TPU v7x, 32 devices: a whole 2x2x4 slice. The times are simulated.
32 devices in a mesh: fsdp: 8 (over z, x), tp: 4 (over y, core).
Axes of the slice: x: 2, y: 2, z: 4, core: 2. Of those that a mesh axis runs over, the one named last changes fastest.
Arguments:
- tokens: bfloat16 [4096, 2048], P('fsdp', 'tp'), may hold values from -6 to 6
- cotangent: bfloat16 [4096, 2048], P('fsdp', 'tp'), may hold values from -6 to 6
- routes: int32 [4096, 8], P('fsdp'), may hold values from 0 to 31, all different within a row; in each aligned block of 256 rows (0 to 255, 256 to 511, ...) at most 128 rows name the same one
- doc_ids: int32 [2, 2048], P(None, 'fsdp'), may hold values from 0 to 3, as said below
- gain_attn: float32 [2048], replicated, may hold values from 0.1 to 1.9
- w_query: bfloat16 [2048, 4096], P('fsdp', 'tp'), may hold values from -0.125 to 0.125
- key_weight: bfloat16 [2048, 512], P('fsdp', 'tp'), may hold values from -0.125 to 0.125
- value_weight: bfloat16 [2048, 512], P('fsdp', 'tp'), may hold values from -0.125 to 0.125
- w_out: bfloat16 [2048, 4096], P('fsdp', 'tp'), may hold values from -1 to 1
- gain_query: float32 [128], replicated, may hold values from 0.1 to 1.9
- key_norm_gain: float32 [128], replicated, may hold values from 0.1 to 1.9
- gain_moe: float32 [2048], replicated, may hold values from 0.1 to 1.9
- router: bfloat16 [2048, 32], replicated, may hold values from -0.0625 to 0.0625
- w_gate: bfloat16 [32, 2048, 768], P(('fsdp', 'tp')), may hold values from -0.125 to 0.125
- w_up: bfloat16 [32, 2048, 768], P(('fsdp', 'tp')), may hold values from -0.125 to 0.125
- w_down: bfloat16 [32, 768, 2048], P(('fsdp', 'tp')), may hold values from -0.875 to 0.875
Outputs:
- block_out: bfloat16 [4096, 2048], P('fsdp', 'tp')
- token_grad: bfloat16 [4096, 2048], P('fsdp', 'tp')
- gain_attn_grad: float32 [2048], replicated
- w_query_grad: float32 [2048, 4096], P('fsdp', 'tp')
- w_key_grad: float32 [2048, 512], P('fsdp', 'tp')
- w_value_grad: float32 [2048, 512], P('fsdp', 'tp')
- w_out_grad: float32 [2048, 4096], P('fsdp', 'tp')
- gain_query_grad: float32 [128], replicated
- gain_key_grad: float32 [128], replicated
- gain_moe_grad: float32 [2048], replicated
- router_grad: float32 [2048, 32], replicated
- w_gate_grad: float32 [32, 2048, 768], P(('fsdp', 'tp'))
- w_up_grad: float32 [32, 2048, 768], P(('fsdp', 'tp'))
- w_down_grad: float32 [32, 768, 2048], P(('fsdp', 'tp'))
Inputs may be any that keep to these rules, and one draw needn't show every extreme that they name: `doc_ids`: row m holds the document numbers of micro-batch m's 2048 positions; they never fall, all 4 numbers occur, and one document begins within the first 256 positions and ends within the last 256. `routes`: A row names 8 different experts. In each aligned block of 256 rows (one fsdp index's tokens of one micro-batch) no expert is named by more than 128 rows, and in some block one expert is named by exactly 128.
All inputs are finite; a program needn't handle non-finite values.
Results may differ from a plain program's by a relative error of at most 0.025.
Values may be sent and summed in bfloat16 or wider, within the bound.
A program may use at most 256 MiB of HBM per device.

v0:
```python
import math

import jax
import jax.numpy as jnp
from jax import lax
from jax.sharding import PartitionSpec as P

TOPK = 8
DOCS = 4


theta_base = 1000000.0
norm_eps = 1e-06
masked_score = -1e30
highest_precision = lax.Precision.HIGHEST


def root_mean_norm(row_block, gain_row):
    return (
        row_block
        * lax.rsqrt(jnp.mean(row_block * row_block, axis=-1, keepdims=True) + norm_eps)
        * gain_row
    )


def rotary_apply(row_block, cosine_lookup, sine_lookup):
    half_width = row_block.shape[-1] // 2
    turned = jnp.concatenate([-row_block[..., half_width:], row_block[..., :half_width]], axis=-1)
    return row_block * cosine_lookup + turned * sine_lookup


def rope_tables(positions, head_width):
    half_width = head_width // 2
    frequency = theta_base ** (
        -2.0 * jnp.arange(half_width, dtype=jnp.int32).astype(jnp.float32) / head_width
    )
    angles = positions.astype(jnp.float32)[:, None] * frequency[None, :]
    cosine_lookup = jnp.cos(angles)
    sine_lookup = jnp.sin(angles)
    return (
        jnp.concatenate([cosine_lookup, cosine_lookup], axis=-1),
        jnp.concatenate([sine_lookup, sine_lookup], axis=-1),
    )


def swiglu(gate_pre, up_pre):
    return jax.nn.silu(gate_pre) * up_pre


def dot_first(left_side, right_side):
    return lax.dot_general(
        left_side, right_side, (((0,), (0,)), ((), ())), preferred_element_type=jnp.float32
    )


def dot_last(left_side, right_side):
    return lax.dot_general(
        left_side, right_side, (((1,), (1,)), ((), ())), preferred_element_type=jnp.float32
    )


def gather_weights(w_query, key_weight, value_weight, w_out):
    return (
        lax.all_gather(w_query, "fsdp", axis=0, tiled=True),
        lax.all_gather(key_weight, "fsdp", axis=0, tiled=True),
        lax.all_gather(value_weight, "fsdp", axis=0, tiled=True),
        lax.all_gather(w_out, "fsdp", axis=0, tiled=True),
    )


def gather_keys(keys_low, values_low):
    return (
        lax.all_gather(keys_low, "fsdp", axis=0, tiled=True),
        lax.all_gather(values_low, "fsdp", axis=0, tiled=True),
    )


def send_rows(buffer):
    return lax.all_to_all(buffer, "fsdp", split_axis=0, concat_axis=0, tiled=True)


def return_rows(buffer):
    return lax.all_to_all(buffer, "fsdp", split_axis=0, concat_axis=0, tiled=True)


def to_heads(per_token, kv_local, group_width):
    token_count, head_total, head_width = per_token.shape
    grouped_heads = per_token.reshape(token_count, kv_local, group_width, head_width)
    return grouped_heads.transpose(1, 2, 0, 3).reshape(
        kv_local, group_width * token_count, head_width
    )


def to_tokens(per_head, group_width):
    kv_local, row_count, head_width = per_head.shape
    token_count = row_count // group_width
    grouped_heads = per_head.reshape(kv_local, group_width, token_count, head_width)
    return grouped_heads.transpose(2, 0, 1, 3).reshape(
        token_count, kv_local * group_width * head_width
    )


def key_block(keys_all, key_start, block_keys, kv_local, head_width):
    return lax.dynamic_slice_in_dim(keys_all, key_start, block_keys, 0).reshape(
        block_keys, kv_local, head_width
    )


def block_scores(queries, keys_part, key_start, query_index, query_start):
    head_width = queries.shape[-1]
    scores = jnp.einsum(
        "hrd,khd->hrk", queries, keys_part, preferred_element_type=jnp.float32
    ) * head_width ** (-0.5)
    key_index = key_start + jnp.arange(keys_part.shape[0])
    allowed = (key_index[None, :] >= query_start[:, None]) & (
        key_index[None, :] <= query_index[:, None]
    )
    return (jnp.where(allowed[None], scores, masked_score), allowed)


def attend_forward(queries, keys_all, values_all, query_index, query_start, block_keys):
    kv_local, row_count, head_width = queries.shape
    lowest_block = jnp.min(query_start) // block_keys
    highest_block = jnp.max(query_index) // block_keys + 1

    def visit_block(block_index, running):
        run_peak, run_total, run_acc = running
        key_start = block_index * block_keys
        keys_part = key_block(keys_all, key_start, block_keys, kv_local, head_width)
        values_part = key_block(values_all, key_start, block_keys, kv_local, head_width)
        scores, allowed = block_scores(queries, keys_part, key_start, query_index, query_start)
        new_peak = jnp.maximum(run_peak, jnp.max(scores, axis=-1))
        weights = jnp.where(allowed[None], jnp.exp(scores - new_peak[..., None]), 0.0)
        factor = jnp.exp(run_peak - new_peak)
        run_total = run_total * factor + jnp.sum(weights, axis=-1)
        run_acc = run_acc * factor[..., None] + jnp.einsum(
            "hrk,khd->hrd",
            weights.astype(jnp.bfloat16),
            values_part,
            preferred_element_type=jnp.float32,
        )
        return (new_peak, run_total, run_acc)

    start_state = (
        jnp.full((kv_local, row_count), masked_score, jnp.float32),
        jnp.zeros((kv_local, row_count), jnp.float32),
        jnp.zeros((kv_local, row_count, head_width), jnp.float32),
    )
    run_peak, run_total, run_acc = lax.fori_loop(
        lowest_block, highest_block, visit_block, start_state
    )
    return (run_acc / run_total[..., None], run_peak + jnp.log(run_total))


def attend_backward(
    queries,
    keys_all,
    values_all,
    query_index,
    query_start,
    block_keys,
    outputs,
    log_total,
    grad_low,
):
    kv_local, row_count, head_width = queries.shape
    key_count = keys_all.shape[0]
    score_scale = head_width ** (-0.5)
    row_delta = jnp.sum(grad_low.astype(jnp.float32) * outputs, axis=-1)
    lowest_block = jnp.min(query_start) // block_keys
    highest_block = jnp.max(query_index) // block_keys + 1

    def visit_block(block_index, running):
        query_acc, key_acc, value_acc = running
        key_start = block_index * block_keys
        keys_part = key_block(keys_all, key_start, block_keys, kv_local, head_width)
        values_part = key_block(values_all, key_start, block_keys, kv_local, head_width)
        scores, allowed = block_scores(queries, keys_part, key_start, query_index, query_start)
        prob_block = jnp.where(allowed[None], jnp.exp(scores - log_total[..., None]), 0.0)
        prob_grad = jnp.einsum(
            "hrd,khd->hrk", grad_low, values_part, preferred_element_type=jnp.float32
        )
        score_grad = (prob_block * (prob_grad - row_delta[..., None])).astype(jnp.bfloat16)
        query_acc = (
            query_acc
            + jnp.einsum("hrk,khd->hrd", score_grad, keys_part, preferred_element_type=jnp.float32)
            * score_scale
        )
        key_part = (
            jnp.einsum("hrk,hrd->khd", score_grad, queries, preferred_element_type=jnp.float32)
            * score_scale
        )
        value_part = jnp.einsum(
            "hrk,hrd->khd",
            prob_block.astype(jnp.bfloat16),
            grad_low,
            preferred_element_type=jnp.float32,
        )
        key_acc = lax.dynamic_update_slice_in_dim(
            key_acc, key_part.reshape(block_keys, kv_local * head_width), key_start, 0
        )
        value_acc = lax.dynamic_update_slice_in_dim(
            value_acc, value_part.reshape(block_keys, kv_local * head_width), key_start, 0
        )
        return (query_acc, key_acc, value_acc)

    start_state = (
        jnp.zeros((kv_local, row_count, head_width), jnp.float32),
        jnp.zeros((key_count, kv_local * head_width), jnp.float32),
        jnp.zeros((key_count, kv_local * head_width), jnp.float32),
    )
    return lax.fori_loop(lowest_block, highest_block, visit_block, start_state)


def body(
    tokens,
    cotangent,
    routes,
    doc_ids,
    gain_attn,
    w_query,
    key_weight,
    value_weight,
    w_out,
    gain_query,
    key_norm_gain,
    gain_moe,
    router,
    w_gate,
    w_up,
    w_down,
):
    shard_count = lax.axis_size("fsdp")
    group_count = lax.axis_size("tp")
    shard_index = lax.axis_index("fsdp")
    group_index = lax.axis_index("tp")
    full_tokens, full_grads = (
        lax.all_gather(tokens, "tp", axis=1, tiled=True),
        lax.all_gather(cotangent, "tp", axis=1, tiled=True),
    )
    slice_width = tokens.shape[1]
    model_width = full_tokens.shape[1]
    micro_count, micro_rows = doc_ids.shape
    head_width = gain_query.shape[0]
    query_local = w_query.shape[1] // head_width
    kv_local = key_weight.shape[1] // head_width
    group_width = query_local // kv_local
    expert_total = router.shape[1]
    capacity = max(2, 2 * micro_rows * TOPK // expert_total)
    slot_total = shard_count * capacity
    pair_total = micro_rows * TOPK
    block_keys = micro_rows * math.gcd(shard_count, max(1, 512 // micro_rows))
    doc_range = jnp.arange(DOCS)
    expert_range = jnp.arange(expert_total)
    local_counts = jnp.sum((doc_ids[:, :, None] == doc_range).astype(jnp.float32), axis=1)
    doc_totals = lax.psum(local_counts, "fsdp")
    doc_begin = (jnp.cumsum(doc_totals, axis=1) - doc_totals).astype(jnp.int32)
    gate_expert = w_gate[0]
    up_expert = w_up[0]
    down_expert = w_down[0]
    router_wide = router.astype(jnp.float32)
    query_acc = jnp.zeros((model_width, query_local * head_width), jnp.float32)
    key_acc = jnp.zeros((model_width, kv_local * head_width), jnp.float32)
    value_acc = jnp.zeros((model_width, kv_local * head_width), jnp.float32)
    out_acc = jnp.zeros((model_width, query_local * head_width), jnp.float32)
    gate_acc = jnp.zeros(gate_expert.shape, jnp.float32)
    up_acc = jnp.zeros(up_expert.shape, jnp.float32)
    down_acc = jnp.zeros(down_expert.shape, jnp.float32)
    router_acc = jnp.zeros(router.shape, jnp.float32)
    gain_attn_acc = jnp.zeros(gain_attn.shape, jnp.float32)
    gain_moe_acc = jnp.zeros(gain_moe.shape, jnp.float32)
    gain_query_acc = jnp.zeros(gain_query.shape, jnp.float32)
    gain_key_acc = jnp.zeros(key_norm_gain.shape, jnp.float32)
    out_parts = []
    grad_parts = []
    for micro_index in range(micro_count):
        row_begin = micro_index * micro_rows
        token_block = full_tokens[row_begin : row_begin + micro_rows].astype(jnp.float32)
        ids_now = doc_ids[micro_index]
        query_index = shard_index * micro_rows + jnp.arange(micro_rows)
        query_start = jnp.sum(
            jnp.where(ids_now[:, None] == doc_range, doc_begin[micro_index][None, :], 0), axis=1
        )
        cosine_lookup, sine_lookup = rope_tables(query_index - query_start, head_width)
        gathered = gather_weights(w_query, key_weight, value_weight, w_out)
        normed, norm_pull = jax.vjp(root_mean_norm, token_block, gain_attn)
        normed_reduced = normed.astype(jnp.bfloat16)
        query_pre = jnp.dot(normed_reduced, gathered[0], preferred_element_type=jnp.float32)
        key_before_norm = jnp.dot(normed_reduced, gathered[1], preferred_element_type=jnp.float32)
        value_reduced = jnp.dot(
            normed_reduced, gathered[2], preferred_element_type=jnp.float32
        ).astype(jnp.bfloat16)

        def shape_heads(query_raw, key_raw, query_gain, key_gain):
            query_heads = rotary_apply(
                root_mean_norm(query_raw.reshape(micro_rows, query_local, head_width), query_gain),
                cosine_lookup[:, None, :],
                sine_lookup[:, None, :],
            )
            key_heads = rotary_apply(
                root_mean_norm(key_raw.reshape(micro_rows, kv_local, head_width), key_gain),
                cosine_lookup[:, None, :],
                sine_lookup[:, None, :],
            )
            return (query_heads, key_heads)

        (query_heads, key_heads), heads_pull = jax.vjp(
            shape_heads, query_pre, key_before_norm, gain_query, key_norm_gain
        )
        queries = to_heads(query_heads.astype(jnp.bfloat16), kv_local, group_width)
        keys_low = key_heads.reshape(micro_rows, kv_local * head_width).astype(jnp.bfloat16)
        keys_all, values_all = gather_keys(keys_low, value_reduced)
        row_index = jnp.tile(query_index, group_width)
        row_start = jnp.tile(query_start, group_width)
        head_out, log_total = attend_forward(
            queries, keys_all, values_all, row_index, row_start, block_keys
        )
        heads_low = to_tokens(head_out, group_width).astype(jnp.bfloat16)
        attn_part = dot_last(heads_low, gathered[3])
        middle = token_block + lax.psum(attn_part.astype(jnp.bfloat16), "tp").astype(jnp.float32)
        moe_normed, moe_pull = jax.vjp(root_mean_norm, middle, gain_moe)
        moe_low = moe_normed.astype(jnp.bfloat16)
        logits = jnp.dot(moe_low, router, preferred_element_type=jnp.float32)
        routes_now = routes[row_begin : row_begin + micro_rows]
        route_match = routes_now[:, :, None] == expert_range
        chosen = jnp.sum(jnp.where(route_match, logits[:, None, :], 0.0), axis=-1)
        gate_weights, softmax_pull = jax.vjp(jax.nn.softmax, chosen)
        mine = routes_now % group_count == group_index
        pair_target = jnp.where(mine, routes_now // group_count, shard_count).reshape(pair_total)
        target_hot = (pair_target[:, None] == jnp.arange(shard_count)).astype(jnp.int32)
        pair_rank = jnp.sum((jnp.cumsum(target_hot, axis=0) - target_hot) * target_hot, axis=1)
        pair_slot = jnp.where(
            pair_target < shard_count, pair_target * capacity + pair_rank, slot_total
        )
        slot_pair = (
            jnp.full((slot_total + 1,), pair_total, jnp.int32)
            .at[pair_slot]
            .set(jnp.arange(pair_total, dtype=jnp.int32))[:slot_total]
        )
        slot_token = slot_pair // TOPK
        slot_grid = pair_slot.reshape(micro_rows, TOPK)
        padded_low = jnp.concatenate([moe_low, jnp.zeros((1, model_width), jnp.bfloat16)], axis=0)
        received = send_rows(
            padded_low[slot_token].reshape(shard_count, capacity, model_width)
        ).reshape(slot_total, model_width)
        gate_pre = jnp.dot(received, gate_expert, preferred_element_type=jnp.float32)
        up_pre = jnp.dot(received, up_expert, preferred_element_type=jnp.float32)
        hidden, swiglu_pull = jax.vjp(swiglu, gate_pre, up_pre)
        hidden_low = hidden.astype(jnp.bfloat16)
        expert_out = jnp.dot(hidden_low, down_expert, preferred_element_type=jnp.float32).astype(
            jnp.bfloat16
        )
        returned = return_rows(expert_out.reshape(shard_count, capacity, model_width)).reshape(
            slot_total, model_width
        )
        padded_out = jnp.concatenate([returned, jnp.zeros((1, model_width), jnp.bfloat16)], axis=0)
        moe_part = jnp.zeros((micro_rows, model_width), jnp.float32)
        for pick_index in range(TOPK):
            moe_part = moe_part + gate_weights[:, pick_index : pick_index + 1] * padded_out[
                slot_grid[:, pick_index]
            ].astype(jnp.float32)
        moe_share = lax.psum_scatter(
            moe_part.astype(jnp.bfloat16), "tp", scatter_dimension=1, tiled=True
        ).astype(jnp.float32)
        middle_slice = lax.dynamic_slice_in_dim(middle, group_index * slice_width, slice_width, 1)
        out_parts.append((middle_slice + moe_share).astype(jnp.bfloat16))
        grad_block = full_grads[row_begin : row_begin + micro_rows].astype(jnp.float32)
        gate_columns = []
        for pick_index in range(TOPK):
            gate_columns.append(
                jnp.sum(
                    grad_block * padded_out[slot_grid[:, pick_index]].astype(jnp.float32), axis=1
                )
            )
        gates_grad = jnp.stack(gate_columns, axis=1)
        flat_gates = jnp.concatenate(
            [gate_weights.reshape(pair_total), jnp.zeros((1,), jnp.float32)]
        )
        padded_grad = jnp.concatenate(
            [grad_block, jnp.zeros((1, model_width), jnp.float32)], axis=0
        )
        send_grad = (padded_grad[slot_token] * flat_gates[slot_pair][:, None]).astype(jnp.bfloat16)
        received_grad = send_rows(send_grad.reshape(shard_count, capacity, model_width)).reshape(
            slot_total, model_width
        )
        hidden_grad = dot_last(received_grad, down_expert)
        down_acc = down_acc + dot_first(hidden_low, received_grad)
        gate_pre_grad, up_pre_grad = swiglu_pull(hidden_grad)
        gate_pre_low = gate_pre_grad.astype(jnp.bfloat16)
        up_pre_low = up_pre_grad.astype(jnp.bfloat16)
        gate_acc = gate_acc + dot_first(received, gate_pre_low)
        up_acc = up_acc + dot_first(received, up_pre_low)
        rows_back = (dot_last(gate_pre_low, gate_expert) + dot_last(up_pre_low, up_expert)).astype(
            jnp.bfloat16
        )
        back_rows = return_rows(rows_back.reshape(shard_count, capacity, model_width)).reshape(
            slot_total, model_width
        )
        padded_back = jnp.concatenate(
            [back_rows, jnp.zeros((1, model_width), jnp.bfloat16)], axis=0
        )
        moe_grad = jnp.zeros((micro_rows, model_width), jnp.float32)
        for pick_index in range(TOPK):
            moe_grad = moe_grad + padded_back[slot_grid[:, pick_index]].astype(jnp.float32)
        (chosen_grad,) = softmax_pull(gates_grad)
        logit_grad = jnp.sum(jnp.where(route_match, chosen_grad[:, :, None], 0.0), axis=1)
        router_acc = router_acc + lax.dot_general(
            moe_low.astype(jnp.float32),
            logit_grad,
            (((0,), (0,)), ((), ())),
            precision=highest_precision,
        )
        moe_grad = moe_grad + lax.dot_general(
            logit_grad, router_wide, (((1,), (1,)), ((), ())), precision=highest_precision
        )
        middle_part, gain_moe_part = moe_pull(moe_grad)
        gain_moe_acc = gain_moe_acc + gain_moe_part
        middle_grad = grad_block + lax.psum(middle_part.astype(jnp.bfloat16), "tp").astype(
            jnp.float32
        )
        middle_low = middle_grad.astype(jnp.bfloat16)
        gathered_back = gather_weights(w_query, key_weight, value_weight, w_out)
        out_acc = out_acc + dot_first(middle_low, heads_low)
        heads_grad = jnp.dot(middle_low, gathered_back[3], preferred_element_type=jnp.float32)
        grad_low = to_heads(
            heads_grad.reshape(micro_rows, query_local, head_width).astype(jnp.bfloat16),
            kv_local,
            group_width,
        )
        query_side, key_side_all, value_side_all = attend_backward(
            queries,
            keys_all,
            values_all,
            row_index,
            row_start,
            block_keys,
            head_out,
            log_total,
            grad_low,
        )
        key_side, value_side = (
            lax.psum_scatter(
                key_side_all.astype(jnp.bfloat16), "fsdp", scatter_dimension=0, tiled=True
            ).astype(jnp.float32),
            lax.psum_scatter(
                value_side_all.astype(jnp.bfloat16), "fsdp", scatter_dimension=0, tiled=True
            ).astype(jnp.float32),
        )
        query_pre_grad, key_pre_grad, gain_query_part, gain_key_part = heads_pull(
            (
                to_tokens(query_side, group_width).reshape(micro_rows, query_local, head_width),
                key_side.reshape(micro_rows, kv_local, head_width),
            )
        )
        gain_query_acc = gain_query_acc + gain_query_part
        gain_key_acc = gain_key_acc + gain_key_part
        query_pre_low = query_pre_grad.astype(jnp.bfloat16)
        key_pre_low = key_pre_grad.astype(jnp.bfloat16)
        value_pre_low = value_side.astype(jnp.bfloat16)
        query_acc = query_acc + dot_first(normed_reduced, query_pre_low)
        key_acc = key_acc + dot_first(normed_reduced, key_pre_low)
        value_acc = value_acc + dot_first(normed_reduced, value_pre_low)
        normed_grad = (
            dot_last(query_pre_low, gathered_back[0])
            + dot_last(key_pre_low, gathered_back[1])
            + dot_last(value_pre_low, gathered_back[2])
        )
        token_part, gain_attn_part = norm_pull(normed_grad)
        gain_attn_acc = gain_attn_acc + gain_attn_part
        token_share = lax.psum_scatter(
            token_part.astype(jnp.bfloat16), "tp", scatter_dimension=1, tiled=True
        ).astype(jnp.float32)
        grad_slice = lax.dynamic_slice_in_dim(
            middle_grad, group_index * slice_width, slice_width, 1
        )
        grad_parts.append((grad_slice + token_share).astype(jnp.bfloat16))
    weight_sums = (
        lax.psum_scatter(
            query_acc.astype(jnp.bfloat16), "fsdp", scatter_dimension=0, tiled=True
        ).astype(jnp.float32),
        lax.psum_scatter(
            key_acc.astype(jnp.bfloat16), "fsdp", scatter_dimension=0, tiled=True
        ).astype(jnp.float32),
        lax.psum_scatter(
            value_acc.astype(jnp.bfloat16), "fsdp", scatter_dimension=0, tiled=True
        ).astype(jnp.float32),
        lax.psum_scatter(
            out_acc.astype(jnp.bfloat16), "fsdp", scatter_dimension=0, tiled=True
        ).astype(jnp.float32),
    )
    small_sums = lax.psum(
        (gain_attn_acc, gain_query_acc, gain_key_acc, gain_moe_acc, router_acc), ("fsdp", "tp")
    )
    return (
        jnp.concatenate(out_parts, axis=0),
        jnp.concatenate(grad_parts, axis=0),
        small_sums[0],
        weight_sums[0],
        weight_sums[1],
        weight_sums[2],
        weight_sums[3],
        small_sums[1],
        small_sums[2],
        small_sums[3],
        small_sums[4],
        gate_acc[None],
        up_acc[None],
        down_acc[None],
    )


def solution(mesh):
    return jax.shard_map(
        body,
        mesh=mesh,
        in_specs=(
            P("fsdp", "tp"),
            P("fsdp", "tp"),
            P("fsdp", None),
            P(None, "fsdp"),
            P(),
            P("fsdp", "tp"),
            P("fsdp", "tp"),
            P("fsdp", "tp"),
            P("fsdp", "tp"),
            P(),
            P(),
            P(),
            P(),
            P(("fsdp", "tp"), None, None),
            P(("fsdp", "tp"), None, None),
            P(("fsdp", "tp"), None, None),
        ),
        out_specs=(
            P("fsdp", "tp"),
            P("fsdp", "tp"),
            P(),
            P("fsdp", "tp"),
            P("fsdp", "tp"),
            P("fsdp", "tp"),
            P("fsdp", "tp"),
            P(),
            P(),
            P(),
            P(),
            P(("fsdp", "tp"), None, None),
            P(("fsdp", "tp"), None, None),
            P(("fsdp", "tp"), None, None),
        ),
        check_vma=False,
    )
```

profile of v0, /device:TPU:0, one launch (start us, length us, event | category | flops | bytes accessed | tf_op | source)
XLA Modules:
  0.0 2330.2 jit_solution(15290187503158480820)
XLA Ops:
  10.7 23.1 psum.70
  48.1 35.1 %all_gather.21 = bf16[2048,128]{1,0:T(8,128)(2,1)} all-gather(bf16[256,128]{1,0:T(8,128)(2,1)} %param.30), channel_id=1, replica_groups=mesh['fsdp'=8,'tp'=4] {'fsdp'}, dimensions={0}, use_global_device_ids=true | all-gather | bytes 589824 | tf_op jit(solution)/shard_map/all_gather | solution.py:65
  83.1 35.2 %all_gather.46 = bf16[2048,128]{1,0:T(8,128)(2,1)} all-gather(bf16[256,128]{1,0:T(8,128)(2,1)} %param.31), channel_id=1, replica_groups=mesh['fsdp'=8,'tp'=4] {'fsdp'}, dimensions={0}, use_global_device_ids=true | all-gather | bytes 589824 | tf_op jit(solution)/shard_map/all_gather | solution.py:66
  142.3 35.3 %all_gather.49 = bf16[2048,128]{0,1:T(8,128)(2,1)} all-gather(bf16[256,128]{0,1:T(8,128)(2,1)} %get-tuple-element.889), channel_id=1, replica_groups=mesh['fsdp'=8,'tp'=4] {'fsdp'}, dimensions={0}, use_global_device_ids=true | all-gather | bytes 589824 | tf_op jit(solution)/shard_map/all_gather | solution.py:73
  181.6 34.7 %all_gather.50 = bf16[2048,128]{1,0:T(8,128)(2,1)} all-gather(bf16[256,128]{1,0:T(8,128)(2,1)S(1)} %convolution_convert_fusion.6), channel_id=1, replica_groups=mesh['fsdp'=8,'tp'=4] {'fsdp'}, dimensions={0}, use_global_device_ids=true | all-gather | bytes 589824 | tf_op jit(solution)/shard_map/all_gather | solution.py:74
  216.3 33.5 %all_gather.44 = bf16[2048,128]{0,1:T(8,128)(2,1)} all-gather(bf16[256,128]{0,1:T(8,128)(2,1)S(1)} %copy-done.104), channel_id=1, replica_groups=mesh['fsdp'=8,'tp'=4] {'fsdp'}, dimensions={0}, use_global_device_ids=true | all-gather | bytes 589824 | tf_op jit(solution)/shard_map/all_gather | solution.py:73
  253.6 33.4 %all_gather.47 = bf16[2048,128]{1,0:T(8,128)(2,1)} all-gather(bf16[256,128]{1,0:T(8,128)(2,1)S(1)} %convolution_convert_fusion.7), channel_id=1, replica_groups=mesh['fsdp'=8,'tp'=4] {'fsdp'}, dimensions={0}, use_global_device_ids=true | all-gather | bytes 589824 | tf_op jit(solution)/shard_map/all_gather | solution.py:74
  355.4 10.6 gather_fusion.18
  366.0 68.9 %all-reduce.27.cloned.1.call-done = (bf16[256,2048]{1,0:T(8,128)(2,1)}, bf16[256,2048]{1,0:T(8,128)(2,1)}) async-done(((bf16[256,2048]{1,0:T(8,128)(2,1)}, bf16[256,2048]{1,0:T(8,128)(2,1)}), (bf16[256,2048]{1,0:T(8,128)(2,1)}, bf16[256,2048]{1,0:T(8,128)(2,1)})) %all-reduce.27.cloned.1.call-update) | async-done | bytes 2097168 | tf_op jit(solution)/shard_map/psum | solution.py:320
  464.2 10.2 gather_fusion
  474.4 80.7 %all-to-all-done.4 = bf16[8,128,2048]{2,1,0:T(8,128)(2,1)} async-done(((bf16[8,128,2048]{2,1,0:T(8,128)(2,1)}), bf16[8,128,2048]{2,1,0:T(8,128)(2,1)}, u32[]{:S(2)}, u32[]{:S(2)}) %all-to-all-start.4) | async-done | bytes 4194336 | tf_op jit(solution)/shard_map/all_to_all | solution.py:79
  580.1 10.6 gather_fusion.28
  605.4 46.8 %all-to-all-done = bf16[8,128,2048]{2,1,0:T(8,128)(2,1)} async-done(((bf16[8,128,2048]{2,1,0:T(8,128)(2,1)}), bf16[8,128,2048]{2,1,0:T(8,128)(2,1)}, u32[]{:S(2)}, u32[]{:S(2)}) %all-to-all-start) | async-done | bytes 4194336 | tf_op jit(solution)/shard_map/all_to_all | solution.py:79
  669.5 80.0 %all-to-all-done.6 = bf16[8,128,2048]{2,1,0:T(8,128)(2,1)} async-done(((bf16[8,128,2048]{2,1,0:T(8,128)(2,1)}), bf16[8,128,2048]{2,1,0:T(8,128)(2,1)}, u32[]{:S(2)}, u32[]{:S(2)}) %all-to-all-start.6) | async-done | bytes 4194336 | tf_op jit(solution)/shard_map/all_to_all | solution.py:79
  780.1 66.6 %all-to-all-done.2 = bf16[8,128,2048]{2,1,0:T(8,128)(2,1)} async-done(((bf16[8,128,2048]{2,1,0:T(8,128)(2,1)}), bf16[8,128,2048]{2,1,0:T(8,128)(2,1)}, u32[]{:S(2)}, u32[]{:S(2)}) %all-to-all-start.2) | async-done | bytes 4194336 | tf_op jit(solution)/shard_map/all_to_all | solution.py:79
  877.6 66.6 %all-to-all-done.1 = bf16[8,128,2048]{2,1,0:T(8,128)(2,1)} async-done(((bf16[8,128,2048]{2,1,0:T(8,128)(2,1)}), bf16[8,128,2048]{2,1,0:T(8,128)(2,1)}, u32[]{:S(2)}, u32[]{:S(2)}) %all-to-all-start.1) | async-done | bytes 4194336 | tf_op jit(solution)/shard_map/all_to_all | solution.py:83
  959.1 82.4 %all-to-all-done.3 = bf16[8,128,2048]{2,1,0:T(8,128)(2,1)} async-done(((bf16[8,128,2048]{2,1,0:T(8,128)(2,1)}), bf16[8,128,2048]{2,1,0:T(8,128)(2,1)}, u32[]{:S(2)}, u32[]{:S(2)}) %all-to-all-start.3) | async-done | bytes 4194336 | tf_op jit(solution)/shard_map/all_to_all | solution.py:83
  1056.1 82.5 %all-to-all-done.5 = bf16[8,128,2048]{2,1,0:T(8,128)(2,1)} async-done(((bf16[8,128,2048]{2,1,0:T(8,128)(2,1)}), bf16[8,128,2048]{2,1,0:T(8,128)(2,1)}, u32[]{:S(2)}, u32[]{:S(2)}) %all-to-all-start.5) | async-done | bytes 4194336 | tf_op jit(solution)/shard_map/all_to_all | solution.py:83
  1390.8 51.6 %all-reduce.25.cloned.1.call-done = (bf16[256,2048]{1,0:T(8,128)(2,1)}, bf16[256,2048]{1,0:T(8,128)(2,1)}) async-done(((bf16[256,2048]{1,0:T(8,128)(2,1)}, bf16[256,2048]{1,0:T(8,128)(2,1)}), (bf16[256,2048]{1,0:T(8,128)(2,1)}, bf16[256,2048]{1,0:T(8,128)(2,1)})) %all-reduce.25.cloned.1.call-update) | async-done | bytes 2097168 | tf_op jit(solution)/shard_map/psum | solution.py:418
  1450.8 13.9 while.63
  1473.5 13.5 while.62
  1516.6 57.4 %reduce-scatter.23.cloned.1.call-done = bf16[256,128]{0,1:T(8,128)(2,1)} async-done(((bf16[2048,128]{0,1:T(8,128)(2,1)}), bf16[256,128]{0,1:T(8,128)(2,1)}) %reduce-scatter.23.cloned.1.call-update) | async-done | bytes 65552 | tf_op jit(solution)/shard_map/reduce_scatter | solution.py:442
  1574.8 64.8 %reduce-scatter.17.cloned.1.call-done = bf16[256,128]{0,1:T(8,128)(2,1)} async-done(((bf16[2048,128]{0,1:T(8,128)(2,1)}), bf16[256,128]{0,1:T(8,128)(2,1)}) %reduce-scatter.17.cloned.1.call-update) | async-done | bytes 65552 | tf_op jit(solution)/shard_map/reduce_scatter | solution.py:442
  1641.7 62.9 %reduce-scatter.19.cloned.1.call-done = bf16[256,128]{1,0:T(8,128)(2,1)} async-done(((bf16[2048,128]{1,0:T(8,128)(2,1)}), bf16[256,128]{1,0:T(8,128)(2,1)}) %reduce-scatter.19.cloned.1.call-update) | async-done | bytes 65552 | tf_op jit(solution)/shard_map/reduce_scatter | solution.py:445
  1707.0 62.0 %reduce-scatter.25.cloned.1.call-done = bf16[256,128]{1,0:T(8,128)(2,1)} async-done(((bf16[2048,128]{1,0:T(8,128)(2,1)}), bf16[256,128]{1,0:T(8,128)(2,1)}) %reduce-scatter.25.cloned.1.call-update) | async-done | bytes 65552 | tf_op jit(solution)/shard_map/reduce_scatter | solution.py:445
  1852.1 40.7 %all-reduce.16 = (f32[2048]{0:T(1024)}, f32[128]{0:T(128)}, f32[128]{0:T(128)}, f32[2048]{0:T(1024)}) all-reduce(f32[2048]{0:T(1024)S(1)} %add.753, f32[128]{0:T(128)S(1)} %add.758, f32[128]{0:T(128)S(1)} %add.759, f32[2048]{0:T(1024)S(1)} %add.760), channel_id=1, replica_groups=mesh['fsdp'=8,'tp'=4] {'fsdp','tp'}, use_global_device_ids=true, to_apply=%region_86.87 | all-reduce | flops 4352 | bytes 34816 | tf_op jit(solution)/shard_map/psum | solution.py:491
  1894.3 58.6 %reduce-scatter.31.cloned.1.call-done = bf16[256,128]{1,0:T(8,128)(2,1)} async-done(((bf16[2048,128]{1,0:T(8,128)(2,1)}), bf16[256,128]{1,0:T(8,128)(2,1)}) %reduce-scatter.31.cloned.1.call-update) | async-done | bytes 65552 | tf_op jit(solution)/shard_map/reduce_scatter | solution.py:481
  1954.4 25.4 %reduce-scatter.21.cloned.1.call-done = bf16[256,512]{1,0:T(8,128)(2,1)} async-done(((bf16[256,2048]{1,0:T(8,128)(2,1)}), bf16[256,512]{1,0:T(8,128)(2,1)}) %reduce-scatter.21.cloned.1.call-update) | async-done | bytes 262160 | tf_op jit(solution)/shard_map/reduce_scatter | solution.py:470
  1981.0 26.8 %reduce-scatter.27.cloned.1.call-done = bf16[256,512]{1,0:T(8,128)(2,1)} async-done(((bf16[256,2048]{1,0:T(8,128)(2,1)}), bf16[256,512]{1,0:T(8,128)(2,1)}) %reduce-scatter.27.cloned.1.call-update) | async-done | bytes 262160 | tf_op jit(solution)/shard_map/reduce_scatter | solution.py:470
  2009.9 89.4 %reduce-scatter.35.cloned.1.call-done = bf16[256,1024]{1,0:T(8,128)(2,1)} async-done(((bf16[2048,1024]{1,0:T(8,128)(2,1)}), bf16[256,1024]{1,0:T(8,128)(2,1)}) %reduce-scatter.35.cloned.1.call-update) | async-done | bytes 524304 | tf_op jit(solution)/shard_map/reduce_scatter | solution.py:487
  2101.4 89.7 %reduce-scatter.29.cloned.1.call-done = bf16[256,1024]{1,0:T(8,128)(2,1)} async-done(((bf16[2048,1024]{1,0:T(8,128)(2,1)}), bf16[256,1024]{1,0:T(8,128)(2,1)}) %reduce-scatter.29.cloned.1.call-update) | async-done | bytes 524304 | tf_op jit(solution)/shard_map/reduce_scatter | solution.py:478
  2193.1 128.7 %all-reduce.23.cloned.1.call-done = f32[2048,32]{0,1:T(8,128)} async-done(((f32[2048,32]{0,1:T(8,128)}), f32[2048,32]{0,1:T(8,128)}) %all-reduce.23.cloned.1.call-update) | async-done | bytes 262160 | tf_op jit(solution)/shard_map/psum | solution.py:491
  (766 shorter events, 725.3 us)
Async XLA Ops:
  7.2 758.5 %copy-start = (bf16[1,768,2048]{2,1,0:T(8,128)(2,1)S(1)}, bf16[1,768,2048]{2,1,0:T(8,128)(2,1)}, u32[]{:S(2)}) copy-start(bf16[1,768,2048]{2,1,0:T(8,128)(2,1)} %param.39) | copy-start | bytes 9437188
  7.2 122.5 %all-gather.5.cloned.1.call-start = ((), (), s32[]{:S(2)}) async-start(), calls=%async_computation.20 | async-start | bytes 2621440 | tf_op jit(solution)/shard_map/all_gather | solution.py:238
  8.0 279.0 %all-gather.7.cloned.1.call-start = ((), (), s32[]{:S(2)}) async-start(), calls=%async_computation.21 | async-start | bytes 4718592 | tf_op jit(solution)/shard_map/all_gather | solution.py:64
  8.7 325.6 %all-gather.9.cloned.1.call-start = ((), (), s32[]{:S(2)}) async-start(), calls=%async_computation.22 | async-start | bytes 4718592 | tf_op jit(solution)/shard_map/all_gather | solution.py:67
  9.4 341.2 %all-gather.11.cloned.1.call-start = ((), (), s32[]{:S(2)}) async-start(), calls=%async_computation.25 | async-start | bytes 2621440 | tf_op jit(solution)/shard_map/all_gather | solution.py:239
  10.0 424.8 %all-reduce.27.cloned.1.call-start = ((), (), s32[]{:S(2)}) async-start(), calls=%async_computation.38 | async-start | bytes 4194304 | tf_op jit(solution)/shard_map/psum | solution.py:320
  456.4 98.7 %all-to-all-start.4 = ((bf16[8,128,2048]{2,1,0:T(8,128)(2,1)}), bf16[8,128,2048]{2,1,0:T(8,128)(2,1)}, u32[]{:S(2)}, u32[]{:S(2)}) async-start(bf16[8,128,2048]{2,1,0:T(8,128)(2,1)} %multiply_convert_fusion.1), calls=%async_computation.6 | async-start | bytes 8388608 | tf_op jit(solution)/shard_map/all_to_all | solution.py:79
  555.1 97.1 %all-to-all-start = ((bf16[8,128,2048]{2,1,0:T(8,128)(2,1)}), bf16[8,128,2048]{2,1,0:T(8,128)(2,1)}, u32[]{:S(2)}, u32[]{:S(2)}) async-start(bf16[8,128,2048]{2,1,0:T(8,128)(2,1)} %bitcast.625), calls=%async_computation | async-start | bytes 8388608 | tf_op jit(solution)/shard_map/all_to_all | solution.py:79
  652.2 97.3 %all-to-all-start.6 = ((bf16[8,128,2048]{2,1,0:T(8,128)(2,1)}), bf16[8,128,2048]{2,1,0:T(8,128)(2,1)}, u32[]{:S(2)}, u32[]{:S(2)}) async-start(bf16[8,128,2048]{2,1,0:T(8,128)(2,1)} %multiply_convert_fusion), calls=%async_computation.11 | async-start | bytes 8388608 | tf_op jit(solution)/shard_map/all_to_all | solution.py:79
  749.5 97.1 %all-to-all-start.2 = ((bf16[8,128,2048]{2,1,0:T(8,128)(2,1)}), bf16[8,128,2048]{2,1,0:T(8,128)(2,1)}, u32[]{:S(2)}, u32[]{:S(2)}) async-start(bf16[8,128,2048]{2,1,0:T(8,128)(2,1)} %bitcast.626), calls=%async_computation.3 | async-start | bytes 8388608 | tf_op jit(solution)/shard_map/all_to_all | solution.py:79
  846.6 97.5 %all-to-all-start.1 = ((bf16[8,128,2048]{2,1,0:T(8,128)(2,1)}), bf16[8,128,2048]{2,1,0:T(8,128)(2,1)}, u32[]{:S(2)}, u32[]{:S(2)}) async-start(bf16[8,128,2048]{2,1,0:T(8,128)(2,1)} %bitcast.628), calls=%async_computation.1 | async-start | bytes 8388608 | tf_op jit(solution)/shard_map/all_to_all | solution.py:83
  944.1 97.4 %all-to-all-start.3 = ((bf16[8,128,2048]{2,1,0:T(8,128)(2,1)}), bf16[8,128,2048]{2,1,0:T(8,128)(2,1)}, u32[]{:S(2)}, u32[]{:S(2)}) async-start(bf16[8,128,2048]{2,1,0:T(8,128)(2,1)} %bitcast.630), calls=%async_computation.4 | async-start | bytes 8388608 | tf_op jit(solution)/shard_map/all_to_all | solution.py:83
  1041.5 97.1 %all-to-all-start.5 = ((bf16[8,128,2048]{2,1,0:T(8,128)(2,1)}), bf16[8,128,2048]{2,1,0:T(8,128)(2,1)}, u32[]{:S(2)}, u32[]{:S(2)}) async-start(bf16[8,128,2048]{2,1,0:T(8,128)(2,1)} %bitcast.629), calls=%async_computation.7 | async-start | bytes 8388608 | tf_op jit(solution)/shard_map/all_to_all | solution.py:83
  1138.6 131.4 %all-to-all-start.7 = ((bf16[8,128,2048]{2,1,0:T(8,128)(2,1)}), bf16[8,128,2048]{2,1,0:T(8,128)(2,1)}, u32[]{:S(2)}, u32[]{:S(2)}) async-start(bf16[8,128,2048]{2,1,0:T(8,128)(2,1)} %bitcast.627), calls=%async_computation.12 | async-start | bytes 8388608 | tf_op jit(solution)/shard_map/all_to_all | solution.py:83
  1143.4 299.0 %all-reduce.25.cloned.1.call-start = ((), (), s32[]{:S(2)}) async-start(), calls=%async_computation.37 | async-start | bytes 4194304 | tf_op jit(solution)/shard_map/psum | solution.py:418
  1390.1 183.8 %reduce-scatter.23.cloned.1.call-start = ((), (), s32[]{:S(2)}) async-start(), calls=%async_computation.29 | async-start | bytes 589824 | tf_op jit(solution)/shard_map/reduce_scatter | solution.py:442
  1470.7 168.9 %reduce-scatter.17.cloned.1.call-start = ((), (), s32[]{:S(2)}) async-start(), calls=%async_computation.26 | async-start | bytes 589824 | tf_op jit(solution)/shard_map/reduce_scatter | solution.py:442
  1487.0 217.6 %reduce-scatter.19.cloned.1.call-start = ((), (), s32[]{:S(2)}) async-start(), calls=%async_computation.27 | async-start | bytes 589824 | tf_op jit(solution)/shard_map/reduce_scatter | solution.py:445
  1487.8 281.3 %reduce-scatter.25.cloned.1.call-start = ((), (), s32[]{:S(2)}) async-start(), calls=%async_computation.30 | async-start | bytes 589824 | tf_op jit(solution)/shard_map/reduce_scatter | solution.py:445
  1488.4 360.4 %reduce-scatter.13.cloned.1.call-start = ((), (), s32[]{:S(2)}) async-start(), calls=%async_computation.23 | async-start | bytes 1310720 | tf_op jit(solution)/shard_map/reduce_scatter | solution.py:362
  1489.1 360.9 %reduce-scatter.15.cloned.1.call-start = ((), (), s32[]{:S(2)}) async-start(), calls=%async_computation.24 | async-start | bytes 1310720 | tf_op jit(solution)/shard_map/reduce_scatter | solution.py:362
  1489.7 403.1 %reduce-scatter.33.cloned.1.call-start = ((), (), s32[]{:S(2)}) async-start(), calls=%async_computation.34 | async-start | bytes 589824 | tf_op jit(solution)/shard_map/reduce_scatter | solution.py:484
  1513.9 190.7 %copy-start.7 = (bf16[512,2048]{1,0:T(8,128)(2,1)S(1)}, bf16[512,2048]{1,0:T(8,128)(2,1)}, u32[]{:S(2)}) copy-start(bf16[512,2048]{1,0:T(8,128)(2,1)} %all-gather.5.cloned.1.call-done) | copy-start | bytes 6291460
  1513.9 190.7 %copy-start.106 = (f32[2048]{0:T(1024)S(1)}, f32[2048]{0:T(1024)}, u32[]{:S(2)}) copy-start(f32[2048]{0:T(1024)} %param.28) | copy-start | bytes 24580
  1574.8 194.2 %copy-start.154 = (f32[256]{0:T(256)S(1)}, f32[256]{0:T(256)}, u32[]{:S(2)}) copy-start(f32[256]{0:T(256)} %copy-done.152) | copy-start | bytes 3076
  1771.7 181.2 %reduce-scatter.31.cloned.1.call-start = ((), (), s32[]{:S(2)}) async-start(), calls=%async_computation.33 | async-start | bytes 589824 | tf_op jit(solution)/shard_map/reduce_scatter | solution.py:481
  1779.3 200.5 %reduce-scatter.21.cloned.1.call-start = ((), (), s32[]{:S(2)}) async-start(), calls=%async_computation.28 | async-start | bytes 1310720 | tf_op jit(solution)/shard_map/reduce_scatter | solution.py:470
  1785.6 222.2 %reduce-scatter.27.cloned.1.call-start = ((), (), s32[]{:S(2)}) async-start(), calls=%async_computation.31 | async-start | bytes 1310720 | tf_op jit(solution)/shard_map/reduce_scatter | solution.py:470
  1786.2 313.0 %reduce-scatter.35.cloned.1.call-start = ((), (), s32[]{:S(2)}) async-start(), calls=%async_computation.35 | async-start | bytes 4718592 | tf_op jit(solution)/shard_map/reduce_scatter | solution.py:487
  1793.0 398.0 %reduce-scatter.29.cloned.1.call-start = ((), (), s32[]{:S(2)}) async-start(), calls=%async_computation.32 | async-start | bytes 4718592 | tf_op jit(solution)/shard_map/reduce_scatter | solution.py:478
  1798.9 523.0 %all-reduce.23.cloned.1.call-start = ((), (), s32[]{:S(2)}) async-start(), calls=%async_computation.36 | async-start | bytes 524288 | tf_op jit(solution)/shard_map/psum | solution.py:491
  2009.0 314.5 %copy-start.1 = (bf16[1,768,2048]{2,1,0:T(8,128)(2,1)S(1)}, bf16[1,768,2048]{2,1,0:T(8,128)(2,1)}, u32[]{:S(2)}) copy-start(bf16[1,768,2048]{2,1,0:T(8,128)(2,1)} %param.39) | copy-start | bytes 9437188
  (183 other events, 2547.5 us)
Sparse Core Ops, SparseCore 0:
  9.6 25.3 all-gather.4
  37.1 86.0 all-gather.6
  125.4 86.5 all-gather.8
  213.4 21.5 all-gather.10
  341.5 93.3 all-reduce.26
  1390.2 52.1 all-reduce.24
  1470.8 103.0 reduce-scatter.22
  1578.2 61.4 reduce-scatter.16
  1643.6 60.9 reduce-scatter.18
  1708.2 60.8 reduce-scatter.24
  1771.6 23.9 reduce-scatter.12
  1798.1 24.8 reduce-scatter.14
  1826.4 61.9 reduce-scatter.32
  1892.0 60.8 reduce-scatter.30
  1955.8 23.9 reduce-scatter.20
  1982.9 24.8 reduce-scatter.26
  2011.3 87.8 reduce-scatter.34
  2103.2 87.8 reduce-scatter.28
  2197.1 124.7 all-reduce.22
where the time goes:
time: 2340 us; the launch traced here: 2330 us
  waiting for transfers between devices  1300 us (56%)
  local copies, waits for them, and re-layouts  358 us (15%)
  blocking collectives  271 us (12%)
  matrix products  222 us (9%)
  other arithmetic  116 us (5%)
  starting transfers between devices  40.2 us (2%)
  between operations  25.1 us (1%)
    all_to_all x4, waiting for transfers between devices, send_rows(): lax.all_to_all(buffer, 'fsdp', split_axis=0, concat_axis=0, tiled=True)  274 us
    all_to_all x4, waiting for transfers between devices, return_rows(): lax.all_to_all(buffer, 'fsdp', split_axis=0, concat_axis=0, tiled=True)  231 us
    psum x1, waiting for transfers between devices, body(): lax.psum((gain_attn_acc, gain_query_acc, gain_key_acc, gain_moe_acc, rout...  129 us
    reduce_scatter x2, waiting for transfers between devices, body(): lax.psum_scatter(value_side_all.astype(jnp.bfloat16), 'fsdp', scatter_dim...  125 us
    reduce_scatter x2, waiting for transfers between devices, body(): lax.psum_scatter(key_side_all.astype(jnp.bfloat16), 'fsdp', scatter_dimen...  122 us
    gather x16, local copies, waits for them, and re-layouts, body(): padded_back[slot_grid[:, pick_index]].astype(jnp.float32)  98.2 us
    gather x16, local copies, waits for them, and re-layouts, body(): padded_out[slot_grid[:, pick_index]].astype(jnp.float32)  97.1 us
    reduce_scatter x1, waiting for transfers between devices, body(): lax.psum_scatter(query_acc.astype(jnp.bfloat16), 'fsdp', scatter_dimensio...  89.7 us
  transfers between devices with their start and end apart: 27, of which 19 were waited for; matrix products, arithmetic and copies ran while one was open for 22% of the time, Pallas kernels for 0%

commit v1 on v0

--- a/solution.py
+++ b/solution.py
@@ -1,8 +1,11 @@
+import functools
 import math
 
 import jax
 import jax.numpy as jnp
 from jax import lax
+from jax.experimental import pallas as pl
+from jax.experimental.pallas import tpu as pltpu
 from jax.sharding import PartitionSpec as P
 
 TOPK = 8
@@ -509,9 +512,1166 @@
     )
 
 
+MESH = pl.DeviceIdType.MESH
+
+
+def place():
+    f = lax.axis_index("fsdp")
+    t = lax.axis_index("tp")
+    return f // 2, f % 2, t // 2, t % 2
+
+
+def device(z, x, y, c):
+    return (z * 2 + x, y * 2 + c)
+
+
+def greet(devices):
+    barrier = pltpu.get_barrier_semaphore()
+    total = 0
+    for valid, where in devices:
+        if valid is None:
+            pl.semaphore_signal(barrier, inc=1, device_id=where, device_id_type=MESH)
+            total = total + 1
+        else:
+            @pl.when(valid)
+            def _():
+                pl.semaphore_signal(barrier, inc=1, device_id=where, device_id_type=MESH)
+            total = total + valid.astype(jnp.int32)
+    pl.semaphore_wait(barrier, total)
+
+
+def remote(src, dst, send, recv, where):
+    return pltpu.make_async_remote_copy(
+        src_ref=src, dst_ref=dst, send_sem=send, recv_sem=recv, device_id=where, device_id_type=MESH
+    )
+
+
+def gather_all_kernel(nz, x_ref, o_ref, lsem, s_p, s_u, s_d, s_x, s_y, s_dx, s_dy,
+                      r_z, r_x, r_y, r_dx, r_dy, r_p):
+    z, x, y, c = place()
+    rows, cols = x_ref.shape
+    half = rows // 2
+    partner = device(z, x, y, 1 - c)
+    xn = device(z, 1 - x, y, c)
+    yn = device(z, x, 1 - y, c)
+    up = device(z + 1, x, y, c)
+    down = device(z - 1, x, y, c)
+    greet([(None, partner), (None, xn), (None, yn), (z < nz - 1, up), (z > 0, down)])
+
+    def block(zz, xx, yy, cc, part=None):
+        start = (zz * 2 + xx) * rows
+        size = rows
+        if part is not None:
+            start = start + part * half
+            size = half
+        return o_ref.at[pl.ds(pl.multiple_of(start, half), size),
+                        pl.ds(pl.multiple_of((yy * 2 + cc) * cols, cols), cols)]
+
+    own = pltpu.make_async_copy(x_ref, block(z, x, y, c), lsem)
+    own.start()
+
+    items = [(0, 0)]
+    for dist in range(1, nz):
+        items += [(dist, -1), (dist, 1)]
+
+    def guard(item, fn):
+        dist, side = item
+        zz = z + side * dist
+        if dist == 0:
+            fn(zz)
+        else:
+            pl.when((zz >= 0) & (zz < nz))(lambda: fn(zz))
+
+    def c_z(zz, src):
+        dst = block(zz, x, y, c)
+        return (remote(src, dst, s_u.at[zz], r_z.at[zz], up),
+                remote(src, dst, s_d.at[zz], r_z.at[zz], down))
+
+    def c_xy(zz, src):
+        dst = block(zz, x, y, c)
+        return (remote(src, dst, s_x.at[zz], r_x.at[zz], xn),
+                remote(src, dst, s_y.at[zz], r_y.at[zz], yn))
+
+    def c_p(zz, rel, src=None):
+        xx = 1 - x if rel in (1, 3, 4) else x
+        yy = 1 - y if rel in (2, 3, 4) else y
+        part = {3: 0, 4: 1}.get(rel)
+        dst = block(zz, xx, yy, c, part)
+        k = zz * 5 + rel
+        return remote(dst if src is None else src, dst, s_p.at[k], r_p.at[k], partner)
+
+    def w_p(zz, rel):
+        xx = 1 - x if rel in (1, 3, 4) else x
+        yy = 1 - y if rel in (2, 3, 4) else y
+        part = {3: 0, 4: 1}.get(rel)
+        dst = block(zz, xx, yy, 1 - c, part)
+        k = zz * 5 + rel
+        return remote(dst, dst, s_p.at[k], r_p.at[k], partner)
+
+    def c_diag(zz):
+        a = block(zz, 1 - x, y, c, 0)
+        b = block(zz, x, 1 - y, c, 1)
+        return (remote(a, a, s_dy.at[zz], r_dy.at[zz], yn),
+                remote(b, b, s_dx.at[zz], r_dx.at[zz], xn))
+
+    def stage_a(item):
+        dist, side = item
+
+        def run(zz):
+            src = x_ref if dist == 0 else block(zz, x, y, c)
+            cu, cd = c_z(zz, src)
+            if dist:
+                cu.wait_recv()
+            if side <= 0:
+                pl.when(z < nz - 1)(cu.start)
+            if dist == 0 or side > 0:
+                pl.when(z > 0)(cd.start)
+            for cc in c_xy(zz, src):
+                cc.start()
+            c_p(zz, 0, src).start()
+
+        guard(item, run)
+
+    def stage_b(item):
+        def run(zz):
+            cx, cy = c_xy(zz, block(zz, x, y, c))
+            dy, dx = c_diag(zz)
+            cx.wait_recv()
+            dy.start()
+            c_p(zz, 1).start()
+            cy.wait_recv()
+            dx.start()
+            c_p(zz, 2).start()
+
+        guard(item, run)
+
+    def stage_c(item):
+        def run(zz):
+            dy, dx = c_diag(zz)
+            dy.wait_recv()
+            c_p(zz, 3).start()
+            dx.wait_recv()
+            c_p(zz, 4).start()
+
+        guard(item, run)
+
+    count = len(items)
+    for k in range(count + 2):
+        if k < count:
+            stage_a(items[k])
+        if 0 <= k - 1 < count:
+            stage_b(items[k - 1])
+        if 0 <= k - 2 < count:
+            stage_c(items[k - 2])
+
+    def finish(zz, carry):
+        for rel in range(5):
+            w_p(zz, rel).wait_recv()
+            c_p(zz, rel).wait_send()
+        cu, cd = c_z(zz, block(zz, x, y, c))
+        pl.when((zz <= z) & (z < nz - 1))(cu.wait_send)
+        pl.when((zz >= z) & (z > 0))(cd.wait_send)
+        for cc in c_xy(zz, block(zz, x, y, c)) + c_diag(zz):
+            cc.wait_send()
+        return carry
+
+    lax.fori_loop(0, nz, finish, 0)
+    own.wait()
+
+
+def gather_all(block, nz, collective_id):
+    rows, cols = block.shape
+    dma = pltpu.SemaphoreType.DMA
+    return pl.pallas_call(
+        functools.partial(gather_all_kernel, nz),
+        out_shape=jax.ShapeDtypeStruct((rows * nz * 2, cols * 4), block.dtype),
+        in_specs=[pl.BlockSpec(memory_space=pl.ANY)],
+        out_specs=pl.BlockSpec(memory_space=pl.ANY),
+        scratch_shapes=[dma] + [dma((5 * nz,))] + [dma((nz,))] * 6 + [dma((nz,))] * 5 + [dma((5 * nz,))],
+        compiler_params=pltpu.CompilerParams(collective_id=collective_id, has_side_effects=True),
+        name="gather_all",
+    )(block)
+
+
+def scatter_all_kernel(nz, p_ref, o_ref, w, lp, rx, rxd, ry, ryd, rz,
+                       s_l, s_p, r_p, s_x, s_y, s_dx, s_dy, s_z, r_x, r_y, r_dx, r_dy, r_z):
+    z, x, y, c = place()
+    rows, cols = o_ref.shape
+    half = rows // 2
+    partner = device(z, x, y, 1 - c)
+    xn = device(z, 1 - x, y, c)
+    yn = device(z, x, 1 - y, c)
+    up = device(z + 1, x, y, c)
+    down = device(z - 1, x, y, c)
+    greet([(None, partner), (None, xn), (None, yn), (z < nz - 1, up), (z > 0, down)])
+    chunk = 64
+
+    def block(zz, rel, cc):
+        xx = 1 - x if rel in (1, 3) else x
+        yy = 1 - y if rel in (2, 3) else y
+        return p_ref.at[pl.ds(pl.multiple_of((zz * 2 + xx) * rows, rows), rows),
+                        pl.ds(pl.multiple_of((yy * 2 + cc) * cols, cols), cols)]
+
+    items = []
+    for dist in range(nz - 1, 0, -1):
+        items += [(dist, -1), (dist, 1)]
+    items += [(0, 0)]
+
+    def guard(item, fn):
+        dist, side = item
+        zz = z + side * dist
+        if dist == 0:
+            fn(zz)
+        else:
+            pl.when((zz >= 0) & (zz < nz))(lambda: fn(zz))
+
+    def c_p(zz, rel):
+        k = zz * 4 + rel
+        return remote(block(zz, rel, 1 - c), lp.at[zz, rel], s_p.at[k], r_p.at[k], partner)
+
+    def c_l(zz, rel):
+        return pltpu.make_async_copy(block(zz, rel, c), w.at[zz, rel], s_l.at[zz * 4 + rel])
+
+    def c_diag(zz):
+        return (remote(w.at[zz, 3, pl.ds(0, half)], rxd.at[zz], s_dx.at[zz], r_dx.at[zz], xn),
+                remote(w.at[zz, 3, pl.ds(half, half)], ryd.at[zz], s_dy.at[zz], r_dy.at[zz], yn))
+
+    def c_xy(zz):
+        return (remote(w.at[zz, 1], rx.at[zz], s_x.at[zz], r_x.at[zz], xn),
+                remote(w.at[zz, 2], ry.at[zz], s_y.at[zz], r_y.at[zz], yn))
+
+    def c_z(zz, slot, where):
+        return remote(w.at[zz, 0], rz.at[slot], s_z.at[zz], r_z.at[slot], where)
+
+    def add(dst, srcs, start, count):
+        def step(i, carry):
+            off = pl.multiple_of(i * chunk, chunk)
+            here = pl.ds(pl.multiple_of(start + off, chunk), chunk)
+            total = dst[here, :].astype(jnp.float32)
+            for src in srcs:
+                total = total + src[pl.ds(off, chunk), :].astype(jnp.float32)
+            dst[here, :] = total.astype(dst.dtype)
+            return carry
+        lax.fori_loop(0, count // chunk, step, 0)
+
+    def stage_0(item):
+        def run(zz):
+            for rel in (3, 1, 2, 0):
+                c_p(zz, rel).start()
+                c_l(zz, rel).start()
+        guard(item, run)
+
+    def stage_d(item):
+        def run(zz):
+            for rel in (3, 1, 2, 0):
+                c_p(zz, rel).wait_recv()
+                c_l(zz, rel).wait()
+                add(w.at[zz, rel], [lp.at[zz, rel]], 0, rows)
+                if rel == 3:
+                    for cc in c_diag(zz):
+                        cc.start()
+        guard(item, run)
+
+    def stage_e(item):
+        def run(zz):
+            dx, dy = c_diag(zz)
+            cx, cy = c_xy(zz)
+            dy.wait_recv()
+            add(w.at[zz, 1], [ryd.at[zz]], half, half)
+            cx.start()
+            dx.wait_recv()
+            add(w.at[zz, 2], [rxd.at[zz]], 0, half)
+            cy.start()
+        guard(item, run)
+
+    def stage_f(item):
+        dist, side = item
+
+        def run(zz):
+            cx, cy = c_xy(zz)
+            cx.wait_recv()
+            cy.wait_recv()
+            if dist:
+                add(w.at[zz, 0], [rx.at[zz], ry.at[zz]], 0, rows)
+                has = z > 0 if side > 0 else z < nz - 1
+                cz = c_z(zz, zz, up if side > 0 else down)
+
+                @pl.when(has)
+                def _():
+                    cz.wait_recv()
+                    add(w.at[zz, 0], [rz.at[zz]], 0, rows)
+                if side > 0:
+                    cz.start()
+                else:
+                    if dist == 1:
+                        c_z(zz, nz, down).start()
+                    else:
+                        cz.start()
+            else:
+                below, above = c_z(zz, zz, up), c_z(zz, nz, down)
+
+                def total(refs):
+                    def step(i, carry):
+                        here = pl.ds(pl.multiple_of(i * chunk, chunk), chunk)
+                        acc = w[zz, 0, here, :].astype(jnp.float32)
+                        for ref in refs:
+                            acc = acc + ref[here, :].astype(jnp.float32)
+                        o_ref[here, :] = acc
+                        return carry
+                    lax.fori_loop(0, rows // chunk, step, 0)
+
+                pl.when(z > 0)(below.wait_recv)
+                pl.when(z < nz - 1)(above.wait_recv)
+                pl.when(z == 0)(lambda: total([rx.at[zz], ry.at[zz], rz.at[nz]]))
+                pl.when(z == nz - 1)(lambda: total([rx.at[zz], ry.at[zz], rz.at[zz]]))
+                pl.when((z > 0) & (z < nz - 1))(
+                    lambda: total([rx.at[zz], ry.at[zz], rz.at[zz], rz.at[nz]]))
+        guard(item, run)
+
+    for item in items:
+        stage_0(item)
+    count = len(items)
+    for k in range(count + 2):
+        if k < count:
+            stage_d(items[k])
+        if 0 <= k - 1 < count:
+            stage_e(items[k - 1])
+        if 0 <= k - 2 < count:
+            stage_f(items[k - 2])
+
+    def finish(zz, carry):
+        for rel in range(4):
+            c_p(zz, rel).wait_send()
+        for cc in c_diag(zz) + c_xy(zz):
+            cc.wait_send()
+        pl.when(zz != z)(c_z(zz, zz, up).wait_send)
+        return carry
+
+    lax.fori_loop(0, nz, finish, 0)
+
+
+def scatter_all(partial, nz, collective_id):
+    rows, cols = partial.shape[0] // (2 * nz), partial.shape[1] // 4
+    half = rows // 2
+    dma = pltpu.SemaphoreType.DMA
+    kind = partial.dtype
+    vm = pltpu.VMEM
+    return pl.pallas_call(
+        functools.partial(scatter_all_kernel, nz),
+        out_shape=jax.ShapeDtypeStruct((rows, cols), jnp.float32),
+        in_specs=[pl.BlockSpec(memory_space=pl.ANY)],
+        out_specs=pl.BlockSpec(memory_space=pltpu.VMEM),
+        scratch_shapes=[vm((nz, 4, rows, cols), kind), vm((nz, 4, rows, cols), kind),
+                        vm((nz, rows, cols), kind), vm((nz, half, cols), kind),
+                        vm((nz, rows, cols), kind), vm((nz, half, cols), kind),
+                        vm((nz + 1, rows, cols), kind)]
+        + [dma((4 * nz,))] * 3 + [dma((nz,))] * 5 + [dma((nz,))] * 4 + [dma((nz + 1,))],
+        compiler_params=pltpu.CompilerParams(collective_id=collective_id, has_side_effects=True,
+                                             vmem_limit_bytes=48 << 20),
+        name="scatter_all",
+    )(partial)
+
+
+def z_items(nz, near_first):
+    items = [(0, 0)] if near_first else []
+    order = range(1, nz) if near_first else range(nz - 1, 0, -1)
+    for dist in order:
+        items += [(dist, -1), (dist, 1)]
+    return items if near_first else items + [(0, 0)]
+
+
+def z_guard(item, z, nz, fn):
+    dist, side = item
+    zz = z + side * dist
+    if dist == 0:
+        fn(zz)
+    else:
+        pl.when((zz >= 0) & (zz < nz))(lambda: fn(zz))
+
+
+def gather_rows_kernel(nz, count, *refs):
+    srcs, outs = refs[:count], refs[count : 2 * count]
+    lsem, s_u, s_d, s_x, r_z, r_x = refs[2 * count :]
+    z, x, y, c = place()
+    xn, up, down = device(z, 1 - x, y, c), device(z + 1, x, y, c), device(z - 1, x, y, c)
+    greet([(None, xn), (z < nz - 1, up), (z > 0, down)])
+
+    def block(n, zz, xx):
+        rows = srcs[n].shape[0]
+        return outs[n].at[pl.ds(pl.multiple_of((zz * 2 + xx) * rows, rows), rows)]
+
+    own = [pltpu.make_async_copy(srcs[n], block(n, z, x), lsem.at[n]) for n in range(count)]
+    for copy in own:
+        copy.start()
+    items = z_items(nz, True)
+
+    def copies(n, zz, src):
+        dst = block(n, zz, x)
+        k = n * nz + zz
+        return (remote(src, dst, s_u.at[k], r_z.at[k], up),
+                remote(src, dst, s_d.at[k], r_z.at[k], down),
+                remote(src, dst, s_x.at[k], r_x.at[k], xn))
+
+    for item in items:
+        dist, side = item
+
+        def run(zz):
+            for n in range(count):
+                src = srcs[n] if dist == 0 else block(n, zz, x)
+                cu, cd, cx = copies(n, zz, src)
+                if dist:
+                    cu.wait_recv()
+                if side <= 0:
+                    pl.when(z < nz - 1)(cu.start)
+                if side > 0 or dist == 0:
+                    pl.when(z > 0)(cd.start)
+                cx.start()
+
+        z_guard(item, z, nz, run)
+
+    def finish(zz, carry):
+        for n in range(count):
+            cu, cd, cx = copies(n, zz, block(n, zz, x))
+            cx.wait_recv()
+            cx.wait_send()
+            pl.when((zz <= z) & (z < nz - 1))(cu.wait_send)
+            pl.when((zz >= z) & (z > 0))(cd.wait_send)
+        return carry
+
+    lax.fori_loop(0, nz, finish, 0)
+    for copy in own:
+        copy.wait()
+
+
+def gather_rows(blocks, nz, collective_id):
+    count = len(blocks)
+    dma = pltpu.SemaphoreType.DMA
+    any_space = pl.BlockSpec(memory_space=pl.ANY)
+    return pl.pallas_call(
+        functools.partial(gather_rows_kernel, nz, count),
+        out_shape=[
+            jax.ShapeDtypeStruct((b.shape[0] * nz * 2,) + b.shape[1:], b.dtype) for b in blocks
+        ],
+        in_specs=[any_space] * count,
+        out_specs=[any_space] * count,
+        scratch_shapes=[dma((count,))] + [dma((count * nz,))] * 5,
+        compiler_params=pltpu.CompilerParams(collective_id=collective_id, has_side_effects=True),
+        name="gather_rows",
+    )(*blocks)
+
+
+def add_blocks(dst, srcs, start, count, out=None, chunk=64):
+    target = dst if out is None else out
+
+    def step(i, carry):
+        off = pl.multiple_of(i * chunk, chunk)
+        here = pl.ds(pl.multiple_of(start + off, chunk), chunk)
+        total = dst[here, :].astype(jnp.float32)
+        for src in srcs:
+            total = total + src[pl.ds(off, chunk), :].astype(jnp.float32)
+        target[here, :] = total.astype(target.dtype)
+        return carry
+
+    lax.fori_loop(0, count // chunk, step, 0)
+
+
+def reduce_rows_kernel(nz, p_ref, o_ref, w, rx, rz, s_l, s_x, s_z, r_x, r_z):
+    z, x, y, c = place()
+    rows = o_ref.shape[0]
+    xn, up, down = device(z, 1 - x, y, c), device(z + 1, x, y, c), device(z - 1, x, y, c)
+    greet([(None, xn), (z < nz - 1, up), (z > 0, down)])
+
+    def block(zz, xx):
+        return p_ref.at[pl.ds(pl.multiple_of((zz * 2 + xx) * rows, rows), rows)]
+
+    def c_x(zz):
+        return remote(block(zz, 1 - x), rx.at[zz], s_x.at[zz], r_x.at[zz], xn)
+
+    def c_l(zz):
+        return pltpu.make_async_copy(block(zz, x), w.at[zz], s_l.at[zz])
+
+    def c_z(zz, slot, where):
+        return remote(w.at[zz], rz.at[slot], s_z.at[zz], r_z.at[slot], where)
+
+    items = z_items(nz, False)
+
+    def start(zz):
+        c_x(zz).start()
+        c_l(zz).start()
+
+    for item in items:
+        z_guard(item, z, nz, start)
+    for item in items:
+        dist, side = item
+
+        def run(zz):
+            c_l(zz).wait()
+            c_x(zz).wait_recv()
+            if dist:
+                add_blocks(w.at[zz], [rx.at[zz]], 0, rows)
+                cz = c_z(zz, zz, up if side > 0 else down)
+
+                @pl.when(z > 0 if side > 0 else z < nz - 1)
+                def _():
+                    cz.wait_recv()
+                    add_blocks(w.at[zz], [rz.at[zz]], 0, rows)
+
+                (c_z(zz, nz, down) if side < 0 and dist == 1 else cz).start()
+            else:
+                pl.when(z > 0)(c_z(zz, zz, up).wait_recv)
+                pl.when(z < nz - 1)(c_z(zz, nz, down).wait_recv)
+                low, high = rz.at[zz], rz.at[nz]
+                pl.when(z == 0)(lambda: add_blocks(w.at[zz], [rx.at[zz], high], 0, rows, o_ref))
+                pl.when(z == nz - 1)(lambda: add_blocks(w.at[zz], [rx.at[zz], low], 0, rows, o_ref))
+                pl.when((z > 0) & (z < nz - 1))(
+                    lambda: add_blocks(w.at[zz], [rx.at[zz], low, high], 0, rows, o_ref)
+                )
+
+        z_guard(item, z, nz, run)
+
+    def finish(zz, carry):
+        c_x(zz).wait_send()
+        pl.when(zz != z)(c_z(zz, zz, up).wait_send)
+        return carry
+
+    lax.fori_loop(0, nz, finish, 0)
+
+
+def reduce_rows(partial, nz, collective_id):
+    rows, cols = partial.shape[0] // (2 * nz), partial.shape[1]
+    dma, vm, kind = pltpu.SemaphoreType.DMA, pltpu.VMEM, partial.dtype
+    return pl.pallas_call(
+        functools.partial(reduce_rows_kernel, nz),
+        out_shape=jax.ShapeDtypeStruct((rows, cols), jnp.float32),
+        in_specs=[pl.BlockSpec(memory_space=pl.ANY)],
+        out_specs=pl.BlockSpec(memory_space=pltpu.VMEM),
+        scratch_shapes=[vm((nz, rows, cols), kind), vm((nz, rows, cols), kind),
+                        vm((nz + 1, rows, cols), kind)]
+        + [dma((nz,))] * 4 + [dma((nz + 1,))],
+        compiler_params=pltpu.CompilerParams(
+            collective_id=collective_id, has_side_effects=True, vmem_limit_bytes=48 << 20
+        ),
+        name="reduce_rows",
+    )(partial)
+
+
+def gather_cols_kernel(x_ref, o_ref, lsem, s_p, s_y, r_p, r_y):
+    z, x, y, c = place()
+    cols = x_ref.shape[1]
+    partner, yn = device(z, x, y, 1 - c), device(z, x, 1 - y, c)
+    greet([(None, partner), (None, yn)])
+
+    def block(yy, cc):
+        return o_ref.at[:, pl.ds(pl.multiple_of((yy * 2 + cc) * cols, cols), cols)]
+
+    own = pltpu.make_async_copy(x_ref, block(y, c), lsem)
+    cy = remote(x_ref, block(y, c), s_y, r_y, yn)
+    cp = remote(x_ref, block(y, c), s_p.at[0], r_p.at[0], partner)
+    cf = remote(block(1 - y, c), block(1 - y, c), s_p.at[1], r_p.at[1], partner)
+    cy.start()
+    cp.start()
+    own.start()
+    cy.wait_recv()
+    cf.start()
+    cp.wait()
+    cf.wait()
+    cy.wait_send()
+    own.wait()
+
+
+def gather_cols(block, collective_id):
+    dma = pltpu.SemaphoreType.DMA
+    any_space = pl.BlockSpec(memory_space=pl.ANY)
+    return pl.pallas_call(
+        gather_cols_kernel,
+        out_shape=jax.ShapeDtypeStruct((block.shape[0], block.shape[1] * 4), block.dtype),
+        in_specs=[any_space],
+        out_specs=any_space,
+        scratch_shapes=[dma, dma((2,)), dma, dma((2,)), dma],
+        compiler_params=pltpu.CompilerParams(collective_id=collective_id, has_side_effects=True),
+        name="gather_cols",
+    )(block)
+
+
+def reduce_cols_kernel(p_ref, o_ref, w, rp, ry, s_l, s_p, s_y, r_p, r_y):
+    z, x, y, c = place()
+    rows, cols = o_ref.shape
+    partner, yn = device(z, x, y, 1 - c), device(z, x, 1 - y, c)
+    greet([(None, partner), (None, yn)])
+
+    def block(yy, cc):
+        return p_ref.at[:, pl.ds(pl.multiple_of((yy * 2 + cc) * cols, cols), cols)]
+
+    sends = [remote(block(yy, 1 - c), rp.at[k], s_p.at[k], r_p.at[k], partner)
+             for k, yy in enumerate((1 - y, y))]
+    loads = [pltpu.make_async_copy(block(yy, c), w.at[k], s_l.at[k])
+             for k, yy in enumerate((1 - y, y))]
+    cy = remote(w.at[0], ry, s_y, r_y, yn)
+    for k in range(2):
+        sends[k].start()
+        loads[k].start()
+    loads[0].wait()
+    sends[0].wait_recv()
+    add_blocks(w.at[0], [rp.at[0]], 0, rows)
+    cy.start()
+    loads[1].wait()
+    sends[1].wait_recv()
+    cy.wait_recv()
+    add_blocks(w.at[1], [rp.at[1], ry], 0, rows, o_ref)
+    for k in range(2):
+        sends[k].wait_send()
+    cy.wait_send()
+
+
+def reduce_cols(partial, collective_id):
+    rows, cols = partial.shape[0], partial.shape[1] // 4
+    dma, vm, kind = pltpu.SemaphoreType.DMA, pltpu.VMEM, partial.dtype
+    return pl.pallas_call(
+        reduce_cols_kernel,
+        out_shape=jax.ShapeDtypeStruct((rows, cols), jnp.float32),
+        in_specs=[pl.BlockSpec(memory_space=pl.ANY)],
+        out_specs=pl.BlockSpec(memory_space=pltpu.VMEM),
+        scratch_shapes=[vm((2, rows, cols), kind), vm((2, rows, cols), kind), vm((rows, cols), kind),
+                        dma((2,)), dma((2,)), dma, dma((2,)), dma],
+        compiler_params=pltpu.CompilerParams(
+            collective_id=collective_id, has_side_effects=True, vmem_limit_bytes=24 << 20
+        ),
+        name="reduce_cols",
+    )(partial)
+
+
+def sum_cols_kernel(v_ref, o_ref, got, s, r):
+    group = lax.axis_index("tp")
+    shard = lax.axis_index("fsdp")
+    peers = [(shard, (group + k) % 4) for k in range(1, 4)]
+    greet([(None, peer) for peer in peers])
+    copies = [remote(v_ref, got.at[k], s.at[k], r.at[k], peer) for k, peer in enumerate(peers)]
+    for copy in copies:
+        copy.start()
+    for copy in copies:
+        copy.wait()
+    o_ref[...] = v_ref[...] + got[0] + got[1] + got[2]
+
+
+def sum_cols(vector, collective_id):
+    dma = pltpu.SemaphoreType.DMA
+    shape = vector.shape
+    return pl.pallas_call(
+        sum_cols_kernel,
+        out_shape=jax.ShapeDtypeStruct(shape, jnp.float32),
+        in_specs=[pl.BlockSpec(memory_space=pltpu.VMEM)],
+        out_specs=pl.BlockSpec(memory_space=pltpu.VMEM),
+        scratch_shapes=[pltpu.VMEM((3,) + shape, jnp.float32), dma((3,)), dma((3,))],
+        compiler_params=pltpu.CompilerParams(collective_id=collective_id, has_side_effects=True),
+        name="sum_cols",
+    )(vector)
+
+
+def greet_all(shard, group, shards, groups):
+    barrier = pltpu.get_barrier_semaphore()
+    total = shards * groups
+
+    def step(k, carry):
+        other = (shard * groups + group + k) % total
+        pl.semaphore_signal(
+            barrier, inc=1, device_id=(other // groups, other % groups), device_id_type=MESH
+        )
+        return carry
+
+    lax.fori_loop(1, total, step, 0)
+    pl.semaphore_wait(barrier, total - 1)
+
+
+def swap_rows_kernel(shards, groups, v_ref, o_ref, s, r):
+    shard, group = lax.axis_index("fsdp"), lax.axis_index("tp")
+    total = shards * groups
+    me = shard * groups + group
+    greet_all(shard, group, shards, groups)
+
+    def copy(k):
+        other = (me + k) % total
+        return remote(v_ref.at[other // groups], o_ref.at[me], s.at[k], r.at[k],
+                      (other // groups, other % groups))
+
+    def start(k, carry):
+        copy(k).start()
+        return carry
+
+    def wait(k, carry):
+        copy(k).wait()
+        return carry
+
+    lax.fori_loop(1, total, start, 0)
+    o_ref[me] = v_ref[shard]
+    lax.fori_loop(1, total, wait, 0)
+
+
+def swap_rows(values, shards, groups, collective_id):
+    dma, total = pltpu.SemaphoreType.DMA, shards * groups
+    return pl.pallas_call(
+        functools.partial(swap_rows_kernel, shards, groups),
+        out_shape=jax.ShapeDtypeStruct((total,) + values.shape[1:], values.dtype),
+        in_specs=[pl.BlockSpec(memory_space=pltpu.VMEM)],
+        out_specs=pl.BlockSpec(memory_space=pltpu.VMEM),
+        scratch_shapes=[dma((total,)), dma((total,))],
+        compiler_params=pltpu.CompilerParams(collective_id=collective_id, has_side_effects=True),
+        name="swap_rows",
+    )(values)
+
+
+def sum_small_kernel(shards, groups, v_ref, o_ref, got, s1, r1, s2, r2):
+    shard, group = lax.axis_index("fsdp"), lax.axis_index("tp")
+    total = shards * groups
+    me = shard * groups + group
+    greet_all(shard, group, shards, groups)
+
+    def first(k):
+        other = (shard + k) % shards
+        return remote(v_ref.at[other], got.at[k], s1.at[k], r1.at[k], (other, group))
+
+    def second(k):
+        other = (me + k) % total
+        return remote(o_ref.at[me], o_ref.at[me], s2.at[k], r2.at[k],
+                      (other // groups, other % groups))
+
+    for k in range(1, shards):
+        first(k).start()
+    acc = v_ref[shard]
+    for k in range(1, shards):
+        first(k).wait()
+        acc = acc + got[k]
+    o_ref[me] = acc
+
+    def start(k, carry):
+        second(k).start()
+        return carry
+
+    def wait(k, carry):
+        second(k).wait()
+        return carry
+
+    lax.fori_loop(1, total, start, 0)
+    lax.fori_loop(1, total, wait, 0)
+
+
+def sum_small(values, shards, groups, collective_id):
+    dma, total = pltpu.SemaphoreType.DMA, shards * groups
+    part = values.shape[1:]
+    return pl.pallas_call(
+        functools.partial(sum_small_kernel, shards, groups),
+        out_shape=jax.ShapeDtypeStruct((total,) + part, values.dtype),
+        in_specs=[pl.BlockSpec(memory_space=pltpu.VMEM)],
+        out_specs=pl.BlockSpec(memory_space=pltpu.VMEM),
+        scratch_shapes=[pltpu.VMEM((shards,) + part, values.dtype), dma((shards,)), dma((shards,)),
+                        dma((total,)), dma((total,))],
+        compiler_params=pltpu.CompilerParams(collective_id=collective_id, has_side_effects=True),
+        name="sum_small",
+    )(values)
+
+
+def dot_plain(left, right):
+    return jnp.dot(left, right, preferred_element_type=jnp.float32)
+
+
+def expert_kernel(slots, block_rows, e_ref, x_ref, g_ref, routes_ref, router_ref, wg, wu, wd,
+                  out_ref, back_ref, gg_ref, gates_ref, dwg, dwu, dwd,
+                  xr, gs, acc_g, acc_u, acc_d, sems):
+    step = pl.program_id(0)
+    rows, width = x_ref.shape
+    blocks = rows // block_rows
+    experts = router_ref.shape[1]
+    chunk = 512
+    f32, low = jnp.float32, jnp.bfloat16
+
+    @pl.when(step == 0)
+    def _():
+        acc_g[...] = jnp.zeros_like(acc_g)
+        acc_u[...] = jnp.zeros_like(acc_u)
+        acc_d[...] = jnp.zeros_like(acc_d)
+
+    lanes = lax.broadcasted_iota(jnp.int32, (rows, experts), 1)
+    routes = routes_ref[...]
+    chosen = routes[:, 0:1] == lanes
+    for j in range(1, TOPK):
+        chosen = chosen | (routes[:, j : j + 1] == lanes)
+    logits = jnp.where(chosen, dot_plain(x_ref[...], router_ref[...]), masked_score)
+    peak = jnp.max(logits, axis=1, keepdims=True)
+    weights = jnp.where(chosen, jnp.exp(logits - peak), 0.0)
+    gates = weights / jnp.sum(weights, axis=1, keepdims=True)
+    gates_ref[...] = gates
+    mine = lanes == e_ref[0]
+    gate_col = jnp.sum(jnp.where(mine, gates, 0.0), axis=1, keepdims=True)
+    match_col = jnp.sum(jnp.where(mine & chosen, 1.0, 0.0), axis=1, keepdims=True)
+    sub = lax.broadcasted_iota(jnp.int32, (block_rows, block_rows), 0)
+    lane = lax.broadcasted_iota(jnp.int32, (block_rows, block_rows), 1)
+    eye = sub == lane
+    before = (sub > lane).astype(low)
+    chosen_low = chosen.astype(f32).astype(low)
+    pick, put, slot_gate = [], [], []
+    slot_lane = lax.broadcasted_iota(jnp.int32, (block_rows, slots), 1).astype(f32)
+    slot_sub = lax.broadcasted_iota(jnp.int32, (slots, block_rows), 0).astype(f32)
+    for b in range(blocks):
+        part = slice(b * block_rows, (b + 1) * block_rows)
+        ranks = dot_plain(before, chosen_low[part])
+        rank = jnp.sum(jnp.where(mine[part], ranks, 0.0), axis=1, keepdims=True)
+        rank = jnp.where(match_col[part] > 0.0, rank, -1.0)
+        rank_row = jnp.sum(jnp.where(eye, rank, 0.0), axis=0, keepdims=True)
+        gate_row = jnp.sum(jnp.where(eye, gate_col[part], 0.0), axis=0, keepdims=True)
+        hot = rank_row == slot_sub
+        pick.append(hot.astype(f32).astype(low))
+        put.append((rank == slot_lane).astype(f32).astype(low))
+        slot_gate.append(jnp.sum(jnp.where(hot, gate_row, 0.0), axis=1, keepdims=True))
+    slot_gate = jnp.concatenate(slot_gate, axis=0)
+
+    def columns(i):
+        return pl.ds(pl.multiple_of(i * chunk, chunk), chunk)
+
+    def gather(ref, cols):
+        return jnp.concatenate(
+            [dot_plain(pick[b], ref[pl.ds(b * block_rows, block_rows), cols]) for b in range(blocks)],
+            axis=0,
+        )
+
+    def scatter(ref, cols, values):
+        for b in range(blocks):
+            ref[pl.ds(b * block_rows, block_rows), cols] = dot_plain(
+                put[b], values[b * slots : (b + 1) * slots]
+            ).astype(low)
+
+    def take(i, carry):
+        cols = columns(i)
+        xr[:, cols] = gather(x_ref, cols).astype(low)
+        return carry
+
+    lax.fori_loop(0, width // chunk, take, 0)
+    gate_pre = dot_plain(xr[...], wg[...])
+    up_pre = dot_plain(xr[...], wu[...])
+    sig = jax.nn.sigmoid(gate_pre)
+    silu = gate_pre * sig
+    hidden_low = (silu * up_pre).astype(low)
+
+    def middle_part(i, carry):
+        total, hidden_grad = carry
+        cols = columns(i)
+        grad = gather(g_ref, cols)
+        expert_out = dot_plain(hidden_low, wd[:, cols]).astype(low).astype(f32)
+        total = total + jnp.sum(grad * expert_out, axis=1, keepdims=True)
+        pair_grad = (grad * slot_gate).astype(low)
+        scatter(out_ref, cols, (expert_out * slot_gate).astype(low))
+        acc_d[:, cols] += dot_first(hidden_low, pair_grad)
+        return total, hidden_grad + dot_last(pair_grad, wd[:, cols])
+
+    gates_grad, hidden_grad = lax.fori_loop(
+        0,
+        width // chunk,
+        middle_part,
+        (jnp.zeros(slot_gate.shape, f32), jnp.zeros(gate_pre.shape, f32)),
+    )
+    for b in range(blocks):
+        part = slice(b * slots, (b + 1) * slots)
+        gg_ref[0, :, pl.ds(b * block_rows, block_rows)] = jnp.sum(
+            pick[b].astype(f32) * gates_grad[part], axis=0, keepdims=True
+        )
+    gate_grad = (hidden_grad * up_pre * (sig * (1.0 + gate_pre * (1.0 - sig)))).astype(low)
+    up_grad = (hidden_grad * silu).astype(low)
+
+    def last_part(i, carry):
+        cols = columns(i)
+        acc_g[cols, :] += dot_first(xr[:, cols], gate_grad)
+        acc_u[cols, :] += dot_first(xr[:, cols], up_grad)
+        row_grad = dot_last(gate_grad, wg[cols, :]) + dot_last(up_grad, wu[cols, :])
+        scatter(back_ref, cols, row_grad.astype(low))
+        return carry
+
+    lax.fori_loop(0, width // chunk, last_part, 0)
+
+    @pl.when(step == pl.num_programs(0) - 1)
+    def _():
+        copies = [
+            pltpu.make_async_copy(src, dst, sems.at[i])
+            for i, (src, dst) in enumerate(((acc_g, dwg), (acc_u, dwu), (acc_d, dwd)))
+        ]
+        for copy in copies:
+            copy.start()
+        for copy in copies:
+            copy.wait()
+
+
+def run_experts(expert, x_all, g_all, routes_all, router, gate_w, up_w, down_w, block_rows, slots):
+    total, width = x_all.shape
+    hidden = gate_w.shape[1]
+    experts = router.shape[1]
+    rows = 2 * block_rows
+    steps = total // rows
+    f32, low = jnp.float32, jnp.bfloat16
+    once = pl.Buffered(1)
+    whole = lambda shape: pl.BlockSpec(shape, lambda i, e: (0, 0), pipeline_mode=once)
+    tile = lambda cols: pl.BlockSpec((rows, cols), lambda i, e: (i, 0))
+    any_space = pl.BlockSpec(memory_space=pl.ANY)
+    return pl.pallas_call(
+        functools.partial(expert_kernel, slots, block_rows),
+        grid_spec=pltpu.PrefetchScalarGridSpec(
+            num_scalar_prefetch=1,
+            grid=(steps,),
+            in_specs=[
+                tile(width), tile(width), tile(routes_all.shape[1]), whole((width, experts)),
+                whole((width, hidden)), whole((width, hidden)), whole((hidden, width)),
+            ],
+            out_specs=[
+                tile(width), tile(width),
+                pl.BlockSpec((1, 1, rows), lambda i, e: (i, 0, 0)),
+                tile(experts), any_space, any_space, any_space,
+            ],
+            scratch_shapes=[
+                pltpu.VMEM((2 * slots, width), low), pltpu.VMEM((2 * slots, width), low),
+                pltpu.VMEM((width, hidden), f32), pltpu.VMEM((width, hidden), f32),
+                pltpu.VMEM((hidden, width), f32), pltpu.SemaphoreType.DMA((3,)),
+            ],
+        ),
+        out_shape=[
+            jax.ShapeDtypeStruct((total, width), low),
+            jax.ShapeDtypeStruct((total, width), low),
+            jax.ShapeDtypeStruct((steps, 1, rows), f32),
+            jax.ShapeDtypeStruct((total, experts), f32),
+            jax.ShapeDtypeStruct((width, hidden), f32),
+            jax.ShapeDtypeStruct((width, hidden), f32),
+            jax.ShapeDtypeStruct((hidden, width), f32),
+        ],
+        compiler_params=pltpu.CompilerParams(
+            dimension_semantics=("arbitrary",), vmem_limit_bytes=60 << 20
+        ),
+        name="experts",
+    )(expert, x_all, g_all, routes_all, router, gate_w, up_w, down_w)
+
+
+def gathered_body(
+    tokens,
+    cotangent,
+    routes,
+    doc_ids,
+    gain_attn,
+    w_query,
+    key_weight,
+    value_weight,
+    w_out,
+    gain_query,
+    key_norm_gain,
+    gain_moe,
+    router,
+    w_gate,
+    w_up,
+    w_down,
+):
+    shard_count = lax.axis_size("fsdp")
+    group_count = lax.axis_size("tp")
+    shard_index = lax.axis_index("fsdp")
+    group_index = lax.axis_index("tp")
+    nz = shard_count // 2
+    f32, low = jnp.float32, jnp.bfloat16
+    row_count, slice_width = tokens.shape
+    model_width = slice_width * group_count
+    micro_count, micro_rows = doc_ids.shape
+    head_width = gain_query.shape[0]
+    query_width, kv_width = w_query.shape[1], key_weight.shape[1]
+    query_local = query_width // head_width
+    kv_local = kv_width // head_width
+    group_width = query_local // kv_local
+    expert_total = router.shape[1]
+    capacity = max(2, 2 * micro_rows * TOPK // expert_total)
+    block_keys = micro_rows * math.gcd(shard_count, max(1, 512 // micro_rows))
+    my_columns = group_index * slice_width
+
+    small = jnp.concatenate([routes, doc_ids.reshape(row_count, 1)], axis=1)
+    small_all = lax.all_gather(small, "fsdp", axis=0, tiled=True)
+    routes_all = small_all[:, :TOPK]
+    ids_all = small_all[:, TOPK].reshape(shard_count, micro_count, micro_rows)
+    doc_range = jnp.arange(DOCS)
+    doc_totals = jnp.sum((ids_all[..., None] == doc_range).astype(jnp.int32), axis=(0, 2))
+    doc_begin = jnp.cumsum(doc_totals, axis=1) - doc_totals
+    query_index = shard_index * micro_rows + jnp.arange(micro_rows)
+    query_start = jnp.sum(
+        jnp.where(doc_ids[:, :, None] == doc_range, doc_begin[:, None, :], 0), axis=2
+    )
+    positions = (query_index[None, :] - query_start).reshape(row_count)
+    cosine_lookup, sine_lookup = rope_tables(positions, head_width)
+
+    full_tokens = gather_cols(tokens, 1).astype(f32)
+    wq_all, wk_all, wv_all, wo_all = gather_rows(
+        [w_query, key_weight, value_weight, w_out], nz, 2
+    )
+    grads_all = gather_all(cotangent, nz, 3)
+    token_mean = jnp.mean(full_tokens * full_tokens, axis=-1, keepdims=True)
+    token_scale = lax.rsqrt(token_mean + norm_eps)
+    normed_low = (full_tokens * token_scale * gain_attn).astype(low)
+    query_pre = jnp.dot(normed_low, wq_all, preferred_element_type=f32)
+    key_pre = jnp.dot(normed_low, wk_all, preferred_element_type=f32)
+    value_low = jnp.dot(normed_low, wv_all, preferred_element_type=f32).astype(low)
+
+    def shape_heads(query_raw, key_raw, query_gain, key_gain):
+        query_heads = rotary_apply(
+            root_mean_norm(query_raw.reshape(row_count, query_local, head_width), query_gain),
+            cosine_lookup[:, None, :],
+            sine_lookup[:, None, :],
+        )
+        key_heads = rotary_apply(
+            root_mean_norm(key_raw.reshape(row_count, kv_local, head_width), key_gain),
+            cosine_lookup[:, None, :],
+            sine_lookup[:, None, :],
+        )
+        return (query_heads, key_heads)
+
+    (query_heads, key_heads), heads_pull = jax.vjp(
+        shape_heads, query_pre, key_pre, gain_query, key_norm_gain
+    )
+    query_low = query_heads.astype(low)
+    key_low = key_heads.reshape(row_count, kv_width).astype(low)
+    keys_got, values_got = gather_rows([key_low, value_low], nz, 4)
+
+    def by_stream(array):
+        return array.reshape(shard_count, micro_count, micro_rows, kv_width).transpose(
+            1, 0, 2, 3
+        ).reshape(micro_count, shard_count * micro_rows, kv_width)
+
+    keys_all, values_all = by_stream(keys_got), by_stream(values_got)
+    row_index = jnp.tile(query_index, group_width)
+    saved, head_parts = [], []
+    for micro_index in range(micro_count):
+        here = slice(micro_index * micro_rows, (micro_index + 1) * micro_rows)
+        queries = to_heads(query_low[here], kv_local, group_width)
+        row_start = jnp.tile(query_start[micro_index], group_width)
+        head_out, log_total = attend_forward(
+            queries, keys_all[micro_index], values_all[micro_index], row_index, row_start, block_keys
+        )
+        saved.append((queries, row_start, head_out, log_total))
+        head_parts.append(to_tokens(head_out, group_width).astype(low))
+    heads_low = jnp.concatenate(head_parts, axis=0)
+    attn_part = dot_last(heads_low, wo_all).astype(low)
+    middle = tokens.astype(f32) + reduce_cols(attn_part, 5)
+
+    def row_mean(values, collective_id):
+        total = jnp.sum(values, axis=1).reshape(row_count // 128, 128)
+        return sum_cols(total, collective_id).reshape(row_count, 1) / model_width
+
+    scale = lax.rsqrt(row_mean(middle * middle, 6) + norm_eps)
+    gain_slice = lax.dynamic_slice_in_dim(gain_moe, my_columns, slice_width)
+    moe_low = (middle * scale * gain_slice).astype(low)
+    moe_all = gather_all(moe_low, nz, 7)
+    expert = (shard_index * group_count + group_index).astype(jnp.int32).reshape(1)
+    out_part, back_part, gates_grad, gates_all, gate_acc, up_acc, down_acc = run_experts(
+        expert, moe_all, grads_all, routes_all, router, w_gate[0], w_up[0], w_down[0],
+        micro_rows, capacity,
+    )
+    back = scatter_all(back_part, nz, 8)
+    gates_grad = swap_rows(
+        gates_grad.reshape(shard_count, row_count // 128, 128), shard_count, group_count, 9
+    ).reshape(expert_total, row_count).T
+    gates = lax.dynamic_slice_in_dim(gates_all, shard_index * row_count, row_count)
+    logit_grad = gates * (gates_grad - jnp.sum(gates * gates_grad, axis=1, keepdims=True))
+    router_slice = lax.dynamic_slice_in_dim(router, my_columns, slice_width).astype(f32)
+    moe_grad = back + lax.dot_general(
+        logit_grad, router_slice, (((1,), (1,)), ((), ())), precision=highest_precision
+    )
+    router_part = lax.dot_general(
+        moe_low.astype(f32), logit_grad, (((0,), (0,)), ((), ())), precision=highest_precision
+    )
+    gain_moe_part = jnp.sum(moe_grad * middle * scale, axis=0)
+    grad_slice = cotangent.astype(f32)
+    inner = gain_slice * moe_grad
+    middle_grad = (
+        grad_slice + scale * inner - middle * scale**3 * row_mean(middle * inner, 10)
+    )
+    middle_low = gather_cols(middle_grad.astype(low), 11)
+    out_grad_part = dot_first(middle_low, heads_low).astype(low)
+    heads_grad = jnp.dot(middle_low, wo_all, preferred_element_type=f32).astype(low)
+    block_out = (middle + scatter_all(out_part, nz, 12)).astype(low)
+    w_out_grad = reduce_rows(out_grad_part, nz, 13)
+    query_sides, key_sides = [], []
+    for micro_index in range(micro_count):
+        here = slice(micro_index * micro_rows, (micro_index + 1) * micro_rows)
+        queries, row_start, head_out, log_total = saved[micro_index]
+        grad_low = to_heads(
+            heads_grad[here].reshape(micro_rows, query_local, head_width), kv_local, group_width
+        )
+        query_side, key_side, value_side = attend_backward(
+            queries,
+            keys_all[micro_index],
+            values_all[micro_index],
+            row_index,
+            row_start,
+            block_keys,
+            head_out,
+            log_total,
+            grad_low,
+        )
+        query_sides.append(to_tokens(query_side, group_width))
+        key_sides.append(jnp.concatenate([key_side, value_side], axis=1).astype(low))
+    sides = jnp.stack(key_sides).reshape(micro_count, shard_count, micro_rows, 2 * kv_width)
+    sides = reduce_rows(
+        sides.transpose(1, 0, 2, 3).reshape(shard_count * row_count, 2 * kv_width), nz, 14
+    )
+    query_pre_grad, key_pre_grad, gain_query_part, gain_key_part = heads_pull(
+        (
+            jnp.concatenate(query_sides, axis=0).reshape(row_count, query_local, head_width),
+            sides[:, :kv_width].reshape(row_count, kv_local, head_width),
+        )
+    )
+    query_pre_low = query_pre_grad.astype(low)
+    key_pre_low = key_pre_grad.astype(low)
+    value_pre_low = sides[:, kv_width:].astype(low)
+    normed_part = (
+        dot_last(query_pre_low, wq_all)
+        + dot_last(key_pre_low, wk_all)
+        + dot_last(value_pre_low, wv_all)
+    ).astype(low)
+    normed_grad = reduce_cols(normed_part, 15)
+    pre_low = jnp.concatenate([query_pre_low, key_pre_low, value_pre_low], axis=1)
+    weight_grad = reduce_rows(dot_first(normed_low, pre_low).astype(low), nz, 16)
+    token_slice = tokens.astype(f32)
+    attn_gain = lax.dynamic_slice_in_dim(gain_attn, my_columns, slice_width)
+    gain_attn_part = jnp.sum(normed_grad * token_slice * token_scale, axis=0)
+    inner = attn_gain * normed_grad
+    token_grad = (
+        middle_grad
+        + token_scale * inner
+        - token_slice * token_scale**3 * row_mean(token_slice * inner, 17)
+    ).astype(low)
+
+    pieces = [router_part.reshape(-1), gain_attn_part, gain_moe_part, gain_query_part, gain_key_part]
+    length = sum(piece.shape[0] for piece in pieces)
+    part_rows = -(-length // (shard_count * 1024)) * 8
+    flat = jnp.concatenate(
+        pieces + [jnp.zeros((shard_count * part_rows * 128 - length,), f32)]
+    ).reshape(shard_count, part_rows, 128)
+    summed = sum_small(flat, shard_count, group_count, 18).reshape(
+        shard_count, group_count, part_rows * 128
+    ).transpose(1, 0, 2).reshape(group_count, shard_count * part_rows * 128)
+    at = 0
+    sums = []
+    for piece in pieces:
+        sums.append(summed[:, at : at + piece.shape[0]])
+        at += piece.shape[0]
+    return (
+        block_out,
+        token_grad,
+        sums[1].reshape(-1),
+        weight_grad[:, :query_width],
+        weight_grad[:, query_width : query_width + kv_width],
+        weight_grad[:, query_width + kv_width :],
+        w_out_grad,
+        jnp.sum(sums[3], axis=0),
+        jnp.sum(sums[4], axis=0),
+        sums[2].reshape(-1),
+        sums[0].reshape(router.shape),
+        gate_acc[None],
+        up_acc[None],
+        down_acc[None],
+    )
+
+
 def solution(mesh):
+    small = mesh.shape["fsdp"] * mesh.shape["tp"] <= 32 and mesh.shape["tp"] == 4
     return jax.shard_map(
-        body,
+        gathered_body if small else body,
         mesh=mesh,
         in_specs=(
             P("fsdp", "tp"),

time: 2340 us -> 1120 us (0.48)
  waiting for transfers between devices: 1300 us -> 0 us
  Pallas kernels: 0 us -> 914 us
  local copies, waits for them, and re-layouts: 358 us -> 38.4 us
  blocking collectives: 271 us -> 45 us
  matrix products: 222 us -> 57.6 us
  other arithmetic: 116 us -> 42.3 us
  starting transfers between devices: 40.2 us -> 0 us
    pallas_call x0 -> x19, Pallas kernels: none -> 914 us  [the longest x3 195 us: reduce_rows(): pl.pallas_call(functools.partial(reduce_rows_kernel, nz), out_shape=jax.S...]
    reduce_scatter x12 -> x0, waiting for transfers between devices: 537 us -> none  [the longest x2 125 us: body(): lax.psum_scatter(value_side_all.astype(jnp.bfloat16), 'fsdp', scatter_dim...]
    all_to_all x8 -> x0, waiting for transfers between devices: 506 us -> none  [the longest x4 274 us: send_rows(): lax.all_to_all(buffer, 'fsdp', split_axis=0, concat_axis=0, tiled=True)]
    psum x3 -> x0, waiting for transfers between devices: 249 us -> none  [the longest x1 129 us: body(): lax.psum((gain_attn_acc, gain_query_acc, gain_key_acc, gain_moe_acc, rout...]
    gather x38 -> x0, local copies, waits for them, and re-layouts: 249 us -> none  [the longest x16 98.2 us: body(): padded_back[slot_grid[:, pick_index]].astype(jnp.float32)]
    all_gather x6 -> x1, blocking collectives: 207 us -> 45 us  [gathered_body(): small_all = lax.all_gather(small, 'fsdp', axis=0, tiled=True)]
    psum x2 -> x0, blocking collectives: 63.7 us -> none  [the longest x1 40.7 us: body(): lax.psum((gain_attn_acc, gain_query_acc, gain_key_acc, gain_moe_acc, rout...]
    dot_general x20 -> x6, matrix products: 69.4 us -> 14.8 us  [the longest x1 4.73 us: gathered_body(): query_pre = jnp.dot(normed_low, wq_all, preferred_element_type=f32)]
  transfers between devices with their start and end apart: 27 -> 0, of which waited for: 19 -> 0; matrix products, arithmetic and copies ran while one was open for 22% -> 0% of each run, Pallas kernels for 0% -> 0%
where the time goes in v1:
time: 1120 us; the launch traced here: 1110 us
  Pallas kernels  914 us (82%)
  matrix products  57.6 us (5%)
  blocking collectives  45 us (4%)
  other arithmetic  42.3 us (4%)
  local copies, waits for them, and re-layouts  38.4 us (3%)
    pallas_call x3, Pallas kernels, reduce_rows(): pl.pallas_call(functools.partial(reduce_rows_kernel, nz), out_shape=jax.S...  195 us
    pallas_call x2, Pallas kernels, gather_all(): pl.pallas_call(functools.partial(gather_all_kernel, nz), out_shape=jax.Sh...  185 us
    pallas_call x2, Pallas kernels, scatter_all(): pl.pallas_call(functools.partial(scatter_all_kernel, nz), out_shape=jax.S...  156 us
    pallas_call x1, Pallas kernels, run_experts(): pl.pallas_call(functools.partial(expert_kernel, slots, block_rows), grid_...  134 us
    pallas_call x2, Pallas kernels, gather_rows(): pl.pallas_call(functools.partial(gather_rows_kernel, nz, count), out_shap...  128 us
    all_gather x1, blocking collectives, gathered_body(): small_all = lax.all_gather(small, 'fsdp', axis=0, tiled=True)  45 us
    pallas_call x2, Pallas kernels, gather_cols(): pl.pallas_call(gather_cols_kernel, out_shape=jax.ShapeDtypeStruct((block....  38.4 us
    pallas_call x2, Pallas kernels, reduce_cols(): pl.pallas_call(reduce_cols_kernel, out_shape=jax.ShapeDtypeStruct((rows,...  31.1 us

profile of v1, /device:TPU:0, one launch (start us, length us, event | category | flops | bytes accessed | tf_op | source)
XLA Modules:
  0.0 1108.0 jit_solution(5936405149478199178)
XLA Ops:
  0.7 20.1 %gather_cols.2 = bf16[512,2048]{1,0:T(8,128)(2,1)} custom-call(bf16[512,512]{1,0:T(8,128)(2,1)} %x_ref.2), custom_call_target="tpu_custom_call" | custom-call | tf_op jit(solution)/shard_map/gather_cols/pallas_call | solution.py:1085
  23.4 105.4 %gather_rows.2 = (bf16[2048,1024]{1,0:T(8,128)(2,1)}, bf16[2048,128]{1,0:T(8,128)(2,1)}, bf16[2048,128]{1,0:T(8,128)(2,1)}, bf16[2048,1024]{1,0:T(8,128)(2,1)}) custom-call(bf16[256,1024]{1,0:T(8,128)(2,1)} %refs_0_.1, bf16[256,128]{1,0:T(8,128)(2,1)} %refs_1_.1, bf16[256,128]{1,0:T(8,128)(2,1)} %refs_2_.1, bf16[256,1024]{1,0:T(8,128)(2,1)} %refs_3_.1), custom_call_target="tpu_custom_call" | custom-call | tf_op jit(solution)/shard_map/gather_rows/pallas_call | solution.py:950
  128.9 2.6 multiply_reduce_fusion.8
  132.2 45.0 %all_gather.3 = s32[4096,9]{1,0:T(8,128)S(1)} all-gather(s32[512,9]{1,0:T(8,128)S(1)} %copy.150), channel_id=1, replica_groups=mesh['fsdp'=8,'tp'=4] {'fsdp'}, dimensions={0}, use_global_device_ids=true | all-gather | bytes 165888 | tf_op jit(solution)/shard_map/all_gather | solution.py:1485
  182.4 4.7 convolution_bitcast_fusion.2
  198.9 3.0 convolution_convert_fusion.4.refs_1_
  202.0 22.8 %gather_rows.3 = (bf16[4096,128]{1,0:T(8,128)(2,1)}, bf16[4096,128]{1,0:T(8,128)(2,1)}) custom-call(bf16[512,128]{1,0:T(8,128)(2,1)} %get-tuple-element.646.refs_0_, bf16[512,128]{1,0:T(8,128)(2,1)} %convolution_convert_fusion.4.refs_1_), custom_call_target="tpu_custom_call" | custom-call | tf_op jit(solution)/shard_map/gather_rows/pallas_call | solution.py:950
  228.2 5.6 while.60
  241.7 4.5 while.61
  249.7 4.9 convolution_convert_fusion.2.p_ref
  254.7 16.5 %reduce_cols.2 = f32[512,512]{1,0:T(8,128)S(1)} custom-call(bf16[512,2048]{1,0:T(8,128)(2,1)S(1)} %convolution_convert_fusion.2.p_ref), custom_call_target="tpu_custom_call" | custom-call | tf_op jit(solution)/shard_map/reduce_cols/pallas_call | solution.py:1129
  272.1 4.9 sum_cols.3
  279.4 100.6 %gather_all.2.x_ref = bf16[4096,2048]{1,0:T(8,128)(2,1)} custom-call(bf16[512,512]{1,0:T(8,128)(2,1)} %multiply_convert_fusion.x_ref), custom_call_target="tpu_custom_call" | custom-call | tf_op jit(solution)/shard_map/gather_all/pallas_call | solution.py:685
  380.0 84.4 %gather_all.3.g_ref = bf16[4096,2048]{1,0:T(8,128)(2,1)} custom-call(bf16[512,512]{1,0:T(8,128)(2,1)} %x_ref.3), custom_call_target="tpu_custom_call" | custom-call | tf_op jit(solution)/shard_map/gather_all/pallas_call | solution.py:685
  465.4 133.7 %experts.1 = (bf16[4096,2048]{1,0:T(8,128)(2,1)}, bf16[4096,2048]{1,0:T(8,128)(2,1)}, f32[8,1,512]{2,1,0:T(1,128)}, f32[4096,32]{1,0:T(8,128)}, f32[2048,768]{1,...) custom-call(s32[1]{0:T(128)} %bitcast.29.e_ref, bf16[4096,2048]{1,0:T(8,128)(2,1)} %gather_all.2.x_ref, ...), custom_call_target="tpu_custom_call" | custom-call | tf_op jit(solution)/shard_map/experts/pallas_call | solution.py:1411
  599.1 9.6 swap_rows.1
  611.9 77.5 %scatter_all.3 = f32[512,512]{1,0:T(8,128)S(1)} custom-call(bf16[4096,2048]{1,0:T(8,128)(2,1)} %get-tuple-element.288.p_ref), custom_call_target="tpu_custom_call" | custom-call | tf_op jit(solution)/shard_map/scatter_all/pallas_call | solution.py:859
  690.9 4.9 sum_cols.4
  696.4 78.3 %scatter_all.2 = f32[512,512]{1,0:T(8,128)S(1)} custom-call(bf16[4096,2048]{1,0:T(8,128)(2,1)} %get-tuple-element.287.p_ref), custom_call_target="tpu_custom_call" | custom-call | tf_op jit(solution)/shard_map/scatter_all/pallas_call | solution.py:859
  776.4 18.4 %gather_cols.3 = bf16[512,2048]{1,0:T(8,128)(2,1)} custom-call(bf16[512,512]{1,0:T(8,128)(2,1)} %get-tuple-element.610.x_ref), custom_call_target="tpu_custom_call" | custom-call | tf_op jit(solution)/shard_map/gather_cols/pallas_call | solution.py:1085
  794.8 4.4 convolution_convert_fusion.1.p_ref
  799.2 55.9 %reduce_rows.5 = f32[256,1024]{1,0:T(8,128)S(1)} custom-call(bf16[2048,1024]{1,0:T(8,128)(2,1)S(1)} %convolution_convert_fusion.1.p_ref), custom_call_target="tpu_custom_call" | custom-call | tf_op jit(solution)/shard_map/reduce_rows/pallas_call | solution.py:1043
  861.3 9.2 while.62
  875.7 8.8 while.63
  886.5 85.2 %reduce_rows.3 = f32[512,256]{1,0:T(8,128)S(1)} custom-call(bf16[4096,256]{1,0:T(8,128)(2,1)S(1)} %bitcast.413), custom_call_target="tpu_custom_call" | custom-call | tf_op jit(solution)/shard_map/reduce_rows/pallas_call | solution.py:1043
  976.4 4.2 multiply_reduce_fusion
  980.9 3.9 fusion.105
  985.1 5.8 convolution_convert_fusion.p_ref
  990.9 54.3 %reduce_rows.4 = f32[256,1280]{1,0:T(8,128)S(1)} custom-call(bf16[2048,1280]{1,0:T(8,128)(2,1)} %convolution_convert_fusion.p_ref), custom_call_target="tpu_custom_call" | custom-call | tf_op jit(solution)/shard_map/reduce_rows/pallas_call | solution.py:1043
  1053.4 14.6 %reduce_cols.3 = f32[512,512]{1,0:T(8,128)S(1)} custom-call(bf16[512,2048]{1,0:T(8,128)(2,1)S(1)} %add_convert_fusion.p_ref), custom_call_target="tpu_custom_call" | custom-call | tf_op jit(solution)/shard_map/reduce_cols/pallas_call | solution.py:1129
  1070.5 21.3 %sum_small.1 = f32[32,24,128]{2,1,0:T(8,128)} custom-call(f32[8,24,128]{2,1,0:T(8,128)} %bitcast.474), custom_call_target="tpu_custom_call" | custom-call | tf_op jit(solution)/shard_map/sum_small/pallas_call | solution.py:1260
  1098.3 5.4 sum_cols.5
  (275 shorter events, 104.6 us)
Async XLA Ops:
  0.6 128.2 %copy-start.57 = (f32[2048]{0:T(1024)S(1)}, f32[2048]{0:T(1024)}, u32[]{:S(2)}) copy-start(f32[2048]{0:T(1024)} %param.28) | copy-start | bytes 24580
  20.7 110.9 %copy-start.54 = (f32[128]{0:T(128)S(1)}, f32[128]{0:T(128)}, u32[]{:S(2)}) copy-start(f32[128]{0:T(128)} %param.34) | copy-start | bytes 1540
  22.8 109.2 %copy-start.53 = (s32[2,256]{1,0:T(2,128)S(1)}, s32[2,256]{1,0:T(2,128)}, u32[]{:S(2)}) copy-start(s32[2,256]{1,0:T(2,128)} %param.27) | copy-start | bytes 6148
  22.8 109.2 %copy-start.47 = (s32[512,8]{0,1:T(8,128)S(1)}, s32[512,8]{0,1:T(8,128)}, u32[]{:S(2)}) copy-start(s32[512,8]{0,1:T(8,128)} %param.26) | copy-start | bytes 49156
  23.4 175.5 %copy-start.44 = (f32[512]{0:T(512)}, f32[512]{0:T(512)S(1)}, u32[]{:S(2)}) copy-start(f32[512]{0:T(512)S(1)} %get-tuple-element.653) | copy-start | bytes 6148
  131.5 50.8 %copy-start.42 = (f32[512]{0:T(512)}, f32[512]{0:T(512)S(1)}, u32[]{:S(2)}) copy-start(f32[512]{0:T(512)S(1)} %fusion.134) | copy-start | bytes 6148
  131.7 50.7 %copy-start.16 = (f32[512,128]{1,0:T(8,128)}, f32[512,128]{1,0:T(8,128)S(1)}, u32[]{:S(2)}) copy-start(f32[512,128]{1,0:T(8,128)S(1)} %copy.152) | copy-start | bytes 786436
  131.8 50.5 %copy-start.10 = (bf16[512,2048]{1,0:T(8,128)(2,1)S(1)}, bf16[512,2048]{1,0:T(8,128)(2,1)}, u32[]{:S(2)}) copy-start(bf16[512,2048]{1,0:T(8,128)(2,1)} %gather_cols.2) | copy-start | bytes 6291460
  182.3 7.7 copy-start.22
  182.3 7.7 copy-start.24
  190.1 8.9 copy-start.36
  246.2 8.5 copy-start.5
  246.2 8.5 copy-start.7
  246.2 8.5 copy-start.19
  246.2 8.5 copy-start.20
  249.7 21.5 %copy-start.12 = (bf16[512,512]{1,0:T(8,128)(2,1)S(1)}, bf16[512,512]{1,0:T(8,128)(2,1)}, u32[]{:S(2)}) copy-start(bf16[512,512]{1,0:T(8,128)(2,1)} %x_ref.2) | copy-start | bytes 1572868
  380.0 84.4 %copy-start.39 = (bf16[2048,32]{0,1:T(8,128)(2,1)S(1)}, bf16[2048,32]{0,1:T(8,128)(2,1)}, u32[]{:S(2)}) copy-start(bf16[2048,32]{0,1:T(8,128)(2,1)} %param.36) | copy-start | bytes 393220
  696.4 78.3 %copy-start.46 = (f32[4,128]{1,0:T(4,128)S(1)}, f32[4,128]{1,0:T(4,128)}, u32[]{:S(2)}) copy-start(f32[4,128]{1,0:T(4,128)} %sum_cols.3) | copy-start | bytes 6148
  696.4 78.3 %copy-start.31 = (bf16[512,512]{1,0:T(8,128)(2,1)S(1)}, bf16[512,512]{1,0:T(8,128)(2,1)}, u32[]{:S(2)}) copy-start(bf16[512,512]{1,0:T(8,128)(2,1)} %x_ref.3) | copy-start | bytes 1572868
  794.8 60.3 %copy-start.59 = (bf16[2048,1024]{1,0:T(8,128)(2,1)S(1)}, bf16[2048,1024]{1,0:T(8,128)(2,1)}, u32[]{:S(2)}) copy-start(bf16[2048,1024]{1,0:T(8,128)(2,1)} %get-tuple-element.286) | copy-start | bytes 12582916
  799.2 55.9 %copy-start.30 = (bf16[512,2048]{1,0:T(8,128)(2,1)S(1)}, bf16[512,2048]{1,0:T(8,128)(2,1)}, u32[]{:S(2)}) copy-start(bf16[512,2048]{1,0:T(8,128)(2,1)} %gather_cols.3) | copy-start | bytes 6291460
  884.5 87.2 %copy-start.27 = (f32[512,64]{1,0:T(8,128)S(1)}, f32[512,64]{1,0:T(8,128)}, u32[]{:S(2)}) copy-start(f32[512,64]{1,0:T(8,128)} %copy-done.26) | copy-start | bytes 393220
  884.5 87.5 %copy-start.17 = (f32[512,128]{1,0:T(8,128)S(1)}, f32[512,128]{1,0:T(8,128)}, u32[]{:S(2)}) copy-start(f32[512,128]{1,0:T(8,128)} %copy-done.16) | copy-start | bytes 786436
  884.5 87.5 %copy-start.29 = (f32[512,64]{1,0:T(8,128)S(1)}, f32[512,64]{1,0:T(8,128)}, u32[]{:S(2)}) copy-start(f32[512,64]{1,0:T(8,128)} %copy-done.28) | copy-start | bytes 393220
  884.5 87.5 %copy-start.43 = (f32[512]{0:T(512)S(1)}, f32[512]{0:T(512)}, u32[]{:S(2)}) copy-start(f32[512]{0:T(512)} %copy-done.42) | copy-start | bytes 6148
  884.5 87.5 %copy-start.55 = (f32[128]{0:T(128)S(1)}, f32[128]{0:T(128)}, u32[]{:S(2)}) copy-start(f32[128]{0:T(128)} %param.34) | copy-start | bytes 1540
  884.6 87.9 %copy-start.52 = (f32[512]{0:T(512)S(1)}, f32[512]{0:T(512)}, u32[]{:S(2)}) copy-start(f32[512]{0:T(512)} %copy-done.51) | copy-start | bytes 6148
  886.5 86.9 %copy-start.3 = (f32[1,2048,128]{2,1,0:T(8,128)S(1)}, f32[1,2048,128]{2,1,0:T(8,128)}, u32[]{:S(2)}) copy-start(f32[1,2048,128]{2,1,0:T(8,128)} %copy-done.2) | copy-start | bytes 3145732
  990.9 56.1 %copy-start.18 = (bf16[512,512]{1,0:T(8,128)(2,1)S(1)}, bf16[512,512]{1,0:T(8,128)(2,1)}, u32[]{:S(2)}) copy-start(bf16[512,512]{1,0:T(8,128)(2,1)} %multiply_convert_fusion.x_ref) | copy-start | bytes 1572868
  1052.6 16.2 %copy-start.13 = (bf16[512,512]{1,0:T(8,128)(2,1)S(1)}, bf16[512,512]{1,0:T(8,128)(2,1)}, u32[]{:S(2)}) copy-start(bf16[512,512]{1,0:T(8,128)(2,1)} %x_ref.2) | copy-start | bytes 1572868
  1053.3 16.5 %copy-start.56 = (f32[128]{0:T(128)S(1)}, f32[128]{0:T(128)}, u32[]{:S(2)}) copy-start(f32[128]{0:T(128)} %get-tuple-element.502) | copy-start | bytes 1540
  1053.3 51.1 %copy-start.50 = (f32[512]{0:T(512)S(1)}, f32[512]{0:T(512)}, u32[]{:S(2)}) copy-start(f32[512]{0:T(512)} %get-tuple-element.652) | copy-start | bytes 6148
  (28 other events, 68.6 us)

commit v2 on v1

--- a/solution.py
+++ b/solution.py
@@ -889,21 +889,46 @@
         pl.when((zz >= 0) & (zz < nz))(lambda: fn(zz))
 
 
-def gather_rows_kernel(nz, count, *refs):
-    srcs, outs = refs[:count], refs[count : 2 * count]
-    lsem, s_u, s_d, s_x, r_z, r_x = refs[2 * count :]
+def gather_rows_kernel(nz, count, columns, *refs):
+    total = count + columns
+    srcs, refs = refs[:total], refs[total:]
+    outs, refs = refs[:total], refs[total:]
+    wide, refs = refs[: min(columns, 1)], refs[min(columns, 1) :]
+    lsem, s_u, s_d, s_x, r_z, r_x, s_c, r_c, s_w, r_w = refs
     z, x, y, c = place()
     xn, up, down = device(z, 1 - x, y, c), device(z + 1, x, y, c), device(z - 1, x, y, c)
-    greet([(None, xn), (z < nz - 1, up), (z > 0, down)])
+    partner, yn = device(z, x, y, 1 - c), device(z, x, 1 - y, c)
+    wanted = [(None, xn), (z < nz - 1, up), (z > 0, down)]
+    greet(wanted + [(None, partner), (None, yn), (None, device(nz - 1 - z, 1 - x, y, c))] * min(columns, 1))
 
     def block(n, zz, xx):
         rows = srcs[n].shape[0]
         return outs[n].at[pl.ds(pl.multiple_of((zz * 2 + xx) * rows, rows), rows)]
 
-    own = [pltpu.make_async_copy(srcs[n], block(n, z, x), lsem.at[n]) for n in range(count)]
-    for copy in own:
+    own = [(srcs[n], block(n, z, x)) for n in range(count)]
+    column_copies, swaps = [], []
+    if columns:
+        mirror = device(nz - 1 - z, 1 - x, y, c)
+        first, out = outs[count], wide[0]
+        rows, cols = first.shape
+        top, bottom = pl.ds(0, rows // 2), pl.ds(rows // 2, rows // 2)
+        for n in range(columns):
+            src, dst = srcs[count + n], outs[count + n]
+            swaps.append(remote(src.at[bottom], dst.at[bottom], s_w.at[n], r_w.at[n], mirror))
+            own.append((src.at[top], dst.at[top]))
+
+        def column(yy):
+            return out.at[:, pl.ds(pl.multiple_of((yy * 2 + c) * cols, cols), cols)]
+
+        column_copies = [
+            remote(first, column(y), s_c.at[0], r_c.at[0], yn),
+            remote(first, column(y), s_c.at[1], r_c.at[1], partner),
+            remote(column(1 - y), column(1 - y), s_c.at[2], r_c.at[2], partner),
+        ]
+        last = pltpu.make_async_copy(first, column(y), lsem.at[total])
+    own = [pltpu.make_async_copy(src, dst, lsem.at[n]) for n, (src, dst) in enumerate(own)]
+    for copy in swaps + own:
         copy.start()
-    items = z_items(nz, True)
 
     def copies(n, zz, src):
         dst = block(n, zz, x)
@@ -912,7 +937,7 @@
                 remote(src, dst, s_d.at[k], r_z.at[k], down),
                 remote(src, dst, s_x.at[k], r_x.at[k], xn))
 
-    for item in items:
+    for item in z_items(nz, True):
         dist, side = item
 
         def run(zz):
@@ -928,6 +953,15 @@
                 cx.start()
 
         z_guard(item, z, nz, run)
+        if columns and dist == 0:
+            own[count].wait()
+            swaps[0].wait_recv()
+            column_copies[0].start()
+            column_copies[1].start()
+            last.start()
+        if columns and item == (1, 1):
+            column_copies[0].wait_recv()
+            column_copies[2].start()
 
     def finish(zz, carry):
         for n in range(count):
@@ -939,24 +973,69 @@
         return carry
 
     lax.fori_loop(0, nz, finish, 0)
-    for copy in own:
+    for n, copy in enumerate(own):
+        if n != count:
+            copy.wait()
+    if columns:
+        column_copies[0].wait_send()
+        column_copies[1].wait()
+        column_copies[2].wait()
+        last.wait()
+        swaps[0].wait_send()
+        for copy in swaps[1:]:
+            copy.wait()
+
+
+def gather_rows(blocks, nz, collective_id, swapped=()):
+    count, columns = len(blocks), len(swapped)
+    dma = pltpu.SemaphoreType.DMA
+    any_space = pl.BlockSpec(memory_space=pl.ANY)
+    shapes = [
+        jax.ShapeDtypeStruct((b.shape[0] * nz * 2,) + b.shape[1:], b.dtype) for b in blocks
+    ] + [jax.ShapeDtypeStruct(b.shape, b.dtype) for b in swapped]
+    if columns:
+        rows, cols = swapped[0].shape
+        shapes.append(jax.ShapeDtypeStruct((rows, cols * 4), swapped[0].dtype))
+    total = count + columns
+    return pl.pallas_call(
+        functools.partial(gather_rows_kernel, nz, count, columns),
+        out_shape=shapes,
+        in_specs=[any_space] * total,
+        out_specs=[any_space] * len(shapes),
+        scratch_shapes=[dma((total + 1,))] + [dma((count * nz,))] * 5 + [dma((3,))] * 2
+        + [dma((max(columns, 1),))] * 2,
+        compiler_params=pltpu.CompilerParams(collective_id=collective_id, has_side_effects=True),
+        name="gather_rows",
+    )(*blocks, *swapped)
+
+
+def swap_back_kernel(nz, *refs):
+    count = (len(refs) - 2) // 2
+    srcs, outs = refs[:count], refs[count : 2 * count]
+    s, r = refs[2 * count :]
+    z, x, y, c = place()
+    mirror = device(nz - 1 - z, 1 - x, y, c)
+    greet([(None, mirror)])
+    copies = [remote(src, out, s.at[n], r.at[n], mirror)
+              for n, (src, out) in enumerate(zip(srcs, outs))]
+    for copy in copies:
+        copy.start()
+    for copy in copies:
         copy.wait()
 
 
-def gather_rows(blocks, nz, collective_id):
+def swap_back(blocks, nz, collective_id):
     count = len(blocks)
     dma = pltpu.SemaphoreType.DMA
     any_space = pl.BlockSpec(memory_space=pl.ANY)
     return pl.pallas_call(
-        functools.partial(gather_rows_kernel, nz, count),
-        out_shape=[
-            jax.ShapeDtypeStruct((b.shape[0] * nz * 2,) + b.shape[1:], b.dtype) for b in blocks
-        ],
+        functools.partial(swap_back_kernel, nz),
+        out_shape=[jax.ShapeDtypeStruct(b.shape, b.dtype) for b in blocks],
         in_specs=[any_space] * count,
         out_specs=[any_space] * count,
-        scratch_shapes=[dma((count,))] + [dma((count * nz,))] * 5,
+        scratch_shapes=[dma((count,))] * 2,
         compiler_params=pltpu.CompilerParams(collective_id=collective_id, has_side_effects=True),
-        name="gather_rows",
+        name="swap_back",
     )(*blocks)
 
 
@@ -1273,175 +1352,348 @@
     return jnp.dot(left, right, preferred_element_type=jnp.float32)
 
 
-def expert_kernel(slots, block_rows, e_ref, x_ref, g_ref, routes_ref, router_ref, wg, wu, wd,
-                  out_ref, back_ref, gg_ref, gates_ref, dwg, dwu, dwd,
-                  xr, gs, acc_g, acc_u, acc_d, sems):
-    step = pl.program_id(0)
-    rows, width = x_ref.shape
+def far_first(nz, z, k):
+    at = 0
+    for here in range(nz):
+        order = sorted(range(nz), key=lambda other: (-abs(other - here), other))
+        for step, other in enumerate(order):
+            at = at + jnp.where((z == here) & (k == step), other, 0)
+    return at
+
+
+def expert_kernel(nz, slots, block_rows, x_all, g_all, routes_all, router_ref, wg, wu, wd,
+                  out_all, back_ref, gg_ref, gates_ref, xr_all, gs_all, hid_all, gp_all, up_all,
+                  x_ref, g_ref, t_ref, o_ref, xr, gs, hid, gp, up, st,
+                  w, lp, rx, rxd, ry, ryd, rz,
+                  s_in, s_out, s_save, s_p, r_p, s_x, s_y, s_dx, s_dy, s_z, r_x, r_y, r_dx, r_dy, r_z):
+    z, x, y, c = place()
+    expert = lax.axis_index("fsdp") * 4 + lax.axis_index("tp")
+    rows, cols = back_ref.shape
+    width = x_ref.shape[1]
+    half = rows // 2
     blocks = rows // block_rows
     experts = router_ref.shape[1]
-    chunk = 512
     f32, low = jnp.float32, jnp.bfloat16
-
-    @pl.when(step == 0)
-    def _():
-        acc_g[...] = jnp.zeros_like(acc_g)
-        acc_u[...] = jnp.zeros_like(acc_u)
-        acc_d[...] = jnp.zeros_like(acc_d)
-
-    lanes = lax.broadcasted_iota(jnp.int32, (rows, experts), 1)
-    routes = routes_ref[...]
-    chosen = routes[:, 0:1] == lanes
-    for j in range(1, TOPK):
-        chosen = chosen | (routes[:, j : j + 1] == lanes)
-    logits = jnp.where(chosen, dot_plain(x_ref[...], router_ref[...]), masked_score)
-    peak = jnp.max(logits, axis=1, keepdims=True)
-    weights = jnp.where(chosen, jnp.exp(logits - peak), 0.0)
-    gates = weights / jnp.sum(weights, axis=1, keepdims=True)
-    gates_ref[...] = gates
-    mine = lanes == e_ref[0]
-    gate_col = jnp.sum(jnp.where(mine, gates, 0.0), axis=1, keepdims=True)
-    match_col = jnp.sum(jnp.where(mine & chosen, 1.0, 0.0), axis=1, keepdims=True)
-    sub = lax.broadcasted_iota(jnp.int32, (block_rows, block_rows), 0)
-    lane = lax.broadcasted_iota(jnp.int32, (block_rows, block_rows), 1)
-    eye = sub == lane
-    before = (sub > lane).astype(low)
-    chosen_low = chosen.astype(f32).astype(low)
-    pick, put, slot_gate = [], [], []
-    slot_lane = lax.broadcasted_iota(jnp.int32, (block_rows, slots), 1).astype(f32)
-    slot_sub = lax.broadcasted_iota(jnp.int32, (slots, block_rows), 0).astype(f32)
-    for b in range(blocks):
-        part = slice(b * block_rows, (b + 1) * block_rows)
-        ranks = dot_plain(before, chosen_low[part])
-        rank = jnp.sum(jnp.where(mine[part], ranks, 0.0), axis=1, keepdims=True)
-        rank = jnp.where(match_col[part] > 0.0, rank, -1.0)
-        rank_row = jnp.sum(jnp.where(eye, rank, 0.0), axis=0, keepdims=True)
-        gate_row = jnp.sum(jnp.where(eye, gate_col[part], 0.0), axis=0, keepdims=True)
-        hot = rank_row == slot_sub
-        pick.append(hot.astype(f32).astype(low))
-        put.append((rank == slot_lane).astype(f32).astype(low))
-        slot_gate.append(jnp.sum(jnp.where(hot, gate_row, 0.0), axis=1, keepdims=True))
-    slot_gate = jnp.concatenate(slot_gate, axis=0)
-
-    def columns(i):
-        return pl.ds(pl.multiple_of(i * chunk, chunk), chunk)
-
-    def gather(ref, cols):
-        return jnp.concatenate(
-            [dot_plain(pick[b], ref[pl.ds(b * block_rows, block_rows), cols]) for b in range(blocks)],
-            axis=0,
-        )
-
-    def scatter(ref, cols, values):
+    partner = device(z, x, y, 1 - c)
+    xn, yn = device(z, 1 - x, y, c), device(z, x, 1 - y, c)
+    up_dev, down_dev = device(z + 1, x, y, c), device(z - 1, x, y, c)
+    greet([(None, partner), (None, xn), (None, yn), (z < nz - 1, up_dev), (z > 0, down_dev)])
+    tiles = 2 * nz
+
+    def tile_of(j):
+        return far_first(nz, z, j // 2) * 2 + jnp.where(j % 2 == 0, 1 - x, x)
+
+    def tile_rows(j):
+        return pl.ds(pl.multiple_of(tile_of(j) * rows, rows), rows)
+
+    def load(j, kind):
+        src, dst = ((x_all, x_ref), (g_all, g_ref), (routes_all, t_ref))[kind]
+        return pltpu.make_async_copy(src.at[tile_rows(j)], dst, s_in.at[kind])
+
+    def save_out(j):
+        return pltpu.make_async_copy(o_ref, out_all.at[tile_rows(j)], s_out)
+
+    def saves(j):
+        pairs = ((xr, xr_all), (gs, gs_all), (hid, hid_all), (gp, gp_all), (up, up_all))
+        return [pltpu.make_async_copy(src, dst.at[j], s_save.at[n])
+                for n, (src, dst) in enumerate(pairs)]
+
+    def c_p(zz, rel, slot):
+        k = zz * 4 + rel
+        return remote(st.at[slot, rel // 2], lp.at[zz, rel], s_p.at[k], r_p.at[k], partner)
+
+    def c_diag(zz):
+        return (remote(w.at[zz, 3, pl.ds(0, half)], rxd.at[zz], s_dx.at[zz], r_dx.at[zz], xn),
+                remote(w.at[zz, 3, pl.ds(half, half)], ryd.at[zz], s_dy.at[zz], r_dy.at[zz], yn))
+
+    def c_xy(zz):
+        return (remote(w.at[zz, 1], rx.at[zz], s_x.at[zz], r_x.at[zz], xn),
+                remote(w.at[zz, 2], ry.at[zz], s_y.at[zz], r_y.at[zz], yn))
+
+    def c_z(zz, slot, where):
+        return remote(w.at[zz, 0], rz.at[slot], s_z.at[zz], r_z.at[slot], where)
+
+    def send_z(zz):
+        pl.when(zz > z)(lambda: c_z(zz, zz, up_dev).start())
+        pl.when(zz == z - 1)(lambda: c_z(zz, nz, down_dev).start())
+        pl.when(zz < z - 1)(lambda: c_z(zz, zz, down_dev).start())
+
+    def stage_d(zz, rel, slot):
+        c_p(zz, rel, slot).wait_recv()
+        add_blocks(w.at[zz, rel], [lp.at[zz, rel]], 0, rows)
+        if rel == 3:
+            for copy in c_diag(zz):
+                copy.start()
+
+    def stage_e(zz):
+        dx, dy = c_diag(zz)
+        cx, cy = c_xy(zz)
+        dy.wait_recv()
+        add_blocks(w.at[zz, 1], [ryd.at[zz]], half, half)
+        cx.start()
+        dx.wait_recv()
+        add_blocks(w.at[zz, 2], [rxd.at[zz]], 0, half)
+        cy.start()
+
+    def passes(zz):
+        return ((zz > z) & (z > 0)) | ((zz < z) & (z < nz - 1))
+
+    def stage_f1(zz):
+        cx, cy = c_xy(zz)
+        cx.wait_recv()
+        cy.wait_recv()
+        add_blocks(w.at[zz, 0], [rx.at[zz], ry.at[zz]], 0, rows)
+        pl.when((zz != z) & jnp.logical_not(passes(zz)))(lambda: send_z(zz))
+
+    def stage_f2(zz):
+        @pl.when((zz != z) & passes(zz))
+        def _():
+            c_z(zz, zz, up_dev).wait_recv()
+            add_blocks(w.at[zz, 0], [rz.at[zz]], 0, rows)
+            send_z(zz)
+
+        @pl.when(zz == z)
+        def _():
+            low_part, high_part = rz.at[zz], rz.at[nz]
+            pl.when(z > 0)(lambda: c_z(zz, zz, up_dev).wait_recv())
+            pl.when(z < nz - 1)(lambda: c_z(zz, nz, down_dev).wait_recv())
+            own = w.at[zz, 0]
+            pl.when(z == 0)(lambda: add_blocks(own, [high_part], 0, rows, back_ref))
+            pl.when(z == nz - 1)(lambda: add_blocks(own, [low_part], 0, rows, back_ref))
+            pl.when((z > 0) & (z < nz - 1))(
+                lambda: add_blocks(own, [low_part, high_part], 0, rows, back_ref)
+            )
+
+    def compute(j):
+        zz = far_first(nz, z, j // 2)
+        slot = j % 2
+        load(j, 2).wait()
+        load(j, 0).wait()
+        lanes = lax.broadcasted_iota(jnp.int32, (rows, experts), 1)
+        routes = t_ref[...]
+        chosen = routes[:, 0:1] == lanes
+        for n in range(1, TOPK):
+            chosen = chosen | (routes[:, n : n + 1] == lanes)
+        logits = jnp.where(chosen, dot_plain(x_ref[...], router_ref[...]), masked_score)
+        peak = jnp.max(logits, axis=1, keepdims=True)
+        weights = jnp.where(chosen, jnp.exp(logits - peak), 0.0)
+        gates = weights / jnp.sum(weights, axis=1, keepdims=True)
+        gates_ref[...] = gates
+        mine = lanes == expert
+        gate_col = jnp.sum(jnp.where(mine, gates, 0.0), axis=1, keepdims=True)
+        match_col = jnp.sum(jnp.where(mine & chosen, 1.0, 0.0), axis=1, keepdims=True)
+        sub = lax.broadcasted_iota(jnp.int32, (block_rows, block_rows), 0)
+        lane = lax.broadcasted_iota(jnp.int32, (block_rows, block_rows), 1)
+        eye = sub == lane
+        before = (sub > lane).astype(f32).astype(low)
+        chosen_low = chosen.astype(f32).astype(low)
+        pick, put, slot_gate = [], [], []
+        slot_lane = lax.broadcasted_iota(jnp.int32, (block_rows, slots), 1).astype(f32)
+        slot_sub = lax.broadcasted_iota(jnp.int32, (slots, block_rows), 0).astype(f32)
         for b in range(blocks):
-            ref[pl.ds(b * block_rows, block_rows), cols] = dot_plain(
-                put[b], values[b * slots : (b + 1) * slots]
-            ).astype(low)
-
-    def take(i, carry):
-        cols = columns(i)
-        xr[:, cols] = gather(x_ref, cols).astype(low)
+            part = slice(b * block_rows, (b + 1) * block_rows)
+            ranks = dot_plain(before, chosen_low[part])
+            rank = jnp.sum(jnp.where(mine[part], ranks, 0.0), axis=1, keepdims=True)
+            rank = jnp.where(match_col[part] > 0.0, rank, -1.0)
+            rank_row = jnp.sum(jnp.where(eye, rank, 0.0), axis=0, keepdims=True)
+            gate_row = jnp.sum(jnp.where(eye, gate_col[part], 0.0), axis=0, keepdims=True)
+            hot = rank_row == slot_sub
+            pick.append(hot.astype(f32).astype(low))
+            put.append((rank == slot_lane).astype(f32).astype(low))
+            slot_gate.append(jnp.sum(jnp.where(hot, gate_row, 0.0), axis=1, keepdims=True))
+        slot_gate = jnp.concatenate(slot_gate, axis=0)
+
+        def gather(ref, at):
+            return jnp.concatenate(
+                [dot_plain(pick[b], ref[pl.ds(b * block_rows, block_rows), at])
+                 for b in range(blocks)],
+                axis=0,
+            )
+
+        def scatter(ref, at, values):
+            for b in range(blocks):
+                ref[pl.ds(b * block_rows, block_rows), at] = dot_plain(
+                    put[b], values[b * slots : (b + 1) * slots]
+                ).astype(low)
+
+        def columns(i):
+            return pl.ds(pl.multiple_of(i * cols, cols), cols)
+
+        @pl.when(j > 0)
+        def _():
+            for copy in saves(j):
+                copy.wait()
+
+        def take(i, carry):
+            xr[:, columns(i)] = gather(x_ref, columns(i)).astype(low)
+            return carry
+
+        lax.fori_loop(0, width // cols, take, 0)
+
+        @pl.when(j < tiles - 1)
+        def _():
+            load(j + 1, 2).start()
+            load(j + 1, 0).start()
+
+        gate_pre = dot_plain(xr[...], wg[...])
+        up_pre = dot_plain(xr[...], wu[...])
+        sig = jax.nn.sigmoid(gate_pre)
+        silu = gate_pre * sig
+        hidden_low = (silu * up_pre).astype(low)
+        hid[...] = hidden_low
+        load(j, 1).wait()
+        pl.when(j > 0)(lambda: save_out(j).wait())
+
+        def middle_part(i, carry):
+            total, hidden_grad = carry
+            at = columns(i)
+            grad = gather(g_ref, at)
+            expert_out = dot_plain(hidden_low, wd[:, at]).astype(low).astype(f32)
+            total = total + jnp.sum(grad * expert_out, axis=1, keepdims=True)
+            pair_grad = (grad * slot_gate).astype(low)
+            gs[:, at] = pair_grad
+            scatter(o_ref, at, (expert_out * slot_gate).astype(low))
+            return total, hidden_grad + dot_last(pair_grad, wd[:, at])
+
+        gates_grad, hidden_grad = lax.fori_loop(
+            0,
+            width // cols,
+            middle_part,
+            (jnp.zeros(slot_gate.shape, f32), jnp.zeros(gate_pre.shape, f32)),
+        )
+        save_out(j).start()
+        pl.when(j < tiles - 1)(lambda: load(j + 1, 1).start())
+        for b in range(blocks):
+            gg_ref[tile_of(j), :, pl.ds(b * block_rows, block_rows)] = jnp.sum(
+                pick[b].astype(f32) * gates_grad[b * slots : (b + 1) * slots],
+                axis=0,
+                keepdims=True,
+            )
+        gate_grad = (hidden_grad * up_pre * (sig * (1.0 + gate_pre * (1.0 - sig)))).astype(low)
+        up_grad = (hidden_grad * silu).astype(low)
+        gp[...] = gate_grad
+        up[...] = up_grad
+        for copy in saves(j):
+            copy.start()
+
+        def part_of(i, yy, cc):
+            at = columns(yy * 2 + cc)
+            row_grad = dot_last(gate_grad, wg[at, :]) + dot_last(up_grad, wu[at, :])
+            return row_grad.astype(low)
+
+        first = jnp.where(slot == 0, 1, 0)
+
+        def to_partner(i, carry):
+            yy = jnp.where(i == 1, 1 - y, y)
+            rel = first + 2 * i
+
+            @pl.when(j >= 2)
+            def _():
+                before_zz = far_first(nz, z, j // 2 - 1)
+                k = before_zz * 4 + rel
+                remote(st.at[slot, i], lp.at[before_zz, rel], s_p.at[k], r_p.at[k], partner).wait_send()
+
+            scatter(st.at[slot, i], slice(None), part_of(i, yy, 1 - c))
+            k = zz * 4 + rel
+            remote(st.at[slot, i], lp.at[zz, rel], s_p.at[k], r_p.at[k], partner).start()
+            return carry
+
+        def to_own(i, carry):
+            yy = jnp.where(i == 1, 1 - y, y)
+            scatter(w.at[zz, first + 2 * i], slice(None), part_of(i, yy, c))
+            return carry
+
+        lax.fori_loop(0, 2, to_partner, 0)
+        lax.fori_loop(0, 2, to_own, 0)
+
+    for kind in (2, 0, 1):
+        load(0, kind).start()
+
+    def step(j, carry):
+        k, odd = j // 2, j % 2 == 1
+        pl.when(j < tiles)(lambda: compute(j))
+
+        @pl.when(odd & (k < nz))
+        def _():
+            zz = far_first(nz, z, k)
+            stage_d(zz, 3, 0)
+            stage_d(zz, 1, 0)
+
+        @pl.when(jnp.logical_not(odd) & (k >= 1) & (k <= nz))
+        def _():
+            zz = far_first(nz, z, k - 1)
+            stage_d(zz, 2, 1)
+            stage_d(zz, 0, 1)
+            stage_e(zz)
+
+        @pl.when((k >= 2) & jnp.logical_not(odd))
+        def _():
+            stage_f1(far_first(nz, z, k - 2))
+
+        @pl.when((k >= 2) & odd)
+        def _():
+            stage_f2(far_first(nz, z, k - 2))
+
         return carry
 
-    lax.fori_loop(0, width // chunk, take, 0)
-    gate_pre = dot_plain(xr[...], wg[...])
-    up_pre = dot_plain(xr[...], wu[...])
-    sig = jax.nn.sigmoid(gate_pre)
-    silu = gate_pre * sig
-    hidden_low = (silu * up_pre).astype(low)
-
-    def middle_part(i, carry):
-        total, hidden_grad = carry
-        cols = columns(i)
-        grad = gather(g_ref, cols)
-        expert_out = dot_plain(hidden_low, wd[:, cols]).astype(low).astype(f32)
-        total = total + jnp.sum(grad * expert_out, axis=1, keepdims=True)
-        pair_grad = (grad * slot_gate).astype(low)
-        scatter(out_ref, cols, (expert_out * slot_gate).astype(low))
-        acc_d[:, cols] += dot_first(hidden_low, pair_grad)
-        return total, hidden_grad + dot_last(pair_grad, wd[:, cols])
-
-    gates_grad, hidden_grad = lax.fori_loop(
-        0,
-        width // chunk,
-        middle_part,
-        (jnp.zeros(slot_gate.shape, f32), jnp.zeros(gate_pre.shape, f32)),
-    )
-    for b in range(blocks):
-        part = slice(b * slots, (b + 1) * slots)
-        gg_ref[0, :, pl.ds(b * block_rows, block_rows)] = jnp.sum(
-            pick[b].astype(f32) * gates_grad[part], axis=0, keepdims=True
-        )
-    gate_grad = (hidden_grad * up_pre * (sig * (1.0 + gate_pre * (1.0 - sig)))).astype(low)
-    up_grad = (hidden_grad * silu).astype(low)
-
-    def last_part(i, carry):
-        cols = columns(i)
-        acc_g[cols, :] += dot_first(xr[:, cols], gate_grad)
-        acc_u[cols, :] += dot_first(xr[:, cols], up_grad)
-        row_grad = dot_last(gate_grad, wg[cols, :]) + dot_last(up_grad, wu[cols, :])
-        scatter(back_ref, cols, row_grad.astype(low))
+    lax.fori_loop(0, 2 * (nz + 2), step, 0)
+    save_out(tiles - 1).wait()
+    for copy in saves(tiles - 1):
+        copy.wait()
+    for slot in range(2):
+        for i in range(2):
+            c_p(z, 1 - slot + 2 * i, slot).wait_send()
+
+    def finish(zz, carry):
+        for copy in c_diag(zz) + c_xy(zz):
+            copy.wait_send()
+        pl.when(zz != z)(c_z(zz, zz, up_dev).wait_send)
         return carry
 
-    lax.fori_loop(0, width // chunk, last_part, 0)
-
-    @pl.when(step == pl.num_programs(0) - 1)
-    def _():
-        copies = [
-            pltpu.make_async_copy(src, dst, sems.at[i])
-            for i, (src, dst) in enumerate(((acc_g, dwg), (acc_u, dwu), (acc_d, dwd)))
-        ]
-        for copy in copies:
-            copy.start()
-        for copy in copies:
-            copy.wait()
-
-
-def run_experts(expert, x_all, g_all, routes_all, router, gate_w, up_w, down_w, block_rows, slots):
+    lax.fori_loop(0, nz, finish, 0)
+
+
+def run_experts(x_all, g_all, routes_all, router, gate_w, up_w, down_w, block_rows, slots, nz,
+                collective_id):
     total, width = x_all.shape
     hidden = gate_w.shape[1]
     experts = router.shape[1]
-    rows = 2 * block_rows
-    steps = total // rows
+    tiles = 2 * nz
+    rows, cols = total // tiles, width // 4
+    pairs = rows // block_rows * slots
+    half = rows // 2
     f32, low = jnp.float32, jnp.bfloat16
-    once = pl.Buffered(1)
-    whole = lambda shape: pl.BlockSpec(shape, lambda i, e: (0, 0), pipeline_mode=once)
-    tile = lambda cols: pl.BlockSpec((rows, cols), lambda i, e: (i, 0))
     any_space = pl.BlockSpec(memory_space=pl.ANY)
+    vmem = pl.BlockSpec(memory_space=pltpu.VMEM)
+    vm, dma, shape = pltpu.VMEM, pltpu.SemaphoreType.DMA, jax.ShapeDtypeStruct
     return pl.pallas_call(
-        functools.partial(expert_kernel, slots, block_rows),
-        grid_spec=pltpu.PrefetchScalarGridSpec(
-            num_scalar_prefetch=1,
-            grid=(steps,),
-            in_specs=[
-                tile(width), tile(width), tile(routes_all.shape[1]), whole((width, experts)),
-                whole((width, hidden)), whole((width, hidden)), whole((hidden, width)),
-            ],
-            out_specs=[
-                tile(width), tile(width),
-                pl.BlockSpec((1, 1, rows), lambda i, e: (i, 0, 0)),
-                tile(experts), any_space, any_space, any_space,
-            ],
-            scratch_shapes=[
-                pltpu.VMEM((2 * slots, width), low), pltpu.VMEM((2 * slots, width), low),
-                pltpu.VMEM((width, hidden), f32), pltpu.VMEM((width, hidden), f32),
-                pltpu.VMEM((hidden, width), f32), pltpu.SemaphoreType.DMA((3,)),
-            ],
-        ),
+        functools.partial(expert_kernel, nz, slots, block_rows),
+        in_specs=[any_space] * 3 + [vmem] * 4,
+        out_specs=[any_space, vmem, vmem, vmem] + [any_space] * 5,
         out_shape=[
-            jax.ShapeDtypeStruct((total, width), low),
-            jax.ShapeDtypeStruct((total, width), low),
-            jax.ShapeDtypeStruct((steps, 1, rows), f32),
-            jax.ShapeDtypeStruct((total, experts), f32),
-            jax.ShapeDtypeStruct((width, hidden), f32),
-            jax.ShapeDtypeStruct((width, hidden), f32),
-            jax.ShapeDtypeStruct((hidden, width), f32),
+            shape((total, width), low), shape((rows, cols), f32), shape((tiles, 1, rows), f32),
+            shape((rows, experts), f32),
+            shape((tiles, pairs, width), low), shape((tiles, pairs, width), low),
+            shape((tiles, pairs, hidden), low), shape((tiles, pairs, hidden), low),
+            shape((tiles, pairs, hidden), low),
         ],
+        scratch_shapes=[
+            vm((rows, width), low), vm((rows, width), low),
+            vm((rows, routes_all.shape[1]), jnp.int32), vm((rows, width), low),
+            vm((pairs, width), low), vm((pairs, width), low),
+            vm((pairs, hidden), low), vm((pairs, hidden), low), vm((pairs, hidden), low),
+            vm((2, 2, rows, cols), low),
+            vm((nz, 4, rows, cols), low), vm((nz, 4, rows, cols), low),
+            vm((nz, rows, cols), low), vm((nz, half, cols), low),
+            vm((nz, rows, cols), low), vm((nz, half, cols), low),
+            vm((nz + 1, rows, cols), low),
+            dma((3,)), dma, dma((5,)), dma((4 * nz,)), dma((4 * nz,)),
+        ] + [dma((nz,))] * 9 + [dma((nz + 1,))],
         compiler_params=pltpu.CompilerParams(
-            dimension_semantics=("arbitrary",), vmem_limit_bytes=60 << 20
+            collective_id=collective_id, has_side_effects=True, vmem_limit_bytes=62 << 20
         ),
         name="experts",
-    )(expert, x_all, g_all, routes_all, router, gate_w, up_w, down_w)
+    )(x_all, g_all, routes_all, router, gate_w, up_w, down_w)
 
 
 def gathered_body(
@@ -1481,24 +1733,39 @@
     block_keys = micro_rows * math.gcd(shard_count, max(1, 512 // micro_rows))
     my_columns = group_index * slice_width
 
-    small = jnp.concatenate([routes, doc_ids.reshape(row_count, 1)], axis=1)
-    small_all = lax.all_gather(small, "fsdp", axis=0, tiled=True)
-    routes_all = small_all[:, :TOPK]
-    ids_all = small_all[:, TOPK].reshape(shard_count, micro_count, micro_rows)
+    mirror_index = shard_count - 1 - shard_index
+    owners = jnp.stack([shard_index, mirror_index])
+
+    def to_owners(array):
+        return jnp.stack([array[:, 0], array[::-1, 1]], axis=1)
+
+    small = jnp.concatenate([routes.reshape(-1), doc_ids.reshape(-1)])
+    small_rows = -(-small.shape[0] // 1024) * 8
+    small = jnp.pad(small, (0, small_rows * 128 - small.shape[0])).reshape(small_rows, 128)
+    small_all, wq_all, wk_all, wv_all, wo_all, tokens, cotangent, full_tokens = gather_rows(
+        [small, w_query, key_weight, value_weight, w_out], nz, 2, [tokens, cotangent]
+    )
+    small_all = small_all.reshape(shard_count, small_rows * 128)
+    routes_all = to_owners(
+        small_all[:, : row_count * TOPK].reshape(shard_count, micro_count, micro_rows, TOPK)
+    ).reshape(shard_count * row_count, TOPK)
+    ids_all = small_all[:, row_count * TOPK : row_count * (TOPK + 1)].reshape(
+        shard_count, micro_count, micro_rows
+    )
     doc_range = jnp.arange(DOCS)
     doc_totals = jnp.sum((ids_all[..., None] == doc_range).astype(jnp.int32), axis=(0, 2))
     doc_begin = jnp.cumsum(doc_totals, axis=1) - doc_totals
-    query_index = shard_index * micro_rows + jnp.arange(micro_rows)
+    query_index = owners[:, None] * micro_rows + jnp.arange(micro_rows)
+    my_ids = jnp.stack(
+        [lax.dynamic_index_in_dim(ids_all[:, m], owners[m], 0, False) for m in range(micro_count)]
+    )
     query_start = jnp.sum(
-        jnp.where(doc_ids[:, :, None] == doc_range, doc_begin[:, None, :], 0), axis=2
-    )
-    positions = (query_index[None, :] - query_start).reshape(row_count)
+        jnp.where(my_ids[:, :, None] == doc_range, doc_begin[:, None, :], 0), axis=2
+    )
+    positions = (query_index - query_start).reshape(row_count)
     cosine_lookup, sine_lookup = rope_tables(positions, head_width)
 
-    full_tokens = gather_cols(tokens, 1).astype(f32)
-    wq_all, wk_all, wv_all, wo_all = gather_rows(
-        [w_query, key_weight, value_weight, w_out], nz, 2
-    )
+    full_tokens = full_tokens.astype(f32)
     grads_all = gather_all(cotangent, nz, 3)
     token_mean = jnp.mean(full_tokens * full_tokens, axis=-1, keepdims=True)
     token_scale = lax.rsqrt(token_mean + norm_eps)
@@ -1528,19 +1795,25 @@
     keys_got, values_got = gather_rows([key_low, value_low], nz, 4)
 
     def by_stream(array):
-        return array.reshape(shard_count, micro_count, micro_rows, kv_width).transpose(
-            1, 0, 2, 3
-        ).reshape(micro_count, shard_count * micro_rows, kv_width)
+        array = array.reshape(shard_count, micro_count, micro_rows, kv_width)
+        return to_owners(array).transpose(1, 0, 2, 3).reshape(
+            micro_count, shard_count * micro_rows, kv_width
+        )
 
     keys_all, values_all = by_stream(keys_got), by_stream(values_got)
-    row_index = jnp.tile(query_index, group_width)
+    row_index = jnp.tile(query_index, (1, group_width))
     saved, head_parts = [], []
     for micro_index in range(micro_count):
         here = slice(micro_index * micro_rows, (micro_index + 1) * micro_rows)
         queries = to_heads(query_low[here], kv_local, group_width)
         row_start = jnp.tile(query_start[micro_index], group_width)
         head_out, log_total = attend_forward(
-            queries, keys_all[micro_index], values_all[micro_index], row_index, row_start, block_keys
+            queries,
+            keys_all[micro_index],
+            values_all[micro_index],
+            row_index[micro_index],
+            row_start,
+            block_keys,
         )
         saved.append((queries, row_start, head_out, log_total))
         head_parts.append(to_tokens(head_out, group_width).astype(low))
@@ -1556,16 +1829,19 @@
     gain_slice = lax.dynamic_slice_in_dim(gain_moe, my_columns, slice_width)
     moe_low = (middle * scale * gain_slice).astype(low)
     moe_all = gather_all(moe_low, nz, 7)
-    expert = (shard_index * group_count + group_index).astype(jnp.int32).reshape(1)
-    out_part, back_part, gates_grad, gates_all, gate_acc, up_acc, down_acc = run_experts(
-        expert, moe_all, grads_all, routes_all, router, w_gate[0], w_up[0], w_down[0],
-        micro_rows, capacity,
-    )
-    back = scatter_all(back_part, nz, 8)
+    out_part, back, gates_grad, gates, *kept = run_experts(
+        moe_all, grads_all, routes_all, router, w_gate[0], w_up[0], w_down[0],
+        micro_rows, capacity, nz, 8,
+    )
+    rows_in, pair_grad, hidden_low, gate_pre_low, up_pre_low = (
+        array.reshape(-1, array.shape[2]) for array in kept
+    )
+    gate_acc = dot_first(rows_in, gate_pre_low)
+    up_acc = dot_first(rows_in, up_pre_low)
+    down_acc = dot_first(hidden_low, pair_grad)
     gates_grad = swap_rows(
         gates_grad.reshape(shard_count, row_count // 128, 128), shard_count, group_count, 9
     ).reshape(expert_total, row_count).T
-    gates = lax.dynamic_slice_in_dim(gates_all, shard_index * row_count, row_count)
     logit_grad = gates * (gates_grad - jnp.sum(gates * gates_grad, axis=1, keepdims=True))
     router_slice = lax.dynamic_slice_in_dim(router, my_columns, slice_width).astype(f32)
     moe_grad = back + lax.dot_general(
@@ -1596,7 +1872,7 @@
             queries,
             keys_all[micro_index],
             values_all[micro_index],
-            row_index,
+            row_index[micro_index],
             row_start,
             block_keys,
             head_out,
@@ -1607,7 +1883,7 @@
         key_sides.append(jnp.concatenate([key_side, value_side], axis=1).astype(low))
     sides = jnp.stack(key_sides).reshape(micro_count, shard_count, micro_rows, 2 * kv_width)
     sides = reduce_rows(
-        sides.transpose(1, 0, 2, 3).reshape(shard_count * row_count, 2 * kv_width), nz, 14
+        to_owners(sides.transpose(1, 0, 2, 3)).reshape(shard_count * row_count, 2 * kv_width), nz, 14
     )
     query_pre_grad, key_pre_grad, gain_query_part, gain_key_part = heads_pull(
         (
@@ -1635,6 +1911,10 @@
         + token_scale * inner
         - token_slice * token_scale**3 * row_mean(token_slice * inner, 17)
     ).astype(low)
+
+    there = swap_back([block_out[micro_rows:], token_grad[micro_rows:]], nz, 19)
+    block_out = jnp.concatenate([block_out[:micro_rows], there[0]], axis=0)
+    token_grad = jnp.concatenate([token_grad[:micro_rows], there[1]], axis=0)
 
     pieces = [router_part.reshape(-1), gain_attn_part, gain_moe_part, gain_query_part, gain_key_part]
     length = sum(piece.shape[0] for piece in pieces)

time: 1120 us -> 1040 us (0.929)
  Pallas kernels: 914 us -> 781 us
  matrix products: 57.6 us -> 121 us
  blocking collectives: 45 us -> 0 us
  local copies, waits for them, and re-layouts: 38.4 us -> 53.9 us
  other arithmetic: 42.3 us -> 54 us
    pallas_call x2 -> x1, Pallas kernels: 156 us -> 77.9 us  [scatter_all(): pl.pallas_call(functools.partial(scatter_all_kernel, nz), out_shape=jax.S...]
    pallas_call x3, Pallas kernels: 195 us -> 143 us  [reduce_rows(): pl.pallas_call(functools.partial(reduce_rows_kernel, nz), out_shape=jax.S...]
    all_gather x1 -> x0, blocking collectives: 45 us -> none  [gathered_body(): small_all = lax.all_gather(small, 'fsdp', axis=0, tiled=True)]
    pallas_call x3 -> x4, Pallas kernels: 262 us -> 301 us  [the longest x2 156 us: gather_rows(): pl.pallas_call(functools.partial(gather_rows_kernel, nz, count, columns),...]
    dot_general x2 -> x5, matrix products: 10.2 us -> 39.4 us  [dot_first(): lax.dot_general(left_side, right_side, (((0,), (0,)), ((), ())), preferre...]
    pallas_call x2 -> x1, Pallas kernels: 38.4 us -> 18.4 us  [gather_cols(): pl.pallas_call(gather_cols_kernel, out_shape=jax.ShapeDtypeStruct((block....]
    pallas_call x2, Pallas kernels: 185 us -> 165 us  [gather_all(): pl.pallas_call(functools.partial(gather_all_kernel, nz), out_shape=jax.Sh...]
where the time goes in v2:
time: 1040 us; the launch traced here: 1020 us
  Pallas kernels  781 us (75%)
  matrix products  121 us (12%)
  other arithmetic  54 us (5%)
  local copies, waits for them, and re-layouts  53.9 us (5%)
  between operations  12.6 us (1%)
    pallas_call x2, Pallas kernels, gather_all(): pl.pallas_call(functools.partial(gather_all_kernel, nz), out_shape=jax.Sh...  165 us
    pallas_call x2, Pallas kernels, gather_rows(): pl.pallas_call(functools.partial(gather_rows_kernel, nz, count, columns),...  156 us
    pallas_call x3, Pallas kernels, reduce_rows(): pl.pallas_call(functools.partial(reduce_rows_kernel, nz), out_shape=jax.S...  143 us
    pallas_call x1, Pallas kernels, run_experts(): pl.pallas_call(functools.partial(expert_kernel, nz, slots, block_rows), i...  129 us
    pallas_call x1, Pallas kernels, scatter_all(): pl.pallas_call(functools.partial(scatter_all_kernel, nz), out_shape=jax.S...  77.9 us
    dot_general x5, matrix products, dot_first(): lax.dot_general(left_side, right_side, (((0,), (0,)), ((), ())), preferre...  39.4 us
    pallas_call x2, Pallas kernels, reduce_cols(): pl.pallas_call(reduce_cols_kernel, out_shape=jax.ShapeDtypeStruct((rows,...  31.5 us

profile of v2, /device:TPU:0, one launch (start us, length us, event | category | flops | bytes accessed | tf_op | source)
XLA Modules:
  0.0 1023.9 jit_solution(7729827440400700078)
XLA Ops:
  3.0 130.9 %gather_rows.2 = (s32[320,128]{1,0:T(8,128)}, bf16[2048,1024]{1,0:T(8,128)(2,1)}, bf16[2048,128]{1,0:T(8,128)(2,1)}, bf16[2048,128]{1,0:T(8,128)(2,1)}, bf16[204...) custom-call(s32[40,128]{1,0:T(8,128)} %pad_bitcast_fusion.refs_0_, ...), custom_call_target="tpu_custom_call" | custom-call | tf_op jit(solution)/shard_map/gather_rows/pallas_call | solution.py:1000
  146.9 3.2 convolution_convert_fusion.4.refs_1_
  150.1 24.8 %gather_rows.3 = (bf16[4096,128]{1,0:T(8,128)(2,1)}, bf16[4096,128]{1,0:T(8,128)(2,1)}) custom-call(bf16[512,128]{1,0:T(8,128)(2,1)} %get-tuple-element.674.refs_0_, bf16[512,128]{1,0:T(8,128)(2,1)} %convolution_convert_fusion.4.refs_1_), custom_call_target="tpu_custom_call" | custom-call | tf_op jit(solution)/shard_map/gather_rows/pallas_call | solution.py:1000
  191.9 5.6 while.60
  208.7 21.9 %while.61 = (s32[]{:T(128)}, f32[1,2048]{1,0:T(1,128)S(1)}, f32[1,2048]{1,0:T(1,128)S(1)}, f32[1,2048,128]{2,1,0:T(8,128)S(1)}, s32[]{:T(128)}, /*index=5*/bf16[...) while((s32[]{:T(128)}, f32[1,2048]{1,0:T(1,128)S(1)}, ...), condition=%wide.region_17.18_spmd.clone, body=%wide.region_14.17_spmd.clone.sunk | while | flops 560468480 | bytes 15706303 | solution.py:152
  234.0 4.9 convolution_convert_fusion.2.p_ref
  239.0 16.5 %reduce_cols.2 = f32[512,512]{1,0:T(8,128)S(1)} custom-call(bf16[512,2048]{1,0:T(8,128)(2,1)S(1)} %convolution_convert_fusion.2.p_ref), custom_call_target="tpu_custom_call" | custom-call | tf_op jit(solution)/shard_map/reduce_cols/pallas_call | solution.py:1208
  256.3 4.8 sum_cols.3
  263.5 82.5 %gather_all.2.x_all = bf16[4096,2048]{1,0:T(8,128)(2,1)} custom-call(bf16[512,512]{1,0:T(8,128)(2,1)} %multiply_convert_fusion.x_ref), custom_call_target="tpu_custom_call" | custom-call | tf_op jit(solution)/shard_map/gather_all/pallas_call | solution.py:685
  352.2 3.1 pad_add_fusion
  355.3 82.7 %gather_all.3.g_all = bf16[4096,2048]{1,0:T(8,128)(2,1)} custom-call(bf16[512,512]{1,0:T(8,128)(2,1)} %get-tuple-element.298.x_ref), custom_call_target="tpu_custom_call" | custom-call | tf_op jit(solution)/shard_map/gather_all/pallas_call | solution.py:685
  439.0 128.7 %experts.1 = (bf16[4096,2048]{1,0:T(8,128)(2,1)}, f32[512,512]{1,0:T(8,128)}, f32[8,1,512]{2,1,0:T(1,128)}, f32[512,32]{1,0:T(8,128)}, bf16[8,256,2048]{2,1,0:T(...) custom-call(bf16[4096,2048]{1,0:T(8,128)(2,1)} %gather_all.2.x_all, ...), custom_call_target="tpu_custom_call" | custom-call | tf_op jit(solution)/shard_map/experts/pallas_call | solution.py:1669
  567.8 11.9 %convolution_bitcast_fusion.2 = f32[1,768,2048]{2,1,0:T(8,128)} fusion(bf16[8,256,768]{2,1,0:T(8,128)(2,1)} %get-tuple-element.316, bf16[8,256,2048]{2,1,0:T(8,128)(2,1)} %get-tuple-element.317), kind=kOutput, calls=%fused_computation.127 | convolution fusion | flops 6442450944 | bytes 17825792 | tf_op jit(solution)/shard_map/dot_general | solution.py:54
  579.7 9.2 convolution_bitcast_fusion.3
  588.9 9.0 convolution_bitcast_fusion.4
  597.9 9.6 swap_rows.1
  611.4 4.9 sum_cols.4
  616.9 77.9 %scatter_all.1 = f32[512,512]{1,0:T(8,128)S(1)} custom-call(bf16[4096,2048]{1,0:T(8,128)(2,1)} %get-tuple-element.299.p_ref), custom_call_target="tpu_custom_call" | custom-call | tf_op jit(solution)/shard_map/scatter_all/pallas_call | solution.py:859
  696.5 18.4 %gather_cols.1 = bf16[512,2048]{1,0:T(8,128)(2,1)} custom-call(bf16[512,512]{1,0:T(8,128)(2,1)} %get-tuple-element.626.x_ref), custom_call_target="tpu_custom_call" | custom-call | tf_op jit(solution)/shard_map/gather_cols/pallas_call | solution.py:1164
  714.9 4.4 convolution_convert_fusion.1.p_ref
  719.3 50.7 %reduce_rows.5 = f32[256,1024]{1,0:T(8,128)S(1)} custom-call(bf16[2048,1024]{1,0:T(8,128)(2,1)S(1)} %convolution_convert_fusion.1.p_ref), custom_call_target="tpu_custom_call" | custom-call | tf_op jit(solution)/shard_map/reduce_rows/pallas_call | solution.py:1122
  776.2 8.8 while.62
  790.4 35.4 %while.63 = (s32[]{:T(128)}, f32[1,2048,128]{2,1,0:T(8,128)S(1)}, bf16[2048,128]{1,0:T(8,128)(2,1)}, bf16[2048,128]{1,0:T(8,128)(2,1)}, s32[]{:T(128)}, /*index=...) while((s32[]{:T(128)}, f32[1,2048,128]{2,1,0:T(8,128)S(1)}, ...), condition=%wide.region_26.27_spmd.clone, body=%wide.region_25.26_spmd.clone.sunk | while | flops 1354301952 | bytes 28268828 | solution.py:215
  833.2 32.6 %reduce_rows.3 = f32[512,256]{1,0:T(8,128)S(1)} custom-call(bf16[4096,256]{1,0:T(8,128)(2,1)S(1)} %bitcast.435), custom_call_target="tpu_custom_call" | custom-call | tf_op jit(solution)/shard_map/reduce_rows/pallas_call | solution.py:1122
  869.9 3.7 multiply_reduce_fusion
  873.8 3.9 fusion.105
  878.0 4.9 convolution_convert_fusion.p_ref
  882.9 60.1 %reduce_rows.4 = f32[256,1280]{1,0:T(8,128)S(1)} custom-call(bf16[2048,1280]{1,0:T(8,128)(2,1)} %convolution_convert_fusion.p_ref), custom_call_target="tpu_custom_call" | custom-call | tf_op jit(solution)/shard_map/reduce_rows/pallas_call | solution.py:1122
  948.8 15.0 %reduce_cols.3 = f32[512,512]{1,0:T(8,128)S(1)} custom-call(bf16[512,2048]{1,0:T(8,128)(2,1)S(1)} %add_convert_fusion.p_ref), custom_call_target="tpu_custom_call" | custom-call | tf_op jit(solution)/shard_map/reduce_cols/pallas_call | solution.py:1208
  966.5 17.8 %sum_small.1 = f32[32,24,128]{2,1,0:T(8,128)} custom-call(f32[8,24,128]{2,1,0:T(8,128)} %bitcast.500), custom_call_target="tpu_custom_call" | custom-call | tf_op jit(solution)/shard_map/sum_small/pallas_call | solution.py:1339
  992.5 5.8 sum_cols.5
  1002.0 17.1 %swap_back.1 = (bf16[256,512]{1,0:T(8,128)(2,1)}, bf16[256,512]{1,0:T(8,128)(2,1)}) custom-call(bf16[256,512]{1,0:T(8,128)(2,1)} %get-tuple-element.668.refs_0_, bf16[256,512]{1,0:T(8,128)(2,1)} %get-tuple-element.666.refs_1_), custom_call_target="tpu_custom_call" | custom-call | tf_op jit(solution)/shard_map/swap_back/pallas_call | solution.py:1031
  (382 shorter events, 170.8 us)
Async XLA Ops:
  0.6 142.0 %copy-start.57 = (f32[2048]{0:T(1024)S(1)}, f32[2048]{0:T(1024)}, u32[]{:S(2)}) copy-start(f32[2048]{0:T(1024)} %param.28) | copy-start | bytes 24580
  133.8 11.7 %copy-start.55 = (f32[128]{0:T(128)S(1)}, f32[128]{0:T(128)}, u32[]{:S(2)}) copy-start(f32[128]{0:T(128)} %param.34) | copy-start | bytes 1540
  134.8 10.6 %copy-start.37 = (s32[8,5120]{1,0:T(8,128)}, s32[8,5120]{1,0:T(8,128)S(1)}, u32[]{:S(2)}) copy-start(s32[8,5120]{1,0:T(8,128)S(1)} %reshape.690) | copy-start | bytes 491524
  142.7 37.7 %copy-start.47 = (f32[512]{0:T(512)}, f32[512]{0:T(512)S(1)}, u32[]{:S(2)}) copy-start(f32[512]{0:T(512)S(1)} %get-tuple-element.683) | copy-start | bytes 6148
  145.5 29.4 %copy-start.11 = (f32[512,128]{1,0:T(8,128)}, f32[512,128]{1,0:T(8,128)S(1)}, u32[]{:S(2)}) copy-start(f32[512,128]{1,0:T(8,128)S(1)} %copy.171) | copy-start | bytes 786436
  146.8 38.9 %copy-start.18 = (f32[512,128]{1,0:T(8,128)}, f32[512,128]{1,0:T(8,128)S(1)}, u32[]{:S(2)}) copy-start(f32[512,128]{1,0:T(8,128)S(1)} %get-tuple-element.673) | copy-start | bytes 786436
  146.8 39.0 %copy-start.20 = (f32[512,128]{1,0:T(8,128)}, f32[512,128]{1,0:T(8,128)S(1)}, u32[]{:S(2)}) copy-start(f32[512,128]{1,0:T(8,128)S(1)} %get-tuple-element.675) | copy-start | bytes 786436
  150.1 30.3 %copy-start.27 = (bf16[512,2048]{1,0:T(8,128)(2,1)S(1)}, bf16[512,2048]{1,0:T(8,128)(2,1)}, u32[]{:S(2)}) copy-start(bf16[512,2048]{1,0:T(8,128)(2,1)} %get-tuple-element.287) | copy-start | bytes 6291460
  197.6 11.0 %copy-start.17 = (bf16[2048,128]{1,0:T(8,128)(2,1)}, bf16[2048,128]{1,0:T(8,128)(2,1)S(1)}, u32[]{:S(2)}) copy-start(bf16[2048,128]{1,0:T(8,128)(2,1)S(1)} %get-tuple-element.1228) | copy-start | bytes 1572868
  230.6 24.9 %copy-start.6 = (f32[1,2048,128]{2,1,0:T(8,128)}, f32[1,2048,128]{2,1,0:T(8,128)S(1)}, u32[]{:S(2)}) copy-start(f32[1,2048,128]{2,1,0:T(8,128)S(1)} %get-tuple-element.295) | copy-start | bytes 3145732
  234.0 21.5 %copy-start.14 = (bf16[512,512]{1,0:T(8,128)(2,1)S(1)}, bf16[512,512]{1,0:T(8,128)(2,1)}, u32[]{:S(2)}) copy-start(bf16[512,512]{1,0:T(8,128)(2,1)} %get-tuple-element.285) | copy-start | bytes 1572868
  263.5 82.5 %slice-start = ((s32[8,5120]{1,0:T(8,128)}), s32[8,4096]{1,0:T(8,128)S(1)}, s32[]{:S(2)}) async-start(s32[8,5120]{1,0:T(8,128)} %copy-done.37), calls=%async_computation | async-start | bytes 262144 | tf_op jit(solution)/shard_map/slice | solution.py:1750
  355.3 82.7 %copy-start.42 = (bf16[2048,32]{0,1:T(8,128)(2,1)S(1)}, bf16[2048,32]{0,1:T(8,128)(2,1)}, u32[]{:S(2)}) copy-start(bf16[2048,32]{0,1:T(8,128)(2,1)} %param.36) | copy-start | bytes 393220
  567.7 12.0 %copy-start.59 = (bf16[8,256,2048]{2,1,0:T(8,128)(2,1)S(1)}, bf16[8,256,2048]{2,1,0:T(8,128)(2,1)}, u32[]{:S(2)}) copy-start(bf16[8,256,2048]{2,1,0:T(8,128)(2,1)} %get-tuple-element.313) | copy-start | bytes 25165828
  567.8 11.9 %copy-start.64 = (bf16[8,256,768]{2,1,0:T(8,128)(2,1)S(1)}, bf16[8,256,768]{2,1,0:T(8,128)(2,1)}, u32[]{:S(2)}) copy-start(bf16[8,256,768]{2,1,0:T(8,128)(2,1)} %get-tuple-element.315) | copy-start | bytes 9437188
  588.9 19.5 %copy-start.35 = (f32[512,32]{1,0:T(8,128)S(1)}, f32[512,32]{1,0:T(8,128)}, u32[]{:S(2)}) copy-start(f32[512,32]{1,0:T(8,128)} %get-tuple-element.301) | copy-start | bytes 196612
  616.9 77.9 %copy-start.49 = (f32[4,128]{1,0:T(4,128)S(1)}, f32[4,128]{1,0:T(4,128)}, u32[]{:S(2)}) copy-start(f32[4,128]{1,0:T(4,128)} %sum_cols.3) | copy-start | bytes 6148
  616.9 77.9 %copy-start.29 = (bf16[512,512]{1,0:T(8,128)(2,1)S(1)}, bf16[512,512]{1,0:T(8,128)(2,1)}, u32[]{:S(2)}) copy-start(bf16[512,512]{1,0:T(8,128)(2,1)} %get-tuple-element.298.x_ref) | copy-start | bytes 1572868
  714.9 55.1 %copy-start.62 = (bf16[2048,1024]{1,0:T(8,128)(2,1)S(1)}, bf16[2048,1024]{1,0:T(8,128)(2,1)}, u32[]{:S(2)}) copy-start(bf16[2048,1024]{1,0:T(8,128)(2,1)} %get-tuple-element.297) | copy-start | bytes 12582916
  719.3 50.7 %copy-start.26 = (bf16[512,2048]{1,0:T(8,128)(2,1)S(1)}, bf16[512,2048]{1,0:T(8,128)(2,1)}, u32[]{:S(2)}) copy-start(bf16[512,2048]{1,0:T(8,128)(2,1)} %gather_cols.1) | copy-start | bytes 6291460
  829.0 36.7 %copy-start.23 = (f32[512,64]{1,0:T(8,128)S(1)}, f32[512,64]{1,0:T(8,128)}, u32[]{:S(2)}) copy-start(f32[512,64]{1,0:T(8,128)} %copy-done.22) | copy-start | bytes 393220
  831.4 34.7 %copy-start.12 = (f32[512,128]{1,0:T(8,128)S(1)}, f32[512,128]{1,0:T(8,128)}, u32[]{:S(2)}) copy-start(f32[512,128]{1,0:T(8,128)} %copy-done.11) | copy-start | bytes 786436
  831.4 34.7 %copy-start.25 = (f32[512,64]{1,0:T(8,128)S(1)}, f32[512,64]{1,0:T(8,128)}, u32[]{:S(2)}) copy-start(f32[512,64]{1,0:T(8,128)} %copy-done.24) | copy-start | bytes 393220
  831.4 34.7 %copy-start.46 = (f32[512]{0:T(512)S(1)}, f32[512]{0:T(512)}, u32[]{:S(2)}) copy-start(f32[512]{0:T(512)} %copy-done.45) | copy-start | bytes 6148
  831.4 34.7 %copy-start.56 = (f32[128]{0:T(128)S(1)}, f32[128]{0:T(128)}, u32[]{:S(2)}) copy-start(f32[128]{0:T(128)} %param.34) | copy-start | bytes 1540
  831.4 35.1 %copy-start.54 = (f32[512]{0:T(512)S(1)}, f32[512]{0:T(512)}, u32[]{:S(2)}) copy-start(f32[512]{0:T(512)} %copy-done.53) | copy-start | bytes 6148
  833.2 33.6 %copy-start.3 = (f32[1,2048,128]{2,1,0:T(8,128)S(1)}, f32[1,2048,128]{2,1,0:T(8,128)}, u32[]{:S(2)}) copy-start(f32[1,2048,128]{2,1,0:T(8,128)} %copy-done.2) | copy-start | bytes 3145732
  882.9 61.9 %copy-start.40 = (bf16[2048,128]{1,0:T(8,128)(2,1)S(1)}, bf16[2048,128]{1,0:T(8,128)(2,1)}, u32[]{:S(2)}) copy-start(bf16[2048,128]{1,0:T(8,128)(2,1)} %get-tuple-element.288) | copy-start | bytes 1572868
  948.0 15.8 %copy-start.15 = (bf16[512,512]{1,0:T(8,128)(2,1)S(1)}, bf16[512,512]{1,0:T(8,128)(2,1)}, u32[]{:S(2)}) copy-start(bf16[512,512]{1,0:T(8,128)(2,1)} %get-tuple-element.285) | copy-start | bytes 1572868
  948.8 16.1 %copy-start.13 = (bf16[512,512]{1,0:T(8,128)(2,1)S(1)}, bf16[512,512]{1,0:T(8,128)(2,1)}, u32[]{:S(2)}) copy-start(bf16[512,512]{1,0:T(8,128)(2,1)} %multiply_convert_fusion.x_ref) | copy-start | bytes 1572868
  963.7 35.3 %copy-start.52 = (f32[512]{0:T(512)S(1)}, f32[512]{0:T(512)}, u32[]{:S(2)}) copy-start(f32[512]{0:T(512)} %get-tuple-element.682) | copy-start | bytes 6148
  984.3 17.0 %copy-start.30 = (bf16[512,512]{1,0:T(8,128)(2,1)S(1)}, bf16[512,512]{1,0:T(8,128)(2,1)}, u32[]{:S(2)}) copy-start(bf16[512,512]{1,0:T(8,128)(2,1)} %get-tuple-element.654) | copy-start | bytes 1572868
  (40 other events, 127.0 us)

commit v3 on v2

--- a/solution.py
+++ b/solution.py
@@ -899,7 +899,7 @@
     xn, up, down = device(z, 1 - x, y, c), device(z + 1, x, y, c), device(z - 1, x, y, c)
     partner, yn = device(z, x, y, 1 - c), device(z, x, 1 - y, c)
     wanted = [(None, xn), (z < nz - 1, up), (z > 0, down)]
-    greet(wanted + [(None, partner), (None, yn), (None, device(nz - 1 - z, 1 - x, y, c))] * min(columns, 1))
+    greet(wanted + [(None, partner), (None, yn), (None, device(nz - 1 - z, x, y, c))] * min(columns, 1))
 
     def block(n, zz, xx):
         rows = srcs[n].shape[0]
@@ -908,7 +908,7 @@
     own = [(srcs[n], block(n, z, x)) for n in range(count)]
     column_copies, swaps = [], []
     if columns:
-        mirror = device(nz - 1 - z, 1 - x, y, c)
+        mirror = device(nz - 1 - z, x, y, c)
         first, out = outs[count], wide[0]
         rows, cols = first.shape
         top, bottom = pl.ds(0, rows // 2), pl.ds(rows // 2, rows // 2)
@@ -1014,7 +1014,7 @@
     srcs, outs = refs[:count], refs[count : 2 * count]
     s, r = refs[2 * count :]
     z, x, y, c = place()
-    mirror = device(nz - 1 - z, 1 - x, y, c)
+    mirror = device(nz - 1 - z, x, y, c)
     greet([(None, mirror)])
     copies = [remote(src, out, s.at[n], r.at[n], mirror)
               for n, (src, out) in enumerate(zip(srcs, outs))]
@@ -1387,8 +1387,15 @@
         return pl.ds(pl.multiple_of(tile_of(j) * rows, rows), rows)
 
     def load(j, kind):
-        src, dst = ((x_all, x_ref), (g_all, g_ref), (routes_all, t_ref))[kind]
+        src, dst = ((x_all, x_ref), None, (routes_all, t_ref))[kind]
         return pltpu.make_async_copy(src.at[tile_rows(j)], dst, s_in.at[kind])
+
+    def load_g(j):
+        tile = tile_of(j)
+        first = pl.ds(pl.multiple_of(tile * rows, half), half)
+        second = pl.ds(pl.multiple_of(mirrored(nz, tile) * rows + half, half), half)
+        return (pltpu.make_async_copy(g_all.at[first], g_ref.at[pl.ds(0, half)], s_in.at[1]),
+                pltpu.make_async_copy(g_all.at[second], g_ref.at[pl.ds(half, half)], s_in.at[3]))
 
     def save_out(j):
         return pltpu.make_async_copy(o_ref, out_all.at[tile_rows(j)], s_out)
@@ -1541,7 +1548,8 @@
         silu = gate_pre * sig
         hidden_low = (silu * up_pre).astype(low)
         hid[...] = hidden_low
-        load(j, 1).wait()
+        for copy in load_g(j):
+            copy.wait()
         pl.when(j > 0)(lambda: save_out(j).wait())
 
         def middle_part(i, carry):
@@ -1562,7 +1570,12 @@
             (jnp.zeros(slot_gate.shape, f32), jnp.zeros(gate_pre.shape, f32)),
         )
         save_out(j).start()
-        pl.when(j < tiles - 1)(lambda: load(j + 1, 1).start())
+
+        @pl.when(j < tiles - 1)
+        def _():
+            for copy in load_g(j + 1):
+                copy.start()
+
         for b in range(blocks):
             gg_ref[tile_of(j), :, pl.ds(b * block_rows, block_rows)] = jnp.sum(
                 pick[b].astype(f32) * gates_grad[b * slots : (b + 1) * slots],
@@ -1606,8 +1619,8 @@
         lax.fori_loop(0, 2, to_partner, 0)
         lax.fori_loop(0, 2, to_own, 0)
 
-    for kind in (2, 0, 1):
-        load(0, kind).start()
+    for copy in (load(0, 2), load(0, 0)) + load_g(0):
+        copy.start()
 
     def step(j, carry):
         k, odd = j // 2, j % 2 == 1
@@ -1687,13 +1700,661 @@
             vm((nz, rows, cols), low), vm((nz, half, cols), low),
             vm((nz, rows, cols), low), vm((nz, half, cols), low),
             vm((nz + 1, rows, cols), low),
-            dma((3,)), dma, dma((5,)), dma((4 * nz,)), dma((4 * nz,)),
+            dma((4,)), dma, dma((5,)), dma((4 * nz,)), dma((4 * nz,)),
         ] + [dma((nz,))] * 9 + [dma((nz + 1,))],
         compiler_params=pltpu.CompilerParams(
             collective_id=collective_id, has_side_effects=True, vmem_limit_bytes=62 << 20
         ),
         name="experts",
     )(x_all, g_all, routes_all, router, gate_w, up_w, down_w)
+
+
+def near_first(nz, z, k):
+    return far_first(nz, z, nz - 1 - k)
+
+
+class GatherAll:
+    sems = 6
+
+    @staticmethod
+    def scratch(nz):
+        dma = pltpu.SemaphoreType.DMA
+        return [dma] + [dma((5 * nz,))] * 2 + [dma((nz,))] * 11
+
+    def __init__(self, nz, src, out, sems, cut):
+        (self.lsem, self.s_p, self.r_p, self.s_u, self.s_d, self.s_x, self.s_y, self.s_dx,
+         self.s_dy, self.r_z, self.r_x, self.r_y, self.r_dx, self.r_dy) = sems
+        self.nz, self.src, self.out, self.cut = nz, src, out, cut
+        self.rows, self.cols = src.shape
+        self.place = z, x, y, c = place()
+        self.partner, self.xn, self.yn = (
+            device(z, x, y, 1 - c), device(z, 1 - x, y, c), device(z, x, 1 - y, c))
+        self.up, self.down = device(z + 1, x, y, c), device(z - 1, x, y, c)
+
+    def block(self, zz, xx, yy, cc, part=None):
+        start, size, unit = (zz * 2 + xx) * self.rows, self.rows, self.rows
+        if part == 0:
+            size, unit = self.cut, self.rows
+        elif part == 1:
+            start, size = start + self.cut, self.rows - self.cut
+            unit = math.gcd(self.cut, self.rows)
+        return self.out.at[pl.ds(pl.multiple_of(start, unit), size),
+                           pl.ds(pl.multiple_of((yy * 2 + cc) * self.cols, self.cols), self.cols)]
+
+    def own(self):
+        z, x, y, c = self.place
+        return pltpu.make_async_copy(self.src, self.block(z, x, y, c), self.lsem)
+
+    def line(self, zz):
+        z, x, y, c = self.place
+        here = self.block(zz, x, y, c)
+        return (remote(here, here, self.s_u.at[zz], self.r_z.at[zz], self.up),
+                remote(here, here, self.s_d.at[zz], self.r_z.at[zz], self.down))
+
+    def sides(self, zz):
+        z, x, y, c = self.place
+        here = self.block(zz, x, y, c)
+        return (remote(here, here, self.s_x.at[zz], self.r_x.at[zz], self.xn),
+                remote(here, here, self.s_y.at[zz], self.r_y.at[zz], self.yn))
+
+    def across(self, zz):
+        z, x, y, c = self.place
+        copies = []
+        if self.cut > 0:
+            here = self.block(zz, 1 - x, y, c, 0)
+            copies.append(remote(here, here, self.s_dy.at[zz], self.r_dy.at[zz], self.yn))
+        if self.cut < self.rows:
+            here = self.block(zz, x, 1 - y, c, 1)
+            copies.append(remote(here, here, self.s_dx.at[zz], self.r_dx.at[zz], self.xn))
+        return copies
+
+    def pair(self, zz, rel, mine=True):
+        z, x, y, c = self.place
+        xx = 1 - x if rel in (1, 3, 4) else x
+        yy = 1 - y if rel in (2, 3, 4) else y
+        here = self.block(zz, xx, yy, c if mine else 1 - c, {3: 0, 4: 1}.get(rel))
+        k = zz * 5 + rel
+        return remote(here, here, self.s_p.at[k], self.r_p.at[k], self.partner)
+
+    def parts(self):
+        return [0, 1, 2] + [3] * (self.cut > 0) + [4] * (self.cut < self.rows)
+
+    def first(self, k):
+        zz, z = near_first(self.nz, self.place[0], k), self.place[0]
+        up, down = self.line(zz)
+        pl.when(k > 0)(lambda: up.wait_recv())
+        pl.when((zz <= z) & (z < self.nz - 1))(lambda: up.start())
+        pl.when((zz >= z) & (z > 0))(lambda: down.start())
+        for copy in self.sides(zz):
+            copy.start()
+        self.pair(zz, 0).start()
+
+    def second(self, k):
+        zz = near_first(self.nz, self.place[0], k)
+        to_x, to_y = self.sides(zz)
+        across = self.across(zz)
+        to_x.wait_recv()
+        if self.cut > 0:
+            across[0].start()
+        self.pair(zz, 1).start()
+        to_y.wait_recv()
+        if self.cut < self.rows:
+            across[-1].start()
+        self.pair(zz, 2).start()
+
+    def third(self, k):
+        zz = near_first(self.nz, self.place[0], k)
+        across = self.across(zz)
+        for rel, copy in zip(self.parts()[3:], across):
+            copy.wait_recv()
+            self.pair(zz, rel).start()
+
+    def finish(self):
+        z = self.place[0]
+
+        def step(zz, carry):
+            for rel in self.parts():
+                self.pair(zz, rel, False).wait_recv()
+                self.pair(zz, rel).wait_send()
+            up, down = self.line(zz)
+            pl.when((zz <= z) & (z < self.nz - 1))(lambda: up.wait_send())
+            pl.when((zz >= z) & (z > 0))(lambda: down.wait_send())
+            for copy in tuple(self.sides(zz)) + tuple(self.across(zz)):
+                copy.wait_send()
+            return carry
+
+        lax.fori_loop(0, self.nz, step, 0)
+
+
+class GatherRows:
+    @staticmethod
+    def scratch(nz):
+        dma = pltpu.SemaphoreType.DMA
+        return [dma] + [dma((nz,))] * 5
+
+    def __init__(self, nz, src, out, sems):
+        self.lsem, self.s_u, self.s_d, self.s_x, self.r_z, self.r_x = sems
+        self.nz, self.src, self.out = nz, src, out
+        self.place = z, x, y, c = place()
+        self.xn = device(z, 1 - x, y, c)
+        self.up, self.down = device(z + 1, x, y, c), device(z - 1, x, y, c)
+
+    def block(self, zz):
+        rows = self.src.shape[0]
+        return self.out.at[pl.ds(pl.multiple_of((zz * 2 + self.place[1]) * rows, rows), rows)]
+
+    def own(self):
+        return pltpu.make_async_copy(self.src, self.block(self.place[0]), self.lsem)
+
+    def copies(self, zz):
+        here = self.block(zz)
+        return (remote(here, here, self.s_u.at[zz], self.r_z.at[zz], self.up),
+                remote(here, here, self.s_d.at[zz], self.r_z.at[zz], self.down),
+                remote(here, here, self.s_x.at[zz], self.r_x.at[zz], self.xn))
+
+    def first(self, k):
+        zz, z = near_first(self.nz, self.place[0], k), self.place[0]
+        up, down, to_x = self.copies(zz)
+        pl.when(k > 0)(lambda: up.wait_recv())
+        pl.when((zz <= z) & (z < self.nz - 1))(lambda: up.start())
+        pl.when((zz >= z) & (z > 0))(lambda: down.start())
+        to_x.start()
+
+    def finish(self):
+        z = self.place[0]
+
+        def step(zz, carry):
+            up, down, to_x = self.copies(zz)
+            to_x.wait()
+            pl.when((zz <= z) & (z < self.nz - 1))(lambda: up.wait_send())
+            pl.when((zz >= z) & (z > 0))(lambda: down.wait_send())
+            return carry
+
+        lax.fori_loop(0, self.nz, step, 0)
+
+
+def mirrored(nz, shard):
+    return (nz - 1 - shard // 2) * 2 + shard % 2
+
+
+def stream_unit(u, nz, block):
+    shard = lax.axis_index("fsdp")
+    later = u > shard
+    micro = jnp.where(later, 1, 0)
+    here = jnp.where(later, mirrored(nz, shard), shard)
+    key_place = here - jnp.where(later, u - shard - 1, u)
+    owner = jnp.where(later, mirrored(nz, key_place), key_place)
+    rows = pl.ds(pl.multiple_of((owner * 2 + micro) * block, block), block)
+    return micro, here, key_place, rows
+
+
+def key_bias(micro, here, key_place, block, start_ref):
+    key = key_place * block + lax.broadcasted_iota(jnp.int32, (block, block), 0)
+    query = here * block + lax.broadcasted_iota(jnp.int32, (block, block), 1)
+    return jnp.where((key >= start_ref[micro]) & (key <= query), 0.0, masked_score)
+
+
+def attend_kernel(nz, q_ref, k_ref, v_ref, start_ref, cot_ref, wo_ref,
+                  heads_ref, out_ref, lse_ref, cot_all, wo_all, acc, peak, total, *sems):
+    shards = 2 * nz
+    width = k_ref.shape[1]
+    block = q_ref.shape[0] // 2
+    heads = q_ref.shape[1] // width
+    z, x, y, c = place()
+    split = len(GatherAll.scratch(nz))
+    cots = GatherAll(nz, cot_ref, cot_all, sems[:split], cot_ref.shape[0])
+    outs = GatherRows(nz, wo_ref, wo_all, sems[split:])
+    greet([(None, cots.partner), (None, cots.xn), (None, cots.yn),
+           (z < nz - 1, cots.up), (z > 0, cots.down)])
+    for part in (outs, cots):
+        part.own().start()
+    peak[...] = jnp.full(peak.shape, masked_score, jnp.float32)
+    total[...] = jnp.zeros_like(total)
+    acc[...] = jnp.zeros_like(acc)
+    for part in (outs, cots):
+        part.own().wait()
+
+    def unit(u, carry):
+        @pl.when(u < nz)
+        def _():
+            outs.first(u)
+            cots.first(u)
+
+        pl.when((u >= 1) & (u <= nz))(lambda: cots.second(u - 1))
+        pl.when((u >= 2) & (u <= nz + 1))(lambda: cots.third(u - 2))
+        pl.when(u < shards + 2 * x)(lambda: attention(u))
+        return carry
+
+    def attention(u):
+        micro, here, key_place, rows = stream_unit(u, nz, block)
+        bias = key_bias(micro, here, key_place, block, start_ref)
+        keys, values = k_ref[rows, :], v_ref[rows, :]
+        q_rows = pl.ds(pl.multiple_of(micro * block, block), block)
+
+        def head(h, carry):
+            at = micro * heads + h
+            query = q_ref[q_rows, pl.ds(pl.multiple_of(h * width, width), width)]
+            scores = dot_last(keys, query) * width ** (-0.5) + bias
+            before = peak[at]
+            now = jnp.maximum(before, jnp.max(scores, axis=0, keepdims=True))
+            weights = jnp.exp(scores - now)
+            factor = jnp.exp(before - now)
+            peak[at] = now
+            total[at] = total[at] * factor + jnp.sum(weights, axis=0, keepdims=True)
+            acc[at] = acc[at] * factor + dot_first(values, weights.astype(jnp.bfloat16))
+            return carry
+
+        lax.fori_loop(0, heads, head, 0, unroll=4)
+
+    lax.fori_loop(0, shards + 2, unit, 0)
+
+    def close(at, carry):
+        micro, h = at // heads, at % heads
+        result = (acc[at] / total[at]).T
+        here = pl.ds(pl.multiple_of(micro * block, block), block)
+        cols = pl.ds(pl.multiple_of(h * width, width), width)
+        out_ref[here, cols] = result
+        heads_ref[here, cols] = result.astype(jnp.bfloat16)
+        lse_ref[at] = peak[at] + jnp.log(total[at])
+        return carry
+
+    lax.fori_loop(0, 2 * heads, close, 0)
+    outs.finish()
+    cots.finish()
+
+
+def attend(query, keys, values, starts, cotangent, w_out, nz, collective_id):
+    rows, columns = query.shape
+    width = keys.shape[1]
+    heads = columns // width
+    block = rows // 2
+    any_space = pl.BlockSpec(memory_space=pl.ANY)
+    vmem = pl.BlockSpec(memory_space=pltpu.VMEM)
+    vm, shape, f32 = pltpu.VMEM, jax.ShapeDtypeStruct, jnp.float32
+    return pl.pallas_call(
+        functools.partial(attend_kernel, nz),
+        in_specs=[vmem] * 4 + [any_space] * 2,
+        out_specs=[vmem] * 3 + [any_space] * 2,
+        out_shape=[
+            shape((rows, columns), jnp.bfloat16),
+            shape((rows, columns), f32),
+            shape((2 * heads, 1, block), f32),
+            shape((rows * 2 * nz, cotangent.shape[1] * 4), cotangent.dtype),
+            shape((w_out.shape[0] * 2 * nz, w_out.shape[1]), w_out.dtype),
+        ],
+        scratch_shapes=[
+            vm((2 * heads, width, block), f32), vm((2 * heads, 1, block), f32),
+            vm((2 * heads, 1, block), f32),
+        ] + GatherAll.scratch(nz) + GatherRows.scratch(nz),
+        compiler_params=pltpu.CompilerParams(
+            collective_id=collective_id, has_side_effects=True, vmem_limit_bytes=40 << 20
+        ),
+        name="attend",
+    )(query, keys, values, starts, cotangent, w_out)
+
+
+class ScatterAll:
+    @staticmethod
+    def scratch(nz, rows, cols, kind, cut):
+        vm, dma = pltpu.VMEM, pltpu.SemaphoreType.DMA
+        return [
+            vm((nz, 4, rows, cols), kind), vm((nz, 4, rows, cols), kind),
+            vm((nz, rows, cols), kind), vm((nz, max(cut, 16), cols), kind),
+            vm((nz, rows, cols), kind), vm((nz, max(rows - cut, 16), cols), kind),
+            vm((nz + 1, rows, cols), kind),
+        ] + [dma((4 * nz,))] * 3 + [dma((nz,))] * 9 + [dma((nz + 1,))]
+
+    def __init__(self, nz, partial, out, refs, cut):
+        (self.w, self.lp, self.rx, self.rxd, self.ry, self.ryd, self.rz,
+         self.s_l, self.s_p, self.r_p, self.s_x, self.s_y, self.s_dx, self.s_dy, self.s_z,
+         self.r_x, self.r_y, self.r_dx, self.r_dy, self.r_z) = refs
+        self.nz, self.partial, self.out, self.cut = nz, partial, out, cut
+        self.rows, self.cols = out.shape
+        self.place = z, x, y, c = place()
+        self.partner, self.xn, self.yn = (
+            device(z, x, y, 1 - c), device(z, 1 - x, y, c), device(z, x, 1 - y, c))
+        self.up, self.down = device(z + 1, x, y, c), device(z - 1, x, y, c)
+
+    def block(self, zz, rel, cc):
+        z, x, y, c = self.place
+        xx = 1 - x if rel in (1, 3) else x
+        yy = 1 - y if rel in (2, 3) else y
+        return self.partial.at[
+            pl.ds(pl.multiple_of((zz * 2 + xx) * self.rows, self.rows), self.rows),
+            pl.ds(pl.multiple_of((yy * 2 + cc) * self.cols, self.cols), self.cols)]
+
+    def pair(self, zz, rel):
+        k = zz * 4 + rel
+        return remote(self.block(zz, rel, 1 - self.place[3]), self.lp.at[zz, rel],
+                      self.s_p.at[k], self.r_p.at[k], self.partner)
+
+    def load(self, zz, rel):
+        return pltpu.make_async_copy(
+            self.block(zz, rel, self.place[3]), self.w.at[zz, rel], self.s_l.at[zz * 4 + rel])
+
+    def across(self, zz):
+        copies = []
+        if self.cut > 0:
+            copies.append(remote(self.w.at[zz, 3, pl.ds(0, self.cut)], self.rxd.at[zz],
+                                 self.s_dx.at[zz], self.r_dx.at[zz], self.xn))
+        if self.cut < self.rows:
+            copies.append(remote(self.w.at[zz, 3, pl.ds(self.cut, self.rows - self.cut)],
+                                 self.ryd.at[zz], self.s_dy.at[zz], self.r_dy.at[zz], self.yn))
+        return copies
+
+    def sides(self, zz):
+        return (remote(self.w.at[zz, 1], self.rx.at[zz], self.s_x.at[zz], self.r_x.at[zz], self.xn),
+                remote(self.w.at[zz, 2], self.ry.at[zz], self.s_y.at[zz], self.r_y.at[zz], self.yn))
+
+    def line(self, zz, slot, where):
+        return remote(self.w.at[zz, 0], self.rz.at[slot], self.s_z.at[zz], self.r_z.at[slot], where)
+
+    def start(self):
+        def step(k, carry):
+            zz = far_first(self.nz, self.place[0], k)
+            for rel in (3, 1, 2, 0):
+                self.pair(zz, rel).start()
+                self.load(zz, rel).start()
+            return carry
+
+        lax.fori_loop(0, self.nz, step, 0)
+
+    def first(self, k):
+        zz = far_first(self.nz, self.place[0], k)
+        for rel in (3, 1, 2, 0):
+            self.pair(zz, rel).wait_recv()
+            self.load(zz, rel).wait()
+            add_blocks(self.w.at[zz, rel], [self.lp.at[zz, rel]], 0, self.rows)
+            if rel == 3:
+                for copy in self.across(zz):
+                    copy.start()
+
+    def second(self, k):
+        zz = far_first(self.nz, self.place[0], k)
+        across, (to_x, to_y) = self.across(zz), self.sides(zz)
+        if self.cut < self.rows:
+            across[-1].wait_recv()
+            add_blocks(self.w.at[zz, 1], [self.ryd.at[zz]], self.cut, self.rows - self.cut)
+        to_x.start()
+        if self.cut > 0:
+            across[0].wait_recv()
+            add_blocks(self.w.at[zz, 2], [self.rxd.at[zz]], 0, self.cut)
+        to_y.start()
+
+    def send_line(self, zz):
+        z = self.place[0]
+        pl.when(zz > z)(lambda: self.line(zz, zz, self.up).start())
+        pl.when(zz == z - 1)(lambda: self.line(zz, self.nz, self.down).start())
+        pl.when(zz < z - 1)(lambda: self.line(zz, zz, self.down).start())
+
+    def passes(self, zz):
+        z = self.place[0]
+        return ((zz > z) & (z > 0)) | ((zz < z) & (z < self.nz - 1))
+
+    def third(self, k):
+        zz, z = far_first(self.nz, self.place[0], k), self.place[0]
+        to_x, to_y = self.sides(zz)
+        to_x.wait_recv()
+        to_y.wait_recv()
+        add_blocks(self.w.at[zz, 0], [self.rx.at[zz], self.ry.at[zz]], 0, self.rows)
+        pl.when((zz != z) & jnp.logical_not(self.passes(zz)))(lambda: self.send_line(zz))
+
+    def fourth(self, k):
+        zz, z, nz = far_first(self.nz, self.place[0], k), self.place[0], self.nz
+
+        @pl.when((zz != z) & self.passes(zz))
+        def _():
+            self.line(zz, zz, self.up).wait_recv()
+            add_blocks(self.w.at[zz, 0], [self.rz.at[zz]], 0, self.rows)
+            self.send_line(zz)
+
+        @pl.when(zz == z)
+        def _():
+            finish_line(self, self.w.at[zz, 0], zz)
+
+    def finish(self):
+        z = self.place[0]
+
+        def step(zz, carry):
+            for rel in range(4):
+                self.pair(zz, rel).wait_send()
+            for copy in tuple(self.across(zz)) + tuple(self.sides(zz)):
+                copy.wait_send()
+            pl.when(zz != z)(lambda: self.line(zz, zz, self.up).wait_send())
+            return carry
+
+        lax.fori_loop(0, self.nz, step, 0)
+
+
+def finish_line(self, own, zz):
+    z, nz = self.place[0], self.nz
+    below, above = self.rz.at[zz], self.rz.at[nz]
+    pl.when(z > 0)(lambda: self.line(zz, zz, self.up).wait_recv())
+    pl.when(z < nz - 1)(lambda: self.line(zz, nz, self.down).wait_recv())
+    pl.when(z == 0)(lambda: add_blocks(own, [above], 0, self.rows, self.out))
+    pl.when(z == nz - 1)(lambda: add_blocks(own, [below], 0, self.rows, self.out))
+    pl.when((z > 0) & (z < nz - 1))(lambda: add_blocks(own, [below, above], 0, self.rows, self.out))
+
+
+class ReduceRows:
+    @staticmethod
+    def scratch(nz, rows, cols, kind):
+        vm, dma = pltpu.VMEM, pltpu.SemaphoreType.DMA
+        return [vm((nz, rows, cols), kind), vm((nz, rows, cols), kind),
+                vm((nz + 1, rows, cols), kind)] + [dma((nz,))] * 4 + [dma((nz + 1,))]
+
+    def __init__(self, nz, partial, out, refs):
+        self.w, self.rx, self.rz, self.s_l, self.s_x, self.s_z, self.r_x, self.r_z = refs
+        self.nz, self.partial, self.out = nz, partial, out
+        self.rows = out.shape[0]
+        self.place = z, x, y, c = place()
+        self.xn = device(z, 1 - x, y, c)
+        self.up, self.down = device(z + 1, x, y, c), device(z - 1, x, y, c)
+
+    def block(self, zz, xx):
+        return self.partial.at[pl.ds(pl.multiple_of((zz * 2 + xx) * self.rows, self.rows), self.rows)]
+
+    def side(self, zz):
+        return remote(self.block(zz, 1 - self.place[1]), self.rx.at[zz],
+                      self.s_x.at[zz], self.r_x.at[zz], self.xn)
+
+    def load(self, zz):
+        return pltpu.make_async_copy(self.block(zz, self.place[1]), self.w.at[zz], self.s_l.at[zz])
+
+    def line(self, zz, slot, where):
+        return remote(self.w.at[zz], self.rz.at[slot], self.s_z.at[zz], self.r_z.at[slot], where)
+
+    def start(self):
+        def step(k, carry):
+            zz = far_first(self.nz, self.place[0], k)
+            self.side(zz).start()
+            self.load(zz).start()
+            return carry
+
+        lax.fori_loop(0, self.nz, step, 0)
+
+    send_line = ScatterAll.send_line
+    passes = ScatterAll.passes
+
+    def first(self, k):
+        zz, z = far_first(self.nz, self.place[0], k), self.place[0]
+        self.load(zz).wait()
+        self.side(zz).wait_recv()
+        add_blocks(self.w.at[zz], [self.rx.at[zz]], 0, self.rows)
+        pl.when((zz != z) & jnp.logical_not(self.passes(zz)))(lambda: self.send_line(zz))
+
+    def second(self, k):
+        zz, z, nz = far_first(self.nz, self.place[0], k), self.place[0], self.nz
+
+        @pl.when((zz != z) & self.passes(zz))
+        def _():
+            self.line(zz, zz, self.up).wait_recv()
+            add_blocks(self.w.at[zz], [self.rz.at[zz]], 0, self.rows)
+            self.send_line(zz)
+
+        @pl.when(zz == z)
+        def _():
+            finish_line(self, self.w.at[zz], zz)
+
+    def finish(self):
+        z = self.place[0]
+
+        def step(zz, carry):
+            self.side(zz).wait_send()
+            pl.when(zz != z)(lambda: self.line(zz, zz, self.up).wait_send())
+            return carry
+
+        lax.fori_loop(0, self.nz, step, 0)
+
+
+def attend_back_kernel(nz, q_ref, k_ref, v_ref, start_ref, lse_ref, delta_ref, grad_ref,
+                       gp_ref, up_ref, hid_ref, xr_all, gs_all, out_part, wo_part,
+                       q_side, sides, out_sum, wo_sum, dwg, dwu, dwd,
+                       acc, k_acc, v_acc, x_panel, g_panel, o_gate, o_up, o_down, s_in, s_out, *refs):
+    shards = 2 * nz
+    shard = lax.axis_index("fsdp")
+    width = k_ref.shape[1]
+    block = q_ref.shape[0] // 2
+    heads = q_ref.shape[1] // width
+    z, x, y, c = place()
+    count = shards + 2 * x
+    panel = x_panel.shape[1]
+    panels = xr_all.shape[1] // panel
+    low = jnp.bfloat16
+    split = len(ScatterAll.scratch(nz, 16, 128, low, 0))
+    outs = ScatterAll(nz, out_part, out_sum, refs[:split], 0)
+    weights = ReduceRows(nz, wo_part, wo_sum, refs[split:])
+    greet([(None, outs.partner), (None, outs.xn), (None, outs.yn),
+           (z < nz - 1, outs.up), (z > 0, outs.down)])
+    outs.start()
+    weights.start()
+
+    def loads(n):
+        at = pl.ds(pl.multiple_of(n * panel, panel), panel)
+        return (pltpu.make_async_copy(xr_all.at[:, at], x_panel, s_in.at[0]),
+                pltpu.make_async_copy(gs_all.at[:, at], g_panel, s_in.at[1]))
+
+    def stores(n):
+        at = pl.ds(pl.multiple_of(n * panel, panel), panel)
+        return (pltpu.make_async_copy(o_gate, dwg.at[at, :], s_out.at[0]),
+                pltpu.make_async_copy(o_up, dwu.at[at, :], s_out.at[1]),
+                pltpu.make_async_copy(o_down, dwd.at[:, at], s_out.at[2]))
+
+    for copy in loads(0):
+        copy.start()
+    sides[...] = jnp.zeros_like(sides)
+    acc[...] = jnp.zeros_like(acc)
+
+    def attention(u):
+        micro, here, key_place, rows = stream_unit(u, nz, block)
+        bias = key_bias(micro, here, key_place, block, start_ref)
+        keys, values = k_ref[rows, :], v_ref[rows, :]
+        q_rows = pl.ds(pl.multiple_of(micro * block, block), block)
+        k_acc[...] = jnp.zeros_like(k_acc)
+        v_acc[...] = jnp.zeros_like(v_acc)
+
+        def head(h, carry):
+            at = micro * heads + h
+            cols = pl.ds(pl.multiple_of(h * width, width), width)
+            query, grad = q_ref[q_rows, cols], grad_ref[q_rows, cols]
+            scores = dot_last(keys, query) * width ** (-0.5) + bias
+            probs = jnp.exp(scores - lse_ref[at])
+            score_grad = (probs * (dot_last(values, grad) - delta_ref[at])).astype(low)
+            v_acc[...] += dot_plain(probs.astype(low), grad)
+            k_acc[...] += dot_plain(score_grad, query)
+            acc[at] += dot_first(keys, score_grad)
+            return carry
+
+        lax.fori_loop(0, heads, head, 0, unroll=2)
+        sides[rows, pl.ds(0, width)] = (k_acc[...] * width ** (-0.5)).astype(low)
+        sides[rows, pl.ds(width, width)] = v_acc[...].astype(low)
+
+    def expert_weights(n):
+        for copy in loads(n):
+            copy.wait()
+
+        @pl.when(n > 0)
+        def _():
+            for copy in stores(n):
+                copy.wait()
+
+        o_gate[...] = dot_first(x_panel[...], gp_ref[...])
+        o_up[...] = dot_first(x_panel[...], up_ref[...])
+        o_down[...] = dot_first(g_panel[...], hid_ref[...]).T
+        for copy in stores(n):
+            copy.start()
+
+        @pl.when(n < panels - 1)
+        def _():
+            for copy in loads(n + 1):
+                copy.start()
+
+    def unit(u, carry):
+        def at(fn, k):
+            pl.when((k >= 0) & (k < nz))(lambda: fn(k))
+
+        at(outs.first, u)
+        at(weights.first, u)
+        at(outs.second, u - 1)
+        at(weights.second, u - 1)
+        at(outs.third, u - 2)
+        at(outs.fourth, u - 3)
+        pl.when(u < count)(lambda: attention(u))
+        pl.when(u < panels)(lambda: expert_weights(u))
+        return carry
+
+    lax.fori_loop(0, max(shards + 2, panels), unit, 0)
+
+    def close(at, carry):
+        micro, h = at // heads, at % heads
+        q_side[pl.ds(pl.multiple_of(micro * block, block), block),
+               pl.ds(pl.multiple_of(h * width, width), width)] = acc[at].T * width ** (-0.5)
+        return carry
+
+    lax.fori_loop(0, 2 * heads, close, 0)
+    for copy in stores(panels - 1):
+        copy.wait()
+    outs.finish()
+    weights.finish()
+
+
+def attend_back(query, keys, values, starts, log_total, delta, grad, gate_grad, up_grad, hidden,
+                rows_in, pair_grad, out_part, wo_part, nz, collective_id):
+    rows, columns = query.shape
+    width = keys.shape[1]
+    heads = columns // width
+    block = rows // 2
+    pairs, features = rows_in.shape
+    hidden_width = hidden.shape[1]
+    panel = 256
+    cols = out_part.shape[1] // 4
+    wo_shape = (wo_part.shape[0] // (2 * nz), wo_part.shape[1])
+    any_space = pl.BlockSpec(memory_space=pl.ANY)
+    vmem = pl.BlockSpec(memory_space=pltpu.VMEM)
+    vm, shape, f32, low = pltpu.VMEM, jax.ShapeDtypeStruct, jnp.float32, jnp.bfloat16
+    dma = pltpu.SemaphoreType.DMA
+    return pl.pallas_call(
+        functools.partial(attend_back_kernel, nz),
+        in_specs=[vmem] * 10 + [any_space] * 4,
+        out_specs=[vmem] * 4 + [any_space] * 3,
+        out_shape=[
+            shape((rows, columns), f32), shape((rows * 2 * nz, 2 * width), low),
+            shape((rows, cols), f32), shape(wo_shape, f32),
+            shape((features, hidden_width), f32), shape((features, hidden_width), f32),
+            shape((hidden_width, features), f32),
+        ],
+        scratch_shapes=[
+            vm((2 * heads, width, block), f32), vm((block, width), f32), vm((block, width), f32),
+            vm((pairs, panel), low), vm((pairs, panel), low),
+            vm((panel, hidden_width), f32), vm((panel, hidden_width), f32),
+            vm((hidden_width, panel), f32), dma((2,)), dma((3,)),
+        ] + ScatterAll.scratch(nz, rows, cols, low, 0) + ReduceRows.scratch(nz, *wo_shape, low),
+        compiler_params=pltpu.CompilerParams(
+            collective_id=collective_id, has_side_effects=True, vmem_limit_bytes=63 << 20
+        ),
+        name="attend_back",
+    )(query, keys, values, starts, log_total, delta, grad, gate_grad, up_grad, hidden,
+      rows_in, pair_grad, out_part, wo_part)
 
 
 def gathered_body(
@@ -1733,17 +2394,18 @@
     block_keys = micro_rows * math.gcd(shard_count, max(1, 512 // micro_rows))
     my_columns = group_index * slice_width
 
-    mirror_index = shard_count - 1 - shard_index
+    mirror_index = mirrored(nz, shard_index)
     owners = jnp.stack([shard_index, mirror_index])
 
     def to_owners(array):
-        return jnp.stack([array[:, 0], array[::-1, 1]], axis=1)
+        second = array[:, 1].reshape((nz, 2) + array.shape[2:])[::-1].reshape(array[:, 1].shape)
+        return jnp.stack([array[:, 0], second], axis=1)
 
     small = jnp.concatenate([routes.reshape(-1), doc_ids.reshape(-1)])
     small_rows = -(-small.shape[0] // 1024) * 8
     small = jnp.pad(small, (0, small_rows * 128 - small.shape[0])).reshape(small_rows, 128)
-    small_all, wq_all, wk_all, wv_all, wo_all, tokens, cotangent, full_tokens = gather_rows(
-        [small, w_query, key_weight, value_weight, w_out], nz, 2, [tokens, cotangent]
+    small_all, wq_all, wk_all, wv_all, tokens, full_tokens = gather_rows(
+        [small, w_query, key_weight, value_weight], nz, 2, [tokens]
     )
     small_all = small_all.reshape(shard_count, small_rows * 128)
     routes_all = to_owners(
@@ -1766,7 +2428,6 @@
     cosine_lookup, sine_lookup = rope_tables(positions, head_width)
 
     full_tokens = full_tokens.astype(f32)
-    grads_all = gather_all(cotangent, nz, 3)
     token_mean = jnp.mean(full_tokens * full_tokens, axis=-1, keepdims=True)
     token_scale = lax.rsqrt(token_mean + norm_eps)
     normed_low = (full_tokens * token_scale * gain_attn).astype(low)
@@ -1794,30 +2455,11 @@
     key_low = key_heads.reshape(row_count, kv_width).astype(low)
     keys_got, values_got = gather_rows([key_low, value_low], nz, 4)
 
-    def by_stream(array):
-        array = array.reshape(shard_count, micro_count, micro_rows, kv_width)
-        return to_owners(array).transpose(1, 0, 2, 3).reshape(
-            micro_count, shard_count * micro_rows, kv_width
-        )
-
-    keys_all, values_all = by_stream(keys_got), by_stream(values_got)
-    row_index = jnp.tile(query_index, (1, group_width))
-    saved, head_parts = [], []
-    for micro_index in range(micro_count):
-        here = slice(micro_index * micro_rows, (micro_index + 1) * micro_rows)
-        queries = to_heads(query_low[here], kv_local, group_width)
-        row_start = jnp.tile(query_start[micro_index], group_width)
-        head_out, log_total = attend_forward(
-            queries,
-            keys_all[micro_index],
-            values_all[micro_index],
-            row_index[micro_index],
-            row_start,
-            block_keys,
-        )
-        saved.append((queries, row_start, head_out, log_total))
-        head_parts.append(to_tokens(head_out, group_width).astype(low))
-    heads_low = jnp.concatenate(head_parts, axis=0)
+    starts = query_start.reshape(micro_count, 1, micro_rows).astype(jnp.int32)
+    heads_low, head_out, log_total, grads_all, wo_all = attend(
+        query_low.reshape(row_count, query_width), keys_got, values_got,
+        starts, cotangent, w_out, nz, 3,
+    )
     attn_part = dot_last(heads_low, wo_all).astype(low)
     middle = tokens.astype(f32) + reduce_cols(attn_part, 5)
 
@@ -1836,9 +2478,6 @@
     rows_in, pair_grad, hidden_low, gate_pre_low, up_pre_low = (
         array.reshape(-1, array.shape[2]) for array in kept
     )
-    gate_acc = dot_first(rows_in, gate_pre_low)
-    up_acc = dot_first(rows_in, up_pre_low)
-    down_acc = dot_first(hidden_low, pair_grad)
     gates_grad = swap_rows(
         gates_grad.reshape(shard_count, row_count // 128, 128), shard_count, group_count, 9
     ).reshape(expert_total, row_count).T
@@ -1851,7 +2490,10 @@
         moe_low.astype(f32), logit_grad, (((0,), (0,)), ((), ())), precision=highest_precision
     )
     gain_moe_part = jnp.sum(moe_grad * middle * scale, axis=0)
-    grad_slice = cotangent.astype(f32)
+    swapped_grad = lax.dynamic_slice(
+        grads_all, (mirror_index * row_count + micro_rows, my_columns), (micro_rows, slice_width)
+    )
+    grad_slice = jnp.concatenate([cotangent[:micro_rows], swapped_grad], axis=0).astype(f32)
     inner = gain_slice * moe_grad
     middle_grad = (
         grad_slice + scale * inner - middle * scale**3 * row_mean(middle * inner, 10)
@@ -1859,35 +2501,20 @@
     middle_low = gather_cols(middle_grad.astype(low), 11)
     out_grad_part = dot_first(middle_low, heads_low).astype(low)
     heads_grad = jnp.dot(middle_low, wo_all, preferred_element_type=f32).astype(low)
-    block_out = (middle + scatter_all(out_part, nz, 12)).astype(low)
-    w_out_grad = reduce_rows(out_grad_part, nz, 13)
-    query_sides, key_sides = [], []
-    for micro_index in range(micro_count):
-        here = slice(micro_index * micro_rows, (micro_index + 1) * micro_rows)
-        queries, row_start, head_out, log_total = saved[micro_index]
-        grad_low = to_heads(
-            heads_grad[here].reshape(micro_rows, query_local, head_width), kv_local, group_width
-        )
-        query_side, key_side, value_side = attend_backward(
-            queries,
-            keys_all[micro_index],
-            values_all[micro_index],
-            row_index[micro_index],
-            row_start,
-            block_keys,
-            head_out,
-            log_total,
-            grad_low,
-        )
-        query_sides.append(to_tokens(query_side, group_width))
-        key_sides.append(jnp.concatenate([key_side, value_side], axis=1).astype(low))
-    sides = jnp.stack(key_sides).reshape(micro_count, shard_count, micro_rows, 2 * kv_width)
-    sides = reduce_rows(
-        to_owners(sides.transpose(1, 0, 2, 3)).reshape(shard_count * row_count, 2 * kv_width), nz, 14
-    )
+    delta = jnp.sum(
+        (heads_grad.astype(f32) * head_out).reshape(micro_count, micro_rows, query_local, head_width),
+        axis=3,
+    ).transpose(0, 2, 1).reshape(micro_count * query_local, 1, micro_rows)
+    query_side, sides, out_sum, w_out_grad, gate_acc, up_acc, down_acc = attend_back(
+        query_low.reshape(row_count, query_width), keys_got, values_got, starts, log_total, delta,
+        heads_grad, gate_pre_low, up_pre_low, hidden_low, rows_in, pair_grad, out_part,
+        out_grad_part, nz, 12,
+    )
+    block_out = (middle + out_sum).astype(low)
+    sides = reduce_rows(sides, nz, 14)
     query_pre_grad, key_pre_grad, gain_query_part, gain_key_part = heads_pull(
         (
-            jnp.concatenate(query_sides, axis=0).reshape(row_count, query_local, head_width),
+            query_side.reshape(row_count, query_local, head_width),
             sides[:, :kv_width].reshape(row_count, kv_local, head_width),
         )
     )

time: 1040 us -> 922 us (0.89)
  matrix products: 121 us -> 32.6 us
    pallas_call x1 -> x2, Pallas kernels: 77.9 us -> 245 us  [the longest x1 128 us: attend_back(): pl.pallas_call(functools.partial(attend_back_kernel, nz), in_specs=[vmem]...]
    pallas_call x2 -> x1, Pallas kernels: 165 us -> 86.9 us  [gather_all(): pl.pallas_call(functools.partial(gather_all_kernel, nz), out_shape=jax.Sh...]
    dot_general x35 -> x0, matrix products: 59 us -> none  [the longest x10 17 us: block_scores(): jnp.einsum('hrd,khd->hrk', queries, keys_part, preferred_element_type=jnp...]
    pallas_call x2, Pallas kernels: 156 us -> 106 us  [gather_rows(): pl.pallas_call(functools.partial(gather_rows_kernel, nz, count, columns),...]
    pallas_call x3 -> x2, Pallas kernels: 143 us -> 100 us  [reduce_rows(): pl.pallas_call(functools.partial(reduce_rows_kernel, nz), out_shape=jax.S...]
    dot_general x5 -> x2, matrix products: 39.4 us -> 10.8 us  [dot_first(): lax.dot_general(left_side, right_side, (((0,), (0,)), ((), ())), preferre...]
    unnamed x141 -> x163, local copies, waits for them, and re-layouts: 12.5 us -> 30.7 us
where the time goes in v3:
time: 922 us; the launch traced here: 912 us
  Pallas kernels  785 us (85%)
  local copies, waits for them, and re-layouts  48.3 us (5%)
  other arithmetic  43.9 us (5%)
  matrix products  32.6 us (4%)
    pallas_call x1, Pallas kernels, run_experts(): pl.pallas_call(functools.partial(expert_kernel, nz, slots, block_rows), i...  132 us
    pallas_call x1, Pallas kernels, attend_back(): pl.pallas_call(functools.partial(attend_back_kernel, nz), in_specs=[vmem]...  128 us
    pallas_call x1, Pallas kernels, attend(): pl.pallas_call(functools.partial(attend_kernel, nz), in_specs=[vmem] * 4...  118 us
    pallas_call x2, Pallas kernels, gather_rows(): pl.pallas_call(functools.partial(gather_rows_kernel, nz, count, columns),...  106 us
    pallas_call x2, Pallas kernels, reduce_rows(): pl.pallas_call(functools.partial(reduce_rows_kernel, nz), out_shape=jax.S...  100 us
    pallas_call x1, Pallas kernels, gather_all(): pl.pallas_call(functools.partial(gather_all_kernel, nz), out_shape=jax.Sh...  86.9 us
    unnamed x163, local copies, waits for them, and re-layouts  30.7 us
    pallas_call x2, Pallas kernels, reduce_cols(): pl.pallas_call(reduce_cols_kernel, out_shape=jax.ShapeDtypeStruct((rows,...  29.4 us

profile of v3, /device:TPU:0, one launch (start us, length us, event | category | flops | bytes accessed | tf_op | source)
XLA Modules:
  0.0 911.9 jit_solution(16465832401042502909)
XLA Ops:
  3.0 81.1 %gather_rows.2 = (s32[320,128]{1,0:T(8,128)}, bf16[2048,1024]{1,0:T(8,128)(2,1)}, bf16[2048,128]{1,0:T(8,128)(2,1)}, bf16[2048,128]{1,0:T(8,128)(2,1)}, bf16[512...) custom-call(s32[40,128]{1,0:T(8,128)} %pad_bitcast_fusion.refs_0_, bf16[256,1024]{1,0:T(8,128)(2,1)} %refs_1_.1, ...), custom_call_target="tpu_custom_call" | custom-call | tf_op jit(solution)/shard_map/gather_rows/pallas_call | solution.py:1000
  86.9 4.6 fusion.39
  94.6 2.7 slice_negate_fusion.1
  103.4 2.4 maximum_multiply_fusion
  110.9 24.9 %gather_rows.3 = (bf16[4096,128]{1,0:T(8,128)(2,1)}, bf16[4096,128]{1,0:T(8,128)(2,1)}) custom-call(bf16[512,128]{1,0:T(8,128)(2,1)} %get-tuple-element.177.refs_0_, bf16[512,128]{1,0:T(8,128)(2,1)} %convolution_convert_fusion.4.refs_1_), custom_call_target="tpu_custom_call" | custom-call | tf_op jit(solution)/shard_map/gather_rows/pallas_call | solution.py:1000
  138.2 117.6 %attend.1 = (bf16[512,1024]{1,0:T(8,128)(2,1)S(1)}, f32[512,1024]{1,0:T(8,128)S(1)}, f32[16,1,256]{2,1,0:T(1,128)S(1)}, bf16[4096,2048]{1,0:T(8,128)(2,1)}, bf16[2048,1024]{1,0:T(8,128)(2,1)S(1)}) custom-call(bf16[512,1024]{1,0:T(8,128)(2,1)S(1)} %fusion.6.q_ref, bf16[4096,128]{1,0:T(8,128)(2,1)S(1)} %copy-done.1, bf16[4096,128]{1,0:T(8,128)(2,1)S(1)} %copy-done.2, ...), custom_call_target="tpu_custom_call" | custom-call | tf_op jit(solution)/shard_map/attend/pallas_call | solution.py:1974
  255.8 2.4 convolution_convert_fusion.2.p_ref
  258.8 14.3 %reduce_cols.2 = f32[512,512]{1,0:T(8,128)S(1)} custom-call(bf16[512,2048]{1,0:T(8,128)(2,1)S(1)} %convolution_convert_fusion.2.p_ref), custom_call_target="tpu_custom_call" | custom-call | tf_op jit(solution)/shard_map/reduce_cols/pallas_call | solution.py:1208
  274.0 5.4 sum_cols.3
  281.8 86.9 %gather_all.1.x_all = bf16[4096,2048]{1,0:T(8,128)(2,1)} custom-call(bf16[512,512]{1,0:T(8,128)(2,1)} %multiply_convert_fusion.x_ref), custom_call_target="tpu_custom_call" | custom-call | tf_op jit(solution)/shard_map/gather_all/pallas_call | solution.py:685
  368.7 2.5 reshape.332
  371.2 2.7 fusion.44
  375.0 3.1 pad_add_fusion
  379.1 132.0 %experts.1 = (bf16[4096,2048]{1,0:T(8,128)(2,1)}, f32[512,512]{1,0:T(8,128)}, f32[8,1,512]{2,1,0:T(1,128)}, f32[512,32]{1,0:T(8,128)}, bf16[8,256,2048]{2,1,0:T(...) custom-call(bf16[4096,2048]{1,0:T(8,128)(2,1)} %gather_all.1.x_all, ...), custom_call_target="tpu_custom_call" | custom-call | tf_op jit(solution)/shard_map/experts/pallas_call | solution.py:1682
  511.2 9.6 %swap_rows.1 = f32[32,4,128]{2,1,0:T(4,128)} custom-call(f32[8,4,128]{2,1,0:T(4,128)} %bitcast.182), custom_call_target="tpu_custom_call" | custom-call | tf_op jit(solution)/shard_map/swap_rows/pallas_call | solution.py:1290
  524.7 2.7 multiply_reduce_fusion.3
  527.3 4.9 sum_cols.4
  535.4 17.6 %gather_cols.1 = bf16[512,2048]{1,0:T(8,128)(2,1)} custom-call(bf16[512,512]{1,0:T(8,128)(2,1)} %get-tuple-element.157.x_ref), custom_call_target="tpu_custom_call" | custom-call | tf_op jit(solution)/shard_map/gather_cols/pallas_call | solution.py:1164
  553.0 5.3 convolution_convert_fusion.3.grad_ref
  561.1 6.0 convolution_convert_fusion.1.wo_part
  567.1 127.6 %attend_back.1 = (f32[512,1024]{1,0:T(8,128)}, bf16[4096,256]{1,0:T(8,128)(2,1)}, f32[512,512]{1,0:T(8,128)}, f32[256,1024]{1,0:T(8,128)}, f32[2048,768]{1,0:T(8...) custom-call(bf16[512,1024]{1,0:T(8,128)(2,1)} %copy-done, bf16[4096,128]{1,0:T(8,128)(2,1)} %get-tuple-element.51.k_ref, ...), custom_call_target="tpu_custom_call" | custom-call | tf_op jit(solution)/shard_map/attend_back/pallas_call | solution.py:2336
  703.8 3.5 fusion.3
  709.7 37.8 %reduce_rows.2 = f32[512,256]{1,0:T(8,128)S(1)} custom-call(bf16[4096,256]{1,0:T(8,128)(2,1)S(1)} %copy-done.3), custom_call_target="tpu_custom_call" | custom-call | tf_op jit(solution)/shard_map/reduce_rows/pallas_call | solution.py:1122
  750.6 15.1 %reduce_cols.3 = f32[512,512]{1,0:T(8,128)S(1)} custom-call(bf16[512,2048]{1,0:T(8,128)(2,1)S(1)} %add_convert_fusion.p_ref), custom_call_target="tpu_custom_call" | custom-call | tf_op jit(solution)/shard_map/reduce_cols/pallas_call | solution.py:1208
  767.6 5.0 sum_cols.5
  774.4 16.2 %swap_back.1 = (bf16[256,512]{1,0:T(8,128)(2,1)}, bf16[256,512]{1,0:T(8,128)(2,1)}) custom-call(bf16[256,512]{1,0:T(8,128)(2,1)} %get-tuple-element.172.refs_0_, bf16[256,512]{1,0:T(8,128)(2,1)} %get-tuple-element.170.refs_1_), custom_call_target="tpu_custom_call" | custom-call | tf_op jit(solution)/shard_map/swap_back/pallas_call | solution.py:1031
  795.8 26.3 %sum_small.1 = f32[32,24,128]{2,1,0:T(8,128)} custom-call(f32[8,24,128]{2,1,0:T(8,128)} %bitcast.179), custom_call_target="tpu_custom_call" | custom-call | tf_op jit(solution)/shard_map/sum_small/pallas_call | solution.py:1339
  824.9 4.9 convolution_convert_fusion.p_ref
  829.7 62.5 %reduce_rows.3 = f32[256,1280]{1,0:T(8,128)S(1)} custom-call(bf16[2048,1280]{1,0:T(8,128)(2,1)} %convolution_convert_fusion.p_ref), custom_call_target="tpu_custom_call" | custom-call | tf_op jit(solution)/shard_map/reduce_rows/pallas_call | solution.py:1122
  898.9 6.5 copy.120
  905.4 2.8 copy.121
  908.7 2.7 copy.122
  (250 shorter events, 70.1 us)
Async XLA Ops:
  0.6 86.2 %copy-start.63 = (f32[2048]{0:T(1024)S(1)}, f32[2048]{0:T(1024)}, u32[]{:S(2)}) copy-start(f32[2048]{0:T(1024)} %param.20) | copy-start | bytes 24580
  98.3 5.1 copy-start.20
  98.5 4.9 copy-start.17
  101.1 4.7 copy-start.29
  109.4 26.4 %copy-start = (bf16[512,1024]{1,0:T(8,128)(2,1)}, bf16[512,1024]{1,0:T(8,128)(2,1)S(1)}, u32[]{:S(2)}) copy-start(bf16[512,1024]{1,0:T(8,128)(2,1)S(1)} %fusion.6.q_ref) | copy-start | bytes 3145732
  109.4 26.3 %copy-start.6 = (bf16[512,512]{1,0:T(8,128)(2,1)S(1)}, bf16[512,512]{1,0:T(8,128)(2,1)}, u32[]{:S(2)}) copy-start(bf16[512,512]{1,0:T(8,128)(2,1)} %cot_ref.1) | copy-start | bytes 1572868
  109.4 26.3 %copy-start.7 = (bf16[256,1024]{1,0:T(8,128)(2,1)S(1)}, bf16[256,1024]{1,0:T(8,128)(2,1)}, u32[]{:S(2)}) copy-start(bf16[256,1024]{1,0:T(8,128)(2,1)} %wo_ref.1) | copy-start | bytes 1572868
  138.2 117.6 %copy-start.8 = (s32[2,1,256]{2,1,0:T(1,128)}, s32[2,1,256]{2,1,0:T(1,128)S(1)}, u32[]{:S(2)}) copy-start(s32[2,1,256]{2,1,0:T(1,128)S(1)} %reshape.330.start_ref) | copy-start | bytes 6148
  258.8 14.3 %copy-start.23 = (bf16[512,512]{1,0:T(8,128)(2,1)S(1)}, bf16[512,512]{1,0:T(8,128)(2,1)}, u32[]{:S(2)}) copy-start(bf16[512,512]{1,0:T(8,128)(2,1)} %get-tuple-element.45) | copy-start | bytes 1572868
  274.0 259.9 %copy-start.15 = (f32[512,512]{1,0:T(8,128)}, f32[512,512]{1,0:T(8,128)S(1)}, u32[]{:S(2)}) copy-start(f32[512,512]{1,0:T(8,128)S(1)} %get-tuple-element.160) | copy-start | bytes 3145732
  522.8 10.0 %copy-start.52 = (f32[4,128]{1,0:T(4,128)S(1)}, f32[4,128]{1,0:T(4,128)}, u32[]{:S(2)}) copy-start(f32[4,128]{1,0:T(4,128)} %sum_cols.3) | copy-start | bytes 6148
  524.7 9.2 %slice-start = ((bf16[512,512]{1,0:T(8,128)(2,1)}), bf16[256,512]{1,0:T(8,128)(2,1)S(1)}, s32[]{:S(2)}) async-start(bf16[512,512]{1,0:T(8,128)(2,1)} %cot_ref.1), calls=%async_computation | async-start | bytes 524288 | tf_op jit(solution)/shard_map/slice | solution.py:2496
  553.0 5.3 copy-start.5
  703.8 3.5 copy-start.66
  709.7 37.8 %copy-start.30 = (f32[512,64]{1,0:T(8,128)S(1)}, f32[512,64]{1,0:T(8,128)}, u32[]{:S(2)}) copy-start(f32[512,64]{1,0:T(8,128)} %copy-done.29) | copy-start | bytes 393220
  709.7 38.1 %copy-start.21 = (f32[512,128]{1,0:T(8,128)S(1)}, f32[512,128]{1,0:T(8,128)}, u32[]{:S(2)}) copy-start(f32[512,128]{1,0:T(8,128)} %copy-done.20) | copy-start | bytes 786436
  709.7 38.1 %copy-start.36 = (f32[512,64]{1,0:T(8,128)S(1)}, f32[512,64]{1,0:T(8,128)}, u32[]{:S(2)}) copy-start(f32[512,64]{1,0:T(8,128)} %copy-done.35) | copy-start | bytes 393220
  709.7 38.1 %copy-start.59 = (f32[128]{0:T(128)S(1)}, f32[128]{0:T(128)}, u32[]{:S(2)}) copy-start(f32[128]{0:T(128)} %param.26) | copy-start | bytes 1540
  750.6 15.9 %copy-start.24 = (bf16[512,512]{1,0:T(8,128)(2,1)S(1)}, bf16[512,512]{1,0:T(8,128)(2,1)}, u32[]{:S(2)}) copy-start(bf16[512,512]{1,0:T(8,128)(2,1)} %get-tuple-element.45) | copy-start | bytes 1572868
  750.6 22.7 %copy-start.26 = (f32[512,512]{1,0:T(8,128)S(1)}, f32[512,512]{1,0:T(8,128)}, u32[]{:S(2)}) copy-start(f32[512,512]{1,0:T(8,128)} %get-tuple-element.158) | copy-start | bytes 3145732
  750.6 22.7 %copy-start.55 = (f32[512]{0:T(512)S(1)}, f32[512]{0:T(512)}, u32[]{:S(2)}) copy-start(f32[512]{0:T(512)} %get-tuple-element.186) | copy-start | bytes 6148
  773.3 17.3 %copy-start.44 = (bf16[256,512]{1,0:T(8,128)(2,1)S(1)}, bf16[256,512]{1,0:T(8,128)(2,1)}, u32[]{:S(2)}) copy-start(bf16[256,512]{1,0:T(8,128)(2,1)} %get-tuple-element.171) | copy-start | bytes 786436
  773.6 20.6 %copy-start.22 = (bf16[512,512]{1,0:T(8,128)(2,1)S(1)}, bf16[512,512]{1,0:T(8,128)(2,1)}, u32[]{:S(2)}) copy-start(bf16[512,512]{1,0:T(8,128)(2,1)} %multiply_convert_fusion.x_ref) | copy-start | bytes 1572868
  773.6 20.6 %copy-start.38 = (f32[512,32]{1,0:T(8,128)S(1)}, f32[512,32]{1,0:T(8,128)}, u32[]{:S(2)}) copy-start(f32[512,32]{1,0:T(8,128)} %copy-done.37) | copy-start | bytes 196612
  774.4 20.7 %copy-start.60 = (f32[512]{0:T(512)S(1)}, f32[512]{0:T(512)}, u32[]{:S(2)}) copy-start(f32[512]{0:T(512)} %get-tuple-element.148) | copy-start | bytes 6148
  774.4 20.8 %copy-start.61 = (f32[128]{0:T(128)S(1)}, f32[128]{0:T(128)}, u32[]{:S(2)}) copy-start(f32[128]{0:T(128)} %get-tuple-element.146) | copy-start | bytes 1540
  774.4 20.8 %copy-start.62 = (f32[128]{0:T(128)S(1)}, f32[128]{0:T(128)}, u32[]{:S(2)}) copy-start(f32[128]{0:T(128)} %get-tuple-element.152) | copy-start | bytes 1540
  792.4 31.5 %copy-start.28 = (bf16[512,8,128]{2,1,0:T(8,128)(2,1)S(1)}, bf16[512,8,128]{2,1,0:T(8,128)(2,1)}, u32[]{:S(2)}) copy-start(bf16[512,8,128]{2,1,0:T(8,128)(2,1)} %copy-done.27) | copy-start | bytes 3145732
  795.0 29.2 %copy-start.65 = (f32[2048]{0:T(1024)S(1)}, f32[2048]{0:T(1024)}, u32[]{:S(2)}) copy-start(f32[2048]{0:T(1024)} %param.20) | copy-start | bytes 24580
  895.2 10.2 %slice-start.3 = ((s8[6291456]{0:T(1024)(128)(4,1)}), s8[2097152]{0:T(1024)(128)(4,1)S(1)}, s32[]{:S(2)}) async-start(s8[6291456]{0:T(1024)(128)(4,1)} %bitcast.159), calls=%async_computation.3 | async-start | bytes 4194304
  898.9 6.5 slice-start.4
  898.9 9.4 %slice-start.1 = ((s8[6291456]{0:T(1024)(128)(4,1)}), s8[4194304]{0:T(1024)(128)(4,1)S(1)}, s32[]{:S(2)}) async-start(s8[6291456]{0:T(1024)(128)(4,1)} %bitcast.156), calls=%async_computation.1 | async-start | bytes 8388608
  (40 other events, 73.4 us)

commit v4 on v3

--- a/solution.py
+++ b/solution.py
@@ -867,7 +867,7 @@
                         vm((nz + 1, rows, cols), kind)]
         + [dma((4 * nz,))] * 3 + [dma((nz,))] * 5 + [dma((nz,))] * 4 + [dma((nz + 1,))],
         compiler_params=pltpu.CompilerParams(collective_id=collective_id, has_side_effects=True,
-                                             vmem_limit_bytes=48 << 20),
+                                             vmem_limit_bytes=62 << 20),
         name="scatter_all",
     )(partial)
 
@@ -915,7 +915,7 @@
         for n in range(columns):
             src, dst = srcs[count + n], outs[count + n]
             swaps.append(remote(src.at[bottom], dst.at[bottom], s_w.at[n], r_w.at[n], mirror))
-            own.append((src.at[top], dst.at[top]))
+            dst[top, :] = src[top, :]
 
         def column(yy):
             return out.at[:, pl.ds(pl.multiple_of((yy * 2 + c) * cols, cols), cols)]
@@ -937,7 +937,8 @@
                 remote(src, dst, s_d.at[k], r_z.at[k], down),
                 remote(src, dst, s_x.at[k], r_x.at[k], xn))
 
-    for item in z_items(nz, True):
+    items = z_items(nz, True)
+    for item in items:
         dist, side = item
 
         def run(zz):
@@ -953,13 +954,12 @@
                 cx.start()
 
         z_guard(item, z, nz, run)
-        if columns and dist == 0:
-            own[count].wait()
+        if columns and item == items[-1]:
             swaps[0].wait_recv()
             column_copies[0].start()
             column_copies[1].start()
             last.start()
-        if columns and item == (1, 1):
+        if columns and item == items[-1]:
             column_copies[0].wait_recv()
             column_copies[2].start()
 
@@ -973,9 +973,8 @@
         return carry
 
     lax.fori_loop(0, nz, finish, 0)
-    for n, copy in enumerate(own):
-        if n != count:
-            copy.wait()
+    for copy in own:
+        copy.wait()
     if columns:
         column_copies[0].wait_send()
         column_copies[1].wait()
@@ -990,6 +989,7 @@
     count, columns = len(blocks), len(swapped)
     dma = pltpu.SemaphoreType.DMA
     any_space = pl.BlockSpec(memory_space=pl.ANY)
+    vmem = pl.BlockSpec(memory_space=pltpu.VMEM)
     shapes = [
         jax.ShapeDtypeStruct((b.shape[0] * nz * 2,) + b.shape[1:], b.dtype) for b in blocks
     ] + [jax.ShapeDtypeStruct(b.shape, b.dtype) for b in swapped]
@@ -1000,11 +1000,12 @@
     return pl.pallas_call(
         functools.partial(gather_rows_kernel, nz, count, columns),
         out_shape=shapes,
-        in_specs=[any_space] * total,
-        out_specs=[any_space] * len(shapes),
+        in_specs=[vmem] * total,
+        out_specs=[any_space] * count + [vmem] * columns + [any_space] * min(columns, 1),
         scratch_shapes=[dma((total + 1,))] + [dma((count * nz,))] * 5 + [dma((3,))] * 2
         + [dma((max(columns, 1),))] * 2,
-        compiler_params=pltpu.CompilerParams(collective_id=collective_id, has_side_effects=True),
+        compiler_params=pltpu.CompilerParams(collective_id=collective_id, has_side_effects=True,
+                                             vmem_limit_bytes=62 << 20),
         name="gather_rows",
     )(*blocks, *swapped)
 
@@ -1128,7 +1129,7 @@
                         vm((nz + 1, rows, cols), kind)]
         + [dma((nz,))] * 4 + [dma((nz + 1,))],
         compiler_params=pltpu.CompilerParams(
-            collective_id=collective_id, has_side_effects=True, vmem_limit_bytes=48 << 20
+            collective_id=collective_id, has_side_effects=True, vmem_limit_bytes=62 << 20
         ),
         name="reduce_rows",
     )(partial)
@@ -1213,7 +1214,7 @@
         scratch_shapes=[vm((2, rows, cols), kind), vm((2, rows, cols), kind), vm((rows, cols), kind),
                         dma((2,)), dma((2,)), dma, dma((2,)), dma],
         compiler_params=pltpu.CompilerParams(
-            collective_id=collective_id, has_side_effects=True, vmem_limit_bytes=24 << 20
+            collective_id=collective_id, has_side_effects=True, vmem_limit_bytes=62 << 20
         ),
         name="reduce_cols",
     )(partial)
@@ -1362,12 +1363,14 @@
 
 
 def expert_kernel(nz, slots, block_rows, x_all, g_all, routes_all, router_ref, wg, wu, wd,
-                  out_all, back_ref, gg_ref, gates_ref, xr_all, gs_all, hid_all, gp_all, up_all,
-                  x_ref, g_ref, t_ref, o_ref, xr, gs, hid, gp, up, st,
+                  out_all, back_ref, gg_got, gates_ref, xr_all, gs_all, hid_all, gp_all, up_all,
+                  gg_ref, x_ref, g_ref, t_ref, o_ref, xr, gs, hid, gp, up, st,
                   w, lp, rx, rxd, ry, ryd, rz,
-                  s_in, s_out, s_save, s_p, r_p, s_x, s_y, s_dx, s_dy, s_z, r_x, r_y, r_dx, r_dy, r_z):
+                  s_in, s_out, s_save, s_p, r_p, s_x, s_y, s_dx, s_dy, s_z, r_x, r_y, r_dx, r_dy, r_z,
+                  s_g, r_g):
     z, x, y, c = place()
-    expert = lax.axis_index("fsdp") * 4 + lax.axis_index("tp")
+    shard, group = lax.axis_index("fsdp"), lax.axis_index("tp")
+    expert = shard * 4 + group
     rows, cols = back_ref.shape
     width = x_ref.shape[1]
     half = rows // 2
@@ -1377,8 +1380,14 @@
     partner = device(z, x, y, 1 - c)
     xn, yn = device(z, 1 - x, y, c), device(z, x, 1 - y, c)
     up_dev, down_dev = device(z + 1, x, y, c), device(z - 1, x, y, c)
-    greet([(None, partner), (None, xn), (None, yn), (z < nz - 1, up_dev), (z > 0, down_dev)])
+    greet_all(shard, group, 2 * nz, 4)
     tiles = 2 * nz
+    devices = 8 * nz
+
+    def swap(k):
+        other = (expert + k) % devices
+        return remote(gg_ref.at[other // 4], gg_got.at[expert], s_g.at[k], r_g.at[k],
+                      (other // 4, other % 4))
 
     def tile_of(j):
         return far_first(nz, z, j // 2) * 2 + jnp.where(j % 2 == 0, 1 - x, x)
@@ -1386,9 +1395,8 @@
     def tile_rows(j):
         return pl.ds(pl.multiple_of(tile_of(j) * rows, rows), rows)
 
-    def load(j, kind):
-        src, dst = ((x_all, x_ref), None, (routes_all, t_ref))[kind]
-        return pltpu.make_async_copy(src.at[tile_rows(j)], dst, s_in.at[kind])
+    def load(j):
+        return pltpu.make_async_copy(x_all.at[tile_rows(j)], x_ref, s_in.at[0])
 
     def load_g(j):
         tile = tile_of(j)
@@ -1396,6 +1404,13 @@
         second = pl.ds(pl.multiple_of(mirrored(nz, tile) * rows + half, half), half)
         return (pltpu.make_async_copy(g_all.at[first], g_ref.at[pl.ds(0, half)], s_in.at[1]),
                 pltpu.make_async_copy(g_all.at[second], g_ref.at[pl.ds(half, half)], s_in.at[3]))
+
+    def load_t(j):
+        tile = tile_of(j)
+        first = pl.ds(pl.multiple_of(tile * rows, half), half)
+        second = pl.ds(pl.multiple_of(mirrored(nz, tile) * rows + half, half), half)
+        return (pltpu.make_async_copy(routes_all.at[first], t_ref.at[pl.ds(0, half)], s_in.at[2]),
+                pltpu.make_async_copy(routes_all.at[second], t_ref.at[pl.ds(half, half)], s_in.at[4]))
 
     def save_out(j):
         return pltpu.make_async_copy(o_ref, out_all.at[tile_rows(j)], s_out)
@@ -1474,8 +1489,9 @@
     def compute(j):
         zz = far_first(nz, z, j // 2)
         slot = j % 2
-        load(j, 2).wait()
-        load(j, 0).wait()
+        load(j).wait()
+        for copy in load_t(j):
+            copy.wait()
         lanes = lax.broadcasted_iota(jnp.int32, (rows, experts), 1)
         routes = t_ref[...]
         chosen = routes[:, 0:1] == lanes
@@ -1539,8 +1555,9 @@
 
         @pl.when(j < tiles - 1)
         def _():
-            load(j + 1, 2).start()
-            load(j + 1, 0).start()
+            load(j + 1).start()
+            for copy in load_t(j + 1):
+                copy.start()
 
         gate_pre = dot_plain(xr[...], wg[...])
         up_pre = dot_plain(xr[...], wu[...])
@@ -1619,12 +1636,17 @@
         lax.fori_loop(0, 2, to_partner, 0)
         lax.fori_loop(0, 2, to_own, 0)
 
-    for copy in (load(0, 2), load(0, 0)) + load_g(0):
+    for copy in (load(0),) + load_t(0) + load_g(0):
         copy.start()
 
     def step(j, carry):
         k, odd = j // 2, j % 2 == 1
         pl.when(j < tiles)(lambda: compute(j))
+
+        @pl.when(j == tiles)
+        def _():
+            gg_got[expert] = gg_ref[shard]
+            loop_from_one(devices, lambda n: swap(n).start())
 
         @pl.when(odd & (k < nz))
         def _():
@@ -1650,6 +1672,7 @@
         return carry
 
     lax.fori_loop(0, 2 * (nz + 2), step, 0)
+    loop_from_one(devices, lambda n: swap(n).wait())
     save_out(tiles - 1).wait()
     for copy in saves(tiles - 1):
         copy.wait()
@@ -1684,14 +1707,14 @@
         in_specs=[any_space] * 3 + [vmem] * 4,
         out_specs=[any_space, vmem, vmem, vmem] + [any_space] * 5,
         out_shape=[
-            shape((total, width), low), shape((rows, cols), f32), shape((tiles, 1, rows), f32),
+            shape((total, width), low), shape((rows, cols), f32), shape((4 * tiles, 1, rows), f32),
             shape((rows, experts), f32),
             shape((tiles, pairs, width), low), shape((tiles, pairs, width), low),
             shape((tiles, pairs, hidden), low), shape((tiles, pairs, hidden), low),
             shape((tiles, pairs, hidden), low),
         ],
         scratch_shapes=[
-            vm((rows, width), low), vm((rows, width), low),
+            vm((tiles, 1, rows), f32), vm((rows, width), low), vm((rows, width), low),
             vm((rows, routes_all.shape[1]), jnp.int32), vm((rows, width), low),
             vm((pairs, width), low), vm((pairs, width), low),
             vm((pairs, hidden), low), vm((pairs, hidden), low), vm((pairs, hidden), low),
@@ -1700,8 +1723,8 @@
             vm((nz, rows, cols), low), vm((nz, half, cols), low),
             vm((nz, rows, cols), low), vm((nz, half, cols), low),
             vm((nz + 1, rows, cols), low),
-            dma((4,)), dma, dma((5,)), dma((4 * nz,)), dma((4 * nz,)),
-        ] + [dma((nz,))] * 9 + [dma((nz + 1,))],
+            dma((5,)), dma, dma((5,)), dma((4 * nz,)), dma((4 * nz,)),
+        ] + [dma((nz,))] * 9 + [dma((nz + 1,))] + [dma((4 * tiles,))] * 2,
         compiler_params=pltpu.CompilerParams(
             collective_id=collective_id, has_side_effects=True, vmem_limit_bytes=62 << 20
         ),
@@ -1826,6 +1849,73 @@
         lax.fori_loop(0, self.nz, step, 0)
 
 
+class GatherCausal:
+    @staticmethod
+    def scratch(nz):
+        dma = pltpu.SemaphoreType.DMA
+        return [dma, dma, dma((2,)), dma((2 * nz,)), dma((2 * nz,)), dma((2 * nz,))]
+
+    def __init__(self, nz, src, out, held, sems):
+        self.s_x, self.r_x, self.lsem, self.s_z, self.r_z, self.l_z = sems
+        self.nz, self.src, self.out, self.held_ref = nz, src, out, held
+        self.place = z, x, y, c = place()
+        self.xn = device(z, 1 - x, y, c)
+        self.near = (device(z + 1, x, y, c), device(z - 1, x, y, c))
+
+    def own(self):
+        z, x = self.place[:2]
+        return [pltpu.make_async_copy(self.src, self.out.at[z, x], self.lsem.at[0]),
+                pltpu.make_async_copy(self.src, self.held_ref.at[z, x], self.lsem.at[1])]
+
+    def side(self):
+        z, x = self.place[:2]
+        return remote(self.src, self.out.at[z, x], self.s_x, self.r_x, self.xn)
+
+    def line(self, zz, micro):
+        here = self.out.at[zz, :, micro]
+        return remote(here, here, self.s_z.at[zz * 2 + micro], self.r_z.at[zz * 2 + micro],
+                      self.near[micro])
+
+    def keep(self, zz, micro):
+        return pltpu.make_async_copy(self.out.at[zz, :, micro], self.held_ref.at[zz, :, micro],
+                                     self.l_z.at[zz * 2 + micro])
+
+    def needed(self, zz, micro):
+        return zz <= self.place[0] if micro == 0 else zz >= self.place[0]
+
+    def sends(self, zz, micro):
+        z = self.place[0]
+        return self.needed(zz, micro) & (z < self.nz - 1 if micro == 0 else z > 0)
+
+    def first(self, k):
+        zz, z = near_first(self.nz, self.place[0], k), self.place[0]
+
+        @pl.when(k == 0)
+        def _():
+            for copy in self.own():
+                copy.wait()
+            self.side().wait_recv()
+
+        for micro in range(2):
+            pl.when((k > 0) & self.needed(zz, micro))(lambda: self.line(zz, micro).wait_recv())
+            pl.when(self.sends(zz, micro))(lambda: self.line(zz, micro).start())
+            pl.when(self.needed(zz, micro))(lambda: self.keep(zz, micro).start())
+
+    def ready(self, zz):
+        for micro in range(2):
+            pl.when(self.needed(zz, micro))(lambda: self.keep(zz, micro).wait())
+
+    def finish(self):
+        self.side().wait_send()
+
+        def step(zz, carry):
+            for micro in range(2):
+                pl.when(self.sends(zz, micro))(lambda: self.line(zz, micro).wait_send())
+            return carry
+
+        lax.fori_loop(0, self.nz, step, 0)
+
+
 class GatherRows:
     @staticmethod
     def scratch(nz):
@@ -1877,15 +1967,14 @@
     return (nz - 1 - shard // 2) * 2 + shard % 2
 
 
-def stream_unit(u, nz, block):
+def stream_unit(u, nz):
     shard = lax.axis_index("fsdp")
     later = u > shard
     micro = jnp.where(later, 1, 0)
     here = jnp.where(later, mirrored(nz, shard), shard)
     key_place = here - jnp.where(later, u - shard - 1, u)
     owner = jnp.where(later, mirrored(nz, key_place), key_place)
-    rows = pl.ds(pl.multiple_of((owner * 2 + micro) * block, block), block)
-    return micro, here, key_place, rows
+    return micro, here, key_place, owner
 
 
 def key_bias(micro, here, key_place, block, start_ref):
@@ -1894,41 +1983,79 @@
     return jnp.where((key >= start_ref[micro]) & (key <= query), 0.0, masked_score)
 
 
-def attend_kernel(nz, q_ref, k_ref, v_ref, start_ref, cot_ref, wo_ref,
-                  heads_ref, out_ref, lse_ref, cot_all, wo_all, acc, peak, total, *sems):
+def norm_turn(raw, gain, cosine, sine):
+    scale = lax.rsqrt(jnp.mean(raw * raw, axis=1, keepdims=True) + norm_eps)
+    normed = raw * scale * gain
+    return normed * cosine + pltpu.roll(normed, raw.shape[1] // 2, 1) * sine
+
+
+def attend_kernel(nz, q_pre, k_pre, v_pre, gq_ref, gk_ref, cos_ref, sin_ref, start_ref, cot_ref, wo_ref,
+                  q_ref, heads_ref, out_ref, lse_ref, kv_all, cot_all, wo_all,
+                  kv_ref, kv, acc, peak, total, *sems):
     shards = 2 * nz
-    width = k_ref.shape[1]
+    width = kv_ref.shape[2] // 2
     block = q_ref.shape[0] // 2
+    low = jnp.bfloat16
     heads = q_ref.shape[1] // width
     z, x, y, c = place()
     split = len(GatherAll.scratch(nz))
+    end = split + len(GatherRows.scratch(nz))
     cots = GatherAll(nz, cot_ref, cot_all, sems[:split], cot_ref.shape[0])
-    outs = GatherRows(nz, wo_ref, wo_all, sems[split:])
+    outs = GatherRows(nz, wo_ref, wo_all, sems[split:end])
+    keys_in = GatherCausal(nz, kv_ref, kv_all, kv, sems[end:])
     greet([(None, cots.partner), (None, cots.xn), (None, cots.yn),
            (z < nz - 1, cots.up), (z > 0, cots.down)])
     for part in (outs, cots):
         part.own().start()
+    turned = norm_turn(k_pre[...], gk_ref[...], cos_ref[...], sin_ref[...]).astype(low)
+    for micro in range(2):
+        rows = slice(micro * block, (micro + 1) * block)
+        kv_ref[micro, :, :width] = turned[rows]
+        kv_ref[micro, :, width:] = v_pre[rows, :]
+    keys_in.side().start()
+    for copy in keys_in.own():
+        copy.start()
     peak[...] = jnp.full(peak.shape, masked_score, jnp.float32)
     total[...] = jnp.zeros_like(total)
     acc[...] = jnp.zeros_like(acc)
     for part in (outs, cots):
         part.own().wait()
 
-    def unit(u, carry):
+    def tick(u, carry):
         @pl.when(u < nz)
         def _():
+            pl.when(u == 0)(lambda: cots.first(u))
+            keys_in.first(u)
+            pl.when(u > 0)(lambda: cots.first(u))
             outs.first(u)
-            cots.first(u)
 
         pl.when((u >= 1) & (u <= nz))(lambda: cots.second(u - 1))
         pl.when((u >= 2) & (u <= nz + 1))(lambda: cots.third(u - 2))
-        pl.when(u < shards + 2 * x)(lambda: attention(u))
+        pl.when((u >= 1) & (u <= nz))(lambda: attend_item(u - 1))
         return carry
 
-    def attention(u):
-        micro, here, key_place, rows = stream_unit(u, nz, block)
+    def attend_item(k):
+        zz = near_first(nz, z, k)
+        own = zz == z
+        keys_in.ready(zz)
+
+        def part(i, carry):
+            micro = jnp.where(own, i // 2, jnp.where(zz < z, 0, 1))
+            xx = jnp.where(own, jnp.where(i % 2 == 0, x, 0), i)
+            valid = jnp.where(own, jnp.where((i % 2 == 0) | (x == 1), 1, 0), jnp.where(i < 2, 1, 0))
+            pl.when(valid == 1)(lambda: attention(micro, zz, xx))
+            return carry
+
+        lax.fori_loop(0, 4, part, 0)
+
+    def attention(micro, zz, xx):
+        def at_place(z_at, x_at):
+            return jnp.where(micro == 0, z_at, nz - 1 - z_at) * 2 + x_at
+
+        here, key_place = at_place(z, x), at_place(zz, xx)
         bias = key_bias(micro, here, key_place, block, start_ref)
-        keys, values = k_ref[rows, :], v_ref[rows, :]
+        both = kv.at[zz, xx, micro]
+        keys, values = both[:, :width], both[:, width:]
         q_rows = pl.ds(pl.multiple_of(micro * block, block), block)
 
         def head(h, carry):
@@ -1946,7 +2073,14 @@
 
         lax.fori_loop(0, heads, head, 0, unroll=4)
 
-    lax.fori_loop(0, shards + 2, unit, 0)
+    def prepare(h, carry):
+        cols = pl.ds(pl.multiple_of(h * width, width), width)
+        q_ref[:, cols] = norm_turn(q_pre[:, cols], gq_ref[...], cos_ref[...], sin_ref[...]).astype(low)
+        return carry
+
+    tick(0, 0)
+    lax.fori_loop(0, heads, prepare, 0)
+    lax.fori_loop(1, nz + 2, tick, 0)
 
     def close(at, carry):
         micro, h = at // heads, at % heads
@@ -1959,38 +2093,41 @@
         return carry
 
     lax.fori_loop(0, 2 * heads, close, 0)
+    keys_in.finish()
     outs.finish()
     cots.finish()
 
 
-def attend(query, keys, values, starts, cotangent, w_out, nz, collective_id):
-    rows, columns = query.shape
-    width = keys.shape[1]
+def attend(q_pre, k_pre, v_low, gain_query, gain_key, cosine, sine, starts, cotangent, w_out, nz,
+           collective_id):
+    rows, columns = q_pre.shape
+    width = k_pre.shape[1]
     heads = columns // width
     block = rows // 2
     any_space = pl.BlockSpec(memory_space=pl.ANY)
     vmem = pl.BlockSpec(memory_space=pltpu.VMEM)
-    vm, shape, f32 = pltpu.VMEM, jax.ShapeDtypeStruct, jnp.float32
+    vm, shape, f32, low = pltpu.VMEM, jax.ShapeDtypeStruct, jnp.float32, jnp.bfloat16
     return pl.pallas_call(
         functools.partial(attend_kernel, nz),
-        in_specs=[vmem] * 4 + [any_space] * 2,
-        out_specs=[vmem] * 3 + [any_space] * 2,
+        in_specs=[vmem] * 10,
+        out_specs=[vmem] * 4 + [any_space] * 3,
         out_shape=[
-            shape((rows, columns), jnp.bfloat16),
-            shape((rows, columns), f32),
+            shape((rows, columns), low), shape((rows, columns), low), shape((rows, columns), f32),
             shape((2 * heads, 1, block), f32),
+            shape((nz, 2, 2, block, 2 * width), low),
             shape((rows * 2 * nz, cotangent.shape[1] * 4), cotangent.dtype),
             shape((w_out.shape[0] * 2 * nz, w_out.shape[1]), w_out.dtype),
         ],
         scratch_shapes=[
+            vm((2, block, 2 * width), low), vm((nz, 2, 2, block, 2 * width), low),
             vm((2 * heads, width, block), f32), vm((2 * heads, 1, block), f32),
             vm((2 * heads, 1, block), f32),
-        ] + GatherAll.scratch(nz) + GatherRows.scratch(nz),
+        ] + GatherAll.scratch(nz) + GatherRows.scratch(nz) + GatherCausal.scratch(nz),
         compiler_params=pltpu.CompilerParams(
-            collective_id=collective_id, has_side_effects=True, vmem_limit_bytes=40 << 20
+            collective_id=collective_id, has_side_effects=True, vmem_limit_bytes=62 << 20
         ),
         name="attend",
-    )(query, keys, values, starts, cotangent, w_out)
+    )(q_pre, k_pre, v_low, gain_query, gain_key, cosine, sine, starts, cotangent, w_out)
 
 
 class ScatterAll:
@@ -2166,12 +2303,15 @@
 
     def start(self):
         def step(k, carry):
-            zz = far_first(self.nz, self.place[0], k)
-            self.side(zz).start()
-            self.load(zz).start()
+            self.send(k)
             return carry
 
         lax.fori_loop(0, self.nz, step, 0)
+
+    def send(self, k):
+        zz = far_first(self.nz, self.place[0], k)
+        self.side(zz).start()
+        self.load(zz).start()
 
     send_line = ScatterAll.send_line
     passes = ScatterAll.passes
@@ -2207,48 +2347,35 @@
         lax.fori_loop(0, self.nz, step, 0)
 
 
-def attend_back_kernel(nz, q_ref, k_ref, v_ref, start_ref, lse_ref, delta_ref, grad_ref,
-                       gp_ref, up_ref, hid_ref, xr_all, gs_all, out_part, wo_part,
-                       q_side, sides, out_sum, wo_sum, dwg, dwu, dwd,
-                       acc, k_acc, v_acc, x_panel, g_panel, o_gate, o_up, o_down, s_in, s_out, *refs):
+def attend_back_kernel(nz, q_ref, q_pre, gq_ref, cos_ref, sin_ref, kv_ref, start_ref, lse_ref,
+                       delta_ref, grad_ref, small_ref, out_part, wo_part, q_grad, gain_grad, sides, out_sum, wo_sum, small_out,
+                       acc, k_acc, v_acc, *refs):
     shards = 2 * nz
     shard = lax.axis_index("fsdp")
-    width = k_ref.shape[1]
+    width = kv_ref.shape[4] // 2
     block = q_ref.shape[0] // 2
     heads = q_ref.shape[1] // width
     z, x, y, c = place()
     count = shards + 2 * x
-    panel = x_panel.shape[1]
-    panels = xr_all.shape[1] // panel
     low = jnp.bfloat16
     split = len(ScatterAll.scratch(nz, 16, 128, low, 0))
     outs = ScatterAll(nz, out_part, out_sum, refs[:split], 0)
-    weights = ReduceRows(nz, wo_part, wo_sum, refs[split:])
-    greet([(None, outs.partner), (None, outs.xn), (None, outs.yn),
-           (z < nz - 1, outs.up), (z > 0, outs.down)])
+    end = split + len(ReduceRows.scratch(nz, 16, 128, low))
+    weights = ReduceRows(nz, wo_part, wo_sum, refs[split:end])
+    smalls = SmallSums(nz, small_ref, small_out, refs[end:])
+    greet_all(lax.axis_index("fsdp"), lax.axis_index("tp"), shards, 4)
+    smalls.start()
     outs.start()
-    weights.start()
-
-    def loads(n):
-        at = pl.ds(pl.multiple_of(n * panel, panel), panel)
-        return (pltpu.make_async_copy(xr_all.at[:, at], x_panel, s_in.at[0]),
-                pltpu.make_async_copy(gs_all.at[:, at], g_panel, s_in.at[1]))
-
-    def stores(n):
-        at = pl.ds(pl.multiple_of(n * panel, panel), panel)
-        return (pltpu.make_async_copy(o_gate, dwg.at[at, :], s_out.at[0]),
-                pltpu.make_async_copy(o_up, dwu.at[at, :], s_out.at[1]),
-                pltpu.make_async_copy(o_down, dwd.at[:, at], s_out.at[2]))
-
-    for copy in loads(0):
-        copy.start()
+
     sides[...] = jnp.zeros_like(sides)
     acc[...] = jnp.zeros_like(acc)
 
     def attention(u):
-        micro, here, key_place, rows = stream_unit(u, nz, block)
+        micro, here, key_place, owner = stream_unit(u, nz)
+        rows = pl.ds(pl.multiple_of((owner * 2 + micro) * block, block), block)
         bias = key_bias(micro, here, key_place, block, start_ref)
-        keys, values = k_ref[rows, :], v_ref[rows, :]
+        both = kv_ref.at[owner // 2, owner % 2, micro]
+        keys, values = both[:, :width], both[:, width:]
         q_rows = pl.ds(pl.multiple_of(micro * block, block), block)
         k_acc[...] = jnp.zeros_like(k_acc)
         v_acc[...] = jnp.zeros_like(v_acc)
@@ -2269,7 +2396,270 @@
         sides[rows, pl.ds(0, width)] = (k_acc[...] * width ** (-0.5)).astype(low)
         sides[rows, pl.ds(width, width)] = v_acc[...].astype(low)
 
+    def close(at, total):
+        micro, h = at // heads, at % heads
+        here = pl.ds(pl.multiple_of(micro * block, block), block)
+        cols = pl.ds(pl.multiple_of(h * width, width), width)
+        turned = acc[at].T * width ** (-0.5)
+        grad = turned * cos_ref[here, :] + pltpu.roll(turned * sin_ref[here, :], width // 2, 1)
+        raw = q_pre[here, cols]
+        scale = lax.rsqrt(jnp.mean(raw * raw, axis=1, keepdims=True) + norm_eps)
+        inner = grad * gq_ref[...]
+        mean = jnp.mean(raw * inner, axis=1, keepdims=True)
+        q_grad[here, cols] = (scale * inner - raw * (scale * scale * scale * mean)).astype(low)
+        return total + jnp.sum(grad * raw * scale, axis=0, keepdims=True)
+
+    def close_all():
+        gain_grad[...] = lax.fori_loop(
+            0, 2 * heads, close, jnp.zeros(gain_grad.shape, jnp.float32)
+        )
+
+    def unit(u, carry):
+        def at(fn, k):
+            pl.when((k >= 0) & (k < nz))(lambda: fn(k))
+
+        at(outs.first, u)
+        at(outs.second, u - 1)
+        at(weights.send, u)
+        pl.when(u == 2)(smalls.second)
+        pl.when(2 * u < count)(lambda: attention(2 * u))
+        pl.when(2 * u + 1 < count)(lambda: attention(2 * u + 1))
+        pl.when(u == (shards + 2) // 2)(close_all)
+        at(outs.third, u - 2)
+        at(outs.fourth, u - 3)
+        at(weights.second, u - 2)
+        at(weights.first, u - 1)
+        return carry
+
+    lax.fori_loop(0, max(nz + 3, nz + 2), unit, 0)
+
+    outs.finish()
+    weights.finish()
+    smalls.finish()
+
+
+def attend_back(query, q_pre, gain_query, cosine, sine, keys_values, starts, log_total, delta,
+                grad, small, out_part, wo_part, nz, collective_id):
+    rows, columns = query.shape
+    width = keys_values.shape[4] // 2
+    heads = columns // width
+    block = rows // 2
+    cols = out_part.shape[1] // 4
+    wo_shape = (wo_part.shape[0] // (2 * nz), wo_part.shape[1])
+    any_space = pl.BlockSpec(memory_space=pl.ANY)
+    vmem = pl.BlockSpec(memory_space=pltpu.VMEM)
+    vm, shape, f32, low = pltpu.VMEM, jax.ShapeDtypeStruct, jnp.float32, jnp.bfloat16
+    return pl.pallas_call(
+        functools.partial(attend_back_kernel, nz),
+        in_specs=[vmem] * 11 + [any_space] * 2,
+        out_specs=[vmem] * 6,
+        out_shape=[
+            shape((rows, columns), low), shape((1, width), f32),
+            shape((rows * 2 * nz, 2 * width), low),
+            shape((rows, cols), f32), shape(wo_shape, f32),
+            shape((8 * nz,) + small.shape[1:], f32),
+        ],
+        scratch_shapes=[
+            vm((2 * heads, width, block), f32), vm((block, width), f32), vm((block, width), f32),
+        ] + ScatterAll.scratch(nz, rows, cols, low, 0) + ReduceRows.scratch(nz, *wo_shape, low)
+        + SmallSums.scratch(nz, small.shape[1:], f32),
+        compiler_params=pltpu.CompilerParams(
+            collective_id=collective_id, has_side_effects=True, vmem_limit_bytes=62 << 20
+        ),
+        name="attend_back",
+    )(query, q_pre, gain_query, cosine, sine, keys_values, starts, log_total, delta, grad, small,
+      out_part, wo_part)
+
+
+def to_row(column, eye):
+    return jnp.sum(jnp.where(eye, column, 0.0), axis=0, keepdims=True)
+
+
+def to_column(row, eye):
+    return jnp.sum(jnp.where(eye, row, 0.0), axis=1, keepdims=True)
+
+
+def diagonal():
+    shape = (128, 128)
+    return lax.broadcasted_iota(jnp.int32, shape, 0) == lax.broadcasted_iota(jnp.int32, shape, 1)
+
+
+class RowSums:
+    @staticmethod
+    def scratch(rows):
+        dma = pltpu.SemaphoreType.DMA
+        return [pltpu.VMEM((4, rows // 128, 128), jnp.float32), dma((3,)), dma((3,))]
+
+    def __init__(self, refs):
+        self.got, s, r = refs
+        shard, group = lax.axis_index("fsdp"), lax.axis_index("tp")
+        self.peers = [(shard, (group + k) % 4) for k in range(1, 4)]
+        self.copies = [
+            remote(self.got.at[0], self.got.at[k + 1], s.at[k], r.at[k], peer)
+            for k, peer in enumerate(self.peers)
+        ]
+
+    def start(self):
+        for copy in self.copies:
+            copy.start()
+
+    def wait(self):
+        for copy in self.copies:
+            copy.wait()
+
+    def total(self, n):
+        return self.got[0, pl.ds(n, 1), :] + self.got[1, pl.ds(n, 1), :] + (
+            self.got[2, pl.ds(n, 1), :] + self.got[3, pl.ds(n, 1), :])
+
+
+class ReduceCols:
+    @staticmethod
+    def scratch(rows, cols, kind):
+        vm, dma = pltpu.VMEM, pltpu.SemaphoreType.DMA
+        return [vm((2, rows, cols), kind), vm((2, rows, cols), kind), vm((rows, cols), kind),
+                dma((2,)), dma((2,)), dma((2,)), dma, dma]
+
+    def __init__(self, partial, out, refs):
+        self.w, self.rp, self.ry, s_l, s_p, r_p, s_y, r_y = refs
+        self.out = out
+        self.rows, cols = out.shape
+        z, x, y, c = place()
+        self.partner, self.yn = device(z, x, y, 1 - c), device(z, x, 1 - y, c)
+
+        def block(yy, cc):
+            return partial.at[:, pl.ds(pl.multiple_of((yy * 2 + cc) * cols, cols), cols)]
+
+        self.sends = [remote(block(yy, 1 - c), self.rp.at[k], s_p.at[k], r_p.at[k], self.partner)
+                      for k, yy in enumerate((1 - y, y))]
+        self.loads = [pltpu.make_async_copy(block(yy, c), self.w.at[k], s_l.at[k])
+                      for k, yy in enumerate((1 - y, y))]
+        self.across = remote(self.w.at[0], self.ry, s_y, r_y, self.yn)
+
+    def start(self):
+        for k in range(2):
+            self.sends[k].start()
+            self.loads[k].start()
+
+    def first(self):
+        self.loads[0].wait()
+        self.sends[0].wait_recv()
+        add_blocks(self.w.at[0], [self.rp.at[0]], 0, self.rows)
+        self.across.start()
+
+    def second(self):
+        self.loads[1].wait()
+        self.sends[1].wait_recv()
+        self.across.wait_recv()
+        add_blocks(self.w.at[1], [self.rp.at[1], self.ry], 0, self.rows, self.out)
+
+    def finish(self):
+        for send in self.sends:
+            send.wait_send()
+        self.across.wait_send()
+
+
+class SmallSums:
+    @staticmethod
+    def scratch(nz, part, kind):
+        dma = pltpu.SemaphoreType.DMA
+        return [pltpu.VMEM((2 * nz,) + part, kind), dma((2 * nz,)), dma((2 * nz,)),
+                dma((8 * nz,)), dma((8 * nz,))]
+
+    def __init__(self, nz, values, out, refs):
+        self.got, self.s_1, self.r_1, self.s_2, self.r_2 = refs
+        self.values, self.out = values, out
+        self.shards, self.devices = 2 * nz, 8 * nz
+        self.shard, self.group = lax.axis_index("fsdp"), lax.axis_index("tp")
+        self.me = self.shard * 4 + self.group
+
+    def share(self, k):
+        other = (self.shard + k) % self.shards
+        return remote(self.values.at[other], self.got.at[k], self.s_1.at[k], self.r_1.at[k],
+                      (other, self.group))
+
+    def spread(self, k):
+        other = (self.me + k) % self.devices
+        return remote(self.out.at[self.me], self.out.at[self.me], self.s_2.at[k], self.r_2.at[k],
+                      (other // 4, other % 4))
+
+    def start(self):
+        loop_from_one(self.shards, lambda k: self.share(k).start())
+
+    def second(self):
+        loop_from_one(self.shards, lambda k: self.share(k).wait())
+        acc = self.values[self.shard]
+        for k in range(1, self.shards):
+            acc = acc + self.got[k]
+        self.out[self.me] = acc
+        loop_from_one(self.devices, lambda k: self.spread(k).start())
+
+    def finish(self):
+        loop_from_one(self.devices, lambda k: self.spread(k).wait())
+
+
+def loop_from_one(count, fn):
+    def step(k, carry):
+        fn(k)
+        return carry
+
+    lax.fori_loop(1, count, step, 0)
+
+
+def tail_kernel(nz, tok_ref, mid_ref, scale_ref, gain_ref, block_ref, small_ref,
+                gp_all, up_all, hid_all, xr_all, gs_all, w_part, normed_part,
+                w_sum, token_out, block_out, small_out, dwg, dwu, dwd,
+                gp_ref, up_ref, hid_ref, x_panel, g_panel, o_gate, o_up, o_down, s_in, s_out,
+                normed, token, s_w, r_w, s_l, s_g, r_g, *refs):
+    z, x, y, c = place()
+    shard, group = lax.axis_index("fsdp"), lax.axis_index("tp")
+    shards = 2 * nz
+    devices = 4 * shards
+    me = shard * 4 + group
+    rows, cols = tok_ref.shape
+    width = cols * 4
+    half = rows // 2
+    panel = x_panel.shape[1]
+    panels = xr_all.shape[1] // panel
+    f32, low = jnp.float32, jnp.bfloat16
+    n_w, n_c = len(ReduceRows.scratch(nz, 16, 128, low)), len(ReduceCols.scratch(16, 128, low))
+    weights = ReduceRows(nz, w_part, w_sum, refs[:n_w])
+    columns = ReduceCols(normed_part, normed, refs[n_w : n_w + n_c])
+    sums = RowSums(refs[n_w + n_c :])
+    mirror = device(nz - 1 - z, x, y, c)
+    greet_all(shard, group, shards, 4)
+    columns.start()
+    weights.start()
+    top, bottom = pl.ds(0, half), pl.ds(half, half)
+    swaps = [remote(src.at[bottom], dst.at[bottom], s_w.at[n], r_w.at[n], mirror)
+             for n, (src, dst) in enumerate(((token, token_out), (block_ref, block_out)))]
+    keeps = [pltpu.make_async_copy(src.at[top], dst.at[top], s_l.at[n])
+             for n, (src, dst) in enumerate(((token, token_out), (block_ref, block_out)))]
+    swaps[1].start()
+    keeps[1].start()
+
+    def loads(n):
+        at = pl.ds(pl.multiple_of(n * panel, panel), panel)
+        return (pltpu.make_async_copy(xr_all.at[:, at], x_panel, s_in.at[0]),
+                pltpu.make_async_copy(gs_all.at[:, at], g_panel, s_in.at[1]))
+
+    def stores(n):
+        at = pl.ds(pl.multiple_of(n * panel, panel), panel)
+        return (pltpu.make_async_copy(o_gate, dwg.at[at, :], s_out.at[0]),
+                pltpu.make_async_copy(o_up, dwu.at[at, :], s_out.at[1]),
+                pltpu.make_async_copy(o_down, dwd.at[:, at], s_out.at[2]))
+
+    whole = [pltpu.make_async_copy(src, dst, s_in.at[2 + n])
+             for n, (src, dst) in enumerate(((gp_all, gp_ref), (up_all, up_ref), (hid_all, hid_ref)))]
+    for copy in tuple(whole) + loads(0):
+        copy.start()
+    small_out[me] = small_ref[...]
+
     def expert_weights(n):
+        @pl.when(n == 0)
+        def _():
+            for copy in whole:
+                copy.wait()
+
         for copy in loads(n):
             copy.wait()
 
@@ -2289,72 +2679,247 @@
             for copy in loads(n + 1):
                 copy.start()
 
+    def token_sums():
+        eye = diagonal()
+
+        def step(n, gains):
+            here = pl.ds(pl.multiple_of(n * 128, 128), 128)
+            tok, grad = tok_ref[here, :].astype(f32), normed[here, :]
+            product = tok * (grad * gain_ref[...])
+            sums.got[0, pl.ds(n, 1), :] = to_row(jnp.sum(product, axis=1, keepdims=True), eye)
+            return gains + jnp.sum(grad * tok * scale_ref[here, :], axis=0, keepdims=True)
+
+        gains = lax.fori_loop(0, rows // 128, step, jnp.zeros((1, cols), f32))
+        for n in range(cols // 128):
+            small_out[me, pl.ds(n, 1), :] = gains[:, n * 128 : (n + 1) * 128]
+
+    def token_grads():
+        eye = diagonal()
+
+        def step(n, carry):
+            here = pl.ds(pl.multiple_of(n * 128, 128), 128)
+            mean = to_column(sums.total(n), eye) / width
+            scale = scale_ref[here, :]
+            token[here, :] = (
+                mid_ref[here, :]
+                + scale * (gain_ref[...] * normed[here, :])
+                - tok_ref[here, :].astype(f32) * (scale * scale * scale * mean)
+            ).astype(low)
+            return carry
+
+        lax.fori_loop(0, rows // 128, step, 0)
+
+    def spread(k):
+        other = (me + k) % devices
+        return remote(small_out.at[me], small_out.at[me], s_g.at[k], r_g.at[k],
+                      (other // 4, other % 4))
+
+    columns.first()
+
     def unit(u, carry):
-        def at(fn, k):
-            pl.when((k >= 0) & (k < nz))(lambda: fn(k))
-
-        at(outs.first, u)
-        at(weights.first, u)
-        at(outs.second, u - 1)
-        at(weights.second, u - 1)
-        at(outs.third, u - 2)
-        at(outs.fourth, u - 3)
-        pl.when(u < count)(lambda: attention(u))
-        pl.when(u < panels)(lambda: expert_weights(u))
+        @pl.when(u == 1)
+        def _():
+            sums.wait()
+            token_grads()
+            swaps[0].start()
+            keeps[0].start()
+
+        pl.when((u >= 1) & (u <= nz))(lambda: weights.second(u - 1))
+
+        @pl.when(u < panels // 2)
+        def _():
+            expert_weights(2 * u)
+            expert_weights(2 * u + 1)
+
+        @pl.when(u == 0)
+        def _():
+            columns.second()
+            token_sums()
+            sums.start()
+            loop_from_one(devices, lambda k: spread(k).start())
+
+        pl.when(u < nz)(lambda: weights.first(u))
         return carry
 
-    lax.fori_loop(0, max(shards + 2, panels), unit, 0)
-
-    def close(at, carry):
-        micro, h = at // heads, at % heads
-        q_side[pl.ds(pl.multiple_of(micro * block, block), block),
-               pl.ds(pl.multiple_of(h * width, width), width)] = acc[at].T * width ** (-0.5)
-        return carry
-
-    lax.fori_loop(0, 2 * heads, close, 0)
+    lax.fori_loop(0, max(nz + 1, panels // 2), unit, 0)
+    loop_from_one(devices, lambda k: spread(k).wait())
+    for copy in swaps + keeps:
+        copy.wait()
     for copy in stores(panels - 1):
         copy.wait()
-    outs.finish()
+    columns.finish()
     weights.finish()
 
 
-def attend_back(query, keys, values, starts, log_total, delta, grad, gate_grad, up_grad, hidden,
-                rows_in, pair_grad, out_part, wo_part, nz, collective_id):
-    rows, columns = query.shape
-    width = keys.shape[1]
-    heads = columns // width
-    block = rows // 2
+def tail(gate_grad, up_grad, hidden, tokens, middle_grad, scale, gain, block_out, small, rows_in,
+         pair_grad, w_part, normed_part, nz, collective_id):
+    rows, cols = tokens.shape
     pairs, features = rows_in.shape
     hidden_width = hidden.shape[1]
     panel = 256
-    cols = out_part.shape[1] // 4
-    wo_shape = (wo_part.shape[0] // (2 * nz), wo_part.shape[1])
+    w_shape = (w_part.shape[0] // (2 * nz), w_part.shape[1])
+    devices = 8 * nz
     any_space = pl.BlockSpec(memory_space=pl.ANY)
     vmem = pl.BlockSpec(memory_space=pltpu.VMEM)
     vm, shape, f32, low = pltpu.VMEM, jax.ShapeDtypeStruct, jnp.float32, jnp.bfloat16
     dma = pltpu.SemaphoreType.DMA
     return pl.pallas_call(
-        functools.partial(attend_back_kernel, nz),
-        in_specs=[vmem] * 10 + [any_space] * 4,
-        out_specs=[vmem] * 4 + [any_space] * 3,
+        functools.partial(tail_kernel, nz),
+        in_specs=[vmem] * 6 + [any_space] * 7,
+        out_specs=[vmem, any_space, any_space, vmem] + [any_space] * 3,
         out_shape=[
-            shape((rows, columns), f32), shape((rows * 2 * nz, 2 * width), low),
-            shape((rows, cols), f32), shape(wo_shape, f32),
+            shape(w_shape, f32), shape((rows, cols), low), shape((rows, cols), low),
+            shape((devices,) + small.shape, f32),
             shape((features, hidden_width), f32), shape((features, hidden_width), f32),
             shape((hidden_width, features), f32),
         ],
-        scratch_shapes=[
-            vm((2 * heads, width, block), f32), vm((block, width), f32), vm((block, width), f32),
+        scratch_shapes=[vm((pairs, hidden_width), low)] * 3 + [
             vm((pairs, panel), low), vm((pairs, panel), low),
             vm((panel, hidden_width), f32), vm((panel, hidden_width), f32),
-            vm((hidden_width, panel), f32), dma((2,)), dma((3,)),
-        ] + ScatterAll.scratch(nz, rows, cols, low, 0) + ReduceRows.scratch(nz, *wo_shape, low),
+            vm((hidden_width, panel), f32), dma((5,)), dma((3,)),
+            vm((rows, cols), f32), vm((rows, cols), low),
+            dma((2,)), dma((2,)), dma((2,)), dma((devices,)), dma((devices,)),
+        ] + ReduceRows.scratch(nz, *w_shape, low) + ReduceCols.scratch(rows, cols, low)
+        + RowSums.scratch(rows),
         compiler_params=pltpu.CompilerParams(
-            collective_id=collective_id, has_side_effects=True, vmem_limit_bytes=63 << 20
+            collective_id=collective_id, has_side_effects=True, vmem_limit_bytes=62 << 20
         ),
-        name="attend_back",
-    )(query, keys, values, starts, log_total, delta, grad, gate_grad, up_grad, hidden,
-      rows_in, pair_grad, out_part, wo_part)
+        name="tail",
+    )(tokens, middle_grad, scale, gain, block_out, small, gate_grad, up_grad, hidden, rows_in,
+      pair_grad, w_part, normed_part)
+
+
+def join_kernel(nz, tok_ref, gain_ref, attn_part, middle_ref, scale_ref, low_ref, all_ref, *refs):
+    z, x, y, c = place()
+    rows, cols = tok_ref.shape
+    f32 = jnp.float32
+    n_c, n_s = len(ReduceCols.scratch(16, 128, jnp.bfloat16)), 3
+    columns = ReduceCols(attn_part, middle_ref, refs[:n_c])
+    sums = RowSums(refs[n_c : n_c + n_s])
+    gather = GatherAll(nz, low_ref, all_ref, refs[n_c + n_s :], rows // 2)
+    greet([(None, gather.xn), (z < nz - 1, gather.up), (z > 0, gather.down)]
+          + [(None, peer) for peer in sums.peers])
+    columns.start()
+    eye = diagonal()
+    columns.first()
+    columns.second()
+
+    def add(n, carry):
+        here = pl.ds(pl.multiple_of(n * 128, 128), 128)
+        total = middle_ref[here, :] + tok_ref[here, :].astype(f32)
+        middle_ref[here, :] = total
+        sums.got[0, pl.ds(n, 1), :] = to_row(jnp.sum(total * total, axis=1, keepdims=True), eye)
+        return carry
+
+    def norm(n, carry):
+        here = pl.ds(pl.multiple_of(n * 128, 128), 128)
+        scale = lax.rsqrt(to_column(sums.total(n), eye) / (4 * cols) + norm_eps)
+        scale_ref[here, :] = scale
+        low_ref[here, :] = (middle_ref[here, :] * scale * gain_ref[...]).astype(low_ref.dtype)
+        return carry
+
+    lax.fori_loop(0, rows // 128, add, 0)
+    sums.start()
+    sums.wait()
+    lax.fori_loop(0, rows // 128, norm, 0)
+    gather.own().start()
+    gather.own().wait()
+
+    def tick(k, carry):
+        pl.when(k < nz)(lambda: gather.first(k))
+        pl.when((k >= 1) & (k <= nz))(lambda: gather.second(k - 1))
+        pl.when(k >= 2)(lambda: gather.third(k - 2))
+        return carry
+
+    lax.fori_loop(0, nz + 2, tick, 0)
+    gather.finish()
+    columns.finish()
+
+
+def join(tokens, gain, attn_part, nz, collective_id):
+    rows, cols = tokens.shape
+    any_space = pl.BlockSpec(memory_space=pl.ANY)
+    vmem = pl.BlockSpec(memory_space=pltpu.VMEM)
+    shape, f32, low = jax.ShapeDtypeStruct, jnp.float32, jnp.bfloat16
+    return pl.pallas_call(
+        functools.partial(join_kernel, nz),
+        in_specs=[vmem] * 2 + [any_space],
+        out_specs=[vmem] * 3 + [any_space],
+        out_shape=[shape((rows, cols), f32), shape((rows, 1), f32), shape((rows, cols), low),
+                   shape((rows * 2 * nz, cols * 4), low)],
+        scratch_shapes=ReduceCols.scratch(rows, cols, low) + RowSums.scratch(rows)
+        + GatherAll.scratch(nz),
+        compiler_params=pltpu.CompilerParams(
+            collective_id=collective_id, has_side_effects=True, vmem_limit_bytes=62 << 20
+        ),
+        name="join",
+    )(tokens, gain, attn_part)
+
+
+def turn_kernel(middle_ref, scale_ref, inner_ref, grad_ref, out_ref, all_ref, low_ref, lsem,
+                s_p, r_p, s_y, r_y, *refs):
+    z, x, y, c = place()
+    rows, cols = middle_ref.shape
+    sums = RowSums(refs)
+    partner, yn = device(z, x, y, 1 - c), device(z, x, 1 - y, c)
+    greet([(None, peer) for peer in sums.peers])
+    eye = diagonal()
+
+    def block(yy):
+        return all_ref.at[:, pl.ds(pl.multiple_of((yy * 2 + c) * cols, cols), cols)]
+
+    def dots(n, carry):
+        here = pl.ds(pl.multiple_of(n * 128, 128), 128)
+        product = middle_ref[here, :] * inner_ref[here, :]
+        sums.got[0, pl.ds(n, 1), :] = to_row(jnp.sum(product, axis=1, keepdims=True), eye)
+        return carry
+
+    def grads(n, carry):
+        here = pl.ds(pl.multiple_of(n * 128, 128), 128)
+        mean = to_column(sums.total(n), eye) / (4 * cols)
+        scale = scale_ref[here, :]
+        out = (grad_ref[here, :] + scale * inner_ref[here, :]
+               - middle_ref[here, :] * (scale * scale * scale * mean))
+        out_ref[here, :] = out
+        low_ref[here, :] = out.astype(low_ref.dtype)
+        return carry
+
+    lax.fori_loop(0, rows // 128, dots, 0)
+    sums.start()
+    sums.wait()
+    lax.fori_loop(0, rows // 128, grads, 0)
+    to_y = remote(low_ref, block(y), s_y, r_y, yn)
+    to_pair = remote(low_ref, block(y), s_p.at[0], r_p.at[0], partner)
+    own = pltpu.make_async_copy(low_ref, block(y), lsem)
+    on = remote(block(1 - y), block(1 - y), s_p.at[1], r_p.at[1], partner)
+    for copy in (to_y, to_pair, own):
+        copy.start()
+    to_y.wait_recv()
+    on.start()
+    to_pair.wait()
+    on.wait()
+    to_y.wait_send()
+    own.wait()
+
+
+def turn(middle, scale, inner, grad, collective_id):
+    rows, cols = middle.shape
+    any_space = pl.BlockSpec(memory_space=pl.ANY)
+    vmem = pl.BlockSpec(memory_space=pltpu.VMEM)
+    shape, f32, low = jax.ShapeDtypeStruct, jnp.float32, jnp.bfloat16
+    dma = pltpu.SemaphoreType.DMA
+    return pl.pallas_call(
+        turn_kernel,
+        in_specs=[vmem] * 4,
+        out_specs=[vmem, any_space],
+        out_shape=[shape((rows, cols), f32), shape((rows, cols * 4), low)],
+        scratch_shapes=[pltpu.VMEM((rows, cols), low), dma, dma((2,)), dma((2,)), dma, dma]
+        + RowSums.scratch(rows),
+        compiler_params=pltpu.CompilerParams(
+            collective_id=collective_id, has_side_effects=True, vmem_limit_bytes=62 << 20
+        ),
+        name="turn",
+    )(middle, scale, inner, grad)
 
 
 def gathered_body(
@@ -2397,10 +2962,6 @@
     mirror_index = mirrored(nz, shard_index)
     owners = jnp.stack([shard_index, mirror_index])
 
-    def to_owners(array):
-        second = array[:, 1].reshape((nz, 2) + array.shape[2:])[::-1].reshape(array[:, 1].shape)
-        return jnp.stack([array[:, 0], second], axis=1)
-
     small = jnp.concatenate([routes.reshape(-1), doc_ids.reshape(-1)])
     small_rows = -(-small.shape[0] // 1024) * 8
     small = jnp.pad(small, (0, small_rows * 128 - small.shape[0])).reshape(small_rows, 128)
@@ -2408,9 +2969,7 @@
         [small, w_query, key_weight, value_weight], nz, 2, [tokens]
     )
     small_all = small_all.reshape(shard_count, small_rows * 128)
-    routes_all = to_owners(
-        small_all[:, : row_count * TOPK].reshape(shard_count, micro_count, micro_rows, TOPK)
-    ).reshape(shard_count * row_count, TOPK)
+    routes_all = small_all[:, : row_count * TOPK].reshape(shard_count * row_count, TOPK)
     ids_all = small_all[:, row_count * TOPK : row_count * (TOPK + 1)].reshape(
         shard_count, micro_count, micro_rows
     )
@@ -2434,43 +2993,18 @@
     query_pre = jnp.dot(normed_low, wq_all, preferred_element_type=f32)
     key_pre = jnp.dot(normed_low, wk_all, preferred_element_type=f32)
     value_low = jnp.dot(normed_low, wv_all, preferred_element_type=f32).astype(low)
-
-    def shape_heads(query_raw, key_raw, query_gain, key_gain):
-        query_heads = rotary_apply(
-            root_mean_norm(query_raw.reshape(row_count, query_local, head_width), query_gain),
-            cosine_lookup[:, None, :],
-            sine_lookup[:, None, :],
-        )
-        key_heads = rotary_apply(
-            root_mean_norm(key_raw.reshape(row_count, kv_local, head_width), key_gain),
-            cosine_lookup[:, None, :],
-            sine_lookup[:, None, :],
-        )
-        return (query_heads, key_heads)
-
-    (query_heads, key_heads), heads_pull = jax.vjp(
-        shape_heads, query_pre, key_pre, gain_query, key_norm_gain
-    )
-    query_low = query_heads.astype(low)
-    key_low = key_heads.reshape(row_count, kv_width).astype(low)
-    keys_got, values_got = gather_rows([key_low, value_low], nz, 4)
-
+    turned_sine = jnp.where(jnp.arange(head_width) < head_width // 2, -sine_lookup, sine_lookup)
+    query_gain, key_gain = gain_query.reshape(1, head_width), key_norm_gain.reshape(1, head_width)
     starts = query_start.reshape(micro_count, 1, micro_rows).astype(jnp.int32)
-    heads_low, head_out, log_total, grads_all, wo_all = attend(
-        query_low.reshape(row_count, query_width), keys_got, values_got,
-        starts, cotangent, w_out, nz, 3,
+    query_low, heads_low, head_out, log_total, keys_values, grads_all, wo_all = attend(
+        query_pre, key_pre, value_low, query_gain, key_gain, cosine_lookup, turned_sine, starts,
+        cotangent, w_out, nz, 3,
     )
     attn_part = dot_last(heads_low, wo_all).astype(low)
-    middle = tokens.astype(f32) + reduce_cols(attn_part, 5)
-
-    def row_mean(values, collective_id):
-        total = jnp.sum(values, axis=1).reshape(row_count // 128, 128)
-        return sum_cols(total, collective_id).reshape(row_count, 1) / model_width
-
-    scale = lax.rsqrt(row_mean(middle * middle, 6) + norm_eps)
     gain_slice = lax.dynamic_slice_in_dim(gain_moe, my_columns, slice_width)
-    moe_low = (middle * scale * gain_slice).astype(low)
-    moe_all = gather_all(moe_low, nz, 7)
+    middle, scale, moe_low, moe_all = join(
+        tokens, gain_slice.reshape(1, slice_width), attn_part, nz, 5
+    )
     out_part, back, gates_grad, gates, *kept = run_experts(
         moe_all, grads_all, routes_all, router, w_gate[0], w_up[0], w_down[0],
         micro_rows, capacity, nz, 8,
@@ -2478,9 +3012,7 @@
     rows_in, pair_grad, hidden_low, gate_pre_low, up_pre_low = (
         array.reshape(-1, array.shape[2]) for array in kept
     )
-    gates_grad = swap_rows(
-        gates_grad.reshape(shard_count, row_count // 128, 128), shard_count, group_count, 9
-    ).reshape(expert_total, row_count).T
+    gates_grad = gates_grad.reshape(expert_total, row_count).T
     logit_grad = gates * (gates_grad - jnp.sum(gates * gates_grad, axis=1, keepdims=True))
     router_slice = lax.dynamic_slice_in_dim(router, my_columns, slice_width).astype(f32)
     moe_grad = back + lax.dot_general(
@@ -2495,30 +3027,30 @@
     )
     grad_slice = jnp.concatenate([cotangent[:micro_rows], swapped_grad], axis=0).astype(f32)
     inner = gain_slice * moe_grad
-    middle_grad = (
-        grad_slice + scale * inner - middle * scale**3 * row_mean(middle * inner, 10)
-    )
-    middle_low = gather_cols(middle_grad.astype(low), 11)
+    middle_grad, middle_low = turn(middle, scale, inner, grad_slice, 11)
     out_grad_part = dot_first(middle_low, heads_low).astype(low)
     heads_grad = jnp.dot(middle_low, wo_all, preferred_element_type=f32).astype(low)
     delta = jnp.sum(
         (heads_grad.astype(f32) * head_out).reshape(micro_count, micro_rows, query_local, head_width),
         axis=3,
     ).transpose(0, 2, 1).reshape(micro_count * query_local, 1, micro_rows)
-    query_side, sides, out_sum, w_out_grad, gate_acc, up_acc, down_acc = attend_back(
-        query_low.reshape(row_count, query_width), keys_got, values_got, starts, log_total, delta,
-        heads_grad, gate_pre_low, up_pre_low, hidden_low, rows_in, pair_grad, out_part,
-        out_grad_part, nz, 12,
+    pieces = [gain_moe_part, router_part.reshape(-1)]
+    length = sum(piece.shape[0] for piece in pieces)
+    part_rows = -(-length // (shard_count * 1024)) * 8
+    flat = jnp.concatenate(
+        pieces + [jnp.zeros((shard_count * part_rows * 128 - length,), f32)]
+    ).reshape(shard_count, part_rows, 128)
+    query_pre_low, gain_query_part, sides, out_sum, w_out_grad, summed = attend_back(
+        query_low, query_pre, query_gain, cosine_lookup, turned_sine, keys_values, starts, log_total,
+        delta, heads_grad, flat, out_part, out_grad_part, nz, 12,
     )
     block_out = (middle + out_sum).astype(low)
     sides = reduce_rows(sides, nz, 14)
-    query_pre_grad, key_pre_grad, gain_query_part, gain_key_part = heads_pull(
-        (
-            query_side.reshape(row_count, query_local, head_width),
-            sides[:, :kv_width].reshape(row_count, kv_local, head_width),
-        )
-    )
-    query_pre_low = query_pre_grad.astype(low)
+
+    def shape_keys(key_raw, key_gain):
+        return rotary_apply(root_mean_norm(key_raw, key_gain), cosine_lookup, sine_lookup)
+
+    key_pre_grad, gain_key_part = jax.vjp(shape_keys, key_pre, key_norm_gain)[1](sides[:, :kv_width])
     key_pre_low = key_pre_grad.astype(low)
     value_pre_low = sides[:, kv_width:].astype(low)
     normed_part = (
@@ -2526,49 +3058,35 @@
         + dot_last(key_pre_low, wk_all)
         + dot_last(value_pre_low, wv_all)
     ).astype(low)
-    normed_grad = reduce_cols(normed_part, 15)
     pre_low = jnp.concatenate([query_pre_low, key_pre_low, value_pre_low], axis=1)
-    weight_grad = reduce_rows(dot_first(normed_low, pre_low).astype(low), nz, 16)
-    token_slice = tokens.astype(f32)
+    weight_part = dot_first(normed_low, pre_low).astype(low)
+    gain_rows = slice_width // 128
+    gains = jnp.concatenate(
+        [jnp.zeros((slice_width,), f32), gain_query_part.reshape(-1), gain_key_part,
+         jnp.zeros(((8 - gain_rows - 2) * 128,), f32)]
+    ).reshape(8, 128)
     attn_gain = lax.dynamic_slice_in_dim(gain_attn, my_columns, slice_width)
-    gain_attn_part = jnp.sum(normed_grad * token_slice * token_scale, axis=0)
-    inner = attn_gain * normed_grad
-    token_grad = (
-        middle_grad
-        + token_scale * inner
-        - token_slice * token_scale**3 * row_mean(token_slice * inner, 17)
-    ).astype(low)
-
-    there = swap_back([block_out[micro_rows:], token_grad[micro_rows:]], nz, 19)
-    block_out = jnp.concatenate([block_out[:micro_rows], there[0]], axis=0)
-    token_grad = jnp.concatenate([token_grad[:micro_rows], there[1]], axis=0)
-
-    pieces = [router_part.reshape(-1), gain_attn_part, gain_moe_part, gain_query_part, gain_key_part]
-    length = sum(piece.shape[0] for piece in pieces)
-    part_rows = -(-length // (shard_count * 1024)) * 8
-    flat = jnp.concatenate(
-        pieces + [jnp.zeros((shard_count * part_rows * 128 - length,), f32)]
-    ).reshape(shard_count, part_rows, 128)
-    summed = sum_small(flat, shard_count, group_count, 18).reshape(
-        shard_count, group_count, part_rows * 128
-    ).transpose(1, 0, 2).reshape(group_count, shard_count * part_rows * 128)
-    at = 0
-    sums = []
-    for piece in pieces:
-        sums.append(summed[:, at : at + piece.shape[0]])
-        at += piece.shape[0]
+    weight_grad, token_grad, block_out, gains, gate_acc, up_acc, down_acc = tail(
+        gate_pre_low, up_pre_low, hidden_low, tokens, middle_grad, token_scale,
+        attn_gain.reshape(1, slice_width), block_out, gains, rows_in, pair_grad, weight_part,
+        normed_part, nz, 15,
+    )
+    summed = summed.reshape(shard_count, group_count, part_rows * 128).transpose(
+        1, 0, 2
+    ).reshape(group_count, shard_count * part_rows * 128)
+    gains = gains.reshape(shard_count, group_count, 8, 128)
     return (
         block_out,
         token_grad,
-        sums[1].reshape(-1),
+        jnp.sum(gains[:, :, :gain_rows], axis=0).reshape(-1),
         weight_grad[:, :query_width],
         weight_grad[:, query_width : query_width + kv_width],
         weight_grad[:, query_width + kv_width :],
         w_out_grad,
-        jnp.sum(sums[3], axis=0),
-        jnp.sum(sums[4], axis=0),
-        sums[2].reshape(-1),
-        sums[0].reshape(router.shape),
+        jnp.sum(gains[:, :, gain_rows], axis=(0, 1)),
+        jnp.sum(gains[:, :, gain_rows + 1], axis=(0, 1)),
+        summed[:, :slice_width].reshape(-1),
+        summed[:, slice_width:length].reshape(router.shape),
         gate_acc[None],
         up_acc[None],
         down_acc[None],

time: 922 us -> 802 us (0.87)
  Pallas kernels: 785 us -> 689 us
  other arithmetic: 43.9 us -> 18 us
  local copies, waits for them, and re-layouts: 48.3 us -> 37.4 us
  matrix products: 32.6 us -> 42.1 us
    pallas_call x2 -> x1, Pallas kernels: 100 us -> 43.3 us  [reduce_rows(): pl.pallas_call(functools.partial(reduce_rows_kernel, nz), out_shape=jax.S...]
    pallas_call x2 -> x1, Pallas kernels: 106 us -> 73.3 us  [gather_rows(): pl.pallas_call(functools.partial(gather_rows_kernel, nz, count, columns),...]
    pallas_call x1, Pallas kernels: 128 us -> 112 us  [attend_back(): pl.pallas_call(functools.partial(attend_back_kernel, nz), in_specs=[vmem]...]
    unnamed x163 -> x70, local copies, waits for them, and re-layouts: 30.7 us -> 20.3 us
    convert_element_type x6 -> x1, other arithmetic: 10.3 us -> 1.11 us  [gathered_body(): jnp.concatenate([cotangent[:micro_rows], swapped_grad], axis=0).astype(f32)]
    pallas_call x11 -> x4, Pallas kernels: 319 us -> 323 us  [the longest x1 119 us: attend(): pl.pallas_call(functools.partial(attend_kernel, nz), in_specs=[vmem] * 10...]
where the time goes in v4:
time: 802 us; the launch traced here: 788 us
  Pallas kernels  689 us (86%)
  matrix products  42.1 us (5%)
  local copies, waits for them, and re-layouts  37.4 us (5%)
  other arithmetic  18 us (2%)
    pallas_call x1, Pallas kernels, run_experts(): pl.pallas_call(functools.partial(expert_kernel, nz, slots, block_rows), i...  137 us
    pallas_call x1, Pallas kernels, attend(): pl.pallas_call(functools.partial(attend_kernel, nz), in_specs=[vmem] * 10...  119 us
    pallas_call x1, Pallas kernels, attend_back(): pl.pallas_call(functools.partial(attend_back_kernel, nz), in_specs=[vmem]...  112 us
    pallas_call x1, Pallas kernels, join(): pl.pallas_call(functools.partial(join_kernel, nz), in_specs=[vmem] * 2 +...  104 us
    pallas_call x1, Pallas kernels, tail(): pl.pallas_call(functools.partial(tail_kernel, nz), in_specs=[vmem] * 6 +...  77.2 us
    pallas_call x1, Pallas kernels, gather_rows(): pl.pallas_call(functools.partial(gather_rows_kernel, nz, count, columns),...  73.3 us
    pallas_call x1, Pallas kernels, reduce_rows(): pl.pallas_call(functools.partial(reduce_rows_kernel, nz), out_shape=jax.S...  43.3 us
    pallas_call x1, Pallas kernels, turn(): pl.pallas_call(turn_kernel, in_specs=[vmem] * 4, out_specs=[vmem, any_spa...  22.8 us

profile of v4, /device:TPU:0, one launch (start us, length us, event | category | flops | bytes accessed | tf_op | source)
XLA Modules:
  0.0 787.9 jit_solution(4039218461991719718)
XLA Ops:
  3.0 73.3 %gather_rows.1 = (s32[320,128]{1,0:T(8,128)}, bf16[2048,1024]{1,0:T(8,128)(2,1)}, bf16[2048,128]{1,0:T(8,128)(2,1)}, bf16[2048,128]{1,0:T(8,128)(2,1)}, bf16[512...) custom-call(s32[40,128]{1,0:T(8,128)} %pad_bitcast_fusion.refs_0_, bf16[256,1024]{1,0:T(8,128)(2,1)} %refs_1_.1, ...), custom_call_target="tpu_custom_call" | custom-call | tf_op jit(solution)/shard_map/gather_rows/pallas_call | solution.py:1000
  81.2 2.1 fusion
  83.3 2.6 multiply_reduce_fusion.3
  86.8 6.7 fusion.22.q_pre
  93.4 1.4 convolution_convert_fusion.4.v_pre
  94.9 119.3 %attend.1 = (bf16[512,1024]{1,0:T(8,128)(2,1)}, bf16[512,1024]{1,0:T(8,128)(2,1)}, f32[512,1024]{1,0:T(8,128)}, f32[16,1,256]{2,1,0:T(1,128)}, bf16[4,2,2,256,25...) custom-call(f32[512,1024]{1,0:T(8,128)} %fusion.22.q_pre, f32[512,128]{1,0:T(8,128)} %copy.61.k_pre, ...), custom_call_target="tpu_custom_call" | custom-call | tf_op jit(solution)/shard_map/attend/pallas_call | solution.py:2110
  214.1 6.2 convolution_convert_fusion.2.attn_part
  220.3 1.4 dynamic_slice.23
  221.7 103.6 %join.1 = (f32[512,512]{1,0:T(8,128)}, f32[512,1]{1,0:T(8,128)}, bf16[512,512]{1,0:T(8,128)(2,1)}, bf16[4096,2048]{1,0:T(8,128)(2,1)}) custom-call(bf16[512,512]{1,0:T(8,128)(2,1)} %get-tuple-element.55.tok_ref, f32[1,512]{1,0:T(1,128)} %bitcast.101, bf16[512,2048]{1,0:T(8,128)(2,1)} %convolution_convert_fusion.2.attn_part), custom_call_target="tpu_custom_call" | custom-call | tf_op jit(solution)/shard_map/join/pallas_call | solution.py:2844
  325.3 2.5 reshape.227.routes_all
  328.8 137.3 %experts.1 = (bf16[4096,2048]{1,0:T(8,128)(2,1)}, f32[512,512]{1,0:T(8,128)}, f32[32,1,512]{2,1,0:T(1,128)}, f32[512,32]{1,0:T(8,128)}, bf16[8,256,2048]{2,1,0:T...) custom-call(bf16[4096,2048]{1,0:T(8,128)(2,1)} %get-tuple-element.65, ...), custom_call_target="tpu_custom_call" | custom-call | tf_op jit(solution)/shard_map/experts/pallas_call | solution.py:1705
  469.4 3.0 multiply_reduce_fusion
  473.5 1.1 maximum_convert_fusion.grad_ref
  474.6 22.8 %turn.1 = (f32[512,512]{1,0:T(8,128)}, bf16[512,2048]{1,0:T(8,128)(2,1)}) custom-call(f32[512,512]{1,0:T(8,128)} %get-tuple-element.63.middle_ref, f32[512,1]{1,0:T(8,128)} %get-tuple-element.64.scale_ref, f32[512,512]{1,0:T(8,128)} %get-tuple-element.146.inner_ref, f32[512,512]{1,0:T(8,128)} %maximum_convert_fusion.grad_ref), custom_call_target="tpu_custom_call" | custom-call | tf_op jit(solution)/shard_map/turn/pallas_call | solution.py:2911
  497.5 6.1 convolution_convert_fusion.1.wo_part
  505.1 5.3 convolution_convert_fusion.3.grad_ref
  512.8 112.1 %attend_back.1 = (bf16[512,1024]{1,0:T(8,128)(2,1)}, f32[1,128]{1,0:T(1,128)}, bf16[4096,256]{1,0:T(8,128)(2,1)}, f32[512,512]{1,0:T(8,128)}, f32[256,1024]{1,0:T(8,128)}, /*index=5*/f32[32,24,128]{2,1,0:T(8,128)}) custom-call(bf16[512,1024]{1,0:T(8,128)(2,1)} %get-tuple-element.71.q_ref, f32[512,1024]{1,0:T(8,128)} %fusion.22.q_pre, f32[1,128]{1,0:T(1,128)} %bitcast.110, ...), custom_call_target="tpu_custom_call" | custom-call | tf_op jit(solution)/shard_map/attend_back/pallas_call | solution.py:2452
  625.0 43.3 %reduce_rows.1 = f32[512,256]{1,0:T(8,128)} custom-call(bf16[4096,256]{1,0:T(8,128)(2,1)} %get-tuple-element.80.p_ref), custom_call_target="tpu_custom_call" | custom-call | tf_op jit(solution)/shard_map/reduce_rows/pallas_call | solution.py:1123
  669.5 1.5 multiply_reduce_fusion.1
  672.0 2.4 fusion.28
  674.4 2.0 add_convert_fusion.normed_part
  676.5 4.9 convolution_convert_fusion.w_part
  684.4 77.2 %tail.1 = (f32[256,1280]{1,0:T(8,128)}, bf16[512,512]{1,0:T(8,128)(2,1)}, bf16[512,512]{1,0:T(8,128)(2,1)}, f32[32,8,128]{2,1,0:T(8,128)}, f32[2048,768]{1,0:T(8...) custom-call(bf16[512,512]{1,0:T(8,128)(2,1)} %get-tuple-element.55.tok_ref, f32[512,512]{1,0:T(8,128)} %get-tuple-element.70.mid_ref, ...), custom_call_target="tpu_custom_call" | custom-call | tf_op jit(solution)/shard_map/tail/pallas_call | solution.py:2766
  761.6 2.4 slice.54
  764.0 1.7 fusion.24
  765.7 1.5 slice_reduce_fusion
  767.2 1.5 slice_reduce_fusion.1
  768.8 1.1 reshape.243
  771.9 1.9 copy.82
  775.6 6.1 copy.85
  781.6 2.8 copy.86
  784.7 2.7 copy.87
  (120 shorter events, 26.6 us)
Async XLA Ops:
  0.6 82.7 %copy-start.20 = (f32[2048]{0:T(1024)S(1)}, f32[2048]{0:T(1024)}, u32[]{:S(2)}) copy-start(f32[2048]{0:T(1024)} %param.20) | copy-start | bytes 24580
  86.8 6.7 copy-start.6
  86.8 6.7 copy-start.11
  220.3 107.5 %copy-start.16 = (bf16[2048,32]{0,1:T(8,128)(2,1)S(1)}, bf16[2048,32]{0,1:T(8,128)(2,1)}, u32[]{:S(2)}) copy-start(bf16[2048,32]{0,1:T(8,128)(2,1)} %param.28) | copy-start | bytes 393220
  328.8 140.6 %copy-start = (f32[512,512]{1,0:T(8,128)S(1)}, f32[512,512]{1,0:T(8,128)}, u32[]{:S(2)}) copy-start(f32[512,512]{1,0:T(8,128)} %get-tuple-element.63.middle_ref) | copy-start | bytes 3145732
  328.8 140.6 %copy-start.17 = (f32[512]{0:T(512)S(1)}, f32[512]{0:T(512)}, u32[]{:S(2)}) copy-start(f32[512]{0:T(512)} %dynamic_slice.23) | copy-start | bytes 6148
  466.1 7.3 slice-start.4
  472.4 25.0 %copy-start.22 = (bf16[512,1024]{1,0:T(8,128)(2,1)S(1)}, bf16[512,1024]{1,0:T(8,128)(2,1)}, u32[]{:S(2)}) copy-start(bf16[512,1024]{1,0:T(8,128)(2,1)} %get-tuple-element.61) | copy-start | bytes 3145732
  497.4 6.1 copy-start.5
  497.4 6.1 copy-start.14
  505.1 5.3 copy-start.8
  510.4 1.0 copy-start.2
  624.9 44.6 %copy-start.3 = (f32[512,128]{1,0:T(8,128)S(1)}, f32[512,128]{1,0:T(8,128)}, u32[]{:S(2)}) copy-start(f32[512,128]{1,0:T(8,128)} %copy.61.k_pre) | copy-start | bytes 786436
  624.9 44.6 %copy-start.18 = (f32[128]{0:T(128)S(1)}, f32[128]{0:T(128)}, u32[]{:S(2)}) copy-start(f32[128]{0:T(128)} %param.26) | copy-start | bytes 1540
  625.0 46.3 %copy-start.13 = (bf16[2048,128]{1,0:T(8,128)(2,1)S(1)}, bf16[2048,128]{1,0:T(8,128)(2,1)}, u32[]{:S(2)}) copy-start(bf16[2048,128]{1,0:T(8,128)(2,1)} %get-tuple-element.58) | copy-start | bytes 1572868
  669.3 2.6 copy-start.21
  669.3 2.6 copy-start.23
  672.0 2.4 copy-start.4
  672.0 2.4 copy-start.12
  674.4 2.1 copy-start.7
  676.5 4.9 copy-start.19
  676.5 5.5 copy-start.1
  676.5 5.5 copy-start.10
  761.6 12.2 %copy-start.15 = (bf16[512,512]{1,0:T(8,128)(2,1)S(1)}, bf16[512,512]{1,0:T(8,128)(2,1)}, u32[]{:S(2)}) copy-start(bf16[512,512]{1,0:T(8,128)(2,1)} %get-tuple-element.172) | copy-start | bytes 1572868
  761.6 13.0 %copy-start.9 = (f32[256,1024]{1,0:T(8,128)S(1)}, f32[256,1024]{1,0:T(8,128)}, u32[]{:S(2)}) copy-start(f32[256,1024]{1,0:T(8,128)} %get-tuple-element.177) | copy-start | bytes 3145732
  773.8 7.8 slice-start.2
  775.6 6.1 slice-start.3
  775.6 8.9 %slice-start = ((s8[6291456]{0:T(1024)(128)(4,1)}), s8[4194304]{0:T(1024)(128)(4,1)S(1)}, s32[]{:S(2)}) async-start(s8[6291456]{0:T(1024)(128)(4,1)} %bitcast.80), calls=%async_computation | async-start | bytes 8388608
  781.6 3.1 slice-start.1

commit v5 on v4

--- a/solution.py
+++ b/solution.py
@@ -1362,12 +1362,45 @@
     return at
 
 
-def expert_kernel(nz, slots, block_rows, x_all, g_all, routes_all, router_ref, wg, wu, wd,
-                  out_all, back_ref, gg_got, gates_ref, xr_all, gs_all, hid_all, gp_all, up_all,
-                  gg_ref, x_ref, g_ref, t_ref, o_ref, xr, gs, hid, gp, up, st,
+def tile_item(nz, z, k):
+    return far_first(nz, z, jnp.where(k == nz - 1, nz - 1, nz - 2 - k))
+
+
+def line_schedule(nz):
+    order = []
+    for here in range(nz):
+        near = sorted(range(nz), key=lambda other: (-abs(other - here), other))[::-1]
+        order.append(near[1:] + near[:1])
+    sent = {}
+    steps = [{} for _ in range(nz)]
+
+    def send(here, to):
+        if (here, to) not in sent:
+            ready = 2 * order[here].index(to) + 2
+            back = here - 1 if to > here else here + 1
+            if 0 <= back < nz:
+                ready = max(ready, send(back, to)) + 1
+                steps[here].setdefault(ready, []).append(to)
+            sent[here, to] = ready
+        return sent[here, to]
+
+    for here in range(nz):
+        for to in range(nz):
+            if to != here:
+                send(here, to)
+    for here in range(nz):
+        arrivals = [send(near, here) for near in (here - 1, here + 1) if 0 <= near < nz]
+        last = max(arrivals + [2 * order[here].index(here) + 2]) + 1
+        steps[here].setdefault(last, []).append(here)
+    return steps
+
+
+def expert_kernel(nz, slots, block_rows, tok_ref, gain_ref, router_ref, attn_part, g_all, routes_all,
+                  wg_all, wu_all, wd_all, middle_ref, scale_ref, low_ref, x_all, out_all, back_ref, gg_got, gates_ref, xr_all, gs_all, hid_all, gp_all, up_all,
+                  wg, wu, wd, s_in_w, gg_ref, x_ref, g_ref, t_ref, o_ref, xr, gs, hid, gp, up, st,
                   w, lp, rx, rxd, ry, ryd, rz,
                   s_in, s_out, s_save, s_p, r_p, s_x, s_y, s_dx, s_dy, s_z, r_x, r_y, r_dx, r_dy, r_z,
-                  s_g, r_g):
+                  s_g, r_g, *refs):
     z, x, y, c = place()
     shard, group = lax.axis_index("fsdp"), lax.axis_index("tp")
     expert = shard * 4 + group
@@ -1380,7 +1413,12 @@
     partner = device(z, x, y, 1 - c)
     xn, yn = device(z, 1 - x, y, c), device(z, x, 1 - y, c)
     up_dev, down_dev = device(z + 1, x, y, c), device(z - 1, x, y, c)
+    n_c, n_s = len(ReduceCols.scratch(16, 128, low)), len(RowSums.scratch(128))
+    columns = ReduceCols(attn_part, middle_ref, refs[:n_c])
+    sums = RowSums(refs[n_c : n_c + n_s])
+    moe_rows = GatherAll(nz, low_ref, x_all, refs[n_c + n_s :], half)
     greet_all(shard, group, 2 * nz, 4)
+    columns.start()
     tiles = 2 * nz
     devices = 8 * nz
 
@@ -1390,7 +1428,7 @@
                       (other // 4, other % 4))
 
     def tile_of(j):
-        return far_first(nz, z, j // 2) * 2 + jnp.where(j % 2 == 0, 1 - x, x)
+        return tile_item(nz, z, j // 2) * 2 + jnp.where(j % 2 == 0, 1 - x, x)
 
     def tile_rows(j):
         return pl.ds(pl.multiple_of(tile_of(j) * rows, rows), rows)
@@ -1487,7 +1525,7 @@
             )
 
     def compute(j):
-        zz = far_first(nz, z, j // 2)
+        zz = tile_item(nz, z, j // 2)
         slot = j % 2
         load(j).wait()
         for copy in load_t(j):
@@ -1553,6 +1591,14 @@
 
         lax.fori_loop(0, width // cols, take, 0)
 
+        pl.when(j == 0)(lambda: moe_rows.second(2))
+        for k in range(3, nz):
+            pl.when(j == 1)(lambda: moe_rows.second(k))
+
+        @pl.when((j % 2 == 1) & (j < tiles - 1))
+        def _():
+            moe_rows.ready(tile_item(nz, z, j // 2 + 1))
+
         @pl.when(j < tiles - 1)
         def _():
             load(j + 1).start()
@@ -1619,7 +1665,7 @@
 
             @pl.when(j >= 2)
             def _():
-                before_zz = far_first(nz, z, j // 2 - 1)
+                before_zz = tile_item(nz, z, j // 2 - 1)
                 k = before_zz * 4 + rel
                 remote(st.at[slot, i], lp.at[before_zz, rel], s_p.at[k], r_p.at[k], partner).wait_send()
 
@@ -1636,42 +1682,88 @@
         lax.fori_loop(0, 2, to_partner, 0)
         lax.fori_loop(0, 2, to_own, 0)
 
-    for copy in (load(0),) + load_t(0) + load_g(0):
+    weights = [pltpu.make_async_copy(src, dst, s_in_w.at[n])
+               for n, (src, dst) in enumerate(((wg_all, wg), (wu_all, wu), (wd_all, wd)))]
+    for copy in load_t(0) + load_g(0) + tuple(weights):
         copy.start()
+
+    corner = diagonal()
+    columns.first()
+    columns.second()
+
+    def residual(n, carry):
+        here = pl.ds(pl.multiple_of(n * 128, 128), 128)
+        total = middle_ref[here, :] + tok_ref[here, :].astype(f32)
+        middle_ref[here, :] = total
+        sums.got[0, pl.ds(n, 1), :] = to_row(jnp.sum(total * total, axis=1, keepdims=True), corner)
+        return carry
+
+    def norm(n, carry):
+        here = pl.ds(pl.multiple_of(n * 128, 128), 128)
+        scale = lax.rsqrt(to_column(sums.total(n), corner) / width + norm_eps)
+        scale_ref[here, :] = scale
+        low_ref[here, :] = (middle_ref[here, :] * scale * gain_ref[...]).astype(low)
+        return carry
+
+    lax.fori_loop(0, rows // 128, residual, 0)
+    sums.start()
+    sums.wait()
+    lax.fori_loop(0, rows // 128, norm, 0)
+    moe_rows.own().start()
+    moe_rows.own().wait()
+    moe_rows.first(0)
+    moe_rows.first(1)
+    moe_rows.second(0)
+    moe_rows.first(2)
+    moe_rows.second(1)
+    moe_rows.third(0)
+    for k in range(3, nz):
+        moe_rows.first(k)
+    moe_rows.third(1)
+    moe_rows.ready(tile_item(nz, z, 0))
+    load(0).start()
+    for copy in weights:
+        copy.wait()
+    schedule = line_schedule(nz)
+    last_step = max(max(steps) for steps in schedule)
 
     def step(j, carry):
         k, odd = j // 2, j % 2 == 1
         pl.when(j < tiles)(lambda: compute(j))
+        pl.when(j == 0)(lambda: moe_rows.third(2))
+        for n in range(3, nz):
+            pl.when(j == 2)(lambda: moe_rows.third(n))
 
         @pl.when(j == tiles)
         def _():
             gg_got[expert] = gg_ref[shard]
             loop_from_one(devices, lambda n: swap(n).start())
 
+        @pl.when(jnp.logical_not(odd) & (k < nz))
+        def _():
+            zz = tile_item(nz, z, k)
+            stage_d(zz, 3, 0)
+            stage_d(zz, 1, 0)
+
         @pl.when(odd & (k < nz))
         def _():
-            zz = far_first(nz, z, k)
-            stage_d(zz, 3, 0)
-            stage_d(zz, 1, 0)
-
-        @pl.when(jnp.logical_not(odd) & (k >= 1) & (k <= nz))
-        def _():
-            zz = far_first(nz, z, k - 1)
+            zz = tile_item(nz, z, k)
             stage_d(zz, 2, 1)
             stage_d(zz, 0, 1)
             stage_e(zz)
 
-        @pl.when((k >= 2) & jnp.logical_not(odd))
+        @pl.when((k >= 1) & (k < nz + 1) & jnp.logical_not(odd))
         def _():
-            stage_f1(far_first(nz, z, k - 2))
-
-        @pl.when((k >= 2) & odd)
-        def _():
-            stage_f2(far_first(nz, z, k - 2))
+            stage_f1(tile_item(nz, z, k - 1))
+
+        for here, steps in enumerate(schedule):
+            for at, places in steps.items():
+                for to in places:
+                    pl.when((z == here) & (j == at))(lambda to=to: stage_f2(jnp.int32(to)))
 
         return carry
 
-    lax.fori_loop(0, 2 * (nz + 2), step, 0)
+    lax.fori_loop(0, last_step + 1, step, 0)
     loop_from_one(devices, lambda n: swap(n).wait())
     save_out(tiles - 1).wait()
     for copy in saves(tiles - 1):
@@ -1687,11 +1779,13 @@
         return carry
 
     lax.fori_loop(0, nz, finish, 0)
-
-
-def run_experts(x_all, g_all, routes_all, router, gate_w, up_w, down_w, block_rows, slots, nz,
-                collective_id):
-    total, width = x_all.shape
+    columns.finish()
+    moe_rows.finish_sends()
+
+
+def run_experts(tokens, gain, router, attn_part, g_all, routes_all, gate_w, up_w, down_w, block_rows,
+                slots, nz, collective_id):
+    total, width = g_all.shape
     hidden = gate_w.shape[1]
     experts = router.shape[1]
     tiles = 2 * nz
@@ -1704,9 +1798,11 @@
     vm, dma, shape = pltpu.VMEM, pltpu.SemaphoreType.DMA, jax.ShapeDtypeStruct
     return pl.pallas_call(
         functools.partial(expert_kernel, nz, slots, block_rows),
-        in_specs=[any_space] * 3 + [vmem] * 4,
-        out_specs=[any_space, vmem, vmem, vmem] + [any_space] * 5,
+        in_specs=[vmem] * 3 + [any_space] * 6,
+        out_specs=[vmem] * 3 + [any_space] * 2 + [vmem] * 3 + [any_space] * 5,
         out_shape=[
+            shape((rows, cols), f32), shape((rows, 1), f32), shape((rows, cols), low),
+            shape((total, width), low),
             shape((total, width), low), shape((rows, cols), f32), shape((4 * tiles, 1, rows), f32),
             shape((rows, experts), f32),
             shape((tiles, pairs, width), low), shape((tiles, pairs, width), low),
@@ -1714,6 +1810,7 @@
             shape((tiles, pairs, hidden), low),
         ],
         scratch_shapes=[
+            vm((width, hidden), low), vm((width, hidden), low), vm((hidden, width), low), dma((3,)),
             vm((tiles, 1, rows), f32), vm((rows, width), low), vm((rows, width), low),
             vm((rows, routes_all.shape[1]), jnp.int32), vm((rows, width), low),
             vm((pairs, width), low), vm((pairs, width), low),
@@ -1724,12 +1821,13 @@
             vm((nz, rows, cols), low), vm((nz, half, cols), low),
             vm((nz + 1, rows, cols), low),
             dma((5,)), dma, dma((5,)), dma((4 * nz,)), dma((4 * nz,)),
-        ] + [dma((nz,))] * 9 + [dma((nz + 1,))] + [dma((4 * tiles,))] * 2,
+        ] + [dma((nz,))] * 9 + [dma((nz + 1,))] + [dma((4 * tiles,))] * 2
+        + ReduceCols.scratch(rows, cols, low) + RowSums.scratch(rows) + GatherAll.scratch(nz),
         compiler_params=pltpu.CompilerParams(
             collective_id=collective_id, has_side_effects=True, vmem_limit_bytes=62 << 20
         ),
         name="experts",
-    )(x_all, g_all, routes_all, router, gate_w, up_w, down_w)
+    )(tokens, gain, router, attn_part, g_all, routes_all, gate_w, up_w, down_w)
 
 
 def near_first(nz, z, k):
@@ -1832,12 +1930,15 @@
             copy.wait_recv()
             self.pair(zz, rel).start()
 
-    def finish(self):
+    def ready(self, zz):
+        for rel in self.parts():
+            self.pair(zz, rel, False).wait_recv()
+
+    def finish_sends(self):
         z = self.place[0]
 
         def step(zz, carry):
             for rel in self.parts():
-                self.pair(zz, rel, False).wait_recv()
                 self.pair(zz, rel).wait_send()
             up, down = self.line(zz)
             pl.when((zz <= z) & (z < self.nz - 1))(lambda: up.wait_send())
@@ -1847,6 +1948,14 @@
             return carry
 
         lax.fori_loop(0, self.nz, step, 0)
+
+    def finish(self):
+        def step(zz, carry):
+            self.ready(zz)
+            return carry
+
+        lax.fori_loop(0, self.nz, step, 0)
+        self.finish_sends()
 
 
 class GatherCausal:
@@ -2277,26 +2386,23 @@
     @staticmethod
     def scratch(nz, rows, cols, kind):
         vm, dma = pltpu.VMEM, pltpu.SemaphoreType.DMA
-        return [vm((nz, rows, cols), kind), vm((nz, rows, cols), kind),
-                vm((nz + 1, rows, cols), kind)] + [dma((nz,))] * 4 + [dma((nz + 1,))]
-
-    def __init__(self, nz, partial, out, refs):
-        self.w, self.rx, self.rz, self.s_l, self.s_x, self.s_z, self.r_x, self.r_z = refs
-        self.nz, self.partial, self.out = nz, partial, out
+        return [vm((nz, rows, cols), kind), vm((nz, rows, cols), kind), vm((nz, rows, cols), kind),
+                vm((nz + 1, rows, cols), kind)] + [dma((nz,))] * 3 + [dma((nz + 1,))]
+
+    def __init__(self, nz, left, right, out, refs):
+        self.w, self.sent, self.rx, self.rz, self.s_x, self.s_z, self.r_x, self.r_z = refs
+        self.nz, self.left, self.right, self.out = nz, left, right, out
         self.rows = out.shape[0]
         self.place = z, x, y, c = place()
         self.xn = device(z, 1 - x, y, c)
         self.up, self.down = device(z + 1, x, y, c), device(z - 1, x, y, c)
 
-    def block(self, zz, xx):
-        return self.partial.at[pl.ds(pl.multiple_of((zz * 2 + xx) * self.rows, self.rows), self.rows)]
+    def make(self, zz, xx, ref):
+        at = pl.ds(pl.multiple_of((zz * 2 + xx) * self.rows, self.rows), self.rows)
+        ref[...] = dot_first(self.left[:, at], self.right[...]).astype(ref.dtype)
 
     def side(self, zz):
-        return remote(self.block(zz, 1 - self.place[1]), self.rx.at[zz],
-                      self.s_x.at[zz], self.r_x.at[zz], self.xn)
-
-    def load(self, zz):
-        return pltpu.make_async_copy(self.block(zz, self.place[1]), self.w.at[zz], self.s_l.at[zz])
+        return remote(self.sent.at[zz], self.rx.at[zz], self.s_x.at[zz], self.r_x.at[zz], self.xn)
 
     def line(self, zz, slot, where):
         return remote(self.w.at[zz], self.rz.at[slot], self.s_z.at[zz], self.r_z.at[slot], where)
@@ -2309,16 +2415,16 @@
         lax.fori_loop(0, self.nz, step, 0)
 
     def send(self, k):
-        zz = far_first(self.nz, self.place[0], k)
+        zz, x = far_first(self.nz, self.place[0], k), self.place[1]
+        self.make(zz, 1 - x, self.sent.at[zz])
         self.side(zz).start()
-        self.load(zz).start()
+        self.make(zz, x, self.w.at[zz])
 
     send_line = ScatterAll.send_line
     passes = ScatterAll.passes
 
     def first(self, k):
         zz, z = far_first(self.nz, self.place[0], k), self.place[0]
-        self.load(zz).wait()
         self.side(zz).wait_recv()
         add_blocks(self.w.at[zz], [self.rx.at[zz]], 0, self.rows)
         pl.when((zz != z) & jnp.logical_not(self.passes(zz)))(lambda: self.send_line(zz))
@@ -2347,9 +2453,76 @@
         lax.fori_loop(0, self.nz, step, 0)
 
 
-def attend_back_kernel(nz, q_ref, q_pre, gq_ref, cos_ref, sin_ref, kv_ref, start_ref, lse_ref,
-                       delta_ref, grad_ref, small_ref, out_part, wo_part, q_grad, gain_grad, sides, out_sum, wo_sum, small_out,
-                       acc, k_acc, v_acc, *refs):
+class ReduceCausal:
+    @staticmethod
+    def scratch(nz, rows, cols, kind):
+        vm, dma = pltpu.VMEM, pltpu.SemaphoreType.DMA
+        return [vm((nz, 2, 2, rows, cols), kind), vm((2, rows, cols), kind),
+                dma((2 * nz,)), dma((2 * nz,)), dma((2,)), dma((2,))]
+
+    def __init__(self, nz, sides, out, refs):
+        self.got, self.across, self.s_z, self.r_z, self.s_x, self.r_x = refs
+        self.nz, self.sides, self.out = nz, sides, out
+        self.place = z, x, y, c = place()
+        self.xn = device(z, 1 - x, y, c)
+        self.to = (device(z - 1, x, y, c), device(z + 1, x, y, c))
+
+    def line(self, zz, micro):
+        k = zz * 2 + micro
+        return remote(self.sides.at[zz, :, micro], self.got.at[zz, :, micro],
+                      self.s_z.at[k], self.r_z.at[k], self.to[micro])
+
+    def side(self, micro):
+        z, x = self.place[:2]
+        return remote(self.sides.at[z, 1 - x, micro], self.across.at[micro],
+                      self.s_x.at[micro], self.r_x.at[micro], self.xn)
+
+    def take(self, zz, micro):
+        first = self.place[0] == (self.nz - 1 if micro == 0 else 0)
+
+        @pl.when(jnp.logical_not(first))
+        def _():
+            self.line(zz, micro).wait_recv()
+            for xx in range(2):
+                add_blocks(self.sides.at[zz, xx, micro], [self.got.at[zz, xx, micro]], 0,
+                           self.sides.shape[3])
+
+    def turn(self, hop):
+        z, nz = self.place[0], self.nz
+        for micro in range(2):
+            @pl.when(hop == (nz - 1 - z if micro == 0 else z))
+            def _():
+                def step(n, carry):
+                    zz = n if micro == 0 else nz - 1 - n
+                    self.take(zz, micro)
+                    self.line(zz, micro).start()
+                    return carry
+
+                lax.fori_loop(0, z if micro == 0 else nz - 1 - z, step, 0)
+                self.take(z, micro)
+                self.side(micro).start()
+
+    def finish(self):
+        z, x = self.place[:2]
+        for micro in range(2):
+            self.side(micro).wait_recv()
+            add_blocks(self.sides.at[z, x, micro], [self.across.at[micro]], 0, self.sides.shape[3],
+                       self.out.at[micro])
+        for micro in range(2):
+            self.side(micro).wait_send()
+
+            def step(n, carry):
+                self.line(n if micro == 0 else self.nz - 1 - n, micro).wait_send()
+                return carry
+
+            lax.fori_loop(0, z if micro == 0 else self.nz - 1 - z, step, 0)
+
+
+def attend_back_kernel(nz, gq_ref, cos_ref, sin_ref, start_ref, lse_ref, delta_ref, small_ref,
+                       mid_all, heads_all, q_all, kv_all, grad_all, pre_all, out_part,
+                       q_grad, gain_grad, kv_sum, out_sum, wo_sum, small_out,
+                       mid_ref, heads_ref, q_ref, kv_ref, grad_ref, q_pre, s_in,
+                       sides, acc, k_acc, v_acc, *refs):
     shards = 2 * nz
     shard = lax.axis_index("fsdp")
     width = kv_ref.shape[4] // 2
@@ -2361,18 +2534,24 @@
     split = len(ScatterAll.scratch(nz, 16, 128, low, 0))
     outs = ScatterAll(nz, out_part, out_sum, refs[:split], 0)
     end = split + len(ReduceRows.scratch(nz, 16, 128, low))
-    weights = ReduceRows(nz, wo_part, wo_sum, refs[split:end])
-    smalls = SmallSums(nz, small_ref, small_out, refs[end:])
+    weights = ReduceRows(nz, mid_ref, heads_ref, wo_sum, refs[split:end])
+    last = end + len(SmallSums.scratch(nz, (8, 128), jnp.float32))
+    smalls = SmallSums(nz, small_ref, small_out, refs[end:last])
+    keys_out = ReduceCausal(nz, sides, kv_sum, refs[last:])
     greet_all(lax.axis_index("fsdp"), lax.axis_index("tp"), shards, 4)
+    outs.start()
+    fetches = [pltpu.make_async_copy(src, dst, s_in.at[n]) for n, (src, dst) in enumerate((
+        (mid_all, mid_ref), (heads_all, heads_ref), (q_all, q_ref), (kv_all, kv_ref),
+        (grad_all, grad_ref), (pre_all, q_pre)))]
+    for copy in fetches:
+        copy.start()
     smalls.start()
-    outs.start()
 
     sides[...] = jnp.zeros_like(sides)
     acc[...] = jnp.zeros_like(acc)
 
     def attention(u):
         micro, here, key_place, owner = stream_unit(u, nz)
-        rows = pl.ds(pl.multiple_of((owner * 2 + micro) * block, block), block)
         bias = key_bias(micro, here, key_place, block, start_ref)
         both = kv_ref.at[owner // 2, owner % 2, micro]
         keys, values = both[:, :width], both[:, width:]
@@ -2393,8 +2572,9 @@
             return carry
 
         lax.fori_loop(0, heads, head, 0, unroll=2)
-        sides[rows, pl.ds(0, width)] = (k_acc[...] * width ** (-0.5)).astype(low)
-        sides[rows, pl.ds(width, width)] = v_acc[...].astype(low)
+        side = sides.at[owner // 2, owner % 2, micro]
+        side[:, :width] = (k_acc[...] * width ** (-0.5)).astype(low)
+        side[:, width:] = v_acc[...].astype(low)
 
     def close(at, total):
         micro, h = at // heads, at % heads
@@ -2418,57 +2598,68 @@
         def at(fn, k):
             pl.when((k >= 0) & (k < nz))(lambda: fn(k))
 
-        at(outs.first, u)
-        at(outs.second, u - 1)
-        at(weights.send, u)
-        pl.when(u == 2)(smalls.second)
-        pl.when(2 * u < count)(lambda: attention(2 * u))
-        pl.when(2 * u + 1 < count)(lambda: attention(2 * u + 1))
-        pl.when(u == (shards + 2) // 2)(close_all)
-        at(outs.third, u - 2)
-        at(outs.fourth, u - 3)
-        at(weights.second, u - 2)
-        at(weights.first, u - 1)
+        for n in range(4):
+            pl.when(4 * u + n < count)(lambda: attention(4 * u + n))
+        at(outs.second, u)
+        at(weights.send, u + 1)
+        at(outs.first, u + 2)
+        pl.when(u == 1)(smalls.second)
+        at(keys_out.turn, u - done)
+        at(outs.third, u - 1)
+        at(outs.fourth, u - 2)
+        at(weights.second, u - 3)
+        at(weights.first, u - 2)
+        pl.when(u == done + 1)(close_all)
         return carry
 
-    lax.fori_loop(0, max(nz + 3, nz + 2), unit, 0)
-
+    done = (shards + 2 - 1) // 4
+    outs.first(0)
+    for copy in fetches:
+        copy.wait()
+    weights.send(0)
+    outs.first(1)
+    lax.fori_loop(0, nz + 3, unit, 0)
+    keys_out.finish()
     outs.finish()
     weights.finish()
     smalls.finish()
 
 
 def attend_back(query, q_pre, gain_query, cosine, sine, keys_values, starts, log_total, delta,
-                grad, small, out_part, wo_part, nz, collective_id):
+                grad, small, middle_grad, heads_low, out_part, nz, collective_id):
     rows, columns = query.shape
     width = keys_values.shape[4] // 2
     heads = columns // width
     block = rows // 2
     cols = out_part.shape[1] // 4
-    wo_shape = (wo_part.shape[0] // (2 * nz), wo_part.shape[1])
+    wo_shape = (middle_grad.shape[1] // (2 * nz), columns)
     any_space = pl.BlockSpec(memory_space=pl.ANY)
     vmem = pl.BlockSpec(memory_space=pltpu.VMEM)
     vm, shape, f32, low = pltpu.VMEM, jax.ShapeDtypeStruct, jnp.float32, jnp.bfloat16
     return pl.pallas_call(
         functools.partial(attend_back_kernel, nz),
-        in_specs=[vmem] * 11 + [any_space] * 2,
+        in_specs=[vmem] * 7 + [any_space] * 7,
         out_specs=[vmem] * 6,
         out_shape=[
             shape((rows, columns), low), shape((1, width), f32),
-            shape((rows * 2 * nz, 2 * width), low),
+            shape((2, block, 2 * width), f32),
             shape((rows, cols), f32), shape(wo_shape, f32),
             shape((8 * nz,) + small.shape[1:], f32),
         ],
-        scratch_shapes=[
+        scratch_shapes=[vm(middle_grad.shape, low)] + [vm((rows, columns), low)] * 2 + [
+            vm((nz, 2, 2, block, 2 * width), low), vm((rows, columns), low),
+            vm((rows, columns), f32), pltpu.SemaphoreType.DMA((6,)),
+            vm((nz, 2, 2, block, 2 * width), low),
             vm((2 * heads, width, block), f32), vm((block, width), f32), vm((block, width), f32),
         ] + ScatterAll.scratch(nz, rows, cols, low, 0) + ReduceRows.scratch(nz, *wo_shape, low)
-        + SmallSums.scratch(nz, small.shape[1:], f32),
+        + SmallSums.scratch(nz, small.shape[1:], f32)
+        + ReduceCausal.scratch(nz, block, 2 * width, low),
         compiler_params=pltpu.CompilerParams(
             collective_id=collective_id, has_side_effects=True, vmem_limit_bytes=62 << 20
         ),
         name="attend_back",
-    )(query, q_pre, gain_query, cosine, sine, keys_values, starts, log_total, delta, grad, small,
-      out_part, wo_part)
+    )(gain_query, cosine, sine, starts, log_total, delta, small, middle_grad, heads_low, query,
+      keys_values, grad, q_pre, out_part)
 
 
 def to_row(column, eye):
@@ -2605,10 +2796,10 @@
     lax.fori_loop(1, count, step, 0)
 
 
-def tail_kernel(nz, tok_ref, mid_ref, scale_ref, gain_ref, block_ref, small_ref,
-                gp_all, up_all, hid_all, xr_all, gs_all, w_part, normed_part,
-                w_sum, token_out, block_out, small_out, dwg, dwu, dwd,
-                gp_ref, up_ref, hid_ref, x_panel, g_panel, o_gate, o_up, o_down, s_in, s_out,
+def tail_kernel(nz, tok_ref, scale_ref, gain_ref, block_ref, small_ref, left_all, right_all, mid_all,
+                gp_all, up_all, hid_all, xr_all, gs_all, normed_part,
+                wq_out, wk_out, wv_out, token_out, block_out, small_out, dwg, dwu, dwd,
+                left_ref, right_ref, mid_ref, s_m, w_sum, gp_ref, up_ref, hid_ref, x_panel, g_panel, o_gate, o_up, o_down, s_in, s_out,
                 normed, token, s_w, r_w, s_l, s_g, r_g, *refs):
     z, x, y, c = place()
     shard, group = lax.axis_index("fsdp"), lax.axis_index("tp")
@@ -2622,12 +2813,18 @@
     panels = xr_all.shape[1] // panel
     f32, low = jnp.float32, jnp.bfloat16
     n_w, n_c = len(ReduceRows.scratch(nz, 16, 128, low)), len(ReduceCols.scratch(16, 128, low))
-    weights = ReduceRows(nz, w_part, w_sum, refs[:n_w])
+    weights = ReduceRows(nz, left_ref, right_ref, w_sum, refs[:n_w])
     columns = ReduceCols(normed_part, normed, refs[n_w : n_w + n_c])
     sums = RowSums(refs[n_w + n_c :])
     mirror = device(nz - 1 - z, x, y, c)
     greet_all(shard, group, shards, 4)
     columns.start()
+    fetches = [pltpu.make_async_copy(src, dst, s_m.at[n]) for n, (src, dst) in enumerate((
+        (left_all, left_ref), (right_all, right_ref), (mid_all, mid_ref)))]
+    for copy in fetches:
+        copy.start()
+    for copy in fetches:
+        copy.wait()
     weights.start()
     top, bottom = pl.ds(0, half), pl.ds(half, half)
     swaps = [remote(src.at[bottom], dst.at[bottom], s_w.at[n], r_w.at[n], mirror)
@@ -2747,17 +2944,22 @@
         copy.wait()
     for copy in stores(panels - 1):
         copy.wait()
+    first, second = wq_out.shape[1], wq_out.shape[1] + wk_out.shape[1]
+    wq_out[...] = w_sum[:, :first]
+    wk_out[...] = w_sum[:, first:second]
+    wv_out[...] = w_sum[:, second:]
     columns.finish()
     weights.finish()
 
 
-def tail(gate_grad, up_grad, hidden, tokens, middle_grad, scale, gain, block_out, small, rows_in,
-         pair_grad, w_part, normed_part, nz, collective_id):
+def tail(gate_grad, up_grad, hidden, tokens, middle_grad, scale, gain, block_out, small, normed_low,
+         pre_grad, query_width, rows_in, pair_grad, normed_part, nz, collective_id):
     rows, cols = tokens.shape
     pairs, features = rows_in.shape
     hidden_width = hidden.shape[1]
     panel = 256
-    w_shape = (w_part.shape[0] // (2 * nz), w_part.shape[1])
+    w_shape = (normed_low.shape[1] // (2 * nz), pre_grad.shape[1])
+    kv_width = (pre_grad.shape[1] - query_width) // 2
     devices = 8 * nz
     any_space = pl.BlockSpec(memory_space=pl.ANY)
     vmem = pl.BlockSpec(memory_space=pltpu.VMEM)
@@ -2765,15 +2967,17 @@
     dma = pltpu.SemaphoreType.DMA
     return pl.pallas_call(
         functools.partial(tail_kernel, nz),
-        in_specs=[vmem] * 6 + [any_space] * 7,
-        out_specs=[vmem, any_space, any_space, vmem] + [any_space] * 3,
+        in_specs=[vmem] * 5 + [any_space] * 9,
+        out_specs=[vmem] * 3 + [any_space, any_space, vmem] + [any_space] * 3,
         out_shape=[
-            shape(w_shape, f32), shape((rows, cols), low), shape((rows, cols), low),
+            shape((w_shape[0], query_width), f32), shape((w_shape[0], kv_width), f32),
+            shape((w_shape[0], kv_width), f32), shape((rows, cols), low), shape((rows, cols), low),
             shape((devices,) + small.shape, f32),
             shape((features, hidden_width), f32), shape((features, hidden_width), f32),
             shape((hidden_width, features), f32),
         ],
-        scratch_shapes=[vm((pairs, hidden_width), low)] * 3 + [
+        scratch_shapes=[vm(normed_low.shape, low), vm(pre_grad.shape, low), vm((rows, cols), f32),
+                        dma((3,)), vm(w_shape, f32)] + [vm((pairs, hidden_width), low)] * 3 + [
             vm((pairs, panel), low), vm((pairs, panel), low),
             vm((panel, hidden_width), f32), vm((panel, hidden_width), f32),
             vm((hidden_width, panel), f32), dma((5,)), dma((3,)),
@@ -2785,8 +2989,8 @@
             collective_id=collective_id, has_side_effects=True, vmem_limit_bytes=62 << 20
         ),
         name="tail",
-    )(tokens, middle_grad, scale, gain, block_out, small, gate_grad, up_grad, hidden, rows_in,
-      pair_grad, w_part, normed_part)
+    )(tokens, scale, gain, block_out, small, normed_low, pre_grad, middle_grad, gate_grad, up_grad,
+      hidden, rows_in, pair_grad, normed_part)
 
 
 def join_kernel(nz, tok_ref, gain_ref, attn_part, middle_ref, scale_ref, low_ref, all_ref, *refs):
@@ -3002,12 +3206,9 @@
     )
     attn_part = dot_last(heads_low, wo_all).astype(low)
     gain_slice = lax.dynamic_slice_in_dim(gain_moe, my_columns, slice_width)
-    middle, scale, moe_low, moe_all = join(
-        tokens, gain_slice.reshape(1, slice_width), attn_part, nz, 5
-    )
-    out_part, back, gates_grad, gates, *kept = run_experts(
-        moe_all, grads_all, routes_all, router, w_gate[0], w_up[0], w_down[0],
-        micro_rows, capacity, nz, 8,
+    middle, scale, moe_low, _, out_part, back, gates_grad, gates, *kept = run_experts(
+        tokens, gain_slice.reshape(1, slice_width), router, attn_part, grads_all, routes_all,
+        w_gate[0], w_up[0], w_down[0], micro_rows, capacity, nz, 8,
     )
     rows_in, pair_grad, hidden_low, gate_pre_low, up_pre_low = (
         array.reshape(-1, array.shape[2]) for array in kept
@@ -3028,7 +3229,6 @@
     grad_slice = jnp.concatenate([cotangent[:micro_rows], swapped_grad], axis=0).astype(f32)
     inner = gain_slice * moe_grad
     middle_grad, middle_low = turn(middle, scale, inner, grad_slice, 11)
-    out_grad_part = dot_first(middle_low, heads_low).astype(low)
     heads_grad = jnp.dot(middle_low, wo_all, preferred_element_type=f32).astype(low)
     delta = jnp.sum(
         (heads_grad.astype(f32) * head_out).reshape(micro_count, micro_rows, query_local, head_width),
@@ -3042,10 +3242,10 @@
     ).reshape(shard_count, part_rows, 128)
     query_pre_low, gain_query_part, sides, out_sum, w_out_grad, summed = attend_back(
         query_low, query_pre, query_gain, cosine_lookup, turned_sine, keys_values, starts, log_total,
-        delta, heads_grad, flat, out_part, out_grad_part, nz, 12,
+        delta, heads_grad, flat, middle_low, heads_low, out_part, nz, 12,
     )
     block_out = (middle + out_sum).astype(low)
-    sides = reduce_rows(sides, nz, 14)
+    sides = sides.reshape(row_count, 2 * kv_width)
 
     def shape_keys(key_raw, key_gain):
         return rotary_apply(root_mean_norm(key_raw, key_gain), cosine_lookup, sine_lookup)
@@ -3059,17 +3259,16 @@
         + dot_last(value_pre_low, wv_all)
     ).astype(low)
     pre_low = jnp.concatenate([query_pre_low, key_pre_low, value_pre_low], axis=1)
-    weight_part = dot_first(normed_low, pre_low).astype(low)
     gain_rows = slice_width // 128
     gains = jnp.concatenate(
         [jnp.zeros((slice_width,), f32), gain_query_part.reshape(-1), gain_key_part,
          jnp.zeros(((8 - gain_rows - 2) * 128,), f32)]
     ).reshape(8, 128)
     attn_gain = lax.dynamic_slice_in_dim(gain_attn, my_columns, slice_width)
-    weight_grad, token_grad, block_out, gains, gate_acc, up_acc, down_acc = tail(
+    w_query_grad, w_key_grad, w_value_grad, token_grad, block_out, gains, *expert_grads = tail(
         gate_pre_low, up_pre_low, hidden_low, tokens, middle_grad, token_scale,
-        attn_gain.reshape(1, slice_width), block_out, gains, rows_in, pair_grad, weight_part,
-        normed_part, nz, 15,
+        attn_gain.reshape(1, slice_width), block_out, gains, normed_low, pre_low, query_width, rows_in,
+        pair_grad, normed_part, nz, 15,
     )
     summed = summed.reshape(shard_count, group_count, part_rows * 128).transpose(
         1, 0, 2
@@ -3079,17 +3278,17 @@
         block_out,
         token_grad,
         jnp.sum(gains[:, :, :gain_rows], axis=0).reshape(-1),
-        weight_grad[:, :query_width],
-        weight_grad[:, query_width : query_width + kv_width],
-        weight_grad[:, query_width + kv_width :],
+        w_query_grad,
+        w_key_grad,
+        w_value_grad,
         w_out_grad,
         jnp.sum(gains[:, :, gain_rows], axis=(0, 1)),
         jnp.sum(gains[:, :, gain_rows + 1], axis=(0, 1)),
         summed[:, :slice_width].reshape(-1),
         summed[:, slice_width:length].reshape(router.shape),
-        gate_acc[None],
-        up_acc[None],
-        down_acc[None],
+        expert_grads[0][None],
+        expert_grads[1][None],
+        expert_grads[2][None],
     )
 
 

time: 802 us -> 758 us (0.945)
  Pallas kernels: 689 us -> 659 us
  matrix products: 42.1 us -> 29.7 us
    pallas_call x3 -> x1, Pallas kernels: 224 us -> 85.7 us  [tail(): pl.pallas_call(functools.partial(tail_kernel, nz), in_specs=[vmem] * 5 +...]
    pallas_call x1, Pallas kernels: 137 us -> 223 us  [run_experts(): pl.pallas_call(functools.partial(expert_kernel, nz, slots, block_rows), i...]
    pallas_call x1, Pallas kernels: 112 us -> 134 us  [attend_back(): pl.pallas_call(functools.partial(attend_back_kernel, nz), in_specs=[vmem]...]
    dot_general x2 -> x0, matrix products: 10.9 us -> none  [dot_first(): lax.dot_general(left_side, right_side, (((0,), (0,)), ((), ())), preferre...]
    unnamed x70 -> x77, local copies, waits for them, and re-layouts: 20.3 us -> 24.6 us
where the time goes in v5:
time: 758 us; the launch traced here: 747 us
  Pallas kernels  659 us (87%)
  local copies, waits for them, and re-layouts  36.5 us (5%)
  matrix products  29.7 us (4%)
  other arithmetic  19.7 us (3%)
    pallas_call x1, Pallas kernels, run_experts(): pl.pallas_call(functools.partial(expert_kernel, nz, slots, block_rows), i...  223 us
    pallas_call x1, Pallas kernels, attend_back(): pl.pallas_call(functools.partial(attend_back_kernel, nz), in_specs=[vmem]...  134 us
    pallas_call x1, Pallas kernels, attend(): pl.pallas_call(functools.partial(attend_kernel, nz), in_specs=[vmem] * 10...  119 us
    pallas_call x1, Pallas kernels, tail(): pl.pallas_call(functools.partial(tail_kernel, nz), in_specs=[vmem] * 5 +...  85.7 us
    pallas_call x1, Pallas kernels, gather_rows(): pl.pallas_call(functools.partial(gather_rows_kernel, nz, count, columns),...  73.3 us
    unnamed x77, local copies, waits for them, and re-layouts  24.6 us
    pallas_call x1, Pallas kernels, turn(): pl.pallas_call(turn_kernel, in_specs=[vmem] * 4, out_specs=[vmem, any_spa...  23.3 us

profile of v5, /device:TPU:0, one launch (start us, length us, event | category | flops | bytes accessed | tf_op | source)
XLA Modules:
  0.0 747.0 jit_solution(15964025054678997067)
XLA Ops:
  3.0 73.3 %gather_rows.1 = (s32[320,128]{1,0:T(8,128)}, bf16[2048,1024]{1,0:T(8,128)(2,1)}, bf16[2048,128]{1,0:T(8,128)(2,1)}, bf16[2048,128]{1,0:T(8,128)(2,1)}, bf16[512...) custom-call(s32[40,128]{1,0:T(8,128)} %pad_bitcast_fusion.refs_0_, bf16[256,1024]{1,0:T(8,128)(2,1)} %refs_1_.1, ...), custom_call_target="tpu_custom_call" | custom-call | tf_op jit(solution)/shard_map/gather_rows/pallas_call | solution.py:1000
  81.3 2.1 fusion
  85.7 5.9 fusion.15.q_pre.pre_all
  91.6 1.4 convolution_convert_fusion.2.v_pre
  93.0 119.3 %attend.1 = (bf16[512,1024]{1,0:T(8,128)(2,1)}, bf16[512,1024]{1,0:T(8,128)(2,1)}, f32[512,1024]{1,0:T(8,128)}, f32[16,1,256]{2,1,0:T(1,128)}, bf16[4,2,2,256,25...) custom-call(f32[512,1024]{1,0:T(8,128)} %fusion.15.q_pre.pre_all, ...), custom_call_target="tpu_custom_call" | custom-call | tf_op jit(solution)/shard_map/attend/pallas_call | solution.py:2219
  212.3 6.2 convolution_convert_fusion.attn_part
  218.5 1.3 dynamic_slice.24
  219.9 2.5 reshape.231.routes_all
  223.4 223.5 %experts.1 = (f32[512,512]{1,0:T(8,128)}, f32[512,1]{1,0:T(8,128)}, bf16[512,512]{1,0:T(8,128)(2,1)}, bf16[4096,2048]{1,0:T(8,128)(2,1)}, bf16[4096,2048]{1,0:T(...) custom-call(bf16[512,512]{1,0:T(8,128)(2,1)} %get-tuple-element.56.t, ...), custom_call_target="tpu_custom_call" | custom-call | tf_op jit(solution)/shard_map/experts/pallas_call | solution.py:1799
  446.8 1.0 copy.63
  447.9 1.1 fusion.4
  449.0 2.0 fusion.6
  451.1 1.1 reduce.2
  452.2 3.0 multiply_reduce_fusion
  456.9 1.1 maximum_convert_fusion.grad_ref
  458.0 23.3 %turn.1 = (f32[512,512]{1,0:T(8,128)}, bf16[512,2048]{1,0:T(8,128)(2,1)}) custom-call(f32[512,512]{1,0:T(8,128)} %get-tuple-element.65.middle_ref, f32[512,1]{1,0:T(8,128)} %get-tuple-element.67.scale_ref, f32[512,512]{1,0:T(8,128)} %get-tuple-element.146.inner_ref, f32[512,512]{1,0:T(8,128)} %maximum_convert_fusion.grad_ref), custom_call_target="tpu_custom_call" | custom-call | tf_op jit(solution)/shard_map/turn/pallas_call | solution.py:3115
  481.4 5.3 convolution_convert_fusion.1.grad_all
  489.1 134.4 %attend_back.1 = (bf16[512,1024]{1,0:T(8,128)(2,1)}, f32[1,128]{1,0:T(1,128)}, f32[2,256,256]{2,1,0:T(8,128)}, f32[512,512]{1,0:T(8,128)}, f32[256,1024]{1,0:T(8,128)}, /*index=5*/f32[32,24,128]{2,1,0:T(8,128)}) custom-call(f32[1,128]{1,0:T(1,128)} %bitcast.116, f32[512,128]{1,0:T(8,128)} %pad_maximum_fusion.1.cos_ref, ...), custom_call_target="tpu_custom_call" | custom-call | tf_op jit(solution)/shard_map/attend_back/pallas_call | solution.py:2639
  623.4 1.1 slice_multiply_fusion
  624.7 1.3 multiply_reduce_fusion.1
  627.2 1.3 copy-done.25
  628.5 2.4 fusion.16
  630.9 2.0 add_convert_fusion.normed_part
  633.0 1.2 pad_maximum_fusion.right_all
  637.5 85.7 %tail.1 = (f32[256,1024]{1,0:T(8,128)}, f32[256,128]{1,0:T(8,128)}, f32[256,128]{1,0:T(8,128)}, bf16[512,512]{1,0:T(8,128)(2,1)}, bf16[512,512]{1,0:T(8,128)(2,1...) custom-call(bf16[512,512]{1,0:T(8,128)(2,1)} %get-tuple-element.56.tok_ref, ...), custom_call_target="tpu_custom_call" | custom-call | tf_op jit(solution)/shard_map/tail/pallas_call | solution.py:2968
  723.2 1.6 slice_reduce_fusion
  724.8 1.5 slice_reduce_fusion.1
  728.5 2.0 copy.85
  730.5 2.0 copy.86
  735.8 3.2 copy.91
  739.0 3.2 copy.92
  743.9 2.7 copy.93
  (124 shorter events, 26.3 us)
Async XLA Ops:
  0.6 82.8 %copy-start.22 = (f32[2048]{0:T(1024)S(1)}, f32[2048]{0:T(1024)}, u32[]{:S(2)}) copy-start(f32[2048]{0:T(1024)} %param.20) | copy-start | bytes 24580
  77.2 0.7 copy-start.16
  77.7 5.7 copy-start.3
  81.3 2.7 copy-start.7
  84.0 7.6 %copy-start = (bf16[512,2048]{1,0:T(8,128)(2,1)}, bf16[512,2048]{1,0:T(8,128)(2,1)S(1)}, u32[]{:S(2)}) copy-start(bf16[512,2048]{1,0:T(8,128)(2,1)S(1)} %fusion.2.left_all) | copy-start | bytes 6291460
  85.7 5.9 copy-start.9
  212.3 7.6 %slice-start.5 = ((s32[8,5120]{1,0:T(8,128)}), s32[8,4096]{1,0:T(8,128)S(1)}, s32[]{:S(2)}) async-start(s32[8,5120]{1,0:T(8,128)} %copy-done.16), calls=%async_computation.5 | async-start | bytes 262144 | tf_op jit(solution)/shard_map/slice | solution.py:3176
  212.3 10.1 %copy-start.18 = (bf16[2048,32]{0,1:T(8,128)(2,1)S(1)}, bf16[2048,32]{0,1:T(8,128)(2,1)}, u32[]{:S(2)}) copy-start(bf16[2048,32]{0,1:T(8,128)(2,1)} %param.28) | copy-start | bytes 393220
  223.4 228.8 %copy-start.21 = (f32[512]{0:T(512)S(1)}, f32[512]{0:T(512)}, u32[]{:S(2)}) copy-start(f32[512]{0:T(512)} %dynamic_slice.24) | copy-start | bytes 6148
  446.8 5.4 copy-start.1
  449.0 7.9 %slice-start.4 = ((bf16[512,512]{1,0:T(8,128)(2,1)}), bf16[256,512]{1,0:T(8,128)(2,1)S(1)}, s32[]{:S(2)}) async-start(bf16[512,512]{1,0:T(8,128)(2,1)} %cot_ref.1), calls=%async_computation.4 | async-start | bytes 524288 | tf_op jit(solution)/shard_map/slice | solution.py:3229
  481.3 5.3 copy-start.8
  486.7 1.0 copy-start.5
  489.0 135.6 %copy-start.6 = (f32[512,128]{1,0:T(8,128)S(1)}, f32[512,128]{1,0:T(8,128)}, u32[]{:S(2)}) copy-start(f32[512,128]{1,0:T(8,128)} %copy.61.k_pre) | copy-start | bytes 786436
  489.0 135.6 %copy-start.23 = (f32[128]{0:T(128)S(1)}, f32[128]{0:T(128)}, u32[]{:S(2)}) copy-start(f32[128]{0:T(128)} %param.26) | copy-start | bytes 1540
  626.0 1.2 copy-start.14
  626.0 2.5 copy-start.25
  628.5 2.4 copy-start.10
  628.5 2.4 copy-start.11
  630.9 3.2 copy-start.24
  633.0 1.8 copy-start.2
  633.0 2.0 copy-start.13
  637.5 88.9 %copy-start.17 = (f32[32,24,128]{2,1,0:T(8,128)S(1)}, f32[32,24,128]{2,1,0:T(8,128)}, u32[]{:S(2)}) copy-start(f32[32,24,128]{2,1,0:T(8,128)} %get-tuple-element.94) | copy-start | bytes 1179652
  723.2 9.4 %copy-start.15 = (f32[256,1024]{1,0:T(8,128)S(1)}, f32[256,1024]{1,0:T(8,128)}, u32[]{:S(2)}) copy-start(f32[256,1024]{1,0:T(8,128)} %get-tuple-element.174) | copy-start | bytes 3145732
  726.9 8.0 %copy-start.12 = (f32[256,1024]{1,0:T(8,128)S(1)}, f32[256,1024]{1,0:T(8,128)}, u32[]{:S(2)}) copy-start(f32[256,1024]{1,0:T(8,128)} %get-tuple-element.177) | copy-start | bytes 3145732
  727.9 5.6 copy-start.20
  727.9 6.3 copy-start.19
  728.5 7.3 copy-start.4
  732.5 6.5 slice-start.2
  735.8 3.2 slice-start.3
  735.8 7.3 slice-start
  739.0 4.8 slice-start.1

commit v6 on v5

--- a/solution.py
+++ b/solution.py
@@ -889,7 +889,7 @@
         pl.when((zz >= 0) & (zz < nz))(lambda: fn(zz))
 
 
-def gather_rows_kernel(nz, count, columns, *refs):
+def gather_rows_kernel(nz, count, columns, narrow, *refs):
     total = count + columns
     srcs, refs = refs[:total], refs[total:]
     outs, refs = refs[:total], refs[total:]
@@ -927,12 +927,17 @@
         ]
         last = pltpu.make_async_copy(first, column(y), lsem.at[total])
     own = [pltpu.make_async_copy(src, dst, lsem.at[n]) for n, (src, dst) in enumerate(own)]
-    for copy in swaps + own:
+    pairs = range(count - narrow, count)
+    sides = [remote(srcs[n], block(n, z, x), s_x.at[n * nz], r_x.at[n * nz], xn) for n in pairs]
+    for copy in swaps + own + sides:
         copy.start()
 
     def copies(n, zz, src):
         dst = block(n, zz, x)
         k = n * nz + zz
+        if n in pairs:
+            rows = 2 * srcs[n].shape[0]
+            dst = src = outs[n].at[pl.ds(pl.multiple_of(zz * rows, rows), rows)]
         return (remote(src, dst, s_u.at[k], r_z.at[k], up),
                 remote(src, dst, s_d.at[k], r_z.at[k], down),
                 remote(src, dst, s_x.at[k], r_x.at[k], xn))
@@ -947,14 +952,18 @@
                 cu, cd, cx = copies(n, zz, src)
                 if dist:
                     cu.wait_recv()
+                elif n in pairs:
+                    own[n].wait()
+                    sides[n - count + narrow].wait_recv()
                 if side <= 0:
                     pl.when(z < nz - 1)(cu.start)
                 if side > 0 or dist == 0:
                     pl.when(z > 0)(cd.start)
-                cx.start()
+                if n not in pairs:
+                    cx.start()
 
         z_guard(item, z, nz, run)
-        if columns and item == items[-1]:
+        if columns and item == items[-3]:
             swaps[0].wait_recv()
             column_copies[0].start()
             column_copies[1].start()
@@ -966,15 +975,18 @@
     def finish(zz, carry):
         for n in range(count):
             cu, cd, cx = copies(n, zz, block(n, zz, x))
-            cx.wait_recv()
-            cx.wait_send()
+            if n not in pairs:
+                cx.wait_recv()
+                cx.wait_send()
             pl.when((zz <= z) & (z < nz - 1))(cu.wait_send)
             pl.when((zz >= z) & (z > 0))(cd.wait_send)
         return carry
 
     lax.fori_loop(0, nz, finish, 0)
-    for copy in own:
+    for copy in own[: count - narrow]:
         copy.wait()
+    for copy in sides:
+        copy.wait_send()
     if columns:
         column_copies[0].wait_send()
         column_copies[1].wait()
@@ -985,7 +997,7 @@
             copy.wait()
 
 
-def gather_rows(blocks, nz, collective_id, swapped=()):
+def gather_rows(blocks, nz, collective_id, swapped=(), narrow=0):
     count, columns = len(blocks), len(swapped)
     dma = pltpu.SemaphoreType.DMA
     any_space = pl.BlockSpec(memory_space=pl.ANY)
@@ -998,7 +1010,7 @@
         shapes.append(jax.ShapeDtypeStruct((rows, cols * 4), swapped[0].dtype))
     total = count + columns
     return pl.pallas_call(
-        functools.partial(gather_rows_kernel, nz, count, columns),
+        functools.partial(gather_rows_kernel, nz, count, columns, narrow),
         out_shape=shapes,
         in_specs=[vmem] * total,
         out_specs=[any_space] * count + [vmem] * columns + [any_space] * min(columns, 1),
@@ -1416,7 +1428,14 @@
     n_c, n_s = len(ReduceCols.scratch(16, 128, low)), len(RowSums.scratch(128))
     columns = ReduceCols(attn_part, middle_ref, refs[:n_c])
     sums = RowSums(refs[n_c : n_c + n_s])
-    moe_rows = GatherAll(nz, low_ref, x_all, refs[n_c + n_s :], half)
+    n_g = len(GatherAll.scratch(nz))
+    moe_rows = [GatherAll(nz, part, x_all, refs[n_c + n_s + n * n_g : n_c + n_s + (n + 1) * n_g],
+                          half // 2, n, 2) for n, part in enumerate(halves(low_ref))]
+
+    def rows_step(name, *args):
+        for part in moe_rows:
+            getattr(part, name)(*args)
+
     greet_all(shard, group, 2 * nz, 4)
     columns.start()
     tiles = 2 * nz
@@ -1591,13 +1610,13 @@
 
         lax.fori_loop(0, width // cols, take, 0)
 
-        pl.when(j == 0)(lambda: moe_rows.second(2))
+        pl.when(j == 0)(lambda: rows_step('second', 2))
         for k in range(3, nz):
-            pl.when(j == 1)(lambda: moe_rows.second(k))
+            pl.when(j == 1)(lambda: rows_step('second', k))
 
         @pl.when((j % 2 == 1) & (j < tiles - 1))
         def _():
-            moe_rows.ready(tile_item(nz, z, j // 2 + 1))
+            rows_step('ready', tile_item(nz, z, j // 2 + 1))
 
         @pl.when(j < tiles - 1)
         def _():
@@ -1709,18 +1728,20 @@
     sums.start()
     sums.wait()
     lax.fori_loop(0, rows // 128, norm, 0)
-    moe_rows.own().start()
-    moe_rows.own().wait()
-    moe_rows.first(0)
-    moe_rows.first(1)
-    moe_rows.second(0)
-    moe_rows.first(2)
-    moe_rows.second(1)
-    moe_rows.third(0)
+    for part in moe_rows:
+        part.own().start()
+    for part in moe_rows:
+        part.own().wait()
+    rows_step('first', 0)
+    rows_step('first', 1)
+    rows_step('second', 0)
+    rows_step('first', 2)
+    rows_step('second', 1)
+    rows_step('third', 0)
     for k in range(3, nz):
-        moe_rows.first(k)
-    moe_rows.third(1)
-    moe_rows.ready(tile_item(nz, z, 0))
+        rows_step('first', k)
+    rows_step('third', 1)
+    rows_step('ready', tile_item(nz, z, 0))
     load(0).start()
     for copy in weights:
         copy.wait()
@@ -1730,9 +1751,9 @@
     def step(j, carry):
         k, odd = j // 2, j % 2 == 1
         pl.when(j < tiles)(lambda: compute(j))
-        pl.when(j == 0)(lambda: moe_rows.third(2))
+        pl.when(j == 0)(lambda: rows_step('third', 2))
         for n in range(3, nz):
-            pl.when(j == 2)(lambda: moe_rows.third(n))
+            pl.when(j == 2)(lambda: rows_step('third', n))
 
         @pl.when(j == tiles)
         def _():
@@ -1780,7 +1801,7 @@
 
     lax.fori_loop(0, nz, finish, 0)
     columns.finish()
-    moe_rows.finish_sends()
+    rows_step('finish_sends')
 
 
 def run_experts(tokens, gain, router, attn_part, g_all, routes_all, gate_w, up_w, down_w, block_rows,
@@ -1822,7 +1843,7 @@
             vm((nz + 1, rows, cols), low),
             dma((5,)), dma, dma((5,)), dma((4 * nz,)), dma((4 * nz,)),
         ] + [dma((nz,))] * 9 + [dma((nz + 1,))] + [dma((4 * tiles,))] * 2
-        + ReduceCols.scratch(rows, cols, low) + RowSums.scratch(rows) + GatherAll.scratch(nz),
+        + ReduceCols.scratch(rows, cols, low) + RowSums.scratch(rows) + GatherAll.scratch(nz) * 2,
         compiler_params=pltpu.CompilerParams(
             collective_id=collective_id, has_side_effects=True, vmem_limit_bytes=62 << 20
         ),
@@ -1834,6 +1855,11 @@
     return far_first(nz, z, nz - 1 - k)
 
 
+def halves(ref):
+    rows = ref.shape[0] // 2
+    return [ref.at[pl.ds(part * rows, rows)] for part in range(2)]
+
+
 class GatherAll:
     sems = 6
 
@@ -1842,18 +1868,19 @@
         dma = pltpu.SemaphoreType.DMA
         return [dma] + [dma((5 * nz,))] * 2 + [dma((nz,))] * 11
 
-    def __init__(self, nz, src, out, sems, cut):
+    def __init__(self, nz, src, out, sems, cut, part=0, parts=1):
         (self.lsem, self.s_p, self.r_p, self.s_u, self.s_d, self.s_x, self.s_y, self.s_dx,
          self.s_dy, self.r_z, self.r_x, self.r_y, self.r_dx, self.r_dy) = sems
         self.nz, self.src, self.out, self.cut = nz, src, out, cut
         self.rows, self.cols = src.shape
+        self.offset, self.stride = part * self.rows, parts * self.rows
         self.place = z, x, y, c = place()
         self.partner, self.xn, self.yn = (
             device(z, x, y, 1 - c), device(z, 1 - x, y, c), device(z, x, 1 - y, c))
         self.up, self.down = device(z + 1, x, y, c), device(z - 1, x, y, c)
 
     def block(self, zz, xx, yy, cc, part=None):
-        start, size, unit = (zz * 2 + xx) * self.rows, self.rows, self.rows
+        start, size, unit = (zz * 2 + xx) * self.stride + self.offset, self.rows, self.rows
         if part == 0:
             size, unit = self.cut, self.rows
         elif part == 1:
@@ -1901,17 +1928,25 @@
         return [0, 1, 2] + [3] * (self.cut > 0) + [4] * (self.cut < self.rows)
 
     def first(self, k):
-        zz, z = near_first(self.nz, self.place[0], k), self.place[0]
+        self.first_to(near_first(self.nz, self.place[0], k))
+
+    def second(self, k):
+        self.second_to(near_first(self.nz, self.place[0], k))
+
+    def third(self, k):
+        self.third_to(near_first(self.nz, self.place[0], k))
+
+    def first_to(self, zz):
+        z = self.place[0]
         up, down = self.line(zz)
-        pl.when(k > 0)(lambda: up.wait_recv())
+        pl.when(zz != z)(lambda: up.wait_recv())
         pl.when((zz <= z) & (z < self.nz - 1))(lambda: up.start())
         pl.when((zz >= z) & (z > 0))(lambda: down.start())
         for copy in self.sides(zz):
             copy.start()
         self.pair(zz, 0).start()
 
-    def second(self, k):
-        zz = near_first(self.nz, self.place[0], k)
+    def second_to(self, zz):
         to_x, to_y = self.sides(zz)
         across = self.across(zz)
         to_x.wait_recv()
@@ -1923,8 +1958,7 @@
             across[-1].start()
         self.pair(zz, 2).start()
 
-    def third(self, k):
-        zz = near_first(self.nz, self.place[0], k)
+    def third_to(self, zz):
         across = self.across(zz)
         for rel, copy in zip(self.parts()[3:], across):
             copy.wait_recv()
@@ -1996,17 +2030,17 @@
         z = self.place[0]
         return self.needed(zz, micro) & (z < self.nz - 1 if micro == 0 else z > 0)
 
-    def first(self, k):
-        zz, z = near_first(self.nz, self.place[0], k), self.place[0]
-
-        @pl.when(k == 0)
+    def first_to(self, zz):
+        z = self.place[0]
+
+        @pl.when(zz == z)
         def _():
             for copy in self.own():
                 copy.wait()
             self.side().wait_recv()
 
         for micro in range(2):
-            pl.when((k > 0) & self.needed(zz, micro))(lambda: self.line(zz, micro).wait_recv())
+            pl.when((zz != z) & self.needed(zz, micro))(lambda: self.line(zz, micro).wait_recv())
             pl.when(self.sends(zz, micro))(lambda: self.line(zz, micro).start())
             pl.when(self.needed(zz, micro))(lambda: self.keep(zz, micro).start())
 
@@ -2031,16 +2065,18 @@
         dma = pltpu.SemaphoreType.DMA
         return [dma] + [dma((nz,))] * 5
 
-    def __init__(self, nz, src, out, sems):
+    def __init__(self, nz, src, out, sems, part=0, parts=1):
         self.lsem, self.s_u, self.s_d, self.s_x, self.r_z, self.r_x = sems
         self.nz, self.src, self.out = nz, src, out
+        self.offset, self.stride = part * src.shape[0], parts * src.shape[0]
         self.place = z, x, y, c = place()
         self.xn = device(z, 1 - x, y, c)
         self.up, self.down = device(z + 1, x, y, c), device(z - 1, x, y, c)
 
     def block(self, zz):
         rows = self.src.shape[0]
-        return self.out.at[pl.ds(pl.multiple_of((zz * 2 + self.place[1]) * rows, rows), rows)]
+        start = (zz * 2 + self.place[1]) * self.stride + self.offset
+        return self.out.at[pl.ds(pl.multiple_of(start, rows), rows)]
 
     def own(self):
         return pltpu.make_async_copy(self.src, self.block(self.place[0]), self.lsem)
@@ -2051,10 +2087,10 @@
                 remote(here, here, self.s_d.at[zz], self.r_z.at[zz], self.down),
                 remote(here, here, self.s_x.at[zz], self.r_x.at[zz], self.xn))
 
-    def first(self, k):
-        zz, z = near_first(self.nz, self.place[0], k), self.place[0]
+    def first_to(self, zz):
+        z = self.place[0]
         up, down, to_x = self.copies(zz)
-        pl.when(k > 0)(lambda: up.wait_recv())
+        pl.when(zz != z)(lambda: up.wait_recv())
         pl.when((zz <= z) & (z < self.nz - 1))(lambda: up.start())
         pl.when((zz >= z) & (z > 0))(lambda: down.start())
         to_x.start()
@@ -2098,53 +2134,97 @@
     return normed * cosine + pltpu.roll(normed, raw.shape[1] // 2, 1) * sine
 
 
-def attend_kernel(nz, q_pre, k_pre, v_pre, gq_ref, gk_ref, cos_ref, sin_ref, start_ref, cot_ref, wo_ref,
-                  q_ref, heads_ref, out_ref, lse_ref, kv_all, cot_all, wo_all,
-                  kv_ref, kv, acc, peak, total, *sems):
+def attend_kernel(nz, gain_ref, gq_ref, gk_ref, cos_ref, sin_ref, start_ref, cot_ref, wo_ref,
+                  tok_all, wq_all, wk_all, wv_all,
+                  normed, scale_ref, q_pre, k_pre, q_ref, heads_ref, lse_ref, kv_all, cot_all, wo_all,
+                  tok_ref, wq, wk, wv, s_in, kv_ref, kv, acc, peak, total, *sems):
     shards = 2 * nz
     width = kv_ref.shape[2] // 2
     block = q_ref.shape[0] // 2
     low = jnp.bfloat16
     heads = q_ref.shape[1] // width
     z, x, y, c = place()
-    split = len(GatherAll.scratch(nz))
-    end = split + len(GatherRows.scratch(nz))
-    cots = GatherAll(nz, cot_ref, cot_all, sems[:split], cot_ref.shape[0])
-    outs = GatherRows(nz, wo_ref, wo_all, sems[split:end])
+    n_c, n_o = len(GatherAll.scratch(nz)), len(GatherRows.scratch(nz))
+    end = 2 * (n_c + n_o)
+    cots = [GatherAll(nz, half, cot_all, sems[n * n_c : (n + 1) * n_c], half.shape[0], n, 2)
+            for n, half in enumerate(halves(cot_ref))]
+    outs = [GatherRows(nz, half, wo_all, sems[2 * n_c + n * n_o : 2 * n_c + (n + 1) * n_o], n, 2)
+            for n, half in enumerate(halves(wo_ref))]
     keys_in = GatherCausal(nz, kv_ref, kv_all, kv, sems[end:])
-    greet([(None, cots.partner), (None, cots.xn), (None, cots.yn),
-           (z < nz - 1, cots.up), (z > 0, cots.down)])
-    for part in (outs, cots):
+    greet([(None, cots[0].partner), (None, cots[0].xn), (None, cots[0].yn),
+           (z < nz - 1, cots[0].up), (z > 0, cots[0].down)])
+    for part in outs + cots:
         part.own().start()
+    fetches = [pltpu.make_async_copy(src, dst, s_in.at[n]) for n, (src, dst) in enumerate((
+        (tok_all, tok_ref), (wk_all, wk), (wv_all, wv), (wq_all, wq)))]
+    for copy in fetches:
+        copy.start()
+    for part in outs + cots:
+        part.own().wait()
+    for part in cots:
+        part.first_to(z)
+    fetches[0].wait()
+
+    def token_norm(n, carry):
+        rows = pl.ds(pl.multiple_of(n * 64, 64), 64)
+        row = tok_ref[rows, :].astype(jnp.float32)
+        scale = lax.rsqrt(jnp.mean(row * row, axis=1, keepdims=True) + norm_eps)
+        scale_ref[rows, :] = scale
+        normed[rows, :] = (row * scale * gain_ref[...]).astype(low)
+        return carry
+
+    lax.fori_loop(0, tok_ref.shape[0] // 64, token_norm, 0)
+    fetches[1].wait()
+    k_pre[...] = dot_plain(normed[...], wk[...])
     turned = norm_turn(k_pre[...], gk_ref[...], cos_ref[...], sin_ref[...]).astype(low)
+    fetches[2].wait()
+    value = dot_plain(normed[...], wv[...]).astype(low)
     for micro in range(2):
         rows = slice(micro * block, (micro + 1) * block)
         kv_ref[micro, :, :width] = turned[rows]
-        kv_ref[micro, :, width:] = v_pre[rows, :]
+        kv_ref[micro, :, width:] = value[rows]
     keys_in.side().start()
     for copy in keys_in.own():
         copy.start()
     peak[...] = jnp.full(peak.shape, masked_score, jnp.float32)
     total[...] = jnp.zeros_like(total)
     acc[...] = jnp.zeros_like(acc)
-    for part in (outs, cots):
-        part.own().wait()
+    fetches[3].wait()
+
+    def at_distance(dist, fn):
+        for side in (-1, 1):
+            zz = z + side * dist
+            valid = (dist >= 0) & (zz >= 0) & (zz < nz) & ((dist > 0) | (side > 0))
+            pl.when(valid)(lambda: fn(zz))
 
     def tick(u, carry):
-        @pl.when(u < nz)
-        def _():
-            pl.when(u == 0)(lambda: cots.first(u))
-            keys_in.first(u)
-            pl.when(u > 0)(lambda: cots.first(u))
-            outs.first(u)
-
-        pl.when((u >= 1) & (u <= nz))(lambda: cots.second(u - 1))
-        pl.when((u >= 2) & (u <= nz + 1))(lambda: cots.third(u - 2))
-        pl.when((u >= 1) & (u <= nz))(lambda: attend_item(u - 1))
+        def gradients(zz):
+            @pl.when(u > 0)
+            def _():
+                for part in cots:
+                    part.first_to(zz)
+
+        def weights(zz):
+            for part in outs:
+                part.first_to(zz)
+
+        def across(zz):
+            for part in cots:
+                part.second_to(zz)
+
+        def onward(zz):
+            for part in cots:
+                part.third_to(zz)
+
+        at_distance(u, keys_in.first_to)
+        at_distance(u, gradients)
+        at_distance(u, weights)
+        at_distance(u - 1, across)
+        at_distance(u - 2, onward)
+        at_distance(u - 1, attend_item)
         return carry
 
-    def attend_item(k):
-        zz = near_first(nz, z, k)
+    def attend_item(zz):
         own = zz == z
         keys_in.ready(zz)
 
@@ -2182,13 +2262,18 @@
 
         lax.fori_loop(0, heads, head, 0, unroll=4)
 
-    def prepare(h, carry):
-        cols = pl.ds(pl.multiple_of(h * width, width), width)
-        q_ref[:, cols] = norm_turn(q_pre[:, cols], gq_ref[...], cos_ref[...], sin_ref[...]).astype(low)
+    def prepare(n, carry):
+        pair = pl.ds(pl.multiple_of(n * 2 * width, 2 * width), 2 * width)
+        q_pre[:, pair] = dot_plain(normed[...], wq[:, pair])
+        for h in range(2):
+            cols = pl.ds(pl.multiple_of((n * 2 + h) * width, width), width)
+            q_ref[:, cols] = norm_turn(
+                q_pre[:, cols], gq_ref[...], cos_ref[...], sin_ref[...]
+            ).astype(low)
         return carry
 
+    lax.fori_loop(0, heads // 2, prepare, 0)
     tick(0, 0)
-    lax.fori_loop(0, heads, prepare, 0)
     lax.fori_loop(1, nz + 2, tick, 0)
 
     def close(at, carry):
@@ -2196,21 +2281,20 @@
         result = (acc[at] / total[at]).T
         here = pl.ds(pl.multiple_of(micro * block, block), block)
         cols = pl.ds(pl.multiple_of(h * width, width), width)
-        out_ref[here, cols] = result
         heads_ref[here, cols] = result.astype(jnp.bfloat16)
         lse_ref[at] = peak[at] + jnp.log(total[at])
         return carry
 
     lax.fori_loop(0, 2 * heads, close, 0)
     keys_in.finish()
-    outs.finish()
-    cots.finish()
-
-
-def attend(q_pre, k_pre, v_low, gain_query, gain_key, cosine, sine, starts, cotangent, w_out, nz,
-           collective_id):
-    rows, columns = q_pre.shape
-    width = k_pre.shape[1]
+    for part in outs + cots:
+        part.finish()
+
+
+def attend(tokens, gain_attn, wq_all, wk_all, wv_all, gain_query, gain_key, cosine, sine, starts,
+           cotangent, w_out, nz, collective_id):
+    rows, features = tokens.shape
+    columns, width = wq_all.shape[1], wk_all.shape[1]
     heads = columns // width
     block = rows // 2
     any_space = pl.BlockSpec(memory_space=pl.ANY)
@@ -2218,25 +2302,30 @@
     vm, shape, f32, low = pltpu.VMEM, jax.ShapeDtypeStruct, jnp.float32, jnp.bfloat16
     return pl.pallas_call(
         functools.partial(attend_kernel, nz),
-        in_specs=[vmem] * 10,
-        out_specs=[vmem] * 4 + [any_space] * 3,
+        in_specs=[vmem] * 8 + [any_space] * 4,
+        out_specs=[vmem] * 7 + [any_space] * 3,
         out_shape=[
-            shape((rows, columns), low), shape((rows, columns), low), shape((rows, columns), f32),
+            shape((rows, features), low), shape((rows, 1), f32),
+            shape((rows, columns), f32), shape((rows, width), f32),
+            shape((rows, columns), low), shape((rows, columns), low),
             shape((2 * heads, 1, block), f32),
             shape((nz, 2, 2, block, 2 * width), low),
             shape((rows * 2 * nz, cotangent.shape[1] * 4), cotangent.dtype),
             shape((w_out.shape[0] * 2 * nz, w_out.shape[1]), w_out.dtype),
         ],
         scratch_shapes=[
+            vm((rows, features), low), vm(wq_all.shape, low), vm(wk_all.shape, low),
+            vm(wv_all.shape, low), pltpu.SemaphoreType.DMA((4,)),
             vm((2, block, 2 * width), low), vm((nz, 2, 2, block, 2 * width), low),
             vm((2 * heads, width, block), f32), vm((2 * heads, 1, block), f32),
             vm((2 * heads, 1, block), f32),
-        ] + GatherAll.scratch(nz) + GatherRows.scratch(nz) + GatherCausal.scratch(nz),
+        ] + GatherAll.scratch(nz) * 2 + GatherRows.scratch(nz) * 2 + GatherCausal.scratch(nz),
         compiler_params=pltpu.CompilerParams(
             collective_id=collective_id, has_side_effects=True, vmem_limit_bytes=62 << 20
         ),
         name="attend",
-    )(q_pre, k_pre, v_low, gain_query, gain_key, cosine, sine, starts, cotangent, w_out)
+    )(gain_attn, gain_query, gain_key, cosine, sine, starts, cotangent, w_out, tokens, wq_all, wk_all,
+      wv_all)
 
 
 class ScatterAll:
@@ -2250,12 +2339,13 @@
             vm((nz + 1, rows, cols), kind),
         ] + [dma((4 * nz,))] * 3 + [dma((nz,))] * 9 + [dma((nz + 1,))]
 
-    def __init__(self, nz, partial, out, refs, cut):
+    def __init__(self, nz, partial, out, refs, cut, part=0, parts=1):
         (self.w, self.lp, self.rx, self.rxd, self.ry, self.ryd, self.rz,
          self.s_l, self.s_p, self.r_p, self.s_x, self.s_y, self.s_dx, self.s_dy, self.s_z,
          self.r_x, self.r_y, self.r_dx, self.r_dy, self.r_z) = refs
         self.nz, self.partial, self.out, self.cut = nz, partial, out, cut
         self.rows, self.cols = out.shape
+        self.offset, self.stride = part * self.rows, parts * self.rows
         self.place = z, x, y, c = place()
         self.partner, self.xn, self.yn = (
             device(z, x, y, 1 - c), device(z, 1 - x, y, c), device(z, x, 1 - y, c))
@@ -2266,7 +2356,7 @@
         xx = 1 - x if rel in (1, 3) else x
         yy = 1 - y if rel in (2, 3) else y
         return self.partial.at[
-            pl.ds(pl.multiple_of((zz * 2 + xx) * self.rows, self.rows), self.rows),
+            pl.ds(pl.multiple_of((zz * 2 + xx) * self.stride + self.offset, self.rows), self.rows),
             pl.ds(pl.multiple_of((yy * 2 + cc) * self.cols, self.cols), self.cols)]
 
     def pair(self, zz, rel):
@@ -2389,16 +2479,18 @@
         return [vm((nz, rows, cols), kind), vm((nz, rows, cols), kind), vm((nz, rows, cols), kind),
                 vm((nz + 1, rows, cols), kind)] + [dma((nz,))] * 3 + [dma((nz + 1,))]
 
-    def __init__(self, nz, left, right, out, refs):
+    def __init__(self, nz, left, right, out, refs, part=0, parts=1):
         self.w, self.sent, self.rx, self.rz, self.s_x, self.s_z, self.r_x, self.r_z = refs
         self.nz, self.left, self.right, self.out = nz, left, right, out
         self.rows = out.shape[0]
+        self.offset, self.stride = part * self.rows, parts * self.rows
         self.place = z, x, y, c = place()
         self.xn = device(z, 1 - x, y, c)
         self.up, self.down = device(z + 1, x, y, c), device(z - 1, x, y, c)
 
     def make(self, zz, xx, ref):
-        at = pl.ds(pl.multiple_of((zz * 2 + xx) * self.rows, self.rows), self.rows)
+        start = (zz * 2 + xx) * self.stride + self.offset
+        at = pl.ds(pl.multiple_of(start, self.rows), self.rows)
         ref[...] = dot_first(self.left[:, at], self.right[...]).astype(ref.dtype)
 
     def side(self, zz):
@@ -2518,11 +2610,24 @@
             lax.fori_loop(0, z if micro == 0 else self.nz - 1 - z, step, 0)
 
 
-def attend_back_kernel(nz, gq_ref, cos_ref, sin_ref, start_ref, lse_ref, delta_ref, small_ref,
-                       mid_all, heads_all, q_all, kv_all, grad_all, pre_all, out_part,
-                       q_grad, gain_grad, kv_sum, out_sum, wo_sum, small_out,
-                       mid_ref, heads_ref, q_ref, kv_ref, grad_ref, q_pre, s_in,
-                       sides, acc, k_acc, v_acc, *refs):
+def norm_turn_back(turned, raw, gain, cosine, sine):
+    grad = turned * cosine + pltpu.roll(turned * sine, raw.shape[1] // 2, 1)
+    scale = lax.rsqrt(jnp.mean(raw * raw, axis=1, keepdims=True) + norm_eps)
+    inner = grad * gain
+    mean = jnp.mean(raw * inner, axis=1, keepdims=True)
+    return (scale * inner - raw * (scale * scale * scale * mean),
+            jnp.sum(grad * raw * scale, axis=0, keepdims=True))
+
+
+def attend_back_kernel(nz, k_pre, gk_ref, gq_ref, cos_ref, sin_ref, start_ref, lse_ref, scale_ref,
+                       gates_ref, gg_ref, router_ref, gain_ref, moe_ref,
+                       middle_all, back_all, slice_all, wo_all, heads_all, q_all, kv_all, pre_all,
+                       out_part, mid_out, q_grad, gain_grad, out_sum, wo_sum, small_out,
+                       low_ref, mid_ref, wo_ref, heads_ref, q_ref, kv_ref,
+                       small_ref, split_ref, grad_ref, delta_ref, q_pre, s_in, s_t, r_t,
+                       kv_sum, sides, acc, k_acc, v_acc, *refs):
+    middle_ref, inner_ref = (q_pre.at[:, pl.ds(n * mid_out.shape[1], mid_out.shape[1])]
+                             for n in range(2))
     shards = 2 * nz
     shard = lax.axis_index("fsdp")
     width = kv_ref.shape[4] // 2
@@ -2531,21 +2636,27 @@
     z, x, y, c = place()
     count = shards + 2 * x
     low = jnp.bfloat16
-    split = len(ScatterAll.scratch(nz, 16, 128, low, 0))
-    outs = ScatterAll(nz, out_part, out_sum, refs[:split], 0)
-    end = split + len(ReduceRows.scratch(nz, 16, 128, low))
-    weights = ReduceRows(nz, mid_ref, heads_ref, wo_sum, refs[split:end])
+    n_o, n_w = len(ScatterAll.scratch(nz, 16, 128, low, 0)), len(ReduceRows.scratch(nz, 16, 128, low))
+    end = 2 * (n_o + n_w)
+    outs = [ScatterAll(nz, out_part, half, refs[n * n_o : (n + 1) * n_o], 0, n, 2)
+            for n, half in enumerate(halves(out_sum))]
+    weights = [ReduceRows(nz, mid_ref, heads_ref, half,
+                          refs[2 * n_o + n * n_w : 2 * n_o + (n + 1) * n_w], n, 2)
+               for n, half in enumerate(halves(wo_sum))]
     last = end + len(SmallSums.scratch(nz, (8, 128), jnp.float32))
     smalls = SmallSums(nz, small_ref, small_out, refs[end:last])
-    keys_out = ReduceCausal(nz, sides, kv_sum, refs[last:])
+    final = last + len(ReduceCausal.scratch(nz, 16, 128, low))
+    keys_out = ReduceCausal(nz, sides, kv_sum, refs[last:final])
+    sums = RowSums(refs[final:])
     greet_all(lax.axis_index("fsdp"), lax.axis_index("tp"), shards, 4)
-    outs.start()
+    for part in outs:
+        part.start()
     fetches = [pltpu.make_async_copy(src, dst, s_in.at[n]) for n, (src, dst) in enumerate((
-        (mid_all, mid_ref), (heads_all, heads_ref), (q_all, q_ref), (kv_all, kv_ref),
-        (grad_all, grad_ref), (pre_all, q_pre)))]
-    for copy in fetches:
+        (middle_all, middle_ref), (back_all, inner_ref), (slice_all, mid_out),
+        (wo_all.at[:, pl.ds(0, wo_ref.shape[1])], wo_ref),
+        (heads_all, heads_ref), (q_all, q_ref), (kv_all, kv_ref), (pre_all, q_pre)))]
+    for copy in fetches[:-1]:
         copy.start()
-    smalls.start()
 
     sides[...] = jnp.zeros_like(sides)
     acc[...] = jnp.zeros_like(acc)
@@ -2580,86 +2691,207 @@
         micro, h = at // heads, at % heads
         here = pl.ds(pl.multiple_of(micro * block, block), block)
         cols = pl.ds(pl.multiple_of(h * width, width), width)
-        turned = acc[at].T * width ** (-0.5)
-        grad = turned * cos_ref[here, :] + pltpu.roll(turned * sin_ref[here, :], width // 2, 1)
-        raw = q_pre[here, cols]
-        scale = lax.rsqrt(jnp.mean(raw * raw, axis=1, keepdims=True) + norm_eps)
-        inner = grad * gq_ref[...]
-        mean = jnp.mean(raw * inner, axis=1, keepdims=True)
-        q_grad[here, cols] = (scale * inner - raw * (scale * scale * scale * mean)).astype(low)
-        return total + jnp.sum(grad * raw * scale, axis=0, keepdims=True)
+        grad, gain = norm_turn_back(acc[at].T * width ** (-0.5), q_pre[here, cols], gq_ref[...],
+                                    cos_ref[here, :], sin_ref[here, :])
+        q_grad[here, cols] = grad.astype(low)
+        return total + gain
 
     def close_all():
-        gain_grad[...] = lax.fori_loop(
-            0, 2 * heads, close, jnp.zeros(gain_grad.shape, jnp.float32)
+        gain_grad[pl.ds(0, 1), :] = lax.fori_loop(
+            0, 2 * heads, close, jnp.zeros((1, width), jnp.float32)
         )
 
     def unit(u, carry):
         def at(fn, k):
             pl.when((k >= 0) & (k < nz))(lambda: fn(k))
 
+        def each(parts, name, k):
+            for part in parts:
+                at(getattr(part, name), k)
+
         for n in range(4):
             pl.when(4 * u + n < count)(lambda: attention(4 * u + n))
-        at(outs.second, u)
-        at(weights.send, u + 1)
-        at(outs.first, u + 2)
+        each(outs, 'second', u + 1)
+        each(weights, 'send', u + 2)
+        each(outs, 'first', u + 3)
         pl.when(u == 1)(smalls.second)
         at(keys_out.turn, u - done)
-        at(outs.third, u - 1)
-        at(outs.fourth, u - 2)
-        at(weights.second, u - 3)
-        at(weights.first, u - 2)
+        each(outs, 'third', u)
+        each(outs, 'fourth', u - 1)
+        each(weights, 'second', u - 2)
+        each(weights, 'first', u - 1)
         pl.when(u == done + 1)(close_all)
         return carry
 
+    rows, cols = mid_out.shape
+    eye = diagonal()
+
+    def column(yy):
+        return mid_ref.at[:, pl.ds(pl.multiple_of((yy * 2 + c) * cols, cols), cols)]
+
+    partner, yn = outs[0].partner, outs[0].yn
+    to_y = remote(low_ref, column(y), s_t.at[0], r_t.at[0], yn)
+    to_pair = remote(low_ref, column(y), s_t.at[1], r_t.at[1], partner)
+    onward = remote(column(1 - y), column(1 - y), s_t.at[2], r_t.at[2], partner)
+
+    def dots(n, carry):
+        here = pl.ds(pl.multiple_of(n * 128, 128), 128)
+        product = middle_ref[here, :] * inner_ref[here, :]
+        sums.got[0, pl.ds(n, 1), :] = to_row(jnp.sum(product, axis=1, keepdims=True), eye)
+        return carry
+
+    def residual(n, carry):
+        here = pl.ds(pl.multiple_of(n * 128, 128), 128)
+        mean = to_column(sums.total(n), eye) / (4 * cols)
+        scale = scale_ref[here, :]
+        out = (mid_out[here, :] + scale * inner_ref[here, :]
+               - middle_ref[here, :] * (scale * scale * scale * mean))
+        mid_out[here, :] = out
+        low_ref[here, :] = out.astype(low)
+        return carry
+
+    def head_grads(part):
+        def step(n, carry):
+            at = pl.ds(pl.multiple_of(n * 256, 256), 256)
+            to = pl.ds(pl.multiple_of(part * wo_ref.shape[1] + n * 256, 256), 256)
+            grad_ref[:, to] = dot_plain(mid_ref[...], wo_ref[:, at]).astype(low)
+            return carry
+
+        lax.fori_loop(0, wo_ref.shape[1] // 256, step, 0)
+
+    def deltas(at, carry):
+        here = pl.ds(pl.multiple_of(at // heads * block, block), block)
+        head = pl.ds(pl.multiple_of(at % heads * width, width), width)
+        product = grad_ref[here, head].astype(jnp.float32) * heads_ref[here, head].astype(jnp.float32)
+        delta_ref[at] = jnp.sum(product.T, axis=0, keepdims=True)
+        return carry
+
     done = (shards + 2 - 1) // 4
-    outs.first(0)
-    for copy in fetches:
+    def each_now(parts, name, k):
+        for part in parts:
+            getattr(part, name)(k)
+
+    gates = gates_ref[...]
+    gates_grad = gg_ref[:, 0, :].T
+    logit_grad = gates * (gates_grad - jnp.sum(gates * gates_grad, axis=1, keepdims=True))
+    each_now(outs, 'first', 0)
+    pieces, rest = [], logit_grad
+    for _ in range(3):
+        pieces.append(rest.astype(low))
+        rest = rest - pieces[-1].astype(jnp.float32)
+    router_grad = sum(dot_first(piece, moe_ref[...]) for piece in pieces)
+    small_ref[...] = jnp.zeros_like(small_ref)
+    blocks = cols // 128
+    per = router_grad.shape[0] // shards
+    for e in range(router_grad.shape[0]):
+        for n in range(blocks):
+            small_ref[e // per, pl.ds(e % per * blocks + n, 1), :] = (
+                router_grad[e : e + 1, n * 128 : (n + 1) * 128])
+    for copy in fetches[:3]:
         copy.wait()
-    weights.send(0)
-    outs.first(1)
-    lax.fori_loop(0, nz + 3, unit, 0)
+
+    def moe_grads(n, total):
+        here = pl.ds(pl.multiple_of(n * 128, 128), 128)
+        grad = inner_ref[here, :]
+        for piece in pieces_ref:
+            grad = grad + dot_last(piece[here, :], router_ref[...])
+        inner_ref[here, :] = grad * gain_ref[...]
+        return total + jnp.sum(grad * middle_ref[here, :] * scale_ref[here, :], axis=0, keepdims=True)
+
+    pieces_ref = [split_ref.at[n] for n in range(3)]
+    for ref, piece in zip(pieces_ref, pieces):
+        ref[...] = piece
+    gain_total = lax.fori_loop(0, rows // 128, moe_grads, jnp.zeros((1, cols), jnp.float32))
+    for n in range(blocks):
+        small_ref[0, pl.ds(per * blocks + n, 1), :] = gain_total[:, n * 128 : (n + 1) * 128]
+    smalls.start()
+    lax.fori_loop(0, rows // 128, dots, 0)
+    sums.start()
+    sums.wait()
+    lax.fori_loop(0, rows // 128, residual, 0)
+    fetches[-1].start()
+    to_y.start()
+    to_pair.start()
+    mid_ref[:, pl.ds(pl.multiple_of((y * 2 + c) * cols, cols), cols)] = low_ref[...]
+    each_now(outs, 'first', 1)
+    to_y.wait_recv()
+    onward.start()
+    each_now(outs, 'second', 0)
+    for copy in fetches[3:]:
+        copy.wait()
+    to_pair.wait()
+    onward.wait()
+    to_y.wait_send()
+    for k in range(2):
+        each_now(weights, 'send', k)
+    each_now(outs, 'first', 2)
+    head_grads(0)
+    more = pltpu.make_async_copy(wo_all.at[:, pl.ds(wo_ref.shape[1], wo_ref.shape[1])], wo_ref,
+                                 s_in.at[3])
+    more.start()
+    more.wait()
+    head_grads(1)
+    lax.fori_loop(0, 2 * heads, deltas, 0)
+    lax.fori_loop(0, nz + 2, unit, 0)
     keys_out.finish()
-    outs.finish()
-    weights.finish()
+    total = jnp.zeros((1, width), jnp.float32)
+    for micro in range(2):
+        here = slice(micro * block, (micro + 1) * block)
+        grad, gain = norm_turn_back(kv_sum[micro, :, :width], k_pre[here, :], gk_ref[...],
+                                    cos_ref[here, :], sin_ref[here, :])
+        q_grad[here, heads * width : (heads + 1) * width] = grad.astype(low)
+        q_grad[here, (heads + 1) * width :] = kv_sum[micro, :, width:].astype(low)
+        total = total + gain
+    gain_grad[pl.ds(1, 1), :] = total
+    for part in outs + weights:
+        part.finish()
     smalls.finish()
 
 
-def attend_back(query, q_pre, gain_query, cosine, sine, keys_values, starts, log_total, delta,
-                grad, small, middle_grad, heads_low, out_part, nz, collective_id):
+def attend_back(query, q_pre, k_pre, gain_key, gain_query, cosine, sine, keys_values, starts, log_total,
+                gates, gates_grad, router, gain, moe_low, middle, scale, back, grad_slice, w_out, heads_low, out_part, nz, collective_id):
     rows, columns = query.shape
     width = keys_values.shape[4] // 2
     heads = columns // width
     block = rows // 2
     cols = out_part.shape[1] // 4
-    wo_shape = (middle_grad.shape[1] // (2 * nz), columns)
+    wo_shape = (w_out.shape[0] // (2 * nz), columns)
+    experts = gates.shape[1]
+    part_rows = -(-(experts // (2 * nz) + 1) * cols // 1024) * 8
+    small = (2 * nz, part_rows, 128)
     any_space = pl.BlockSpec(memory_space=pl.ANY)
     vmem = pl.BlockSpec(memory_space=pltpu.VMEM)
     vm, shape, f32, low = pltpu.VMEM, jax.ShapeDtypeStruct, jnp.float32, jnp.bfloat16
+    dma = pltpu.SemaphoreType.DMA
     return pl.pallas_call(
         functools.partial(attend_back_kernel, nz),
-        in_specs=[vmem] * 7 + [any_space] * 7,
+        in_specs=[vmem] * 13 + [any_space] * 9,
         out_specs=[vmem] * 6,
         out_shape=[
-            shape((rows, columns), low), shape((1, width), f32),
-            shape((2, block, 2 * width), f32),
+            shape((rows, cols), f32),
+            shape((rows, columns + 2 * width), low), shape((2, width), f32),
             shape((rows, cols), f32), shape(wo_shape, f32),
-            shape((8 * nz,) + small.shape[1:], f32),
+            shape((8 * nz,) + small[1:], f32),
         ],
-        scratch_shapes=[vm(middle_grad.shape, low)] + [vm((rows, columns), low)] * 2 + [
-            vm((nz, 2, 2, block, 2 * width), low), vm((rows, columns), low),
-            vm((rows, columns), f32), pltpu.SemaphoreType.DMA((6,)),
-            vm((nz, 2, 2, block, 2 * width), low),
+        scratch_shapes=[
+            vm((rows, cols), low),
+            vm((rows, 4 * cols), low), vm((w_out.shape[0], columns // 2), low), vm((rows, columns), low),
+            vm((rows, columns), low), vm((nz, 2, 2, block, 2 * width), low),
+            vm(small, f32), vm((3, rows, experts), low), vm((rows, columns), low),
+            vm((2 * heads, 1, block), f32), vm((rows, columns), f32), dma((8,)), dma((3,)), dma((3,)),
+            vm((2, block, 2 * width), f32), vm((nz, 2, 2, block, 2 * width), low),
             vm((2 * heads, width, block), f32), vm((block, width), f32), vm((block, width), f32),
-        ] + ScatterAll.scratch(nz, rows, cols, low, 0) + ReduceRows.scratch(nz, *wo_shape, low)
-        + SmallSums.scratch(nz, small.shape[1:], f32)
-        + ReduceCausal.scratch(nz, block, 2 * width, low),
+        ] + ScatterAll.scratch(nz, rows // 2, cols, low, 0) * 2
+        + ReduceRows.scratch(nz, wo_shape[0] // 2, wo_shape[1], low) * 2
+        + SmallSums.scratch(nz, small[1:], f32)
+        + ReduceCausal.scratch(nz, block, 2 * width, low) + RowSums.scratch(rows),
         compiler_params=pltpu.CompilerParams(
             collective_id=collective_id, has_side_effects=True, vmem_limit_bytes=62 << 20
         ),
         name="attend_back",
-    )(gain_query, cosine, sine, starts, log_total, delta, small, middle_grad, heads_low, query,
-      keys_values, grad, q_pre, out_part)
+    )(k_pre, gain_key, gain_query, cosine, sine, starts, log_total, scale, gates, gates_grad, router,
+      gain, moe_low, middle, back, grad_slice, w_out,
+      heads_low, query, keys_values, q_pre, out_part)
 
 
 def to_row(column, eye):
@@ -2797,10 +3029,10 @@
 
 
 def tail_kernel(nz, tok_ref, scale_ref, gain_ref, block_ref, small_ref, left_all, right_all, mid_all,
-                gp_all, up_all, hid_all, xr_all, gs_all, normed_part,
-                wq_out, wk_out, wv_out, token_out, block_out, small_out, dwg, dwu, dwd,
-                left_ref, right_ref, mid_ref, s_m, w_sum, gp_ref, up_ref, hid_ref, x_panel, g_panel, o_gate, o_up, o_down, s_in, s_out,
-                normed, token, s_w, r_w, s_l, s_g, r_g, *refs):
+                wq_all, wk_all, wv_all, gp_all, up_all, hid_all, xr_all, gs_all,
+                wq_out, wk_out, wv_out, token_out, block_out, gain_out, head_out, dwg, dwu, dwd,
+                left_ref, right_ref, mid_ref, wq, wk, wv, part_ref, s_m, w_sum, gp_ref, up_ref, hid_ref, x_panel, g_panel, o_gate, o_up, o_down, s_in, s_out,
+                small_out, normed, token, s_w, r_w, s_l, s_g, r_g, *refs):
     z, x, y, c = place()
     shard, group = lax.axis_index("fsdp"), lax.axis_index("tp")
     shards = 2 * nz
@@ -2813,19 +3045,39 @@
     panels = xr_all.shape[1] // panel
     f32, low = jnp.float32, jnp.bfloat16
     n_w, n_c = len(ReduceRows.scratch(nz, 16, 128, low)), len(ReduceCols.scratch(16, 128, low))
-    weights = ReduceRows(nz, left_ref, right_ref, w_sum, refs[:n_w])
-    columns = ReduceCols(normed_part, normed, refs[n_w : n_w + n_c])
-    sums = RowSums(refs[n_w + n_c :])
+    weights = [ReduceRows(nz, left_ref, right_ref, half, refs[n * n_w : (n + 1) * n_w], n, 2)
+               for n, half in enumerate(halves(w_sum))]
+    columns = ReduceCols(part_ref, normed, refs[2 * n_w : 2 * n_w + n_c])
+    sums = RowSums(refs[2 * n_w + n_c :])
     mirror = device(nz - 1 - z, x, y, c)
     greet_all(shard, group, shards, 4)
-    columns.start()
     fetches = [pltpu.make_async_copy(src, dst, s_m.at[n]) for n, (src, dst) in enumerate((
-        (left_all, left_ref), (right_all, right_ref), (mid_all, mid_ref)))]
+        (left_all, left_ref), (right_all, right_ref), (wq_all, wq), (wk_all, wk), (wv_all, wv),
+        (mid_all, mid_ref)))]
     for copy in fetches:
         copy.start()
-    for copy in fetches:
+    for copy in fetches[:2]:
         copy.wait()
-    weights.start()
+    for part in weights:
+        part.send(0)
+    for copy in fetches[2:]:
+        copy.wait()
+    first, second = wq_out.shape[1], wq_out.shape[1] + wk_out.shape[1]
+
+    def normed_parts(n, carry):
+        at = pl.ds(pl.multiple_of(n * cols, cols), cols)
+        part_ref[:, at] = (
+            dot_last(right_ref[:, :first], wq[at, :])
+            + dot_last(right_ref[:, first:second], wk[at, :])
+            + dot_last(right_ref[:, second:], wv[at, :])
+        ).astype(low)
+        return carry
+
+    lax.fori_loop(0, 4, normed_parts, 0)
+    columns.start()
+    for k in range(1, nz):
+        for part in weights:
+            part.send(k)
     top, bottom = pl.ds(0, half), pl.ds(half, half)
     swaps = [remote(src.at[bottom], dst.at[bottom], s_w.at[n], r_w.at[n], mirror)
              for n, (src, dst) in enumerate(((token, token_out), (block_ref, block_out)))]
@@ -2921,7 +3173,10 @@
             swaps[0].start()
             keeps[0].start()
 
-        pl.when((u >= 1) & (u <= nz))(lambda: weights.second(u - 1))
+        @pl.when((u >= 1) & (u <= nz))
+        def _():
+            for part in weights:
+                part.second(u - 1)
 
         @pl.when(u < panels // 2)
         def _():
@@ -2935,31 +3190,45 @@
             sums.start()
             loop_from_one(devices, lambda k: spread(k).start())
 
-        pl.when(u < nz)(lambda: weights.first(u))
+        @pl.when(u < nz)
+        def _():
+            for part in weights:
+                part.first(u)
+
         return carry
 
     lax.fori_loop(0, max(nz + 1, panels // 2), unit, 0)
     loop_from_one(devices, lambda k: spread(k).wait())
+    gain_rows = cols // 128
+    for g in range(4):
+        rows_of = small_out[g, pl.ds(0, gain_rows), :]
+        for f in range(1, shards):
+            rows_of = rows_of + small_out[f * 4 + g, pl.ds(0, gain_rows), :]
+        gain_out[g] = rows_of
+    total = small_out[0, pl.ds(gain_rows, 2), :]
+    for d in range(1, devices):
+        total = total + small_out[d, pl.ds(gain_rows, 2), :]
+    head_out[...] = total
     for copy in swaps + keeps:
         copy.wait()
     for copy in stores(panels - 1):
         copy.wait()
-    first, second = wq_out.shape[1], wq_out.shape[1] + wk_out.shape[1]
     wq_out[...] = w_sum[:, :first]
     wk_out[...] = w_sum[:, first:second]
     wv_out[...] = w_sum[:, second:]
     columns.finish()
-    weights.finish()
+    for part in weights:
+        part.finish()
 
 
 def tail(gate_grad, up_grad, hidden, tokens, middle_grad, scale, gain, block_out, small, normed_low,
-         pre_grad, query_width, rows_in, pair_grad, normed_part, nz, collective_id):
+         pre_grad, wq_all, wk_all, wv_all, rows_in, pair_grad, nz, collective_id):
     rows, cols = tokens.shape
     pairs, features = rows_in.shape
     hidden_width = hidden.shape[1]
     panel = 256
     w_shape = (normed_low.shape[1] // (2 * nz), pre_grad.shape[1])
-    kv_width = (pre_grad.shape[1] - query_width) // 2
+    query_width, kv_width = wq_all.shape[1], wk_all.shape[1]
     devices = 8 * nz
     any_space = pl.BlockSpec(memory_space=pl.ANY)
     vmem = pl.BlockSpec(memory_space=pltpu.VMEM)
@@ -2967,30 +3236,31 @@
     dma = pltpu.SemaphoreType.DMA
     return pl.pallas_call(
         functools.partial(tail_kernel, nz),
-        in_specs=[vmem] * 5 + [any_space] * 9,
-        out_specs=[vmem] * 3 + [any_space, any_space, vmem] + [any_space] * 3,
+        in_specs=[vmem] * 5 + [any_space] * 11,
+        out_specs=[vmem] * 3 + [any_space, any_space, vmem, vmem] + [any_space] * 3,
         out_shape=[
             shape((w_shape[0], query_width), f32), shape((w_shape[0], kv_width), f32),
             shape((w_shape[0], kv_width), f32), shape((rows, cols), low), shape((rows, cols), low),
-            shape((devices,) + small.shape, f32),
+            shape((4, cols // 128, 128), f32), shape((2, 128), f32),
             shape((features, hidden_width), f32), shape((features, hidden_width), f32),
             shape((hidden_width, features), f32),
         ],
         scratch_shapes=[vm(normed_low.shape, low), vm(pre_grad.shape, low), vm((rows, cols), f32),
-                        dma((3,)), vm(w_shape, f32)] + [vm((pairs, hidden_width), low)] * 3 + [
+                        vm(wq_all.shape, low), vm(wk_all.shape, low), vm(wv_all.shape, low),
+                        vm((rows, 4 * cols), low), dma((6,)), vm(w_shape, f32)] + [vm((pairs, hidden_width), low)] * 3 + [
             vm((pairs, panel), low), vm((pairs, panel), low),
             vm((panel, hidden_width), f32), vm((panel, hidden_width), f32),
             vm((hidden_width, panel), f32), dma((5,)), dma((3,)),
-            vm((rows, cols), f32), vm((rows, cols), low),
+            vm((devices,) + small.shape, f32), vm((rows, cols), f32), vm((rows, cols), low),
             dma((2,)), dma((2,)), dma((2,)), dma((devices,)), dma((devices,)),
-        ] + ReduceRows.scratch(nz, *w_shape, low) + ReduceCols.scratch(rows, cols, low)
+        ] + ReduceRows.scratch(nz, w_shape[0] // 2, w_shape[1], low) * 2 + ReduceCols.scratch(rows, cols, low)
         + RowSums.scratch(rows),
         compiler_params=pltpu.CompilerParams(
             collective_id=collective_id, has_side_effects=True, vmem_limit_bytes=62 << 20
         ),
         name="tail",
-    )(tokens, scale, gain, block_out, small, normed_low, pre_grad, middle_grad, gate_grad, up_grad,
-      hidden, rows_in, pair_grad, normed_part)
+    )(tokens, scale, gain, block_out, small, normed_low, pre_grad, middle_grad, wq_all, wk_all, wv_all,
+      gate_grad, up_grad, hidden, rows_in, pair_grad)
 
 
 def join_kernel(nz, tok_ref, gain_ref, attn_part, middle_ref, scale_ref, low_ref, all_ref, *refs):
@@ -3170,7 +3440,7 @@
     small_rows = -(-small.shape[0] // 1024) * 8
     small = jnp.pad(small, (0, small_rows * 128 - small.shape[0])).reshape(small_rows, 128)
     small_all, wq_all, wk_all, wv_all, tokens, full_tokens = gather_rows(
-        [small, w_query, key_weight, value_weight], nz, 2, [tokens]
+        [small, w_query, key_weight, value_weight], nz, 2, [tokens], 2
     )
     small_all = small_all.reshape(shard_count, small_rows * 128)
     routes_all = small_all[:, : row_count * TOPK].reshape(shard_count * row_count, TOPK)
@@ -3190,19 +3460,13 @@
     positions = (query_index - query_start).reshape(row_count)
     cosine_lookup, sine_lookup = rope_tables(positions, head_width)
 
-    full_tokens = full_tokens.astype(f32)
-    token_mean = jnp.mean(full_tokens * full_tokens, axis=-1, keepdims=True)
-    token_scale = lax.rsqrt(token_mean + norm_eps)
-    normed_low = (full_tokens * token_scale * gain_attn).astype(low)
-    query_pre = jnp.dot(normed_low, wq_all, preferred_element_type=f32)
-    key_pre = jnp.dot(normed_low, wk_all, preferred_element_type=f32)
-    value_low = jnp.dot(normed_low, wv_all, preferred_element_type=f32).astype(low)
     turned_sine = jnp.where(jnp.arange(head_width) < head_width // 2, -sine_lookup, sine_lookup)
     query_gain, key_gain = gain_query.reshape(1, head_width), key_norm_gain.reshape(1, head_width)
     starts = query_start.reshape(micro_count, 1, micro_rows).astype(jnp.int32)
-    query_low, heads_low, head_out, log_total, keys_values, grads_all, wo_all = attend(
-        query_pre, key_pre, value_low, query_gain, key_gain, cosine_lookup, turned_sine, starts,
-        cotangent, w_out, nz, 3,
+    (normed_low, token_scale, query_pre, key_pre, query_low, heads_low, log_total, keys_values,
+     grads_all, wo_all) = attend(
+        full_tokens, gain_attn.reshape(1, model_width), wq_all, wk_all, wv_all, query_gain, key_gain,
+        cosine_lookup, turned_sine, starts, cotangent, w_out, nz, 3,
     )
     attn_part = dot_last(heads_low, wo_all).astype(low)
     gain_slice = lax.dynamic_slice_in_dim(gain_moe, my_columns, slice_width)
@@ -3213,79 +3477,46 @@
     rows_in, pair_grad, hidden_low, gate_pre_low, up_pre_low = (
         array.reshape(-1, array.shape[2]) for array in kept
     )
-    gates_grad = gates_grad.reshape(expert_total, row_count).T
-    logit_grad = gates * (gates_grad - jnp.sum(gates * gates_grad, axis=1, keepdims=True))
-    router_slice = lax.dynamic_slice_in_dim(router, my_columns, slice_width).astype(f32)
-    moe_grad = back + lax.dot_general(
-        logit_grad, router_slice, (((1,), (1,)), ((), ())), precision=highest_precision
-    )
-    router_part = lax.dot_general(
-        moe_low.astype(f32), logit_grad, (((0,), (0,)), ((), ())), precision=highest_precision
-    )
-    gain_moe_part = jnp.sum(moe_grad * middle * scale, axis=0)
+    router_slice = lax.dynamic_slice_in_dim(router, my_columns, slice_width)
     swapped_grad = lax.dynamic_slice(
         grads_all, (mirror_index * row_count + micro_rows, my_columns), (micro_rows, slice_width)
     )
     grad_slice = jnp.concatenate([cotangent[:micro_rows], swapped_grad], axis=0).astype(f32)
-    inner = gain_slice * moe_grad
-    middle_grad, middle_low = turn(middle, scale, inner, grad_slice, 11)
-    heads_grad = jnp.dot(middle_low, wo_all, preferred_element_type=f32).astype(low)
-    delta = jnp.sum(
-        (heads_grad.astype(f32) * head_out).reshape(micro_count, micro_rows, query_local, head_width),
-        axis=3,
-    ).transpose(0, 2, 1).reshape(micro_count * query_local, 1, micro_rows)
-    pieces = [gain_moe_part, router_part.reshape(-1)]
-    length = sum(piece.shape[0] for piece in pieces)
-    part_rows = -(-length // (shard_count * 1024)) * 8
-    flat = jnp.concatenate(
-        pieces + [jnp.zeros((shard_count * part_rows * 128 - length,), f32)]
-    ).reshape(shard_count, part_rows, 128)
-    query_pre_low, gain_query_part, sides, out_sum, w_out_grad, summed = attend_back(
-        query_low, query_pre, query_gain, cosine_lookup, turned_sine, keys_values, starts, log_total,
-        delta, heads_grad, flat, middle_low, heads_low, out_part, nz, 12,
+    middle_grad, pre_low, head_gains, out_sum, w_out_grad, summed = attend_back(
+        query_low, query_pre, key_pre, key_gain, query_gain, cosine_lookup, turned_sine, keys_values,
+        starts, log_total, gates, gates_grad, router_slice, gain_slice.reshape(1, slice_width), moe_low,
+        middle, scale, back, grad_slice, wo_all, heads_low, out_part, nz, 12,
     )
     block_out = (middle + out_sum).astype(low)
-    sides = sides.reshape(row_count, 2 * kv_width)
-
-    def shape_keys(key_raw, key_gain):
-        return rotary_apply(root_mean_norm(key_raw, key_gain), cosine_lookup, sine_lookup)
-
-    key_pre_grad, gain_key_part = jax.vjp(shape_keys, key_pre, key_norm_gain)[1](sides[:, :kv_width])
-    key_pre_low = key_pre_grad.astype(low)
-    value_pre_low = sides[:, kv_width:].astype(low)
-    normed_part = (
-        dot_last(query_pre_low, wq_all)
-        + dot_last(key_pre_low, wk_all)
-        + dot_last(value_pre_low, wv_all)
-    ).astype(low)
-    pre_low = jnp.concatenate([query_pre_low, key_pre_low, value_pre_low], axis=1)
     gain_rows = slice_width // 128
     gains = jnp.concatenate(
-        [jnp.zeros((slice_width,), f32), gain_query_part.reshape(-1), gain_key_part,
+        [jnp.zeros((slice_width,), f32), head_gains.reshape(-1),
          jnp.zeros(((8 - gain_rows - 2) * 128,), f32)]
     ).reshape(8, 128)
     attn_gain = lax.dynamic_slice_in_dim(gain_attn, my_columns, slice_width)
-    w_query_grad, w_key_grad, w_value_grad, token_grad, block_out, gains, *expert_grads = tail(
+    (w_query_grad, w_key_grad, w_value_grad, token_grad, block_out, attn_gains, head_gains,
+     *expert_grads) = tail(
         gate_pre_low, up_pre_low, hidden_low, tokens, middle_grad, token_scale,
-        attn_gain.reshape(1, slice_width), block_out, gains, normed_low, pre_low, query_width, rows_in,
-        pair_grad, normed_part, nz, 15,
+        attn_gain.reshape(1, slice_width), block_out, gains, normed_low, pre_low, wq_all, wk_all, wv_all,
+        rows_in, pair_grad, nz, 15,
     )
-    summed = summed.reshape(shard_count, group_count, part_rows * 128).transpose(
-        1, 0, 2
-    ).reshape(group_count, shard_count * part_rows * 128)
-    gains = gains.reshape(shard_count, group_count, 8, 128)
+    per = expert_total // shard_count
+    summed = summed.reshape(shard_count, group_count, -1, 128)
+    router_grad = summed[:, :, : per * gain_rows].reshape(
+        shard_count, group_count, per, slice_width
+    ).transpose(1, 3, 0, 2).reshape(router.shape)
     return (
         block_out,
         token_grad,
-        jnp.sum(gains[:, :, :gain_rows], axis=0).reshape(-1),
+        attn_gains.reshape(-1),
         w_query_grad,
         w_key_grad,
         w_value_grad,
         w_out_grad,
-        jnp.sum(gains[:, :, gain_rows], axis=(0, 1)),
-        jnp.sum(gains[:, :, gain_rows + 1], axis=(0, 1)),
-        summed[:, :slice_width].reshape(-1),
-        summed[:, slice_width:length].reshape(router.shape),
+        head_gains[0],
+        head_gains[1],
+        summed[0, :, per * gain_rows : (per + 1) * gain_rows].reshape(-1),
+        router_grad,
         expert_grads[0][None],
         expert_grads[1][None],
         expert_grads[2][None],

time: 758 us -> 717 us (0.946)
  matrix products: 29.7 us -> 6.23 us
  other arithmetic: 19.7 us -> 7.91 us
    pallas_call x3 -> x2, Pallas kernels: 216 us -> 194 us  [the longest x1 119 us: attend(): pl.pallas_call(functools.partial(attend_kernel, nz), in_specs=[vmem] * 8...]
    pallas_call x1, Pallas kernels: 134 us -> 157 us  [attend_back(): pl.pallas_call(functools.partial(attend_back_kernel, nz), in_specs=[vmem]...]
    dot_general x6 -> x0, matrix products: 18.4 us -> none  [the longest x1 5.89 us: gathered_body(): query_pre = jnp.dot(normed_low, wq_all, preferred_element_type=f32)]
    pallas_call x1, Pallas kernels: 223 us -> 212 us  [run_experts(): pl.pallas_call(functools.partial(expert_kernel, nz, slots, block_rows), i...]
    reduce_sum x6 -> x0, other arithmetic: 8.3 us -> none  [the longest x1 2.13 us: gathered_body(): token_mean = jnp.mean(full_tokens * full_tokens, axis=-1, keepdims=True)]
    pallas_call x1, Pallas kernels: 85.7 us -> 93.4 us  [tail(): pl.pallas_call(functools.partial(tail_kernel, nz), in_specs=[vmem] * 5 +...]
    unnamed x77 -> x41, local copies, waits for them, and re-layouts: 24.6 us -> 22.1 us
where the time goes in v6:
time: 717 us; the launch traced here: 705 us
  Pallas kernels  656 us (91%)
  local copies, waits for them, and re-layouts  34.2 us (5%)
  other arithmetic  7.91 us (1%)
    pallas_call x1, Pallas kernels, run_experts(): pl.pallas_call(functools.partial(expert_kernel, nz, slots, block_rows), i...  212 us
    pallas_call x1, Pallas kernels, attend_back(): pl.pallas_call(functools.partial(attend_back_kernel, nz), in_specs=[vmem]...  157 us
    pallas_call x1, Pallas kernels, attend(): pl.pallas_call(functools.partial(attend_kernel, nz), in_specs=[vmem] * 8...  119 us
    pallas_call x1, Pallas kernels, tail(): pl.pallas_call(functools.partial(tail_kernel, nz), in_specs=[vmem] * 5 +...  93.4 us
    pallas_call x1, Pallas kernels, gather_rows(): pl.pallas_call(functools.partial(gather_rows_kernel, nz, count, columns,...  74.4 us
    unnamed x41, local copies, waits for them, and re-layouts  22.1 us

profile of v6, /device:TPU:0, one launch (start us, length us, event | category | flops | bytes accessed | tf_op | source)
XLA Modules:
  0.0 705.4 jit_solution(9011010112830004530)
XLA Ops:
  0.7 0.8 copy.39
  1.7 0.7 copy.43
  3.0 74.4 %gather_rows.1 = (s32[320,128]{1,0:T(8,128)}, bf16[2048,1024]{1,0:T(8,128)(2,1)}, bf16[2048,128]{1,0:T(8,128)(2,1)}, bf16[2048,128]{1,0:T(8,128)(2,1)}, bf16[512...) custom-call(s32[40,128]{1,0:T(8,128)} %pad_bitcast_fusion.refs_0_, bf16[256,1024]{1,0:T(8,128)(2,1)} %refs_1_.1, ...), custom_call_target="tpu_custom_call" | custom-call | tf_op jit(solution)/shard_map/gather_rows/pallas_call | solution.py:1012
  77.4 0.9 reshape.163
  79.1 1.0 multiply_sine_fusion
  80.1 0.8 negate_select_fusion.sin_ref
  80.9 0.8 pad_maximum_fusion.cos_ref
  82.4 119.1 %attend.1 = (bf16[512,2048]{1,0:T(8,128)(2,1)}, f32[512,1]{1,0:T(8,128)}, f32[512,1024]{1,0:T(8,128)}, f32[512,128]{1,0:T(8,128)}, bf16[512,1024]{1,0:T(8,128)(2...) custom-call(f32[1,2048]{1,0:T(1,128)} %bitcast.73, ...), custom_call_target="tpu_custom_call" | custom-call | tf_op jit(solution)/shard_map/attend/pallas_call | solution.py:2303
  201.5 6.2 convolution_convert_fusion.attn_part
  207.7 1.3 dynamic_slice.28
  209.1 2.5 reshape.168.routes_all
  211.6 1.0 copy.40.router_ref
  212.6 212.5 %experts.1 = (f32[512,512]{1,0:T(8,128)}, f32[512,1]{1,0:T(8,128)}, bf16[512,512]{1,0:T(8,128)(2,1)}, bf16[4096,2048]{1,0:T(8,128)(2,1)}, bf16[4096,2048]{1,0:T(...) custom-call(bf16[512,512]{1,0:T(8,128)(2,1)} %get-tuple-element.58.t, ...), custom_call_target="tpu_custom_call" | custom-call | tf_op jit(solution)/shard_map/experts/pallas_call | solution.py:1820
  425.0 1.0 dynamic_slice.30
  426.0 1.1 maximum_convert_fusion.slice_all
  427.1 1.6 constant_dynamic-slice_fusion.router_ref
  428.7 156.6 %attend_back.1 = (f32[512,512]{1,0:T(8,128)}, bf16[512,1280]{1,0:T(8,128)(2,1)}, f32[2,128]{1,0:T(2,128)}, f32[512,512]{1,0:T(8,128)}, f32[256,1024]{1,0:T(8,128)}, /*index=5*/f32[32,24,128]{2,1,0:T(8,128)}) custom-call(f32[512,128]{1,0:T(8,128)} %get-tuple-element.69.k_pre, f32[1,128]{1,0:T(1,128)} %bitcast.82, f32[1,128]{1,0:T(1,128)} %bitcast.80, ...), custom_call_target="tpu_custom_call" | custom-call | tf_op jit(solution)/shard_map/attend_back/pallas_call | solution.py:2866
  585.3 2.2 add_convert_fusion.block_ref
  587.5 1.3 maximum_bitcast_fusion.small_ref
  588.7 1.3 dynamic_slice.27
  590.1 93.4 %tail.1 = (f32[256,1024]{1,0:T(8,128)}, f32[256,128]{1,0:T(8,128)}, f32[256,128]{1,0:T(8,128)}, bf16[512,512]{1,0:T(8,128)(2,1)}, bf16[512,512]{1,0:T(8,128)(2,1...) custom-call(bf16[512,512]{1,0:T(8,128)(2,1)} %get-tuple-element.58.t, ...), custom_call_target="tpu_custom_call" | custom-call | tf_op jit(solution)/shard_map/tail/pallas_call | solution.py:3237
  683.5 1.3 slice_bitcast_fusion
  685.1 0.8 copy.45
  686.5 2.2 copy.56
  688.7 1.9 copy.57
  691.2 1.0 copy.59
  693.5 1.0 copy.62
  694.4 3.2 copy.63
  697.7 3.2 copy.64
  700.9 0.9 slice-done
  701.7 0.8 slice-done.1
  702.5 2.7 copy.65
  (55 shorter events, 4.8 us)
Async XLA Ops:
  201.5 10.1 %copy-start.5 = (bf16[2048,32]{0,1:T(8,128)(2,1)S(1)}, bf16[2048,32]{0,1:T(8,128)(2,1)}, u32[]{:S(2)}) copy-start(bf16[2048,32]{0,1:T(8,128)(2,1)} %param.28) | copy-start | bytes 393220
  212.6 213.5 %slice-start.4 = ((bf16[512,512]{1,0:T(8,128)(2,1)}), bf16[256,512]{1,0:T(8,128)(2,1)S(1)}, s32[]{:S(2)}) async-start(bf16[512,512]{1,0:T(8,128)(2,1)} %cot_ref.1), calls=%async_computation.4 | async-start | bytes 524288 | tf_op jit(solution)/shard_map/slice | solution.py:3484
  428.7 156.6 %copy-start.1 = (f32[512,512]{1,0:T(8,128)S(1)}, f32[512,512]{1,0:T(8,128)}, u32[]{:S(2)}) copy-start(f32[512,512]{1,0:T(8,128)} %get-tuple-element.68.middle_all) | copy-start | bytes 3145732
  590.1 94.7 %copy-start.4 = (f32[32,24,128]{2,1,0:T(8,128)S(1)}, f32[32,24,128]{2,1,0:T(8,128)}, u32[]{:S(2)}) copy-start(f32[32,24,128]{2,1,0:T(8,128)} %get-tuple-element.98) | copy-start | bytes 1179652
  683.5 7.1 %copy-start.8 = (f32[4,4,128]{2,1,0:T(4,128)S(1)}, f32[4,4,128]{2,1,0:T(4,128)}, u32[]{:S(2)}) copy-start(f32[4,4,128]{2,1,0:T(4,128)} %get-tuple-element.92) | copy-start | bytes 24580
  683.5 7.7 %copy-start.3 = (f32[256,1024]{1,0:T(8,128)S(1)}, f32[256,1024]{1,0:T(8,128)}, u32[]{:S(2)}) copy-start(f32[256,1024]{1,0:T(8,128)} %get-tuple-element.127) | copy-start | bytes 3145732
  683.5 8.7 %copy-start.7 = (f32[256,128]{1,0:T(8,128)S(1)}, f32[256,128]{1,0:T(8,128)}, u32[]{:S(2)}) copy-start(f32[256,128]{1,0:T(8,128)} %get-tuple-element.128) | copy-start | bytes 393220
  683.5 9.3 %copy-start.6 = (f32[256,128]{1,0:T(8,128)S(1)}, f32[256,128]{1,0:T(8,128)}, u32[]{:S(2)}) copy-start(f32[256,128]{1,0:T(8,128)} %get-tuple-element.129) | copy-start | bytes 393220
  683.5 9.9 %copy-start.2 = (f32[256,1024]{1,0:T(8,128)S(1)}, f32[256,1024]{1,0:T(8,128)}, u32[]{:S(2)}) copy-start(f32[256,1024]{1,0:T(8,128)} %get-tuple-element.130) | copy-start | bytes 3145732
  684.9 9.5 %copy-start = (f32[2048,768]{1,0:T(8,128)S(1)}, f32[2048,768]{1,0:T(8,128)}, u32[]{:S(2)}) copy-start(f32[2048,768]{1,0:T(8,128)} %get-tuple-element.99) | copy-start | bytes 18874372
  691.2 6.5 slice-start.2
  694.4 3.2 slice-start.3
  694.4 7.3 %slice-start = ((s8[6291456]{0:T(1024)(128)(4,1)}), s8[4194304]{0:T(1024)(128)(4,1)S(1)}, s32[]{:S(2)}) async-start(s8[6291456]{0:T(1024)(128)(4,1)} %bitcast.52), calls=%async_computation | async-start | bytes 8388608
  697.6 4.8 slice-start.1

commit v7 on v6

--- a/solution.py
+++ b/solution.py
@@ -1721,7 +1721,8 @@
         here = pl.ds(pl.multiple_of(n * 128, 128), 128)
         scale = lax.rsqrt(to_column(sums.total(n), corner) / width + norm_eps)
         scale_ref[here, :] = scale
-        low_ref[here, :] = (middle_ref[here, :] * scale * gain_ref[...]).astype(low)
+        gain = gain_ref[:, pl.ds(pl.multiple_of(group * cols, cols), cols)]
+        low_ref[here, :] = (middle_ref[here, :] * scale * gain).astype(low)
         return carry
 
     lax.fori_loop(0, rows // 128, residual, 0)
@@ -2620,10 +2621,10 @@
 
 
 def attend_back_kernel(nz, k_pre, gk_ref, gq_ref, cos_ref, sin_ref, start_ref, lse_ref, scale_ref,
-                       gates_ref, gg_ref, router_ref, gain_ref, moe_ref,
-                       middle_all, back_all, slice_all, wo_all, heads_all, q_all, kv_all, pre_all,
+                       gates_ref, gg_ref, router_all, gain_ref, moe_ref,
+                       middle_all, back_all, cot_part, cot_all, wo_all, heads_all, q_all, kv_all, pre_all,
                        out_part, mid_out, q_grad, gain_grad, out_sum, wo_sum, small_out,
-                       low_ref, mid_ref, wo_ref, heads_ref, q_ref, kv_ref,
+                       router_ref, low_ref, mid_ref, wo_ref, heads_ref, q_ref, kv_ref,
                        small_ref, split_ref, grad_ref, delta_ref, q_pre, s_in, s_t, r_t,
                        kv_sum, sides, acc, k_acc, v_acc, *refs):
     middle_ref, inner_ref = (q_pre.at[:, pl.ds(n * mid_out.shape[1], mid_out.shape[1])]
@@ -2651,8 +2652,15 @@
     greet_all(lax.axis_index("fsdp"), lax.axis_index("tp"), shards, 4)
     for part in outs:
         part.start()
+    group = lax.axis_index("tp")
+    rows, cols = mid_out.shape
+    half = rows // 2
+    mine = pl.ds(pl.multiple_of(group * cols, cols), cols)
+    there = pl.ds(pl.multiple_of(mirrored(nz, shard) * rows + half, half), half)
     fetches = [pltpu.make_async_copy(src, dst, s_in.at[n]) for n, (src, dst) in enumerate((
-        (middle_all, middle_ref), (back_all, inner_ref), (slice_all, mid_out),
+        (router_all.at[mine], router_ref), (middle_all, middle_ref), (back_all, inner_ref),
+        (cot_part.at[pl.ds(0, half)], low_ref.at[pl.ds(0, half)]),
+        (cot_all.at[there, mine], low_ref.at[pl.ds(half, half)]),
         (wo_all.at[:, pl.ds(0, wo_ref.shape[1])], wo_ref),
         (heads_all, heads_ref), (q_all, q_ref), (kv_all, kv_ref), (pre_all, q_pre)))]
     for copy in fetches[:-1]:
@@ -2723,7 +2731,6 @@
         pl.when(u == done + 1)(close_all)
         return carry
 
-    rows, cols = mid_out.shape
     eye = diagonal()
 
     def column(yy):
@@ -2744,7 +2751,7 @@
         here = pl.ds(pl.multiple_of(n * 128, 128), 128)
         mean = to_column(sums.total(n), eye) / (4 * cols)
         scale = scale_ref[here, :]
-        out = (mid_out[here, :] + scale * inner_ref[here, :]
+        out = (low_ref[here, :].astype(jnp.float32) + scale * inner_ref[here, :]
                - middle_ref[here, :] * (scale * scale * scale * mean))
         mid_out[here, :] = out
         low_ref[here, :] = out.astype(low)
@@ -2787,7 +2794,7 @@
         for n in range(blocks):
             small_ref[e // per, pl.ds(e % per * blocks + n, 1), :] = (
                 router_grad[e : e + 1, n * 128 : (n + 1) * 128])
-    for copy in fetches[:3]:
+    for copy in fetches[:5]:
         copy.wait()
 
     def moe_grads(n, total):
@@ -2795,7 +2802,7 @@
         grad = inner_ref[here, :]
         for piece in pieces_ref:
             grad = grad + dot_last(piece[here, :], router_ref[...])
-        inner_ref[here, :] = grad * gain_ref[...]
+        inner_ref[here, :] = grad * gain_ref[:, mine]
         return total + jnp.sum(grad * middle_ref[here, :] * scale_ref[here, :], axis=0, keepdims=True)
 
     pieces_ref = [split_ref.at[n] for n in range(3)]
@@ -2817,7 +2824,7 @@
     to_y.wait_recv()
     onward.start()
     each_now(outs, 'second', 0)
-    for copy in fetches[3:]:
+    for copy in fetches[5:]:
         copy.wait()
     to_pair.wait()
     onward.wait()
@@ -2827,7 +2834,7 @@
     each_now(outs, 'first', 2)
     head_grads(0)
     more = pltpu.make_async_copy(wo_all.at[:, pl.ds(wo_ref.shape[1], wo_ref.shape[1])], wo_ref,
-                                 s_in.at[3])
+                                 s_in.at[5])
     more.start()
     more.wait()
     head_grads(1)
@@ -2849,7 +2856,7 @@
 
 
 def attend_back(query, q_pre, k_pre, gain_key, gain_query, cosine, sine, keys_values, starts, log_total,
-                gates, gates_grad, router, gain, moe_low, middle, scale, back, grad_slice, w_out, heads_low, out_part, nz, collective_id):
+                gates, gates_grad, router, gain, moe_low, middle, scale, back, cotangent, cot_all, w_out, heads_low, out_part, nz, collective_id):
     rows, columns = query.shape
     width = keys_values.shape[4] // 2
     heads = columns // width
@@ -2865,7 +2872,7 @@
     dma = pltpu.SemaphoreType.DMA
     return pl.pallas_call(
         functools.partial(attend_back_kernel, nz),
-        in_specs=[vmem] * 13 + [any_space] * 9,
+        in_specs=[vmem] * 10 + [any_space] + [vmem] * 2 + [any_space] * 10,
         out_specs=[vmem] * 6,
         out_shape=[
             shape((rows, cols), f32),
@@ -2874,11 +2881,11 @@
             shape((8 * nz,) + small[1:], f32),
         ],
         scratch_shapes=[
-            vm((rows, cols), low),
+            vm((cols, experts), low), vm((rows, cols), low),
             vm((rows, 4 * cols), low), vm((w_out.shape[0], columns // 2), low), vm((rows, columns), low),
             vm((rows, columns), low), vm((nz, 2, 2, block, 2 * width), low),
             vm(small, f32), vm((3, rows, experts), low), vm((rows, columns), low),
-            vm((2 * heads, 1, block), f32), vm((rows, columns), f32), dma((8,)), dma((3,)), dma((3,)),
+            vm((2 * heads, 1, block), f32), vm((rows, columns), f32), dma((10,)), dma((3,)), dma((3,)),
             vm((2, block, 2 * width), f32), vm((nz, 2, 2, block, 2 * width), low),
             vm((2 * heads, width, block), f32), vm((block, width), f32), vm((block, width), f32),
         ] + ScatterAll.scratch(nz, rows // 2, cols, low, 0) * 2
@@ -2890,7 +2897,7 @@
         ),
         name="attend_back",
     )(k_pre, gain_key, gain_query, cosine, sine, starts, log_total, scale, gates, gates_grad, router,
-      gain, moe_low, middle, back, grad_slice, w_out,
+      gain, moe_low, middle, back, cotangent, cot_all, w_out,
       heads_low, query, keys_values, q_pre, out_part)
 
 
@@ -3101,7 +3108,8 @@
              for n, (src, dst) in enumerate(((gp_all, gp_ref), (up_all, up_ref), (hid_all, hid_ref)))]
     for copy in tuple(whole) + loads(0):
         copy.start()
-    small_out[me] = small_ref[...]
+    small_out[me] = jnp.zeros(small_out.shape[1:], f32)
+    small_out[me, pl.ds(cols // 128, 2), :] = small_ref[...]
 
     def expert_weights(n):
         @pl.when(n == 0)
@@ -3134,7 +3142,7 @@
         def step(n, gains):
             here = pl.ds(pl.multiple_of(n * 128, 128), 128)
             tok, grad = tok_ref[here, :].astype(f32), normed[here, :]
-            product = tok * (grad * gain_ref[...])
+            product = tok * (grad * gain_ref[:, pl.ds(pl.multiple_of(group * cols, cols), cols)])
             sums.got[0, pl.ds(n, 1), :] = to_row(jnp.sum(product, axis=1, keepdims=True), eye)
             return gains + jnp.sum(grad * tok * scale_ref[here, :], axis=0, keepdims=True)
 
@@ -3151,7 +3159,7 @@
             scale = scale_ref[here, :]
             token[here, :] = (
                 mid_ref[here, :]
-                + scale * (gain_ref[...] * normed[here, :])
+                + scale * (gain_ref[:, pl.ds(pl.multiple_of(group * cols, cols), cols)] * normed[here, :])
                 - tok_ref[here, :].astype(f32) * (scale * scale * scale * mean)
             ).astype(low)
             return carry
@@ -3251,7 +3259,7 @@
             vm((pairs, panel), low), vm((pairs, panel), low),
             vm((panel, hidden_width), f32), vm((panel, hidden_width), f32),
             vm((hidden_width, panel), f32), dma((5,)), dma((3,)),
-            vm((devices,) + small.shape, f32), vm((rows, cols), f32), vm((rows, cols), low),
+            vm((devices, 8, 128), f32), vm((rows, cols), f32), vm((rows, cols), low),
             dma((2,)), dma((2,)), dma((2,)), dma((devices,)), dma((devices,)),
         ] + ReduceRows.scratch(nz, w_shape[0] // 2, w_shape[1], low) * 2 + ReduceCols.scratch(rows, cols, low)
         + RowSums.scratch(rows),
@@ -3469,35 +3477,25 @@
         cosine_lookup, turned_sine, starts, cotangent, w_out, nz, 3,
     )
     attn_part = dot_last(heads_low, wo_all).astype(low)
-    gain_slice = lax.dynamic_slice_in_dim(gain_moe, my_columns, slice_width)
+    gain_row = gain_moe.reshape(1, model_width)
     middle, scale, moe_low, _, out_part, back, gates_grad, gates, *kept = run_experts(
-        tokens, gain_slice.reshape(1, slice_width), router, attn_part, grads_all, routes_all,
+        tokens, gain_row, router, attn_part, grads_all, routes_all,
         w_gate[0], w_up[0], w_down[0], micro_rows, capacity, nz, 8,
     )
     rows_in, pair_grad, hidden_low, gate_pre_low, up_pre_low = (
         array.reshape(-1, array.shape[2]) for array in kept
     )
-    router_slice = lax.dynamic_slice_in_dim(router, my_columns, slice_width)
-    swapped_grad = lax.dynamic_slice(
-        grads_all, (mirror_index * row_count + micro_rows, my_columns), (micro_rows, slice_width)
-    )
-    grad_slice = jnp.concatenate([cotangent[:micro_rows], swapped_grad], axis=0).astype(f32)
     middle_grad, pre_low, head_gains, out_sum, w_out_grad, summed = attend_back(
         query_low, query_pre, key_pre, key_gain, query_gain, cosine_lookup, turned_sine, keys_values,
-        starts, log_total, gates, gates_grad, router_slice, gain_slice.reshape(1, slice_width), moe_low,
-        middle, scale, back, grad_slice, wo_all, heads_low, out_part, nz, 12,
+        starts, log_total, gates, gates_grad, router, gain_row, moe_low, middle, scale,
+        back, cotangent, grads_all, wo_all, heads_low, out_part, nz, 12,
     )
     block_out = (middle + out_sum).astype(low)
     gain_rows = slice_width // 128
-    gains = jnp.concatenate(
-        [jnp.zeros((slice_width,), f32), head_gains.reshape(-1),
-         jnp.zeros(((8 - gain_rows - 2) * 128,), f32)]
-    ).reshape(8, 128)
-    attn_gain = lax.dynamic_slice_in_dim(gain_attn, my_columns, slice_width)
     (w_query_grad, w_key_grad, w_value_grad, token_grad, block_out, attn_gains, head_gains,
      *expert_grads) = tail(
         gate_pre_low, up_pre_low, hidden_low, tokens, middle_grad, token_scale,
-        attn_gain.reshape(1, slice_width), block_out, gains, normed_low, pre_low, wq_all, wk_all, wv_all,
+        gain_attn.reshape(1, model_width), block_out, head_gains, normed_low, pre_low, wq_all, wk_all, wv_all,
         rows_in, pair_grad, nz, 15,
     )
     per = expert_total // shard_count

time: 717 us -> 718 us (level); the launches traced: 705 us -> 714 us
  Pallas kernels: 656 us -> 671 us
    pallas_call x1, Pallas kernels: 157 us -> 168 us  [attend_back(): pl.pallas_call(functools.partial(attend_back_kernel, nz), in_specs=[vmem]...]
    unnamed x41 -> x39, local copies, waits for them, and re-layouts: 22.1 us -> 23.1 us
where the time goes in v7:
time: 718 us; the launch traced here: 714 us
  Pallas kernels  671 us (93%)
  local copies, waits for them, and re-layouts  30 us (4%)
    pallas_call x1, Pallas kernels, run_experts(): pl.pallas_call(functools.partial(expert_kernel, nz, slots, block_rows), i...  212 us
    pallas_call x1, Pallas kernels, attend_back(): pl.pallas_call(functools.partial(attend_back_kernel, nz), in_specs=[vmem]...  168 us
    pallas_call x1, Pallas kernels, attend(): pl.pallas_call(functools.partial(attend_kernel, nz), in_specs=[vmem] * 8...  119 us
    pallas_call x1, Pallas kernels, tail(): pl.pallas_call(functools.partial(tail_kernel, nz), in_specs=[vmem] * 5 +...  97.4 us
    pallas_call x1, Pallas kernels, gather_rows(): pl.pallas_call(functools.partial(gather_rows_kernel, nz, count, columns,...  74.4 us
    unnamed x39, local copies, waits for them, and re-layouts  23.1 us

profile of v7, /device:TPU:0, one launch (start us, length us, event | category | flops | bytes accessed | tf_op | source)
XLA Modules:
  0.0 713.7 jit_solution(12716608239509420708)
XLA Ops:
  0.8 0.7 copy.43
  1.4 0.8 copy.39
  2.5 0.6 pad_bitcast_fusion.refs_0_
  3.1 1.9 copy.40.router_ref.router_all
  5.0 74.4 %gather_rows.1 = (s32[320,128]{1,0:T(8,128)}, bf16[2048,1024]{1,0:T(8,128)(2,1)}, bf16[2048,128]{1,0:T(8,128)(2,1)}, bf16[2048,128]{1,0:T(8,128)(2,1)}, bf16[512...) custom-call(s32[40,128]{1,0:T(8,128)} %pad_bitcast_fusion.refs_0_, bf16[256,1024]{1,0:T(8,128)(2,1)} %refs_1_.1, ...), custom_call_target="tpu_custom_call" | custom-call | tf_op jit(solution)/shard_map/gather_rows/pallas_call | solution.py:1012
  79.4 0.9 reshape.154
  81.0 0.6 reshape.156.start_ref
  81.6 1.0 multiply_sine_fusion
  82.6 0.8 negate_select_fusion.sin_ref
  83.4 0.8 pad_maximum_fusion.cos_ref
  84.3 2.5 reshape.158.routes_all
  86.7 119.3 %attend.1 = (bf16[512,2048]{1,0:T(8,128)(2,1)}, f32[512,1]{1,0:T(8,128)}, f32[512,1024]{1,0:T(8,128)}, f32[512,128]{1,0:T(8,128)}, bf16[512,1024]{1,0:T(8,128)(2...) custom-call(f32[1,2048]{1,0:T(1,128)} %bitcast.67, ...), custom_call_target="tpu_custom_call" | custom-call | tf_op jit(solution)/shard_map/attend/pallas_call | solution.py:2304
  206.0 6.2 convolution_convert_fusion.attn_part
  212.2 212.1 %experts.1 = (f32[512,512]{1,0:T(8,128)}, f32[512,1]{1,0:T(8,128)}, bf16[512,512]{1,0:T(8,128)(2,1)}, bf16[4096,2048]{1,0:T(8,128)(2,1)}, bf16[4096,2048]{1,0:T(...) custom-call(bf16[512,512]{1,0:T(8,128)(2,1)} %get-tuple-element.58.t, ...), custom_call_target="tpu_custom_call" | custom-call | tf_op jit(solution)/shard_map/experts/pallas_call | solution.py:1821
  424.4 167.6 %attend_back.1 = (f32[512,512]{1,0:T(8,128)}, bf16[512,1280]{1,0:T(8,128)(2,1)}, f32[2,128]{1,0:T(2,128)}, f32[512,512]{1,0:T(8,128)}, f32[256,1024]{1,0:T(8,128)}, /*index=5*/f32[32,24,128]{2,1,0:T(8,128)}) custom-call(f32[512,128]{1,0:T(8,128)} %get-tuple-element.69.k_pre, f32[1,128]{1,0:T(1,128)} %bitcast.78, f32[1,128]{1,0:T(1,128)} %bitcast.76, ...), custom_call_target="tpu_custom_call" | custom-call | tf_op jit(solution)/shard_map/attend_back/pallas_call | solution.py:2873
  592.0 2.2 add_convert_fusion.block_ref
  594.2 97.4 %tail.1 = (f32[256,1024]{1,0:T(8,128)}, f32[256,128]{1,0:T(8,128)}, f32[256,128]{1,0:T(8,128)}, bf16[512,512]{1,0:T(8,128)(2,1)}, bf16[512,512]{1,0:T(8,128)(2,1...) custom-call(bf16[512,512]{1,0:T(8,128)(2,1)} %get-tuple-element.58.t, ...), custom_call_target="tpu_custom_call" | custom-call | tf_op jit(solution)/shard_map/tail/pallas_call | solution.py:3245
  691.7 1.3 slice_bitcast_fusion
  693.0 0.6 slice.36
  693.8 0.8 copy.45
  694.6 2.4 copy.56
  697.0 1.9 copy.57
  698.8 0.6 copy.58
  699.5 1.0 copy.59
  700.4 0.7 copy.60
  701.1 0.7 copy.61
  701.7 1.0 copy.62
  702.7 3.2 copy.63
  705.9 3.2 copy.64
  709.1 0.9 slice-done
  710.0 0.8 slice-done.1
  710.8 2.7 copy.65
  (43 shorter events, 1.1 us)
Async XLA Ops:
  424.4 167.7 %copy-start.1 = (f32[512,512]{1,0:T(8,128)S(1)}, f32[512,512]{1,0:T(8,128)}, u32[]{:S(2)}) copy-start(f32[512,512]{1,0:T(8,128)} %get-tuple-element.68.middle_all) | copy-start | bytes 3145732
  594.2 98.8 %copy-start.4 = (f32[32,24,128]{2,1,0:T(8,128)S(1)}, f32[32,24,128]{2,1,0:T(8,128)}, u32[]{:S(2)}) copy-start(f32[32,24,128]{2,1,0:T(8,128)} %get-tuple-element.98) | copy-start | bytes 1179652
  691.6 7.2 %copy-start.7 = (f32[4,4,128]{2,1,0:T(4,128)S(1)}, f32[4,4,128]{2,1,0:T(4,128)}, u32[]{:S(2)}) copy-start(f32[4,4,128]{2,1,0:T(4,128)} %get-tuple-element.92) | copy-start | bytes 24580
  691.6 7.8 %copy-start.3 = (f32[256,1024]{1,0:T(8,128)S(1)}, f32[256,1024]{1,0:T(8,128)}, u32[]{:S(2)}) copy-start(f32[256,1024]{1,0:T(8,128)} %get-tuple-element.127) | copy-start | bytes 3145732
  691.6 8.8 %copy-start.6 = (f32[256,128]{1,0:T(8,128)S(1)}, f32[256,128]{1,0:T(8,128)}, u32[]{:S(2)}) copy-start(f32[256,128]{1,0:T(8,128)} %get-tuple-element.128) | copy-start | bytes 393220
  691.7 9.4 %copy-start.5 = (f32[256,128]{1,0:T(8,128)S(1)}, f32[256,128]{1,0:T(8,128)}, u32[]{:S(2)}) copy-start(f32[256,128]{1,0:T(8,128)} %get-tuple-element.129) | copy-start | bytes 393220
  691.7 10.1 %copy-start.2 = (f32[256,1024]{1,0:T(8,128)S(1)}, f32[256,1024]{1,0:T(8,128)}, u32[]{:S(2)}) copy-start(f32[256,1024]{1,0:T(8,128)} %get-tuple-element.130) | copy-start | bytes 3145732
  693.7 9.0 %copy-start = (f32[2048,768]{1,0:T(8,128)S(1)}, f32[2048,768]{1,0:T(8,128)}, u32[]{:S(2)}) copy-start(f32[2048,768]{1,0:T(8,128)} %get-tuple-element.99) | copy-start | bytes 18874372
  699.4 6.5 slice-start.2
  702.7 3.2 slice-start.3
  702.7 7.3 %slice-start = ((s8[6291456]{0:T(1024)(128)(4,1)}), s8[4194304]{0:T(1024)(128)(4,1)S(1)}, s32[]{:S(2)}) async-start(s8[6291456]{0:T(1024)(128)(4,1)} %bitcast.48), calls=%async_computation | async-start | bytes 8388608
  705.9 4.8 slice-start.1

commit v8 on v7

--- a/solution.py
+++ b/solution.py
@@ -1650,6 +1650,7 @@
             width // cols,
             middle_part,
             (jnp.zeros(slot_gate.shape, f32), jnp.zeros(gate_pre.shape, f32)),
+            unroll=2,
         )
         save_out(j).start()
 
@@ -3125,9 +3126,9 @@
             for copy in stores(n):
                 copy.wait()
 
-        o_gate[...] = dot_first(x_panel[...], gp_ref[...])
-        o_up[...] = dot_first(x_panel[...], up_ref[...])
-        o_down[...] = dot_first(g_panel[...], hid_ref[...]).T
+        o_gate[...] = dot_first(x_panel[...], gp_ref[...]).astype(low)
+        o_up[...] = dot_first(x_panel[...], up_ref[...]).astype(low)
+        o_down[...] = dot_first(g_panel[...], hid_ref[...]).T.astype(low)
         for copy in stores(n):
             copy.start()
 
@@ -3250,15 +3251,15 @@
             shape((w_shape[0], query_width), f32), shape((w_shape[0], kv_width), f32),
             shape((w_shape[0], kv_width), f32), shape((rows, cols), low), shape((rows, cols), low),
             shape((4, cols // 128, 128), f32), shape((2, 128), f32),
-            shape((features, hidden_width), f32), shape((features, hidden_width), f32),
-            shape((hidden_width, features), f32),
+            shape((features, hidden_width), low), shape((features, hidden_width), low),
+            shape((hidden_width, features), low),
         ],
         scratch_shapes=[vm(normed_low.shape, low), vm(pre_grad.shape, low), vm((rows, cols), f32),
                         vm(wq_all.shape, low), vm(wk_all.shape, low), vm(wv_all.shape, low),
                         vm((rows, 4 * cols), low), dma((6,)), vm(w_shape, f32)] + [vm((pairs, hidden_width), low)] * 3 + [
             vm((pairs, panel), low), vm((pairs, panel), low),
-            vm((panel, hidden_width), f32), vm((panel, hidden_width), f32),
-            vm((hidden_width, panel), f32), dma((5,)), dma((3,)),
+            vm((panel, hidden_width), low), vm((panel, hidden_width), low),
+            vm((hidden_width, panel), low), dma((5,)), dma((3,)),
             vm((devices, 8, 128), f32), vm((rows, cols), f32), vm((rows, cols), low),
             dma((2,)), dma((2,)), dma((2,)), dma((devices,)), dma((devices,)),
         ] + ReduceRows.scratch(nz, w_shape[0] // 2, w_shape[1], low) * 2 + ReduceCols.scratch(rows, cols, low)
@@ -3515,9 +3516,9 @@
         head_gains[1],
         summed[0, :, per * gain_rows : (per + 1) * gain_rows].reshape(-1),
         router_grad,
-        expert_grads[0][None],
-        expert_grads[1][None],
-        expert_grads[2][None],
+        expert_grads[0][None].astype(f32),
+        expert_grads[1][None].astype(f32),
+        expert_grads[2][None].astype(f32),
     )
 
 

time: 718 us -> 708 us (0.986); the launches traced: 714 us -> 696 us
  Pallas kernels: 671 us -> 655 us
  local copies, waits for them, and re-layouts: 30 us -> 16.6 us
  other arithmetic: 5.52 us -> 17.5 us
    unnamed x39 -> x34, local copies, waits for them, and re-layouts: 23.1 us -> 9.7 us
    convert_element_type x0 -> x3, other arithmetic: none -> 12 us  [the longest x1 5.23 us: gathered_body(): expert_grads[0][None].astype(f32)]
    pallas_call x1, Pallas kernels: 168 us -> 157 us  [attend_back(): pl.pallas_call(functools.partial(attend_back_kernel, nz), in_specs=[vmem]...]
where the time goes in v8:
time: 708 us; the launch traced here: 696 us
  Pallas kernels  655 us (93%)
  other arithmetic  17.5 us (2%)
  local copies, waits for them, and re-layouts  16.6 us (2%)
    pallas_call x1, Pallas kernels, run_experts(): pl.pallas_call(functools.partial(expert_kernel, nz, slots, block_rows), i...  209 us
    pallas_call x1, Pallas kernels, attend_back(): pl.pallas_call(functools.partial(attend_back_kernel, nz), in_specs=[vmem]...  157 us
    pallas_call x1, Pallas kernels, attend(): pl.pallas_call(functools.partial(attend_kernel, nz), in_specs=[vmem] * 8...  119 us
    pallas_call x1, Pallas kernels, tail(): pl.pallas_call(functools.partial(tail_kernel, nz), in_specs=[vmem] * 5 +...  94.2 us
    pallas_call x1, Pallas kernels, gather_rows(): pl.pallas_call(functools.partial(gather_rows_kernel, nz, count, columns,...  74.4 us

profile of v8, /device:TPU:0, one launch (start us, length us, event | category | flops | bytes accessed | tf_op | source)
XLA Modules:
  0.0 695.9 jit_solution(9193735559135342719)
XLA Ops:
  0.8 0.7 copy.43
  1.4 0.8 copy.39
  2.5 0.6 pad_bitcast_fusion.refs_0_
  3.1 1.9 copy.40.router_ref.router_all
  5.0 74.4 %gather_rows.1 = (s32[320,128]{1,0:T(8,128)}, bf16[2048,1024]{1,0:T(8,128)(2,1)}, bf16[2048,128]{1,0:T(8,128)(2,1)}, bf16[2048,128]{1,0:T(8,128)(2,1)}, bf16[512...) custom-call(s32[40,128]{1,0:T(8,128)} %pad_bitcast_fusion.refs_0_, bf16[256,1024]{1,0:T(8,128)(2,1)} %refs_1_.1, ...), custom_call_target="tpu_custom_call" | custom-call | tf_op jit(solution)/shard_map/gather_rows/pallas_call | solution.py:1012
  79.4 0.9 reshape.160
  80.4 0.2 convert_reduce_fusion
  80.6 0.2 reduce_window_sum.11
  81.0 0.6 reshape.162.start_ref
  81.6 1.0 multiply_sine_fusion
  82.6 0.8 negate_select_fusion.sin_ref
  83.4 0.8 pad_maximum_fusion.cos_ref
  84.3 2.5 reshape.164.routes_all
  86.7 119.3 %attend.1 = (bf16[512,2048]{1,0:T(8,128)(2,1)}, f32[512,1]{1,0:T(8,128)}, f32[512,1024]{1,0:T(8,128)}, f32[512,128]{1,0:T(8,128)}, bf16[512,1024]{1,0:T(8,128)(2...) custom-call(f32[1,2048]{1,0:T(1,128)} %bitcast.66, ...), custom_call_target="tpu_custom_call" | custom-call | tf_op jit(solution)/shard_map/attend/pallas_call | solution.py:2305
  206.1 6.2 convolution_convert_fusion.attn_part
  212.3 209.2 %experts.1 = (f32[512,512]{1,0:T(8,128)}, f32[512,1]{1,0:T(8,128)}, bf16[512,512]{1,0:T(8,128)(2,1)}, bf16[4096,2048]{1,0:T(8,128)(2,1)}, bf16[4096,2048]{1,0:T(...) custom-call(bf16[512,512]{1,0:T(8,128)(2,1)} %get-tuple-element.58.t, ...), custom_call_target="tpu_custom_call" | custom-call | tf_op jit(solution)/shard_map/experts/pallas_call | solution.py:1822
  421.5 157.5 %attend_back.1 = (f32[512,512]{1,0:T(8,128)}, bf16[512,1280]{1,0:T(8,128)(2,1)}, f32[2,128]{1,0:T(2,128)}, f32[512,512]{1,0:T(8,128)}, f32[256,1024]{1,0:T(8,128)}, /*index=5*/f32[32,24,128]{2,1,0:T(8,128)}) custom-call(f32[512,128]{1,0:T(8,128)} %get-tuple-element.69.k_pre, f32[1,128]{1,0:T(1,128)} %bitcast.77, f32[1,128]{1,0:T(1,128)} %bitcast.75, ...), custom_call_target="tpu_custom_call" | custom-call | tf_op jit(solution)/shard_map/attend_back/pallas_call | solution.py:2874
  579.0 2.2 add_convert_fusion.block_ref
  581.2 94.2 %tail.1 = (f32[256,1024]{1,0:T(8,128)}, f32[256,128]{1,0:T(8,128)}, f32[256,128]{1,0:T(8,128)}, bf16[512,512]{1,0:T(8,128)(2,1)}, bf16[512,512]{1,0:T(8,128)(2,1...) custom-call(bf16[512,512]{1,0:T(8,128)(2,1)} %get-tuple-element.58.t, ...), custom_call_target="tpu_custom_call" | custom-call | tf_op jit(solution)/shard_map/tail/pallas_call | solution.py:3246
  675.4 1.3 slice_bitcast_fusion
  676.6 0.6 slice.36
  677.5 0.8 copy.45
  678.3 5.2 bitcast_convert_fusion.2
  683.5 3.2 bitcast_convert_fusion.1
  686.7 3.6 bitcast_convert_fusion
  690.3 0.8 copy.53
  691.1 0.8 copy.54
  691.9 0.6 copy.55
  692.5 1.0 copy.56
  693.4 0.7 copy.57
  694.1 0.7 copy.58
  694.8 1.0 copy.59
  (39 shorter events, 0.7 us)
Async XLA Ops:
  421.5 157.5 %copy-start = (f32[512,512]{1,0:T(8,128)S(1)}, f32[512,512]{1,0:T(8,128)}, u32[]{:S(2)}) copy-start(f32[512,512]{1,0:T(8,128)} %get-tuple-element.68.middle_all) | copy-start | bytes 3145732
  581.2 95.5 %copy-start.7 = (f32[32,24,128]{2,1,0:T(8,128)S(1)}, f32[32,24,128]{2,1,0:T(8,128)}, u32[]{:S(2)}) copy-start(f32[32,24,128]{2,1,0:T(8,128)} %get-tuple-element.98) | copy-start | bytes 1179652
  678.3 5.2 copy-start.2
  683.5 3.2 copy-start.1
  686.7 3.6 copy-start.6
  686.7 4.4 copy-start.5
  686.7 5.2 copy-start.10
  686.7 5.8 copy-start.4
  690.3 3.2 copy-start.9
  690.3 3.8 copy-start.8
  690.3 4.5 copy-start.3
